TPU v7x, 256 devices: a whole 4x4x8 slice. The times are simulated.
256 devices in a mesh: row: 16 (over x, y_hi, core), col: 16 (over z, y_lo).
Axes of the slice: x: 4, y: 4 (y_hi: 2, y_lo: 2; y = y_hi * 2 + y_lo), z: 8, core: 2. Of those that a mesh axis runs over, the one named last changes fastest.
Arguments:
- activations: bfloat16 [1024, 8192], P(None, 'row'), may hold values from -10 to 10
- cotangents: bfloat16 [1024, 8192], P(None, 'row'), may hold values from -10 to 10
- act_factor: bfloat16 [8192, 8192], P('row', 'col'), may hold values from -0.5 to 1.5
- grad_factor: bfloat16 [8192, 8192], P('row', 'col'), may hold values from -0.5 to 1.5
Outputs:
- act_updated: bfloat16 [8192, 8192], P('row', 'col')
- grad_updated: bfloat16 [8192, 8192], P('row', 'col')
All inputs are finite; a program needn't handle non-finite values.
Results may differ from a plain program's by a relative error of at most 0.0057.
Values may be sent and summed in bfloat16 or wider, within the bound.
No kernel may reach another device: no remote copies, remote signals or barrier semaphores. Data moves between devices by JAX's collectives and lax.ppermute only.
A program may use at most 64 MiB of HBM per device.

v0:
```python
import jax
import jax.numpy as jnp
from jax import lax
from jax.sharding import PartitionSpec as P

D = 8192
TOKENS = 1024


keep_scale = 1.45
gram_scale = 0.5


def times_transposed(factor_block, projected):
    return lax.dot_general(
        factor_block, projected, (((1,), (1,)), ((), ())), preferred_element_type=jnp.float32
    )


def local(activations, cotangents, act_factor, grad_factor):
    width = act_factor.shape[1]
    own_rows = lax.psum_scatter(
        jnp.concatenate(
            [
                jnp.dot(activations, act_factor, preferred_element_type=jnp.float32),
                jnp.dot(cotangents, grad_factor, preferred_element_type=jnp.float32),
            ],
            axis=1,
        ),
        "row",
        scatter_dimension=0,
        tiled=True,
    ).astype(jnp.bfloat16)
    projected = lax.all_gather(own_rows, "row", axis=0, tiled=True)
    squares = jnp.square(own_rows.astype(jnp.float32))
    act_total, grad_total = lax.psum(
        (jnp.sum(squares[:, :width]), jnp.sum(squares[:, width:])), ("row", "col")
    )
    act_mean = act_total / (TOKENS * D)
    grad_mean = grad_total / (TOKENS * D)
    act_proj = projected[:, :width]
    grad_proj = projected[:, width:]
    act_image, grad_image = lax.psum(
        (times_transposed(act_factor, act_proj), times_transposed(grad_factor, grad_proj)), "col"
    )
    act_image = act_image.astype(jnp.bfloat16)
    grad_image = grad_image.astype(jnp.bfloat16)
    act_change = jnp.dot(act_image, act_proj, preferred_element_type=jnp.float32)
    grad_change = jnp.dot(grad_image, grad_proj, preferred_element_type=jnp.float32)
    act_updated = (
        keep_scale * act_factor.astype(jnp.float32) - gram_scale * grad_mean / TOKENS * act_change
    ).astype(jnp.bfloat16)
    grad_updated = (
        keep_scale * grad_factor.astype(jnp.float32) - gram_scale * act_mean / TOKENS * grad_change
    ).astype(jnp.bfloat16)
    return (act_updated, grad_updated)


def solution(mesh):
    return jax.shard_map(
        local,
        mesh=mesh,
        in_specs=(P(None, "row"), P(None, "row"), P("row", "col"), P("row", "col")),
        out_specs=(P("row", "col"), P("row", "col")),
        check_vma=False,
    )
```

profile of v0, /device:TPU:8, one launch (start us, length us, event | category | flops | bytes accessed | tf_op | source)
XLA Modules:
  0.0 385.2 jit_solution(4529226681538673235)
XLA Ops:
  7.2 0.0 copy-start
  7.2 0.0 copy-start.3
  7.2 0.0 copy-start.5
  7.2 0.0 reduce-scatter.4.cloned.1.call-start
  7.2 1.1 copy-done
  8.4 1.8 fusion.10
  10.2 0.8 fusion.11
  11.0 2.5 pad_maximum_fusion
  13.5 5.3 %copy.7 = f32[1024,1024]{1,0:T(8,128)} copy(f32[1024,1024]{0,1:T(8,128)} %pad_maximum_fusion) | data formatting | bytes 8388608
  18.8 0.0 reduce-scatter.4.cloned.1.call-update
  18.8 0.0 all-gather.2.cloned.1.call-start
  18.9 90.2 %reduce-scatter.4.cloned.1.call-done = f32[64,1024]{1,0:T(8,128)} async-done(((f32[1024,1024]{1,0:T(8,128)}), f32[64,1024]{1,0:T(8,128)}) %reduce-scatter.4.cloned.1.call-update) | async-done | bytes 262160
  109.1 1.1 copy.8
  110.3 0.8 copy.6
  111.0 0.0 all-gather.2.cloned.1.call-update
  111.1 0.7 slice_reduce_fusion
  111.8 74.6 %all-reduce = (f32[]{:T(128)}, f32[]{:T(128)}) all-reduce(f32[]{:T(128)} %get-tuple-element.3, f32[]{:T(128)} %get-tuple-element.2), channel_id=1, replica_groups=mesh['row'=16,'col'=16] {'row','col'}, use_global_device_ids=true, to_apply=%region_2.0 | all-reduce | flops 2 | bytes 16 | tf_op jit(solution)/shard_map/psum | solution.py:36
  187.6 0.0 all-gather.2.cloned.1.call-done
  187.6 2.2 convolution_bitcast_fusion
  189.9 3.1 convolution_bitcast_fusion.1
  193.0 180.5 %all-reduce.3 = (bf16[512,1024]{0,1:T(8,128)(2,1)}, bf16[512,1024]{0,1:T(8,128)(2,1)}) all-reduce(f32[512,1024]{0,1:T(8,128)} %convolution_bitcast_fusion.1, f32[512,1024]{0,1:T(8,128)S(1)} %convolution_bitcast_fusion), channel_id=1, replica_groups=mesh['row'=16,'col'=16] {'col'}, use_global_device_ids=true, to_apply=%region_3.0 | all-reduce | flops 1048576 | bytes 6291456 | tf_op jit(solution)/shard_map/psum | solution.py:43
  373.4 3.4 fusion.2
  376.8 0.0 copy-done.2
  376.8 1.5 fusion.3
  (10 shorter events, 0.1 us)
Async XLA Ops:
  7.2 1.2 copy-start
  7.2 3.0 copy-start.3
  7.2 3.0 copy-start.5
  7.2 101.9 %reduce-scatter.4.cloned.1.call-start = ((), (), s32[]{:S(2)}) async-start(), calls=%async_computation.2 | async-start | bytes 4456448
  18.8 168.8 %all-gather.2.cloned.1.call-start = ((), (), s32[]{:S(2)}) async-start(), calls=%async_computation.1 | async-start | bytes 2228224 | tf_op jit(solution)/shard_map/all_gather | solution.py:34
  187.6 2.3 copy-start.1
  373.4 3.4 copy-start.2
  373.4 3.4 copy-start.4
  373.4 3.4 copy-start.6
Sparse Core Ops, SparseCore 0:
  19.0 90.1 reduce-scatter.3
  112.8 52.2 all-gather.1
where the time goes:
time: 388 us; the launch traced here: 385 us
  blocking collectives  255 us (66%)
  waiting for transfers between devices  90.3 us (23%)
  between operations  15.3 us (4%)
  matrix products  12.8 us (3%)
  local copies, waits for them, and re-layouts  8.43 us (2%)
    psum x1, blocking collectives, local(): lax.psum((times_transposed(act_factor, act_proj), times_transposed(grad_f...  180 us
    unnamed x3, waiting for transfers between devices  90.3 us
    psum x1, blocking collectives, local(): lax.psum((jnp.sum(squares[:, :width]), jnp.sum(squares[:, width:])), ('ro...  74.6 us
  transfers between devices with their start and end apart: 2, of which 1 were waited for; matrix products, arithmetic and copies ran while one was open for 0% of the time, Pallas kernels for 0%

commit v1 on v0

v1 whole, which is shorter than its diff:
```python
import jax
import jax.numpy as jnp
from jax import lax
from jax.sharding import Mesh, PartitionSpec as P

D = 8192
TOKENS = 1024
X, YH, CORE, Z, YL = 4, 2, 2, 8, 2
ROW = ("x", "yh", "core")
COL = ("z", "yl")

keep_scale = 1.45
gram_scale = 0.5

f32 = jnp.float32
bf16 = jnp.bfloat16


def dot(a, b):
    return jnp.dot(a, b, preferred_element_type=f32)


def dot_t(a, b):
    return lax.dot_general(a, b, (((1,), (1,)), ((), ())), preferred_element_type=f32)


def shift(a, axis, size, by=1):
    return lax.ppermute(a, axis, [(i, (i + by) % size) for i in range(size)])


def half(a, which):
    rows = a.shape[0] // 2
    return lax.dynamic_slice_in_dim(a, which * rows, rows, 0)


def reduce_direct(a, axes, n):
    parts = lax.all_to_all(a.astype(bf16).reshape(n, -1, a.shape[1]), axes, 0, 0, tiled=True)
    return jnp.sum(parts.astype(f32), axis=0).astype(bf16)


def gather_direct(a, axes, n):
    copies = jnp.broadcast_to(a[None], (n,) + a.shape)
    return lax.all_to_all(copies, axes, 0, 0, tiled=True).reshape(-1, a.shape[1])


def project(rows, factor):
    core = lax.axis_index("core")
    away = shift(dot(half(rows, 1 - core), factor).astype(bf16), "core", CORE)
    total = dot(half(rows, core), factor) + away.astype(f32)
    own = reduce_direct(total, ("x", "yh"), X * YH)
    mine = gather_direct(own, ("x", "yh"), X * YH)
    other = shift(mine, "core", CORE)
    return jnp.concatenate([mine, other], axis=0)


def image_of(factor, proj):
    yl = lax.axis_index("yl")
    away = shift(dot_t(half(factor, 1 - yl), proj).astype(bf16), "yl", YL)
    total = dot_t(half(factor, yl), proj) + away.astype(f32)
    own = reduce_direct(total, "z", Z)
    mine = gather_direct(own, "z", Z)
    other = shift(mine, "yl", YL)
    first = jnp.where(yl == 0, mine, other)
    second = jnp.where(yl == 0, other, mine)
    return jnp.concatenate([first, second], axis=0)


def col_sum(a):
    a = a + shift(a, "yl", YL)
    for by in (1, 2, 4):
        a = a + shift(a, "z", Z, by)
    return a


def local(activations, cotangents, act_factor, grad_factor):
    act_proj = project(activations, act_factor)
    grad_proj = project(cotangents, grad_factor)
    squares = jnp.stack(
        [jnp.sum(jnp.square(p.astype(f32))) for p in (act_proj, grad_proj)]
    )
    means = col_sum(jnp.broadcast_to(squares[:, None], (2, 128))) / (TOKENS * D)
    outs = []
    for factor, proj, mean in (
        (act_factor, act_proj, means[1, 0]),
        (grad_factor, grad_proj, means[0, 0]),
    ):
        change = dot(image_of(factor, proj), proj)
        outs.append(
            (keep_scale * factor.astype(f32) - gram_scale * mean / TOKENS * change).astype(bf16)
        )
    return tuple(outs)


def solution(mesh):
    fine = Mesh(mesh.devices.reshape(X, YH, CORE, Z, YL), ROW + COL)
    return jax.shard_map(
        local,
        mesh=fine,
        in_specs=(P(None, ROW), P(None, ROW), P(ROW, COL), P(ROW, COL)),
        out_specs=(P(ROW, COL), P(ROW, COL)),
        check_vma=False,
    )
```

time: 388 us -> 195 us (0.50)
  blocking collectives: 255 us -> 0 us
  starting transfers between devices: 0.08 us -> 52.6 us
  between operations: 15.3 us -> 2.12 us
  waiting for transfers between devices: 90.3 us -> 103 us
  matrix products: 12.8 us -> 21 us
  other arithmetic: 3.21 us -> 7.66 us
    psum x2 -> x0, blocking collectives: 255 us -> none  [the longest x1 180 us: local(): lax.psum((times_transposed(act_factor, act_proj), times_transposed(grad_f...]
    unnamed x3 -> x0, waiting for transfers between devices: 90.3 us -> none
    all_to_all x0 -> x8, waiting for transfers between devices: none -> 65.2 us  [the longest x4 35.2 us: reduce_direct(): lax.all_to_all(a.astype(bf16).reshape(n, -1, a.shape[1]), axes, 0, 0, til...]
    all_to_all x0 -> x8, starting transfers between devices: none -> 38.8 us  [the longest x4 24.9 us: reduce_direct(): lax.all_to_all(a.astype(bf16).reshape(n, -1, a.shape[1]), axes, 0, 0, til...]
    ppermute x0 -> x12, waiting for transfers between devices: none -> 37.8 us  [shift(): return lax.ppermute(a, axis, [(i, (i + by) % size) for i in range(size)])]
    ppermute x0 -> x12, starting transfers between devices: none -> 13.7 us  [shift(): return lax.ppermute(a, axis, [(i, (i + by) % size) for i in range(size)])]
    dot_general x6 -> x10, matrix products: 12.8 us -> 21 us  [the longest x6 12.4 us: dot(): return jnp.dot(a, b, preferred_element_type=f32)]
    unnamed x16, local copies, waits for them, and re-layouts: 7.64 us -> 1.24 us
  transfers between devices with their start and end apart: 2 -> 20, of which waited for: 1 -> 15; matrix products, arithmetic and copies ran while one was open for 0% -> 12% of each run, Pallas kernels for 0% -> 0%
where the time goes in v1:
time: 195 us; the launch traced here: 192 us
  waiting for transfers between devices  103 us (53%)
  starting transfers between devices  52.6 us (27%)
  matrix products  21 us (11%)
  other arithmetic  7.66 us (4%)
  local copies, waits for them, and re-layouts  5.22 us (3%)
  between operations  2.12 us (1%)
    ppermute x12, waiting for transfers between devices, shift(): return lax.ppermute(a, axis, [(i, (i + by) % size) for i in range(size)])  37.8 us
    all_to_all x4, waiting for transfers between devices, reduce_direct(): lax.all_to_all(a.astype(bf16).reshape(n, -1, a.shape[1]), axes, 0, 0, til...  35.2 us
    all_to_all x4, waiting for transfers between devices, gather_direct(): lax.all_to_all(copies, axes, 0, 0, tiled=True).reshape(-1, a.shape[1])  30 us
    all_to_all x4, starting transfers between devices, reduce_direct(): lax.all_to_all(a.astype(bf16).reshape(n, -1, a.shape[1]), axes, 0, 0, til...  24.9 us
    all_to_all x4, starting transfers between devices, gather_direct(): lax.all_to_all(copies, axes, 0, 0, tiled=True).reshape(-1, a.shape[1])  14 us
    ppermute x12, starting transfers between devices, shift(): return lax.ppermute(a, axis, [(i, (i + by) % size) for i in range(size)])  13.7 us
    dot_general x6, matrix products, dot(): return jnp.dot(a, b, preferred_element_type=f32)  12.4 us
    dot_general x4, matrix products, dot_t(): lax.dot_general(a, b, (((1,), (1,)), ((), ())), preferred_element_type=f32)  8.59 us
  transfers between devices with their start and end apart: 20, of which 15 were waited for; matrix products, arithmetic and copies ran while one was open for 12% of the time, Pallas kernels for 0%

profile of v1, /device:TPU:8, one launch (start us, length us, event | category | flops | bytes accessed | tf_op | source)
XLA Modules:
  0.0 191.5 jit_solution(11089702678364961902)
XLA Ops:
  6.6 6.2 %all-to-all-start.2 = ((bf16[8,64,512]{2,1,0:T(8,128)(2,1)}), bf16[8,64,512]{2,1,0:T(8,128)(2,1)S(1)}, u32[]{:S(2)}, u32[]{:S(2)}) async-start(bf16[8,64,512]{2,1,0:T(8,128)(2,1)} %bitcast.3), calls=%async_computation.2 | async-start | bytes 1048576 | tf_op jit(solution)/shard_map/all_to_all | solution.py:37
  15.0 8.9 %all-to-all-done.2 = bf16[8,64,512]{2,1,0:T(8,128)(2,1)S(1)} async-done(((bf16[8,64,512]{2,1,0:T(8,128)(2,1)}), bf16[8,64,512]{2,1,0:T(8,128)(2,1)S(1)}, u32[]{:S(2)}, u32[]{:S(2)}) %all-to-all-start.2) | async-done | bytes 524320 | tf_op jit(solution)/shard_map/all_to_all | solution.py:37
  24.8 3.5 %all-to-all-start.3 = ((bf16[8,64,512]{2,1,0:T(8,128)(2,1)}), bf16[8,64,512]{2,1,0:T(8,128)(2,1)S(1)}, u32[]{:S(2)}, u32[]{:S(2)}) async-start(bf16[8,64,512]{2,1,0:T(8,128)(2,1)} %broadcast_in_dim.11), calls=%async_computation.3 | async-start | bytes 1048576 | tf_op jit(solution)/shard_map/all_to_all | solution.py:43
  30.6 8.4 %all-to-all-done.3 = bf16[8,64,512]{2,1,0:T(8,128)(2,1)S(1)} async-done(((bf16[8,64,512]{2,1,0:T(8,128)(2,1)}), bf16[8,64,512]{2,1,0:T(8,128)(2,1)S(1)}, u32[]{:S(2)}, u32[]{:S(2)}) %all-to-all-start.3) | async-done | bytes 524320 | tf_op jit(solution)/shard_map/all_to_all | solution.py:43
  39.0 3.5 %all-to-all-start = ((bf16[8,64,512]{2,1,0:T(8,128)(2,1)}), bf16[8,64,512]{2,1,0:T(8,128)(2,1)S(1)}, u32[]{:S(2)}, u32[]{:S(2)}) async-start(bf16[8,64,512]{2,1,0:T(8,128)(2,1)} %bitcast), calls=%async_computation | async-start | bytes 1048576 | tf_op jit(solution)/shard_map/all_to_all | solution.py:37
  42.6 10.3 %all-to-all-done = bf16[8,64,512]{2,1,0:T(8,128)(2,1)S(1)} async-done(((bf16[8,64,512]{2,1,0:T(8,128)(2,1)}), bf16[8,64,512]{2,1,0:T(8,128)(2,1)S(1)}, u32[]{:S(2)}, u32[]{:S(2)}) %all-to-all-start) | async-done | bytes 524320 | tf_op jit(solution)/shard_map/all_to_all | solution.py:37
  53.8 3.5 %all-to-all-start.1 = ((bf16[8,64,512]{2,1,0:T(8,128)(2,1)}), bf16[8,64,512]{2,1,0:T(8,128)(2,1)S(1)}, u32[]{:S(2)}, u32[]{:S(2)}) async-start(bf16[8,64,512]{2,1,0:T(8,128)(2,1)} %broadcast_in_dim.10), calls=%async_computation.1 | async-start | bytes 1048576 | tf_op jit(solution)/shard_map/all_to_all | solution.py:43
  61.0 6.8 %all-to-all-done.1 = bf16[8,64,512]{2,1,0:T(8,128)(2,1)S(1)} async-done(((bf16[8,64,512]{2,1,0:T(8,128)(2,1)}), bf16[8,64,512]{2,1,0:T(8,128)(2,1)S(1)}, u32[]{:S(2)}, u32[]{:S(2)}) %all-to-all-start.1) | async-done | bytes 524320 | tf_op jit(solution)/shard_map/all_to_all | solution.py:43
  67.7 8.4 %collective-permute-done.10 = bf16[256,1024]{1,0:T(8,128)(2,1)} collective-permute-done((bf16[256,1024]{1,0:T(8,128)(2,1)}, bf16[256,1024]{1,0:T(8,128)(2,1)}, u32[]{:S(2)}, u32[]{:S(2)}) %collective-permute-start.10) | collective-permute-done | bytes 524320 | tf_op jit(solution)/shard_map/ppermute | solution.py:28
  76.2 2.5 %fusion.3 = bf16[256,1024]{1,0:T(8,128)(2,1)} fusion(bf16[256,1024]{1,0:T(8,128)(2,1)} %collective-permute-done.10, bf16[512,512]{1,0:T(8,128)(2,1)S(1)} %copy-done.1, s32[]{:T(128)S(6)} %select_n.39, bf16[512,512]{1,0:T(8,128)(2,1)} %collective-permute-done.3, bf16[512,512]{1,0:T(8,128)(2,1)S(1)} %bitcast.24), kind=kOutput, calls=%fused_computation.13 | convolution fusion | flops 271319040 | bytes 2359300 | tf_op jit(solution)/shard_map/dot_general | solution.py:24
  78.7 8.5 %all-to-all-start.6 = ((bf16[8,32,1024]{2,1,0:T(8,128)(2,1)}), bf16[8,32,1024]{2,1,0:T(8,128)(2,1)S(1)}, u32[]{:S(2)}, u32[]{:S(2)}) async-start(bf16[8,32,1024]{2,1,0:T(8,128)(2,1)} %bitcast.32), calls=%async_computation.6 | async-start | bytes 1048576 | tf_op jit(solution)/shard_map/all_to_all | solution.py:37
  89.4 12.7 %collective-permute-done.8 = bf16[256,1024]{1,0:T(8,128)(2,1)S(1)} collective-permute-done((bf16[256,1024]{1,0:T(8,128)(2,1)S(1)}, bf16[256,1024]{1,0:T(8,128)(2,1)S(1)}, u32[]{:S(2)}, u32[]{:S(2)}) %collective-permute-start.8) | collective-permute-done | bytes 524320 | tf_op jit(solution)/shard_map/ppermute | solution.py:28
  104.6 6.7 %all-to-all-start.4 = ((bf16[8,32,1024]{2,1,0:T(8,128)(2,1)}), bf16[8,32,1024]{2,1,0:T(8,128)(2,1)S(1)}, u32[]{:S(2)}, u32[]{:S(2)}) async-start(bf16[8,32,1024]{2,1,0:T(8,128)(2,1)} %bitcast.33), calls=%async_computation.4 | async-start | bytes 1048576 | tf_op jit(solution)/shard_map/all_to_all | solution.py:37
  111.4 15.9 %all-to-all-done.4 = bf16[8,32,1024]{2,1,0:T(8,128)(2,1)S(1)} async-done(((bf16[8,32,1024]{2,1,0:T(8,128)(2,1)}), bf16[8,32,1024]{2,1,0:T(8,128)(2,1)S(1)}, u32[]{:S(2)}, u32[]{:S(2)}) %all-to-all-start.4) | async-done | bytes 524320 | tf_op jit(solution)/shard_map/all_to_all | solution.py:37
  128.1 3.5 %all-to-all-start.7 = ((bf16[8,32,1024]{2,1,0:T(8,128)(2,1)}), bf16[8,32,1024]{2,1,0:T(8,128)(2,1)S(1)}, u32[]{:S(2)}, u32[]{:S(2)}) async-start(bf16[8,32,1024]{2,1,0:T(8,128)(2,1)} %broadcast_in_dim.14), calls=%async_computation.7 | async-start | bytes 1048576 | tf_op jit(solution)/shard_map/all_to_all | solution.py:43
  131.7 14.8 %all-to-all-done.7 = bf16[8,32,1024]{2,1,0:T(8,128)(2,1)S(1)} async-done(((bf16[8,32,1024]{2,1,0:T(8,128)(2,1)}), bf16[8,32,1024]{2,1,0:T(8,128)(2,1)S(1)}, u32[]{:S(2)}, u32[]{:S(2)}) %all-to-all-start.7) | async-done | bytes 524320 | tf_op jit(solution)/shard_map/all_to_all | solution.py:43
  147.4 3.5 %all-to-all-start.5 = ((bf16[8,32,1024]{2,1,0:T(8,128)(2,1)}), bf16[8,32,1024]{2,1,0:T(8,128)(2,1)S(1)}, u32[]{:S(2)}, u32[]{:S(2)}) async-start(bf16[8,32,1024]{2,1,0:T(8,128)(2,1)} %broadcast_in_dim.13), calls=%async_computation.5 | async-start | bytes 1048576 | tf_op jit(solution)/shard_map/all_to_all | solution.py:43
  150.9 2.4 %multiply_reduce_fusion = f32[]{:T(128)} fusion(bf16[512,512]{1,0:T(8,128)(2,1)} %collective-permute-done.3, bf16[512,512]{1,0:T(8,128)(2,1)} %bitcast.25), kind=kLoop, calls=%fused_computation | loop fusion | flops 3145727 | bytes 1048580 | tf_op jit(solution)/shard_map/reduce_sum | solution.py:79
  157.6 2.9 %collective-permute-done.4 = f32[2,128]{1,0:T(2,128)S(1)} collective-permute-done((f32[2,128]{1,0:T(2,128)S(1)}, f32[2,128]{1,0:T(2,128)S(1)}, u32[]{:S(2)}, u32[]{:S(2)}) %collective-permute-start.4) | collective-permute-done | bytes 1056 | tf_op jit(solution)/shard_map/ppermute | solution.py:28
  167.1 4.1 %collective-permute-done.6 = f32[2,128]{1,0:T(2,128)S(1)} collective-permute-done((f32[2,128]{1,0:T(2,128)S(1)}, f32[2,128]{1,0:T(2,128)S(1)}, u32[]{:S(2)}, u32[]{:S(2)}) %collective-permute-start.6) | collective-permute-done | bytes 1056 | tf_op jit(solution)/shard_map/ppermute | solution.py:28
  171.2 5.9 %collective-permute-start.7 = (f32[2,128]{1,0:T(2,128)S(1)}, f32[2,128]{1,0:T(2,128)S(1)}, u32[]{:S(2)}, u32[]{:S(2)}) collective-permute-start(f32[2,128]{1,0:T(2,128)S(1)} %add.46), channel_id=1, source_target_pairs={{0,8},{2,10},{4,12},{6,14},{8,0},{10,2},{12,4},{14,6},{1,9},{3,11}... | collective-permute-start | bytes 3080 | tf_op jit(solution)/shard_map/ppermute | solution.py:28
  181.6 4.7 %collective-permute-done.9 = bf16[256,1024]{1,0:T(8,128)(2,1)S(1)} collective-permute-done((bf16[256,1024]{1,0:T(8,128)(2,1)S(1)}, bf16[256,1024]{1,0:T(8,128)(2,1)S(1)}, u32[]{:S(2)}, u32[]{:S(2)}) %collective-permute-start.9) | collective-permute-done | bytes 524320 | tf_op jit(solution)/shard_map/ppermute | solution.py:28
  186.4 2.6 %fusion.5 = bf16[512,512]{1,0:T(8,128)(2,1)} fusion(bf16[256,1024]{1,0:T(8,128)(2,1)S(1)} %get-tuple-element.3, bf16[256,1024]{1,0:T(8,128)(2,1)S(1)} %get-tuple-element.2, bf16[512,512]{1,0:T(8,128)(2,1)S(1)} %copy-done.1, f32[]{:T(128)} %bitcast.9, bf16[512,512]{1,0:T(8,128)(2,1)} %collective-permute-done.3, bf16[512,512]{1,0:T(8,128)(2,1)S(1)} %bitcast.26), kind=kOutput, calls=%fused_computation.15 | convolution fusion | flops 542375936 | bytes 3145732 | tf_op jit(solution)/shard_map/dot_general | solution.py:20
  189.0 2.5 %fusion.4 = bf16[512,512]{1,0:T(8,128)(2,1)} fusion(bf16[256,1024]{1,0:T(8,128)(2,1)S(1)} %get-tuple-element.5, bf16[256,1024]{1,0:T(8,128)(2,1)S(1)} %get-tuple-element.4, bf16[512,512]{1,0:T(8,128)(2,1)S(1)} %copy-done.2, f32[]{:T(128)} %bitcast.6, bf16[512,512]{1,0:T(8,128)(2,1)} %collective-permute-done.1, bf16[512,512]{1,0:T(8,128)(2,1)S(1)} %bitcast.31), kind=kOutput, calls=%fused_computation.14 | convolution fusion | flops 542375936 | bytes 3145732 | tf_op jit(solution)/shard_map/dot_general | solution.py:20
  (61 shorter events, 36.9 us)
Async XLA Ops:
  3.3 2.0 %collective-permute-start.2 = (bf16[512,512]{1,0:T(8,128)(2,1)S(1)}, bf16[512,512]{1,0:T(8,128)(2,1)S(1)}, u32[]{:S(2)}, u32[]{:S(2)}) collective-permute-start(bf16[512,512]{1,0:T(8,128)(2,1)S(1)} %convolution_convert_fusion.2), channel_id=1, source_target_pairs={{0,16},{16,0},{1,17},{17,1},{2,18},{18,2},{3,19},{19,3},{4,20},{20... | collective-permute-start | bytes 1572872 | tf_op jit(solution)/shard_map/ppermute | solution.py:28
  6.6 6.2 %copy-start.2 = (bf16[512,512]{1,0:T(8,128)(2,1)S(1)}, bf16[512,512]{1,0:T(8,128)(2,1)}, u32[]{:S(2)}) copy-start(bf16[512,512]{1,0:T(8,128)(2,1)} %param.6) | copy-start | bytes 1572868
  6.6 17.3 %all-to-all-start.2 = ((bf16[8,64,512]{2,1,0:T(8,128)(2,1)}), bf16[8,64,512]{2,1,0:T(8,128)(2,1)S(1)}, u32[]{:S(2)}, u32[]{:S(2)}) async-start(bf16[8,64,512]{2,1,0:T(8,128)(2,1)} %bitcast.3), calls=%async_computation.2 | async-start | bytes 1048576 | tf_op jit(solution)/shard_map/all_to_all | solution.py:37
  15.0 13.3 %collective-permute-start = (bf16[512,512]{1,0:T(8,128)(2,1)}, bf16[512,512]{1,0:T(8,128)(2,1)S(1)}, u32[]{:S(2)}, u32[]{:S(2)}) collective-permute-start(bf16[512,512]{1,0:T(8,128)(2,1)} %convolution_convert_fusion.3), channel_id=1, source_target_pairs={{0,16},{16,0},{1,17},{17,1},{2,18},{18,2},{3,19},{19,3},{4,20},{20... | collective-permute-start | bytes 1572872 | tf_op jit(solution)/shard_map/ppermute | solution.py:28
  24.8 14.2 %all-to-all-start.3 = ((bf16[8,64,512]{2,1,0:T(8,128)(2,1)}), bf16[8,64,512]{2,1,0:T(8,128)(2,1)S(1)}, u32[]{:S(2)}, u32[]{:S(2)}) async-start(bf16[8,64,512]{2,1,0:T(8,128)(2,1)} %broadcast_in_dim.11), calls=%async_computation.3 | async-start | bytes 1048576 | tf_op jit(solution)/shard_map/all_to_all | solution.py:43
  39.0 37.2 %copy-start.3 = (bf16[8,64,512]{2,1,0:T(8,128)(2,1)}, bf16[8,64,512]{2,1,0:T(8,128)(2,1)S(1)}, u32[]{:S(2)}) copy-start(bf16[8,64,512]{2,1,0:T(8,128)(2,1)S(1)} %all-to-all-done.3) | copy-start | bytes 1572868
  39.0 13.9 %all-to-all-start = ((bf16[8,64,512]{2,1,0:T(8,128)(2,1)}), bf16[8,64,512]{2,1,0:T(8,128)(2,1)S(1)}, u32[]{:S(2)}, u32[]{:S(2)}) async-start(bf16[8,64,512]{2,1,0:T(8,128)(2,1)} %bitcast), calls=%async_computation | async-start | bytes 1048576 | tf_op jit(solution)/shard_map/all_to_all | solution.py:37
  42.5 14.8 %collective-permute-start.3 = (bf16[512,512]{1,0:T(8,128)(2,1)S(1)}, bf16[512,512]{1,0:T(8,128)(2,1)}, u32[]{:S(2)}, u32[]{:S(2)}) collective-permute-start(bf16[512,512]{1,0:T(8,128)(2,1)S(1)} %bitcast.22), channel_id=1, source_target_pairs={{0,16},{16,0},{1,17},{17,1},{2,18},{18,2},{3,19},{19,3},{4,20},{20... | collective-permute-start | bytes 1572872 | tf_op jit(solution)/shard_map/ppermute | solution.py:28
  53.8 14.0 %all-to-all-start.1 = ((bf16[8,64,512]{2,1,0:T(8,128)(2,1)}), bf16[8,64,512]{2,1,0:T(8,128)(2,1)S(1)}, u32[]{:S(2)}, u32[]{:S(2)}) async-start(bf16[8,64,512]{2,1,0:T(8,128)(2,1)} %broadcast_in_dim.10), calls=%async_computation.1 | async-start | bytes 1048576 | tf_op jit(solution)/shard_map/all_to_all | solution.py:43
  59.6 16.6 %collective-permute-start.10 = (bf16[256,1024]{1,0:T(8,128)(2,1)}, bf16[256,1024]{1,0:T(8,128)(2,1)}, u32[]{:S(2)}, u32[]{:S(2)}) collective-permute-start(bf16[256,1024]{1,0:T(8,128)(2,1)} %convolution_convert_fusion), channel_id=1, source_target_pairs={{0,1},{1,0},{2,3},{3,2},{4,5},{5,4},{6,7},{7,6},{8,9},{9,8},{10,11... | collective-permute-start | bytes 1572872 | tf_op jit(solution)/shard_map/ppermute | solution.py:28
  67.7 34.3 %copy-start.5 = (bf16[8,64,512]{2,1,0:T(8,128)(2,1)}, bf16[8,64,512]{2,1,0:T(8,128)(2,1)S(1)}, u32[]{:S(2)}) copy-start(bf16[8,64,512]{2,1,0:T(8,128)(2,1)S(1)} %all-to-all-done.1) | copy-start | bytes 1572868
  67.7 19.4 %collective-permute-start.1 = (bf16[512,512]{1,0:T(8,128)(2,1)S(1)}, bf16[512,512]{1,0:T(8,128)(2,1)}, u32[]{:S(2)}, u32[]{:S(2)}) collective-permute-start(bf16[512,512]{1,0:T(8,128)(2,1)S(1)} %bitcast.27), channel_id=1, source_target_pairs={{0,16},{16,0},{1,17},{17,1},{2,18},{18,2},{3,19},{19,3},{4,20},{20... | collective-permute-start | bytes 1572872 | tf_op jit(solution)/shard_map/ppermute | solution.py:28
  78.7 25.9 %all-to-all-start.6 = ((bf16[8,32,1024]{2,1,0:T(8,128)(2,1)}), bf16[8,32,1024]{2,1,0:T(8,128)(2,1)S(1)}, u32[]{:S(2)}, u32[]{:S(2)}) async-start(bf16[8,32,1024]{2,1,0:T(8,128)(2,1)} %bitcast.32), calls=%async_computation.6 | async-start | bytes 1048576 | tf_op jit(solution)/shard_map/all_to_all | solution.py:37
  88.7 13.4 %collective-permute-start.8 = (bf16[256,1024]{1,0:T(8,128)(2,1)S(1)}, bf16[256,1024]{1,0:T(8,128)(2,1)S(1)}, u32[]{:S(2)}, u32[]{:S(2)}) collective-permute-start(bf16[256,1024]{1,0:T(8,128)(2,1)S(1)} %convolution_convert_fusion.1), channel_id=1, source_target_pairs={{0,1},{1,0},{2,3},{3,2},{4,5},{5,4},{6,7},{7,6},{8,9},{9,8},{10,11... | collective-permute-start | bytes 1572872 | tf_op jit(solution)/shard_map/ppermute | solution.py:28
  104.6 22.7 %all-to-all-start.4 = ((bf16[8,32,1024]{2,1,0:T(8,128)(2,1)}), bf16[8,32,1024]{2,1,0:T(8,128)(2,1)S(1)}, u32[]{:S(2)}, u32[]{:S(2)}) async-start(bf16[8,32,1024]{2,1,0:T(8,128)(2,1)} %bitcast.33), calls=%async_computation.4 | async-start | bytes 1048576 | tf_op jit(solution)/shard_map/all_to_all | solution.py:37
  128.1 18.4 %all-to-all-start.7 = ((bf16[8,32,1024]{2,1,0:T(8,128)(2,1)}), bf16[8,32,1024]{2,1,0:T(8,128)(2,1)S(1)}, u32[]{:S(2)}, u32[]{:S(2)}) async-start(bf16[8,32,1024]{2,1,0:T(8,128)(2,1)} %broadcast_in_dim.14), calls=%async_computation.7 | async-start | bytes 1048576 | tf_op jit(solution)/shard_map/all_to_all | solution.py:43
  147.4 29.7 %all-to-all-start.5 = ((bf16[8,32,1024]{2,1,0:T(8,128)(2,1)}), bf16[8,32,1024]{2,1,0:T(8,128)(2,1)S(1)}, u32[]{:S(2)}, u32[]{:S(2)}) async-start(bf16[8,32,1024]{2,1,0:T(8,128)(2,1)} %broadcast_in_dim.13), calls=%async_computation.5 | async-start | bytes 1048576 | tf_op jit(solution)/shard_map/all_to_all | solution.py:43
  157.0 3.6 %collective-permute-start.4 = (f32[2,128]{1,0:T(2,128)S(1)}, f32[2,128]{1,0:T(2,128)S(1)}, u32[]{:S(2)}, u32[]{:S(2)}) collective-permute-start(f32[2,128]{1,0:T(2,128)S(1)} %broadcast_in_dim.12), channel_id=1, source_target_pairs={{0,1},{1,0},{2,3},{3,2},{4,5},{5,4},{6,7},{7,6},{8,9},{9,8},{10,11... | collective-permute-start | bytes 3080 | tf_op jit(solution)/shard_map/ppermute | solution.py:28
  160.6 4.8 %collective-permute-start.5 = (f32[2,128]{1,0:T(2,128)S(1)}, f32[2,128]{1,0:T(2,128)S(1)}, u32[]{:S(2)}, u32[]{:S(2)}) collective-permute-start(f32[2,128]{1,0:T(2,128)S(1)} %broadcast_add_fusion), channel_id=1, source_target_pairs={{0,2},{2,4},{4,6},{6,8},{8,10},{10,12},{12,14},{14,0},{1,3},{3,5},... | collective-permute-start | bytes 3080 | tf_op jit(solution)/shard_map/ppermute | solution.py:28
  162.5 17.9 %collective-permute-start.11 = (bf16[256,1024]{1,0:T(8,128)(2,1)S(1)}, bf16[256,1024]{1,0:T(8,128)(2,1)}, u32[]{:S(2)}, u32[]{:S(2)}) collective-permute-start(bf16[256,1024]{1,0:T(8,128)(2,1)S(1)} %bitcast.20), channel_id=1, source_target_pairs={{0,1},{1,0},{2,3},{3,2},{4,5},{5,4},{6,7},{7,6},{8,9},{9,8},{10,11... | collective-permute-start | bytes 1572872 | tf_op jit(solution)/shard_map/ppermute | solution.py:28
  165.5 5.7 %collective-permute-start.6 = (f32[2,128]{1,0:T(2,128)S(1)}, f32[2,128]{1,0:T(2,128)S(1)}, u32[]{:S(2)}, u32[]{:S(2)}) collective-permute-start(f32[2,128]{1,0:T(2,128)S(1)} %fusion.41), channel_id=1, source_target_pairs={{0,4},{2,6},{4,8},{6,10},{8,12},{10,14},{12,0},{14,2},{1,5},{3,7},... | collective-permute-start | bytes 3080 | tf_op jit(solution)/shard_map/ppermute | solution.py:28
  171.2 7.5 %collective-permute-start.7 = (f32[2,128]{1,0:T(2,128)S(1)}, f32[2,128]{1,0:T(2,128)S(1)}, u32[]{:S(2)}, u32[]{:S(2)}) collective-permute-start(f32[2,128]{1,0:T(2,128)S(1)} %add.46), channel_id=1, source_target_pairs={{0,8},{2,10},{4,12},{6,14},{8,0},{10,2},{12,4},{14,6},{1,9},{3,11}... | collective-permute-start | bytes 3080 | tf_op jit(solution)/shard_map/ppermute | solution.py:28
  177.1 9.2 %collective-permute-start.9 = (bf16[256,1024]{1,0:T(8,128)(2,1)S(1)}, bf16[256,1024]{1,0:T(8,128)(2,1)S(1)}, u32[]{:S(2)}, u32[]{:S(2)}) collective-permute-start(bf16[256,1024]{1,0:T(8,128)(2,1)S(1)} %bitcast.21), channel_id=1, source_target_pairs={{0,1},{1,0},{2,3},{3,2},{4,5},{5,4},{6,7},{7,6},{8,9},{9,8},{10,11... | collective-permute-start | bytes 1572872 | tf_op jit(solution)/shard_map/ppermute | solution.py:28
  181.6 4.8 %copy-start.4 = (bf16[8,64,512]{2,1,0:T(8,128)(2,1)S(1)}, bf16[8,64,512]{2,1,0:T(8,128)(2,1)}, u32[]{:S(2)}) copy-start(bf16[8,64,512]{2,1,0:T(8,128)(2,1)} %copy-done.3) | copy-start | bytes 1572868
  (4 other events, 11.0 us)

commit v2 on v1

v2 whole, which is shorter than its diff:
```python
import jax
import jax.numpy as jnp
from jax import lax
from jax.sharding import Mesh, PartitionSpec as P

D = 8192
TOKENS = 1024
X, YH, CORE, Z, YL = 4, 2, 2, 8, 2
ROW = ("x", "yh", "core")
COL = ("z", "yl")

keep_scale = 1.45
gram_scale = 0.5

f32 = jnp.float32
bf16 = jnp.bfloat16


def dot(a, b):
    return jnp.dot(a, b, preferred_element_type=f32)


def dot_t(a, b):
    return lax.dot_general(a, b, (((1,), (1,)), ((), ())), preferred_element_type=f32)


def shift(a, axis, size, by=1):
    return lax.ppermute(a, axis, [(i, (i + by) % size) for i in range(size)])


def piece(a, index, rows):
    return lax.dynamic_slice_in_dim(a, index * rows, rows, 0)


def half(a, which):
    return piece(a, which, a.shape[0] // 2)


def add_up(first, parts):
    for part in parts:
        first = first + part.astype(f32)
    return first


def after(*arrays):
    return sum(jnp.minimum(jnp.abs(a.reshape(-1)[0].astype(f32)), 0.0) for a in arrays)


def core_sum(rows, factor):
    core = lax.axis_index("core")
    away = shift(dot(half(rows, 1 - core), factor).astype(bf16), "core", CORE)
    return dot(half(rows, core), factor) + away.astype(f32)


def x_parts(total):
    x = lax.axis_index("x")
    size = total.shape[0] // X
    return [
        shift(piece(total, lax.rem(x + by, X), size).astype(bf16), "x", X, by)
        for by in range(1, X)
    ]


def gathered(total, parts):
    x, yh = lax.axis_index("x"), lax.axis_index("yh")
    total = add_up(piece(total, x, total.shape[0] // X), parts)
    away = shift(half(total, 1 - yh).astype(bf16), "yh", YH)
    own = (half(total, yh) + away.astype(f32)).astype(bf16)
    pair = jnp.concatenate([own, shift(own, "yh", YH)], axis=0)
    mine = jnp.concatenate([pair] + [shift(pair, "x", X, by) for by in range(1, X)], axis=0)
    return jnp.concatenate([mine, shift(mine, "core", CORE)], axis=0)


def image_sum(factor, proj):
    yl = lax.axis_index("yl")
    away = shift(dot_t(half(factor, 1 - yl), proj).astype(bf16), "yl", YL)
    return dot_t(half(factor, yl), proj) + away.astype(f32)


def reduce_z(a):
    parts = lax.all_to_all(a.astype(bf16).reshape(Z, -1, a.shape[1]), "z", 0, 0, tiled=True)
    return add_up(parts[0].astype(f32), [parts[k] for k in range(1, Z)]).astype(bf16)


def gather_z(a):
    copies = jnp.broadcast_to(a[None], (Z,) + a.shape)
    return lax.all_to_all(copies, "z", 0, 0, tiled=True).reshape(-1, a.shape[1])


def whole_image(mine):
    yl = lax.axis_index("yl")
    other = shift(mine, "yl", YL)
    first = jnp.where(yl == 0, mine, other)
    second = jnp.where(yl == 0, other, mine)
    return jnp.concatenate([first, second], axis=0)


def col_sum(a):
    a = a + shift(a, "yl", YL)
    for by in (1, 2, 4):
        a = a + shift(a, "z", Z, by)
    return a


def updated(factor, image, proj, mean):
    change = dot(image, proj)
    return (keep_scale * factor.astype(f32) - gram_scale * mean / TOKENS * change).astype(bf16)


def local(activations, cotangents, act_factor, grad_factor):
    act_total = core_sum(activations, act_factor)
    act_parts = x_parts(act_total)
    grad_total = core_sum(cotangents, grad_factor) + after(*act_parts)
    grad_parts = x_parts(grad_total)
    act_proj = gathered(act_total, act_parts)
    grad_proj = gathered(grad_total, grad_parts)
    squares = [jnp.sum(jnp.square(p.astype(f32))) for p in (act_proj, grad_proj)]
    row = lax.broadcasted_iota(jnp.int32, (8, 128), 0)
    means = col_sum(jnp.where(row == 0, squares[0], squares[1])) / (TOKENS * D)
    act_own = reduce_z(image_sum(act_factor, act_proj))
    grad_own = reduce_z(image_sum(grad_factor, grad_proj) + after(means))
    act_image = whole_image(gather_z(act_own))
    grad_image = whole_image(gather_z(grad_own))
    return (
        updated(act_factor, act_image, act_proj, means[1, 0]),
        updated(grad_factor, grad_image, grad_proj, means[0, 0]),
    )


def solution(mesh):
    fine = Mesh(mesh.devices.reshape(X, YH, CORE, Z, YL), ROW + COL)
    return jax.shard_map(
        local,
        mesh=fine,
        in_specs=(P(None, ROW), P(None, ROW), P(ROW, COL), P(ROW, COL)),
        out_specs=(P(ROW, COL), P(ROW, COL)),
        check_vma=False,
    )
```

time: 195 us -> 188 us (0.964)
  waiting for transfers between devices: 103 us -> 83.7 us
  starting transfers between devices: 52.6 us -> 66 us
  matrix products: 21 us -> 15.1 us
  between operations: 2.12 us -> 4.87 us
    all_to_all x8 -> x4, waiting for transfers between devices: 65.2 us -> 34.2 us  [the longest x2 21.3 us: gather_z(): return lax.all_to_all(copies, 'z', 0, 0, tiled=True).reshape(-1, a.shape[1])]
    ppermute x12 -> x28, starting transfers between devices: 13.7 us -> 42.2 us  [shift(): return lax.ppermute(a, axis, [(i, (i + by) % size) for i in range(size)])]
    all_to_all x8 -> x4, starting transfers between devices: 38.8 us -> 23.7 us  [the longest x2 15.4 us: reduce_z(): lax.all_to_all(a.astype(bf16).reshape(Z, -1, a.shape[1]), 'z', 0, 0, tile...]
    ppermute x12 -> x28, waiting for transfers between devices: 37.8 us -> 49.4 us  [shift(): return lax.ppermute(a, axis, [(i, (i + by) % size) for i in range(size)])]
    dot_general x4, matrix products: 8.59 us -> 5.63 us  [dot_t(): lax.dot_general(a, b, (((1,), (1,)), ((), ())), preferred_element_type=f32)]
    dot_general x6, matrix products: 12.4 us -> 9.49 us  [dot(): return jnp.dot(a, b, preferred_element_type=f32)]
    reduce_sum x2, other arithmetic: 4.66 us -> 2.24 us  [local(): jnp.sum(jnp.square(p.astype(f32)))]
    select_n x2 -> x3, other arithmetic: 1.22 us -> 3.57 us  [the longest x2 2.39 us: whole_image(): first = jnp.where(yl == 0, mine, other)]
  transfers between devices with their start and end apart: 20 -> 32, of which waited for: 15 -> 17; matrix products, arithmetic and copies ran while one was open for 12% -> 12% of each run, Pallas kernels for 0% -> 0%
where the time goes in v2:
time: 188 us; the launch traced here: 185 us
  waiting for transfers between devices  83.7 us (45%)
  starting transfers between devices  66 us (35%)
  matrix products  15.1 us (8%)
  other arithmetic  8.43 us (4%)
  local copies, waits for them, and re-layouts  6.84 us (4%)
  between operations  4.87 us (3%)
    ppermute x28, waiting for transfers between devices, shift(): return lax.ppermute(a, axis, [(i, (i + by) % size) for i in range(size)])  49.4 us
    ppermute x28, starting transfers between devices, shift(): return lax.ppermute(a, axis, [(i, (i + by) % size) for i in range(size)])  42.2 us
    all_to_all x2, waiting for transfers between devices, gather_z(): return lax.all_to_all(copies, 'z', 0, 0, tiled=True).reshape(-1, a.shape[1])  21.3 us
    all_to_all x2, starting transfers between devices, reduce_z(): lax.all_to_all(a.astype(bf16).reshape(Z, -1, a.shape[1]), 'z', 0, 0, tile...  15.4 us
    all_to_all x2, waiting for transfers between devices, reduce_z(): lax.all_to_all(a.astype(bf16).reshape(Z, -1, a.shape[1]), 'z', 0, 0, tile...  13 us
    dot_general x6, matrix products, dot(): return jnp.dot(a, b, preferred_element_type=f32)  9.49 us
    all_to_all x2, starting transfers between devices, gather_z(): return lax.all_to_all(copies, 'z', 0, 0, tiled=True).reshape(-1, a.shape[1])  8.31 us
    dot_general x4, matrix products, dot_t(): lax.dot_general(a, b, (((1,), (1,)), ((), ())), preferred_element_type=f32)  5.63 us
  transfers between devices with their start and end apart: 32, of which 17 were waited for; matrix products, arithmetic and copies ran while one was open for 12% of the time, Pallas kernels for 0%

profile of v2, /device:TPU:8, one launch (start us, length us, event | category | flops | bytes accessed | tf_op | source)
XLA Modules:
  0.0 184.9 jit_solution(13788140684717302829)
XLA Ops:
  1.9 2.3 %convolution_convert_fusion.3 = bf16[512,512]{1,0:T(8,128)(2,1)} fusion(bf16[512,512]{1,0:T(8,128)(2,1)} %param.6, bf16[1024,512]{1,0:T(8,128)(2,1)S(1)} %copy-done, s32[]{:T(128)S(6)} %select_n.66), kind=kOutput, calls=%fused_computation.12 | convolution fusion | flops 268697600 | bytes 1572868 | tf_op jit(solution)/shard_map/dot_general | solution.py:20
  10.1 2.7 %collective-permute-start.2 = (bf16[128,512]{1,0:T(8,128)(2,1)}, bf16[128,512]{1,0:T(8,128)(2,1)S(1)}, u32[]{:S(2)}, u32[]{:S(2)}) collective-permute-start(bf16[128,512]{1,0:T(8,128)(2,1)} %get-tuple-element.15), channel_id=1, source_target_pairs={{0,128},{64,192},{128,0},{192,64},{1,129},{65,193},{129,1},{193,65... | collective-permute-start | bytes 393224 | tf_op jit(solution)/shard_map/ppermute | solution.py:28
  16.8 2.6 %collective-permute-done.2 = bf16[128,512]{1,0:T(8,128)(2,1)S(1)} collective-permute-done((bf16[128,512]{1,0:T(8,128)(2,1)}, bf16[128,512]{1,0:T(8,128)(2,1)S(1)}, u32[]{:S(2)}, u32[]{:S(2)}) %collective-permute-start.2) | collective-permute-done | bytes 131104 | tf_op jit(solution)/shard_map/ppermute | solution.py:28
  22.0 2.4 %collective-permute-start.4 = (bf16[64,512]{1,0:T(8,128)(2,1)S(1)}, bf16[64,512]{1,0:T(8,128)(2,1)S(1)}, u32[]{:S(2)}, u32[]{:S(2)}) collective-permute-start(bf16[64,512]{1,0:T(8,128)(2,1)S(1)} %dynamic-slice_convert_fusion.7), channel_id=1, source_target_pairs={{0,32},{32,0},{1,33},{33,1},{2,34},{34,2},{3,35},{35,3},{4,36},{36... | collective-permute-start | bytes 196616 | tf_op jit(solution)/shard_map/ppermute | solution.py:28
  26.3 2.2 %collective-permute-start.12 = (bf16[128,512]{1,0:T(8,128)(2,1)S(1)}, bf16[128,512]{1,0:T(8,128)(2,1)S(1)}, u32[]{:S(2)}, u32[]{:S(2)}) collective-permute-start(bf16[128,512]{1,0:T(8,128)(2,1)S(1)} %get-tuple-element.10), channel_id=1, source_target_pairs={{0,128},{64,192},{128,0},{192,64},{1,129},{65,193},{129,1},{193,65... | collective-permute-start | bytes 393224 | tf_op jit(solution)/shard_map/ppermute | solution.py:28
  31.4 4.5 %collective-permute-done.5 = bf16[64,512]{1,0:T(8,128)(2,1)S(1)} collective-permute-done((bf16[64,512]{1,0:T(8,128)(2,1)S(1)}, bf16[64,512]{1,0:T(8,128)(2,1)S(1)}, u32[]{:S(2)}, u32[]{:S(2)}) %collective-permute-start.5) | collective-permute-done | bytes 65568 | tf_op jit(solution)/shard_map/ppermute | solution.py:28
  38.2 2.5 %collective-permute-start.8 = (bf16[128,512]{1,0:T(8,128)(2,1)S(1)}, bf16[128,512]{1,0:T(8,128)(2,1)S(1)}, u32[]{:S(2)}, u32[]{:S(2)}) collective-permute-start(bf16[128,512]{1,0:T(8,128)(2,1)S(1)} %pad_maximum_fusion), channel_id=1, source_target_pairs={{0,192},{64,0},{128,64},{192,128},{1,193},{65,1},{129,65},{193,129... | collective-permute-start | bytes 393224 | tf_op jit(solution)/shard_map/ppermute | solution.py:28
  42.2 4.7 %collective-permute-done.14 = bf16[64,512]{1,0:T(8,128)(2,1)S(1)} collective-permute-done((bf16[64,512]{1,0:T(8,128)(2,1)S(1)}, bf16[64,512]{1,0:T(8,128)(2,1)S(1)}, u32[]{:S(2)}, u32[]{:S(2)}) %collective-permute-start.14) | collective-permute-done | bytes 65568 | tf_op jit(solution)/shard_map/ppermute | solution.py:28
  48.7 4.1 %collective-permute-done.15 = bf16[64,512]{1,0:T(8,128)(2,1)S(1)} collective-permute-done((bf16[64,512]{1,0:T(8,128)(2,1)S(1)}, bf16[64,512]{1,0:T(8,128)(2,1)S(1)}, u32[]{:S(2)}, u32[]{:S(2)}) %collective-permute-start.15) | collective-permute-done | bytes 65568 | tf_op jit(solution)/shard_map/ppermute | solution.py:28
  54.8 2.5 %collective-permute-start.18 = (bf16[128,512]{1,0:T(8,128)(2,1)S(1)}, bf16[128,512]{1,0:T(8,128)(2,1)S(1)}, u32[]{:S(2)}, u32[]{:S(2)}) collective-permute-start(bf16[128,512]{1,0:T(8,128)(2,1)S(1)} %pad_maximum_fusion.1), channel_id=1, source_target_pairs={{0,192},{64,0},{128,64},{192,128},{1,193},{65,1},{129,65},{193,129... | collective-permute-start | bytes 393224 | tf_op jit(solution)/shard_map/ppermute | solution.py:28
  57.4 3.3 %collective-permute-done.16 = bf16[128,512]{1,0:T(8,128)(2,1)S(1)} collective-permute-done((bf16[128,512]{1,0:T(8,128)(2,1)S(1)}, bf16[128,512]{1,0:T(8,128)(2,1)S(1)}, u32[]{:S(2)}, u32[]{:S(2)}) %collective-permute-start.16) | collective-permute-done | bytes 131104 | tf_op jit(solution)/shard_map/ppermute | solution.py:28
  70.7 6.3 %collective-permute-done.24 = bf16[256,1024]{1,0:T(8,128)(2,1)S(1)} collective-permute-done((bf16[256,1024]{1,0:T(8,128)(2,1)S(1)}, bf16[256,1024]{1,0:T(8,128)(2,1)S(1)}, u32[]{:S(2)}, u32[]{:S(2)}) %collective-permute-start.24) | collective-permute-done | bytes 524320 | tf_op jit(solution)/shard_map/ppermute | solution.py:28
  78.3 8.5 %all-to-all-start = ((bf16[8,32,1024]{2,1,0:T(8,128)(2,1)}), bf16[8,32,1024]{2,1,0:T(8,128)(2,1)}, u32[]{:S(2)}, u32[]{:S(2)}) async-start(bf16[8,32,1024]{2,1,0:T(8,128)(2,1)} %bitcast.33), calls=%async_computation | async-start | bytes 1048576 | tf_op jit(solution)/shard_map/all_to_all | solution.py:81
  90.0 8.8 %collective-permute-done.21 = f32[8,128]{1,0:T(8,128)S(1)} collective-permute-done((f32[8,128]{1,0:T(8,128)S(1)}, f32[8,128]{1,0:T(8,128)S(1)}, u32[]{:S(2)}, u32[]{:S(2)}) %collective-permute-start.21) | collective-permute-done | bytes 4128 | tf_op jit(solution)/shard_map/ppermute | solution.py:28
  100.2 4.4 %collective-permute-done.22 = f32[8,128]{1,0:T(8,128)S(1)} collective-permute-done((f32[8,128]{1,0:T(8,128)S(1)}, f32[8,128]{1,0:T(8,128)S(1)}, u32[]{:S(2)}, u32[]{:S(2)}) %collective-permute-start.22) | collective-permute-done | bytes 4128 | tf_op jit(solution)/shard_map/ppermute | solution.py:28
  104.6 5.7 %collective-permute-start.23 = (f32[8,128]{1,0:T(8,128)S(1)}, f32[8,128]{1,0:T(8,128)S(1)}, u32[]{:S(2)}, u32[]{:S(2)}) collective-permute-start(f32[8,128]{1,0:T(8,128)S(1)} %add.205), channel_id=1, source_target_pairs={{0,8},{2,10},{4,12},{6,14},{8,0},{10,2},{12,4},{14,6},{1,9},{3,11}... | collective-permute-start | bytes 12296 | tf_op jit(solution)/shard_map/ppermute | solution.py:28
  113.3 2.6 %fusion.4 = bf16[256,1024]{1,0:T(8,128)(2,1)} fusion(bf16[1024,512]{1,0:T(8,128)(2,1)} %copy-done.2, bf16[256,1024]{1,0:T(8,128)(2,1)} %collective-permute-done.26, f32[]{:T(128)} %bitcast.7, bf16[512,512]{1,0:T(8,128)(2,1)S(1)} %copy-done.4, s32[]{:T(128)S(6)} %select_n.75), kind=kOutput, calls=%fused_computation.14 | convolution fusion | flops 269484032 | bytes 2359304 | tf_op jit(solution)/shard_map/dot_general | solution.py:24
  115.9 6.9 %all-to-all-start.2 = ((bf16[8,32,1024]{2,1,0:T(8,128)(2,1)}), bf16[8,32,1024]{2,1,0:T(8,128)(2,1)}, u32[]{:S(2)}, u32[]{:S(2)}) async-start(bf16[8,32,1024]{2,1,0:T(8,128)(2,1)} %bitcast.37), calls=%async_computation.2 | async-start | bytes 1048576 | tf_op jit(solution)/shard_map/all_to_all | solution.py:81
  124.0 13.0 %all-to-all-done.2 = bf16[8,32,1024]{2,1,0:T(8,128)(2,1)} async-done(((bf16[8,32,1024]{2,1,0:T(8,128)(2,1)}), bf16[8,32,1024]{2,1,0:T(8,128)(2,1)}, u32[]{:S(2)}, u32[]{:S(2)}) %all-to-all-start.2) | async-done | bytes 524320 | tf_op jit(solution)/shard_map/all_to_all | solution.py:81
  137.8 4.2 %all-to-all-start.1 = ((bf16[8,32,1024]{2,1,0:T(8,128)(2,1)}), bf16[8,32,1024]{2,1,0:T(8,128)(2,1)}, u32[]{:S(2)}, u32[]{:S(2)}) async-start(bf16[8,32,1024]{2,1,0:T(8,128)(2,1)} %broadcast_in_dim.27), calls=%async_computation.1 | async-start | bytes 1048576 | tf_op jit(solution)/shard_map/all_to_all | solution.py:87
  143.1 12.1 %all-to-all-done.1 = bf16[8,32,1024]{2,1,0:T(8,128)(2,1)} async-done(((bf16[8,32,1024]{2,1,0:T(8,128)(2,1)}), bf16[8,32,1024]{2,1,0:T(8,128)(2,1)}, u32[]{:S(2)}, u32[]{:S(2)}) %all-to-all-start.1) | async-done | bytes 524320 | tf_op jit(solution)/shard_map/all_to_all | solution.py:87
  156.1 4.2 %all-to-all-start.3 = ((bf16[8,32,1024]{2,1,0:T(8,128)(2,1)}), bf16[8,32,1024]{2,1,0:T(8,128)(2,1)}, u32[]{:S(2)}, u32[]{:S(2)}) async-start(bf16[8,32,1024]{2,1,0:T(8,128)(2,1)} %broadcast_in_dim.29), calls=%async_computation.3 | async-start | bytes 1048576 | tf_op jit(solution)/shard_map/all_to_all | solution.py:87
  163.7 9.1 %all-to-all-done.3 = bf16[8,32,1024]{2,1,0:T(8,128)(2,1)} async-done(((bf16[8,32,1024]{2,1,0:T(8,128)(2,1)}), bf16[8,32,1024]{2,1,0:T(8,128)(2,1)}, u32[]{:S(2)}, u32[]{:S(2)}) %all-to-all-start.3) | async-done | bytes 524320 | tf_op jit(solution)/shard_map/all_to_all | solution.py:87
  177.2 5.0 %collective-permute-done.27 = bf16[256,1024]{1,0:T(8,128)(2,1)S(1)} collective-permute-done((bf16[256,1024]{1,0:T(8,128)(2,1)}, bf16[256,1024]{1,0:T(8,128)(2,1)S(1)}, u32[]{:S(2)}, u32[]{:S(2)}) %collective-permute-start.27) | collective-permute-done | bytes 524320 | tf_op jit(solution)/shard_map/ppermute | solution.py:28
  (108 shorter events, 55.5 us)
Async XLA Ops:
  5.4 19.0 %collective-permute-start.10 = (bf16[512,512]{1,0:T(8,128)(2,1)}, bf16[512,512]{1,0:T(8,128)(2,1)}, u32[]{:S(2)}, u32[]{:S(2)}) collective-permute-start(bf16[512,512]{1,0:T(8,128)(2,1)} %convolution_convert_fusion.2), channel_id=1, source_target_pairs={{0,16},{16,0},{1,17},{17,1},{2,18},{18,2},{3,19},{19,3},{4,20},{20... | collective-permute-start | bytes 1572872 | tf_op jit(solution)/shard_map/ppermute | solution.py:28
  10.1 9.3 %collective-permute-start.2 = (bf16[128,512]{1,0:T(8,128)(2,1)}, bf16[128,512]{1,0:T(8,128)(2,1)S(1)}, u32[]{:S(2)}, u32[]{:S(2)}) collective-permute-start(bf16[128,512]{1,0:T(8,128)(2,1)} %get-tuple-element.15), channel_id=1, source_target_pairs={{0,128},{64,192},{128,0},{192,64},{1,129},{65,193},{129,1},{193,65... | collective-permute-start | bytes 393224 | tf_op jit(solution)/shard_map/ppermute | solution.py:28
  12.9 7.8 %collective-permute-start.3 = (bf16[128,512]{1,0:T(8,128)(2,1)}, bf16[128,512]{1,0:T(8,128)(2,1)S(1)}, u32[]{:S(2)}, u32[]{:S(2)}) collective-permute-start(bf16[128,512]{1,0:T(8,128)(2,1)} %get-tuple-element.14), channel_id=1, source_target_pairs={{0,192},{64,0},{128,64},{192,128},{1,193},{65,1},{129,65},{193,129... | collective-permute-start | bytes 393224 | tf_op jit(solution)/shard_map/ppermute | solution.py:28
  22.0 8.1 %collective-permute-start.4 = (bf16[64,512]{1,0:T(8,128)(2,1)S(1)}, bf16[64,512]{1,0:T(8,128)(2,1)S(1)}, u32[]{:S(2)}, u32[]{:S(2)}) collective-permute-start(bf16[64,512]{1,0:T(8,128)(2,1)S(1)} %dynamic-slice_convert_fusion.7), channel_id=1, source_target_pairs={{0,32},{32,0},{1,33},{33,1},{2,34},{34,2},{3,35},{35,3},{4,36},{36... | collective-permute-start | bytes 196616 | tf_op jit(solution)/shard_map/ppermute | solution.py:28
  25.9 12.3 %collective-permute-start.11 = (bf16[128,512]{1,0:T(8,128)(2,1)S(1)}, bf16[128,512]{1,0:T(8,128)(2,1)S(1)}, u32[]{:S(2)}, u32[]{:S(2)}) collective-permute-start(bf16[128,512]{1,0:T(8,128)(2,1)S(1)} %get-tuple-element.8), channel_id=1, source_target_pairs={{0,64},{64,128},{128,192},{192,0},{1,65},{65,129},{129,193},{193,1... | collective-permute-start | bytes 393224 | tf_op jit(solution)/shard_map/ppermute | solution.py:28
  26.3 14.4 %collective-permute-start.12 = (bf16[128,512]{1,0:T(8,128)(2,1)S(1)}, bf16[128,512]{1,0:T(8,128)(2,1)S(1)}, u32[]{:S(2)}, u32[]{:S(2)}) collective-permute-start(bf16[128,512]{1,0:T(8,128)(2,1)S(1)} %get-tuple-element.10), channel_id=1, source_target_pairs={{0,128},{64,192},{128,0},{192,64},{1,129},{65,193},{129,1},{193,65... | collective-permute-start | bytes 393224 | tf_op jit(solution)/shard_map/ppermute | solution.py:28
  28.5 12.3 %collective-permute-start.13 = (bf16[128,512]{1,0:T(8,128)(2,1)S(1)}, bf16[128,512]{1,0:T(8,128)(2,1)S(1)}, u32[]{:S(2)}, u32[]{:S(2)}) collective-permute-start(bf16[128,512]{1,0:T(8,128)(2,1)S(1)} %get-tuple-element.9), channel_id=1, source_target_pairs={{0,192},{64,0},{128,64},{192,128},{1,193},{65,1},{129,65},{193,129... | collective-permute-start | bytes 393224 | tf_op jit(solution)/shard_map/ppermute | solution.py:28
  35.9 12.6 %collective-permute-start.6 = (bf16[128,512]{1,0:T(8,128)(2,1)S(1)}, bf16[128,512]{1,0:T(8,128)(2,1)S(1)}, u32[]{:S(2)}, u32[]{:S(2)}) collective-permute-start(bf16[128,512]{1,0:T(8,128)(2,1)S(1)} %pad_maximum_fusion), channel_id=1, source_target_pairs={{0,64},{64,128},{128,192},{192,0},{1,65},{65,129},{129,193},{193,1... | collective-permute-start | bytes 393224 | tf_op jit(solution)/shard_map/ppermute | solution.py:28
  36.5 12.1 %collective-permute-start.7 = (bf16[128,512]{1,0:T(8,128)(2,1)S(1)}, bf16[128,512]{1,0:T(8,128)(2,1)S(1)}, u32[]{:S(2)}, u32[]{:S(2)}) collective-permute-start(bf16[128,512]{1,0:T(8,128)(2,1)S(1)} %pad_maximum_fusion), channel_id=1, source_target_pairs={{0,128},{64,192},{128,0},{192,64},{1,129},{65,193},{129,1},{193,65... | collective-permute-start | bytes 393224 | tf_op jit(solution)/shard_map/ppermute | solution.py:28
  38.2 10.4 %collective-permute-start.8 = (bf16[128,512]{1,0:T(8,128)(2,1)S(1)}, bf16[128,512]{1,0:T(8,128)(2,1)S(1)}, u32[]{:S(2)}, u32[]{:S(2)}) collective-permute-start(bf16[128,512]{1,0:T(8,128)(2,1)S(1)} %pad_maximum_fusion), channel_id=1, source_target_pairs={{0,192},{64,0},{128,64},{192,128},{1,193},{65,1},{129,65},{193,129... | collective-permute-start | bytes 393224 | tf_op jit(solution)/shard_map/ppermute | solution.py:28
  48.6 13.1 %collective-permute-start.9 = (bf16[512,512]{1,0:T(8,128)(2,1)S(1)}, bf16[512,512]{1,0:T(8,128)(2,1)S(1)}, u32[]{:S(2)}, u32[]{:S(2)}) collective-permute-start(bf16[512,512]{1,0:T(8,128)(2,1)S(1)} %get-tuple-element.22), channel_id=1, source_target_pairs={{0,16},{16,0},{1,17},{17,1},{2,18},{18,2},{3,19},{19,3},{4,20},{20... | collective-permute-start | bytes 1572872 | tf_op jit(solution)/shard_map/ppermute | solution.py:28
  52.8 7.8 %collective-permute-start.16 = (bf16[128,512]{1,0:T(8,128)(2,1)S(1)}, bf16[128,512]{1,0:T(8,128)(2,1)S(1)}, u32[]{:S(2)}, u32[]{:S(2)}) collective-permute-start(bf16[128,512]{1,0:T(8,128)(2,1)S(1)} %pad_maximum_fusion.1), channel_id=1, source_target_pairs={{0,64},{64,128},{128,192},{192,0},{1,65},{65,129},{129,193},{193,1... | collective-permute-start | bytes 393224 | tf_op jit(solution)/shard_map/ppermute | solution.py:28
  53.1 7.6 %collective-permute-start.17 = (bf16[128,512]{1,0:T(8,128)(2,1)S(1)}, bf16[128,512]{1,0:T(8,128)(2,1)S(1)}, u32[]{:S(2)}, u32[]{:S(2)}) collective-permute-start(bf16[128,512]{1,0:T(8,128)(2,1)S(1)} %pad_maximum_fusion.1), channel_id=1, source_target_pairs={{0,128},{64,192},{128,0},{192,64},{1,129},{65,193},{129,1},{193,65... | collective-permute-start | bytes 393224 | tf_op jit(solution)/shard_map/ppermute | solution.py:28
  62.2 14.8 %collective-permute-start.24 = (bf16[256,1024]{1,0:T(8,128)(2,1)S(1)}, bf16[256,1024]{1,0:T(8,128)(2,1)S(1)}, u32[]{:S(2)}, u32[]{:S(2)}) collective-permute-start(bf16[256,1024]{1,0:T(8,128)(2,1)S(1)} %convolution_convert_fusion.1), channel_id=1, source_target_pairs={{0,1},{1,0},{2,3},{3,2},{4,5},{5,4},{6,7},{7,6},{8,9},{9,8},{10,11... | collective-permute-start | bytes 1572872 | tf_op jit(solution)/shard_map/ppermute | solution.py:28
  66.3 47.0 %collective-permute-start.26 = (bf16[256,1024]{1,0:T(8,128)(2,1)}, bf16[256,1024]{1,0:T(8,128)(2,1)}, u32[]{:S(2)}, u32[]{:S(2)}) collective-permute-start(bf16[256,1024]{1,0:T(8,128)(2,1)} %convolution_convert_fusion), channel_id=1, source_target_pairs={{0,1},{1,0},{2,3},{3,2},{4,5},{5,4},{6,7},{7,6},{8,9},{9,8},{10,11... | collective-permute-start | bytes 1572872 | tf_op jit(solution)/shard_map/ppermute | solution.py:28
  69.1 18.8 %collective-permute-start.20 = (f32[8,128]{1,0:T(8,128)S(1)}, f32[8,128]{1,0:T(8,128)S(1)}, u32[]{:S(2)}, u32[]{:S(2)}) collective-permute-start(f32[8,128]{1,0:T(8,128)S(1)} %iota.7), channel_id=1, source_target_pairs={{0,1},{1,0},{2,3},{3,2},{4,5},{5,4},{6,7},{7,6},{8,9},{9,8},{10,11... | collective-permute-start | bytes 12296 | tf_op jit(solution)/shard_map/ppermute | solution.py:28
  78.3 37.6 %all-to-all-start = ((bf16[8,32,1024]{2,1,0:T(8,128)(2,1)}), bf16[8,32,1024]{2,1,0:T(8,128)(2,1)}, u32[]{:S(2)}, u32[]{:S(2)}) async-start(bf16[8,32,1024]{2,1,0:T(8,128)(2,1)} %bitcast.33), calls=%async_computation | async-start | bytes 1048576 | tf_op jit(solution)/shard_map/all_to_all | solution.py:81
  88.0 10.7 %collective-permute-start.21 = (f32[8,128]{1,0:T(8,128)S(1)}, f32[8,128]{1,0:T(8,128)S(1)}, u32[]{:S(2)}, u32[]{:S(2)}) collective-permute-start(f32[8,128]{1,0:T(8,128)S(1)} %broadcast_add_fusion), channel_id=1, source_target_pairs={{0,2},{2,4},{4,6},{6,8},{8,10},{10,12},{12,14},{14,0},{1,3},{3,5},... | collective-permute-start | bytes 12296 | tf_op jit(solution)/shard_map/ppermute | solution.py:28
  104.6 7.5 %collective-permute-start.23 = (f32[8,128]{1,0:T(8,128)S(1)}, f32[8,128]{1,0:T(8,128)S(1)}, u32[]{:S(2)}, u32[]{:S(2)}) collective-permute-start(f32[8,128]{1,0:T(8,128)S(1)} %add.205), channel_id=1, source_target_pairs={{0,8},{2,10},{4,12},{6,14},{8,0},{10,2},{12,4},{14,6},{1,9},{3,11}... | collective-permute-start | bytes 12296 | tf_op jit(solution)/shard_map/ppermute | solution.py:28
  115.9 21.0 %all-to-all-start.2 = ((bf16[8,32,1024]{2,1,0:T(8,128)(2,1)}), bf16[8,32,1024]{2,1,0:T(8,128)(2,1)}, u32[]{:S(2)}, u32[]{:S(2)}) async-start(bf16[8,32,1024]{2,1,0:T(8,128)(2,1)} %bitcast.37), calls=%async_computation.2 | async-start | bytes 1048576 | tf_op jit(solution)/shard_map/all_to_all | solution.py:81
  137.8 17.4 %all-to-all-start.1 = ((bf16[8,32,1024]{2,1,0:T(8,128)(2,1)}), bf16[8,32,1024]{2,1,0:T(8,128)(2,1)}, u32[]{:S(2)}, u32[]{:S(2)}) async-start(bf16[8,32,1024]{2,1,0:T(8,128)(2,1)} %broadcast_in_dim.27), calls=%async_computation.1 | async-start | bytes 1048576 | tf_op jit(solution)/shard_map/all_to_all | solution.py:87
  156.1 16.7 %all-to-all-start.3 = ((bf16[8,32,1024]{2,1,0:T(8,128)(2,1)}), bf16[8,32,1024]{2,1,0:T(8,128)(2,1)}, u32[]{:S(2)}, u32[]{:S(2)}) async-start(bf16[8,32,1024]{2,1,0:T(8,128)(2,1)} %broadcast_in_dim.29), calls=%async_computation.3 | async-start | bytes 1048576 | tf_op jit(solution)/shard_map/all_to_all | solution.py:87
  160.3 14.2 %collective-permute-start.25 = (bf16[256,1024]{1,0:T(8,128)(2,1)}, bf16[256,1024]{1,0:T(8,128)(2,1)}, u32[]{:S(2)}, u32[]{:S(2)}) collective-permute-start(bf16[256,1024]{1,0:T(8,128)(2,1)} %bitcast.4), channel_id=1, source_target_pairs={{0,1},{1,0},{2,3},{3,2},{4,5},{5,4},{6,7},{7,6},{8,9},{9,8},{10,11... | collective-permute-start | bytes 1572872 | tf_op jit(solution)/shard_map/ppermute | solution.py:28
  172.8 9.4 %collective-permute-start.27 = (bf16[256,1024]{1,0:T(8,128)(2,1)}, bf16[256,1024]{1,0:T(8,128)(2,1)S(1)}, u32[]{:S(2)}, u32[]{:S(2)}) collective-permute-start(bf16[256,1024]{1,0:T(8,128)(2,1)} %bitcast.10), channel_id=1, source_target_pairs={{0,1},{1,0},{2,3},{3,2},{4,5},{5,4},{6,7},{7,6},{8,9},{9,8},{10,11... | collective-permute-start | bytes 1572872 | tf_op jit(solution)/shard_map/ppermute | solution.py:28
  (15 other events, 72.4 us)

commit v3 on v1

v3 whole, which is shorter than its diff:
```python
import jax
import jax.numpy as jnp
from jax import lax
from jax.experimental import pallas as pl
from jax.experimental.pallas import tpu as pltpu
from jax.sharding import Mesh, PartitionSpec as P

D = 8192
TOKENS = 1024
X, YH, CORE, Z, YL = 4, 2, 2, 8, 2
ROW = ("x", "yh", "core")
COL = ("z", "yl")
ROWS = D // (X * YH * CORE)
WIDTH = D // (Z * YL)
HALF = TOKENS // CORE
SMALL = 256
LARGE = TOKENS - SMALL
PART = ROWS // (Z * YL)

keep_scale = 1.45
gram_scale = 0.5

f32 = jnp.float32
bf16 = jnp.bfloat16


def dot(a, b):
    return jnp.dot(a, b, preferred_element_type=f32)


def dot_t(a, b):
    return lax.dot_general(a, b, (((1,), (1,)), ((), ())), preferred_element_type=f32)


def shift(a, axis, size, by=1):
    return lax.ppermute(a, axis, [(i, (i + by) % size) for i in range(size)])


def kernel_call(body, outs, *args, index=None, unread=(), flops=0):
    specs = [pl.BlockSpec(memory_space=pltpu.VMEM)] * len(args)
    specs += [pl.BlockSpec(memory_space=pl.ANY)] * len(unread)
    if index is not None:
        specs = [pl.BlockSpec(memory_space=pltpu.SMEM)] + specs
        args = (index.astype(jnp.int32).reshape(1),) + args
    size = sum(a.size * a.dtype.itemsize for a in args)
    return pl.pallas_call(
        body,
        out_shape=[jax.ShapeDtypeStruct(shape, dtype) for shape, dtype in outs],
        in_specs=specs,
        out_specs=[pl.BlockSpec(memory_space=pltpu.VMEM)] * len(outs),
        compiler_params=pltpu.CompilerParams(vmem_limit_bytes=48 * 2**20),
        cost_estimate=pl.CostEstimate(flops=flops, bytes_accessed=size, transcendentals=0),
    )(*args, *unread)


def project_away(which, acts, cots, act_factor, grad_factor, out):
    rows = pl.ds(pl.multiple_of(which[0] * HALF, HALF), HALF)
    out[:, :WIDTH] = dot(acts[rows, :], act_factor[...]).astype(bf16)
    out[:, WIDTH:] = dot(cots[rows, :], grad_factor[...]).astype(bf16)


def project_own(which, acts, cots, act_factor, grad_factor, came, out):
    rows = pl.ds(pl.multiple_of(which[0] * HALF, HALF), HALF)
    for rows_ref, factor, start in ((acts, act_factor, 0), (cots, grad_factor, WIDTH)):
        cols = slice(start, start + WIDTH)
        total = dot(rows_ref[rows, :], factor[...]) + came[:, cols].astype(f32)
        out[:, cols] = total.astype(bf16)


def project_sum(parts, copies, squares):
    total = parts[0].astype(f32)
    for k in range(1, X * YH):
        total = total + parts[k].astype(f32)
    own = total.astype(bf16)
    for k in range(X * YH):
        copies[k] = own
    own = jnp.square(own.astype(f32))
    row = lax.broadcasted_iota(jnp.int32, (8, 128), 0)
    squares[...] = jnp.where(row == 0, jnp.sum(own[:, :WIDTH]), jnp.sum(own[:, WIDTH:]))


def factor_columns(f):
    return slice(f * WIDTH, (f + 1) * WIDTH)


def image_small(act_factor, grad_factor, mine, _, out):
    for f, factor in enumerate((act_factor, grad_factor)):
        image = dot_t(factor[...].reshape(ROWS, WIDTH), mine[:SMALL, factor_columns(f)])
        out[:, f] = image.astype(bf16).reshape(Z, YL * PART, SMALL)


def half_image(factor, which, mine, other, f):
    rows = factor[:, pl.ds(which, 1)].reshape(ROWS // YL, WIDTH)
    return (
        dot_t(rows, mine[SMALL:, factor_columns(f)]),
        dot_t(rows, other[:, factor_columns(f)]),
    )


def image_away(which, act_factor, grad_factor, mine, other, out):
    for f, factor in enumerate((act_factor, grad_factor)):
        first, second = half_image(factor, which[0], mine, other, f)
        out[f, :, : HALF - SMALL] = first.astype(bf16)
        out[f, :, HALF - SMALL :] = second.astype(bf16)


def image_own(which, act_factor, grad_factor, mine, other, came, _, out):
    cut = HALF - SMALL
    for f, factor in enumerate((act_factor, grad_factor)):
        first, second = half_image(factor, which[0], mine, other, f)
        first = (first + came[f, :, :cut].astype(f32)).astype(bf16)
        second = (second + came[f, :, cut:].astype(f32)).astype(bf16)
        out[:, f, :, :cut] = first.reshape(Z, PART, cut)
        out[:, f, :, cut:] = second.reshape(Z, PART, LARGE - cut)


def small_sum(which, parts, away, own):
    def total(side):
        out = parts[0, :, pl.ds(side, 1)].astype(f32)
        for k in range(1, Z):
            out = out + parts[k, :, pl.ds(side, 1)].astype(f32)
        return out.reshape(2, PART, SMALL)

    own[...] = total(which[0])
    away[...] = total(1 - which[0]).astype(bf16)


def small_copies(own, other, _, copies):
    for k in range(Z):
        copies[k, 0] = own[...]
        copies[k, 1] = other[...]


def large_sum(parts, _, copies):
    total = parts[0].astype(f32)
    for k in range(1, Z):
        total = total + parts[k].astype(f32)
    own = total.astype(bf16)
    for k in range(Z):
        copies[k] = own


def update(which, squares, act_factor, grad_factor, mine, other, own_large, other_large, small, act_out, grad_out):
    cut = HALF - SMALL
    for f, (factor, out) in enumerate(((act_factor, act_out), (grad_factor, grad_out))):
        scale = squares[1 - f : 2 - f, :1] / (TOKENS * D) * (gram_scale / TOKENS)
        for side, large in enumerate((own_large, other_large)):
            where = pl.ds(which[0] if side == 0 else 1 - which[0], 1)
            image = large[:, f].reshape(ROWS // YL, LARGE)
            change = dot(image[:, :cut], mine[SMALL:, factor_columns(f)])
            change += dot(image[:, cut:], other[:, factor_columns(f)])
            image = small[:, side, f].reshape(ROWS // YL, SMALL)
            change += dot(image, mine[:SMALL, factor_columns(f)])
            kept = factor[:, where].reshape(ROWS // YL, WIDTH).astype(f32)
            new = (keep_scale * kept - scale * change).astype(bf16)
            out[:, where] = new.reshape(Z, 1, PART, WIDTH)


def local(activations, cotangents, act_factor, grad_factor):
    core, yl = lax.axis_index("core"), lax.axis_index("yl")
    product = 4 * HALF * ROWS * WIDTH
    given = (activations, cotangents, act_factor, grad_factor)
    (away,) = kernel_call(project_away, [((HALF, 2 * WIDTH), bf16)], *given, index=1 - core, flops=product)
    came = shift(away, "core", CORE)
    (total,) = kernel_call(project_own, [((HALF, 2 * WIDTH), bf16)], *given, came, index=core, flops=product)
    group = X * YH
    chunks = (group, HALF // group, 2 * WIDTH)
    parts = lax.all_to_all(total.reshape(chunks), ("x", "yh"), 0, 0, tiled=True)
    copies, squares = kernel_call(project_sum, [(chunks, bf16), ((8, 128), f32)], parts)
    mine = lax.all_to_all(copies, ("x", "yh"), 0, 0, tiled=True).reshape(HALF, 2 * WIDTH)
    for by in (1, 2, 4):
        squares = squares + shift(squares, "z", Z, by)
    other = shift(mine, "core", CORE)

    factors = [f.reshape(Z, YL, PART, WIDTH) for f in (act_factor, grad_factor)]
    (part,) = kernel_call(image_small, [((Z, 2, YL * PART, SMALL), bf16)], *factors, mine, unread=(squares,), flops=product // 2)
    small_parts = lax.all_to_all(part, "z", 0, 0, tiled=True)
    for axis, size, by in (("x", X, 1), ("x", X, 2), ("core", CORE, 1), ("yh", YH, 1), ("yl", YL, 1)):
        squares = squares + shift(squares, axis, size, by)
    (away,) = kernel_call(image_away, [((2, ROWS // YL, LARGE), bf16)], *factors, mine, other, index=1 - yl, flops=product // 2)
    came = shift(away, "yl", YL)
    (part,) = kernel_call(image_own, [((Z, 2, PART, LARGE), bf16)], *factors, mine, other, came, index=yl, unread=(small_parts,), flops=product // 2)
    shape = (2, PART, SMALL)
    away, own = kernel_call(small_sum, [(shape, bf16), (shape, f32)], small_parts.reshape(Z, 2, YL, PART, SMALL), index=yl)
    large_parts = lax.all_to_all(part, "z", 0, 0, tiled=True)
    own = (own + shift(away, "yl", YL).astype(f32)).astype(bf16)
    from_other = shift(own, "yl", YL)
    (copies,) = kernel_call(large_sum, [((Z, 2, PART, LARGE), bf16)], large_parts, unread=(squares,))
    own_large = lax.all_to_all(copies, "z", 0, 0, tiled=True)
    (copies,) = kernel_call(small_copies, [((Z, YL) + shape, bf16)], own, from_other, unread=(own_large,))
    small = lax.all_to_all(copies, "z", 0, 0, tiled=True)
    other_large = shift(own_large, "yl", YL)
    outs = kernel_call(
        update, [((Z, YL, PART, WIDTH), bf16)] * 2, squares, *factors, mine, other, own_large, other_large, small, index=yl, flops=2 * product
    )
    return tuple(out.reshape(ROWS, WIDTH) for out in outs)


def solution(mesh):
    fine = Mesh(mesh.devices.reshape(X, YH, CORE, Z, YL), ROW + COL)
    return jax.shard_map(
        local,
        mesh=fine,
        in_specs=(P(None, ROW), P(None, ROW), P(ROW, COL), P(ROW, COL)),
        out_specs=(P(ROW, COL), P(ROW, COL)),
        check_vma=False,
    )
```

time: 195 us -> 186 us (0.954); the launches traced: 192 us -> 185 us
  blocking collectives: 0 us -> 42.2 us
  waiting for transfers between devices: 103 us -> 81.5 us
  matrix products: 21 us -> 0 us
  starting transfers between devices: 52.6 us -> 39.4 us
  Pallas kernels: 0 us -> 11.2 us
  other arithmetic: 7.66 us -> 0.03 us
  local copies, waits for them, and re-layouts: 5.22 us -> 9.96 us
    all_to_all x0 -> x2, blocking collectives: none -> 42.2 us  [the longest x1 23 us: local(): parts = lax.all_to_all(total.reshape(chunks), ('x', 'yh'), 0, 0, tiled=True)]
    all_to_all x8 -> x4, waiting for transfers between devices: 65.2 us -> 24.1 us  [the longest x1 12.2 us: local(): own_large = lax.all_to_all(copies, 'z', 0, 0, tiled=True)]
    dot_general x10 -> x0, matrix products: 21 us -> none  [the longest x6 12.4 us: dot(): return jnp.dot(a, b, preferred_element_type=f32)]
    ppermute x12 -> x14, waiting for transfers between devices: 37.8 us -> 57.4 us  [shift(): return lax.ppermute(a, axis, [(i, (i + by) % size) for i in range(size)])]
    all_to_all x8 -> x4, starting transfers between devices: 38.8 us -> 24.1 us  [the longest x1 7.21 us: local(): own_large = lax.all_to_all(copies, 'z', 0, 0, tiled=True)]
    pallas_call x0 -> x10, Pallas kernels: none -> 11.2 us  [kernel_call(): pl.pallas_call(body, out_shape=[jax.ShapeDtypeStruct(shape, dtype) for sh...]
    unnamed x16 -> x26, local copies, waits for them, and re-layouts: 1.24 us -> 9.96 us
    reduce_sum x6 -> x0, other arithmetic: 4.97 us -> none  [the longest x2 4.66 us: local(): jnp.sum(jnp.square(p.astype(f32)))]
  transfers between devices with their start and end apart: 20 -> 18, of which waited for: 15 -> 15; matrix products, arithmetic and copies ran while one was open for 12% -> 0% of each run, Pallas kernels for 0% -> 2%
where the time goes in v3:
time: 186 us; the launch traced here: 185 us
  waiting for transfers between devices  81.5 us (44%)
  blocking collectives  42.2 us (23%)
  starting transfers between devices  39.4 us (21%)
  Pallas kernels  11.2 us (6%)
  local copies, waits for them, and re-layouts  9.96 us (5%)
    ppermute x14, waiting for transfers between devices, shift(): return lax.ppermute(a, axis, [(i, (i + by) % size) for i in range(size)])  57.4 us
    all_to_all x1, blocking collectives, local(): parts = lax.all_to_all(total.reshape(chunks), ('x', 'yh'), 0, 0, tiled=True)  23 us
    all_to_all x1, blocking collectives, local(): lax.all_to_all(copies, ('x', 'yh'), 0, 0, tiled=True)  19.2 us
    ppermute x14, starting transfers between devices, shift(): return lax.ppermute(a, axis, [(i, (i + by) % size) for i in range(size)])  15.3 us
    all_to_all x1, waiting for transfers between devices, local(): own_large = lax.all_to_all(copies, 'z', 0, 0, tiled=True)  12.2 us
    all_to_all x1, waiting for transfers between devices, local(): small_parts = lax.all_to_all(part, 'z', 0, 0, tiled=True)  12 us
    pallas_call x10, Pallas kernels, kernel_call(): pl.pallas_call(body, out_shape=[jax.ShapeDtypeStruct(shape, dtype) for sh...  11.2 us
    unnamed x26, local copies, waits for them, and re-layouts  9.96 us
  transfers between devices with their start and end apart: 18, of which 15 were waited for; matrix products, arithmetic and copies ran while one was open for 0% of the time, Pallas kernels for 2%

profile of v3, /device:TPU:8, one launch (start us, length us, event | category | flops | bytes accessed | tf_op | source)
XLA Modules:
  0.0 185.1 jit_solution(18048827335172567041)
XLA Ops:
  6.0 2.6 %collective-permute-done.came = bf16[512,1024]{1,0:T(8,128)(2,1)S(1)} collective-permute-done((bf16[512,1024]{1,0:T(8,128)(2,1)S(1)}, bf16[512,1024]{1,0:T(8,128)(2,1)S(1)}, u32[]{:S(2)}, u32[]{:S(2)}) %collective-permute-start) | collective-permute-done | bytes 1048608 | tf_op jit(solution)/shard_map/ppermute | solution.py:36
  9.4 23.0 %all_to_all.30.parts = bf16[8,64,1024]{2,1,0:T(8,128)(2,1)S(1)} all-to-all(bf16[8,64,1024]{2,1,0:T(8,128)(2,1)S(1)} %bitcast.24), channel_id=1, replica_groups=mesh['x'=4,'yh'=2,'core'=2,'z'=8,'yl'=2] {'x','yh'}, dimensions={0} | all-to-all | bytes 2097152 | tf_op jit(solution)/shard_map/all_to_all | solution.py:168
  32.7 19.2 %all_to_all.31 = bf16[8,64,1024]{2,1,0:T(8,128)(2,1)S(1)} all-to-all(bf16[8,64,1024]{2,1,0:T(8,128)(2,1)S(1)} %get-tuple-element.9), channel_id=1, replica_groups=mesh['x'=4,'yh'=2,'core'=2,'z'=8,'yl'=2] {'x','yh'}, dimensions={0} | all-to-all | bytes 2097152 | tf_op jit(solution)/shard_map/all_to_all | solution.py:170
  51.9 1.9 %collective-permute-start.1 = (f32[8,128]{1,0:T(8,128)S(1)}, f32[8,128]{1,0:T(8,128)S(1)}, u32[]{:S(2)}, u32[]{:S(2)}) collective-permute-start(f32[8,128]{1,0:T(8,128)S(1)} %get-tuple-element.8), channel_id=1, source_target_pairs={{0,2},{2,4},{4,6},{6,8},{8,10},{10,12},{12,14},{14,0},{1,3},{3,5},... | collective-permute-start | bytes 12296 | tf_op jit(solution)/shard_map/ppermute | solution.py:36
  53.8 5.5 %collective-permute-done.1 = f32[8,128]{1,0:T(8,128)S(1)} collective-permute-done((f32[8,128]{1,0:T(8,128)S(1)}, f32[8,128]{1,0:T(8,128)S(1)}, u32[]{:S(2)}, u32[]{:S(2)}) %collective-permute-start.1) | collective-permute-done | bytes 4128 | tf_op jit(solution)/shard_map/ppermute | solution.py:36
  59.3 5.7 %collective-permute-done.2 = f32[8,128]{1,0:T(8,128)S(1)} collective-permute-done((f32[8,128]{1,0:T(8,128)S(1)}, f32[8,128]{1,0:T(8,128)S(1)}, u32[]{:S(2)}, u32[]{:S(2)}) %collective-permute-start.2) | collective-permute-done | bytes 4128 | tf_op jit(solution)/shard_map/ppermute | solution.py:36
  65.1 4.6 %collective-permute-start.3 = (f32[8,128]{1,0:T(8,128)S(1)}, f32[8,128]{1,0:T(8,128)S(1)}, u32[]{:S(2)}, u32[]{:S(2)}) collective-permute-start(f32[8,128]{1,0:T(8,128)S(1)} %add.28), channel_id=1, source_target_pairs={{0,8},{2,10},{4,12},{6,14},{8,0},{10,2},{12,4},{14,6},{1,9},{3,11}... | collective-permute-start | bytes 12296 | tf_op jit(solution)/shard_map/ppermute | solution.py:36
  69.6 2.9 %collective-permute-done.3 = f32[8,128]{1,0:T(8,128)S(1)} collective-permute-done((f32[8,128]{1,0:T(8,128)S(1)}, f32[8,128]{1,0:T(8,128)S(1)}, u32[]{:S(2)}, u32[]{:S(2)}) %collective-permute-start.3) | collective-permute-done | bytes 4128 | tf_op jit(solution)/shard_map/ppermute | solution.py:36
  73.9 5.8 %all-to-all-start.2 = ((bf16[8,2,64,256]{3,2,1,0:T(8,128)(2,1)}), bf16[8,2,64,256]{3,2,1,0:T(8,128)(2,1)}, u32[]{:S(2)}, u32[]{:S(2)}) async-start(bf16[8,2,64,256]{3,2,1,0:T(8,128)(2,1)} %copy-done.9), calls=%async_computation.2 | async-start | bytes 1048576 | tf_op jit(solution)/shard_map/all_to_all | solution.py:177
  82.5 12.0 %all-to-all-done.2._ = bf16[8,2,64,256]{3,2,1,0:T(8,128)(2,1)} async-done(((bf16[8,2,64,256]{3,2,1,0:T(8,128)(2,1)}), bf16[8,2,64,256]{3,2,1,0:T(8,128)(2,1)}, u32[]{:S(2)}, u32[]{:S(2)}) %all-to-all-start.2) | async-done | bytes 524320 | tf_op jit(solution)/shard_map/all_to_all | solution.py:177
  94.5 3.2 %collective-permute-done.10.came = bf16[2,256,768]{2,1,0:T(8,128)(2,1)} collective-permute-done((bf16[2,256,768]{2,1,0:T(8,128)(2,1)}, bf16[2,256,768]{2,1,0:T(8,128)(2,1)}, u32[]{:S(2)}, u32[]{:S(2)}) %collective-permute-start.10) | collective-permute-done | bytes 786464 | tf_op jit(solution)/shard_map/ppermute | solution.py:36
  97.7 1.7 shard_map.64
  100.4 6.9 %all-to-all-start.3 = ((bf16[8,2,32,768]{3,2,1,0:T(8,128)(2,1)}), bf16[8,2,32,768]{3,2,1,0:T(8,128)(2,1)}, u32[]{:S(2)}, u32[]{:S(2)}) async-start(bf16[8,2,32,768]{3,2,1,0:T(8,128)(2,1)} %copy-done.8), calls=%async_computation.3 | async-start | bytes 1572864 | tf_op jit(solution)/shard_map/all_to_all | solution.py:185
  107.6 4.6 %collective-permute-done.4 = f32[8,128]{1,0:T(8,128)S(1)} collective-permute-done((f32[8,128]{1,0:T(8,128)S(1)}, f32[8,128]{1,0:T(8,128)S(1)}, u32[]{:S(2)}, u32[]{:S(2)}) %collective-permute-start.4) | collective-permute-done | bytes 4128 | tf_op jit(solution)/shard_map/ppermute | solution.py:36
  112.4 4.9 %collective-permute-done.5 = f32[8,128]{1,0:T(8,128)S(1)} collective-permute-done((f32[8,128]{1,0:T(8,128)S(1)}, f32[8,128]{1,0:T(8,128)S(1)}, u32[]{:S(2)}, u32[]{:S(2)}) %collective-permute-start.5) | collective-permute-done | bytes 4128 | tf_op jit(solution)/shard_map/ppermute | solution.py:36
  119.6 3.9 %collective-permute-done.7 = f32[8,128]{1,0:T(8,128)S(1)} collective-permute-done((f32[8,128]{1,0:T(8,128)S(1)}, f32[8,128]{1,0:T(8,128)S(1)}, u32[]{:S(2)}, u32[]{:S(2)}) %collective-permute-start.7) | collective-permute-done | bytes 4128 | tf_op jit(solution)/shard_map/ppermute | solution.py:36
  124.9 2.3 %collective-permute-done.8 = f32[8,128]{1,0:T(8,128)S(1)} collective-permute-done((f32[8,128]{1,0:T(8,128)S(1)}, f32[8,128]{1,0:T(8,128)S(1)}, u32[]{:S(2)}, u32[]{:S(2)}) %collective-permute-start.8) | collective-permute-done | bytes 4128 | tf_op jit(solution)/shard_map/ppermute | solution.py:36
  129.3 7.2 %all-to-all-start.4 = ((bf16[8,2,32,768]{3,2,1,0:T(8,128)(2,1)}), bf16[8,2,32,768]{3,2,1,0:T(8,128)(2,1)}, u32[]{:S(2)}, u32[]{:S(2)}) async-start(bf16[8,2,32,768]{3,2,1,0:T(8,128)(2,1)} %copy-done.7), calls=%async_computation.4 | async-start | bytes 1572864 | tf_op jit(solution)/shard_map/all_to_all | solution.py:189
  139.1 2.6 %collective-permute-done.12 = bf16[2,32,256]{2,1,0:T(8,128)(2,1)S(1)} collective-permute-done((bf16[2,32,256]{2,1,0:T(8,128)(2,1)S(1)}, bf16[2,32,256]{2,1,0:T(8,128)(2,1)S(1)}, u32[]{:S(2)}, u32[]{:S(2)}) %collective-permute-start.12) | collective-permute-done | bytes 32800 | tf_op jit(solution)/shard_map/ppermute | solution.py:36
  143.1 2.6 %collective-permute-done.13.other = bf16[2,32,256]{2,1,0:T(8,128)(2,1)S(1)} collective-permute-done((bf16[2,32,256]{2,1,0:T(8,128)(2,1)S(1)}, bf16[2,32,256]{2,1,0:T(8,128)(2,1)S(1)}, u32[]{:S(2)}, u32[]{:S(2)}) %collective-permute-start.13) | collective-permute-done | bytes 32800 | tf_op jit(solution)/shard_map/ppermute | solution.py:36
  145.6 12.2 %all-to-all-done.4._.own_large = bf16[8,2,32,768]{3,2,1,0:T(8,128)(2,1)} async-done(((bf16[8,2,32,768]{3,2,1,0:T(8,128)(2,1)}), bf16[8,2,32,768]{3,2,1,0:T(8,128)(2,1)}, u32[]{:S(2)}, u32[]{:S(2)}) %all-to-all-start.4) | async-done | bytes 786464 | tf_op jit(solution)/shard_map/all_to_all | solution.py:189
  158.6 4.1 %all-to-all-start.5 = ((bf16[8,2,2,32,256]{4,3,2,1,0:T(8,128)(2,1)}), bf16[8,2,2,32,256]{4,3,2,1,0:T(8,128)(2,1)}, u32[]{:S(2)}, u32[]{:S(2)}) async-start(bf16[8,2,2,32,256]{4,3,2,1,0:T(8,128)(2,1)} %copy-done.10), calls=%async_computation.5 | async-start | bytes 1048576 | tf_op jit(solution)/shard_map/all_to_all | solution.py:191
  164.2 15.5 %collective-permute-done.11.other_large = bf16[8,2,32,768]{3,2,1,0:T(8,128)(2,1)S(1)} collective-permute-done((bf16[8,2,32,768]{3,2,1,0:T(8,128)(2,1)}, bf16[8,2,32,768]{3,2,1,0:T(8,128)(2,1)S(1)}, u32[]{:S(2)}, u32[]{:S(2)}) %collective-permute-start.11) | collective-permute-done | bytes 786464 | tf_op jit(solution)/shard_map/ppermute | solution.py:36
  181.8 3.4 %shard_map.68 = (bf16[8,2,32,512]{3,2,1,0:T(8,128)(2,1)}, bf16[8,2,32,512]{3,2,1,0:T(8,128)(2,1)}) custom-call(s32[1]{0:T(128)} %bitcast.which, f32[8,128]{1,0:T(8,128)S(1)} %add.34._.squares, bf16[8,2,32,512]{3,2,1,0:T(8,128)(2,1)S(1)} %bitcast.19, bf16[8,2,32,512]{3,2,1,0:T(8,128)(2,1)S(1)} %bitcast.23, bf16[512,1024]{1,0:T(8,128)(2,1)S(1)} %bitcast.15, ...), custom_call_target="tpu_custom_call" | custom-call | flops 1073741824 | bytes 5246980 | tf_op jit(solution)/shard_map/pallas_call | solution.py:46
  (59 shorter events, 26.1 us)
Async XLA Ops:
  2.7 1.2 copy-start.4
  3.9 1.2 copy-start.6
  5.2 3.5 %copy-start.1 = (bf16[512,512]{1,0:T(8,128)(2,1)S(1)}, bf16[512,512]{1,0:T(8,128)(2,1)}, u32[]{:S(2)}) copy-start(bf16[512,512]{1,0:T(8,128)(2,1)} %act_factor.3) | copy-start | bytes 1572868
  5.2 3.5 %copy-start.3 = (bf16[512,512]{1,0:T(8,128)(2,1)S(1)}, bf16[512,512]{1,0:T(8,128)(2,1)}, u32[]{:S(2)}) copy-start(bf16[512,512]{1,0:T(8,128)(2,1)} %grad_factor.3) | copy-start | bytes 1572868
  5.2 3.5 %copy-start.5 = (bf16[1024,512]{1,0:T(8,128)(2,1)S(1)}, bf16[1024,512]{1,0:T(8,128)(2,1)}, u32[]{:S(2)}) copy-start(bf16[1024,512]{1,0:T(8,128)(2,1)} %acts.3) | copy-start | bytes 3145732
  5.9 2.7 %collective-permute-start = (bf16[512,1024]{1,0:T(8,128)(2,1)S(1)}, bf16[512,1024]{1,0:T(8,128)(2,1)S(1)}, u32[]{:S(2)}, u32[]{:S(2)}) collective-permute-start(bf16[512,1024]{1,0:T(8,128)(2,1)S(1)} %shard_map.59), channel_id=1, source_target_pairs={{0,16},{16,0},{1,17},{17,1},{2,18},{18,2},{3,19},{19,3},{4,20},{20... | collective-permute-start | bytes 3145736 | tf_op jit(solution)/shard_map/ppermute | solution.py:36
  51.9 27.8 %collective-permute-start.9 = (bf16[512,1024]{1,0:T(8,128)(2,1)S(1)}, bf16[512,1024]{1,0:T(8,128)(2,1)S(1)}, u32[]{:S(2)}, u32[]{:S(2)}) collective-permute-start(bf16[512,1024]{1,0:T(8,128)(2,1)S(1)} %bitcast.11), channel_id=1, source_target_pairs={{0,16},{16,0},{1,17},{17,1},{2,18},{18,2},{3,19},{19,3},{4,20},{20... | collective-permute-start | bytes 3145736 | tf_op jit(solution)/shard_map/ppermute | solution.py:36
  51.9 7.4 %collective-permute-start.1 = (f32[8,128]{1,0:T(8,128)S(1)}, f32[8,128]{1,0:T(8,128)S(1)}, u32[]{:S(2)}, u32[]{:S(2)}) collective-permute-start(f32[8,128]{1,0:T(8,128)S(1)} %get-tuple-element.8), channel_id=1, source_target_pairs={{0,2},{2,4},{4,6},{6,8},{8,10},{10,12},{12,14},{14,0},{1,3},{3,5},... | collective-permute-start | bytes 12296 | tf_op jit(solution)/shard_map/ppermute | solution.py:36
  59.3 5.7 %collective-permute-start.2 = (f32[8,128]{1,0:T(8,128)S(1)}, f32[8,128]{1,0:T(8,128)S(1)}, u32[]{:S(2)}, u32[]{:S(2)}) collective-permute-start(f32[8,128]{1,0:T(8,128)S(1)} %add.27), channel_id=1, source_target_pairs={{0,4},{2,6},{4,8},{6,10},{8,12},{10,14},{12,0},{14,2},{1,5},{3,7},... | collective-permute-start | bytes 12296 | tf_op jit(solution)/shard_map/ppermute | solution.py:36
  65.1 7.5 %collective-permute-start.3 = (f32[8,128]{1,0:T(8,128)S(1)}, f32[8,128]{1,0:T(8,128)S(1)}, u32[]{:S(2)}, u32[]{:S(2)}) collective-permute-start(f32[8,128]{1,0:T(8,128)S(1)} %add.28), channel_id=1, source_target_pairs={{0,8},{2,10},{4,12},{6,14},{8,0},{10,2},{12,4},{14,6},{1,9},{3,11}... | collective-permute-start | bytes 12296 | tf_op jit(solution)/shard_map/ppermute | solution.py:36
  73.9 20.7 %all-to-all-start.2 = ((bf16[8,2,64,256]{3,2,1,0:T(8,128)(2,1)}), bf16[8,2,64,256]{3,2,1,0:T(8,128)(2,1)}, u32[]{:S(2)}, u32[]{:S(2)}) async-start(bf16[8,2,64,256]{3,2,1,0:T(8,128)(2,1)} %copy-done.9), calls=%async_computation.2 | async-start | bytes 1048576 | tf_op jit(solution)/shard_map/all_to_all | solution.py:177
  81.2 16.5 %collective-permute-start.10 = (bf16[2,256,768]{2,1,0:T(8,128)(2,1)}, bf16[2,256,768]{2,1,0:T(8,128)(2,1)}, u32[]{:S(2)}, u32[]{:S(2)}) collective-permute-start(bf16[2,256,768]{2,1,0:T(8,128)(2,1)} %shard_map.62), channel_id=1, source_target_pairs={{0,1},{1,0},{2,3},{3,2},{4,5},{5,4},{6,7},{7,6},{8,9},{9,8},{10,11... | collective-permute-start | bytes 2359304 | tf_op jit(solution)/shard_map/ppermute | solution.py:36
  100.4 26.8 %all-to-all-start.3 = ((bf16[8,2,32,768]{3,2,1,0:T(8,128)(2,1)}), bf16[8,2,32,768]{3,2,1,0:T(8,128)(2,1)}, u32[]{:S(2)}, u32[]{:S(2)}) async-start(bf16[8,2,32,768]{3,2,1,0:T(8,128)(2,1)} %copy-done.8), calls=%async_computation.3 | async-start | bytes 1572864 | tf_op jit(solution)/shard_map/all_to_all | solution.py:185
  107.3 4.8 %collective-permute-start.4 = (f32[8,128]{1,0:T(8,128)S(1)}, f32[8,128]{1,0:T(8,128)S(1)}, u32[]{:S(2)}, u32[]{:S(2)}) collective-permute-start(f32[8,128]{1,0:T(8,128)S(1)} %add.29._), channel_id=1, source_target_pairs={{0,64},{64,128},{128,192},{192,0},{1,65},{65,129},{129,193},{193,1... | collective-permute-start | bytes 12296 | tf_op jit(solution)/shard_map/ppermute | solution.py:36
  112.1 5.1 %collective-permute-start.5 = (f32[8,128]{1,0:T(8,128)S(1)}, f32[8,128]{1,0:T(8,128)S(1)}, u32[]{:S(2)}, u32[]{:S(2)}) collective-permute-start(f32[8,128]{1,0:T(8,128)S(1)} %add.30), channel_id=1, source_target_pairs={{0,128},{64,192},{128,0},{192,64},{1,129},{65,193},{129,1},{193,65... | collective-permute-start | bytes 12296 | tf_op jit(solution)/shard_map/ppermute | solution.py:36
  117.3 1.2 collective-permute-start.6
  118.4 5.1 %collective-permute-start.7 = (f32[8,128]{1,0:T(8,128)S(1)}, f32[8,128]{1,0:T(8,128)S(1)}, u32[]{:S(2)}, u32[]{:S(2)}) collective-permute-start(f32[8,128]{1,0:T(8,128)S(1)} %add.32), channel_id=1, source_target_pairs={{0,32},{32,0},{1,33},{33,1},{2,34},{34,2},{3,35},{35,3},{4,36},{36... | collective-permute-start | bytes 12296 | tf_op jit(solution)/shard_map/ppermute | solution.py:36
  123.5 3.6 %collective-permute-start.8 = (f32[8,128]{1,0:T(8,128)S(1)}, f32[8,128]{1,0:T(8,128)S(1)}, u32[]{:S(2)}, u32[]{:S(2)}) collective-permute-start(f32[8,128]{1,0:T(8,128)S(1)} %add.33), channel_id=1, source_target_pairs={{0,1},{1,0},{2,3},{3,2},{4,5},{5,4},{6,7},{7,6},{8,9},{9,8},{10,11... | collective-permute-start | bytes 12296 | tf_op jit(solution)/shard_map/ppermute | solution.py:36
  129.3 28.5 %all-to-all-start.4 = ((bf16[8,2,32,768]{3,2,1,0:T(8,128)(2,1)}), bf16[8,2,32,768]{3,2,1,0:T(8,128)(2,1)}, u32[]{:S(2)}, u32[]{:S(2)}) async-start(bf16[8,2,32,768]{3,2,1,0:T(8,128)(2,1)} %copy-done.7), calls=%async_computation.4 | async-start | bytes 1572864 | tf_op jit(solution)/shard_map/all_to_all | solution.py:189
  137.6 4.0 %collective-permute-start.12 = (bf16[2,32,256]{2,1,0:T(8,128)(2,1)S(1)}, bf16[2,32,256]{2,1,0:T(8,128)(2,1)S(1)}, u32[]{:S(2)}, u32[]{:S(2)}) collective-permute-start(bf16[2,32,256]{2,1,0:T(8,128)(2,1)S(1)} %get-tuple-element.11), channel_id=1, source_target_pairs={{0,1},{1,0},{2,3},{3,2},{4,5},{5,4},{6,7},{7,6},{8,9},{9,8},{10,11... | collective-permute-start | bytes 98312 | tf_op jit(solution)/shard_map/ppermute | solution.py:36
  141.6 4.0 %collective-permute-start.13 = (bf16[2,32,256]{2,1,0:T(8,128)(2,1)S(1)}, bf16[2,32,256]{2,1,0:T(8,128)(2,1)S(1)}, u32[]{:S(2)}, u32[]{:S(2)}) collective-permute-start(bf16[2,32,256]{2,1,0:T(8,128)(2,1)S(1)} %add_convert_fusion.own), channel_id=1, source_target_pairs={{0,1},{1,0},{2,3},{3,2},{4,5},{5,4},{6,7},{7,6},{8,9},{9,8},{10,11... | collective-permute-start | bytes 98312 | tf_op jit(solution)/shard_map/ppermute | solution.py:36
  158.6 22.0 %all-to-all-start.5 = ((bf16[8,2,2,32,256]{4,3,2,1,0:T(8,128)(2,1)}), bf16[8,2,2,32,256]{4,3,2,1,0:T(8,128)(2,1)}, u32[]{:S(2)}, u32[]{:S(2)}) async-start(bf16[8,2,2,32,256]{4,3,2,1,0:T(8,128)(2,1)} %copy-done.10), calls=%async_computation.5 | async-start | bytes 1048576 | tf_op jit(solution)/shard_map/all_to_all | solution.py:191
  162.8 16.9 %collective-permute-start.11 = (bf16[8,2,32,768]{3,2,1,0:T(8,128)(2,1)}, bf16[8,2,32,768]{3,2,1,0:T(8,128)(2,1)S(1)}, u32[]{:S(2)}, u32[]{:S(2)}) collective-permute-start(bf16[8,2,32,768]{3,2,1,0:T(8,128)(2,1)} %all-to-all-done.4._.own_large), channel_id=1, source_target_pairs={{0,1},{1,0},{2,3},{3,2},{4,5},{5,4},{6,7},{7,6},{8,9},{9,8},{10,11... | collective-permute-start | bytes 2359304 | tf_op jit(solution)/shard_map/ppermute | solution.py:36
  180.6 1.1 copy-start.12
  (7 other events, 6.4 us)

commit v4 on v3

v4 whole, which is shorter than its diff:
```python
import jax
import jax.numpy as jnp
from jax import lax
from jax.experimental import pallas as pl
from jax.experimental.pallas import tpu as pltpu
from jax.sharding import Mesh, PartitionSpec as P

D = 8192
TOKENS = 1024
X, YH, CORE, Z, YL = 4, 2, 2, 8, 2
ROW = ("x", "yh", "core")
COL = ("z", "yl")
ROWS = D // (X * YH * CORE)
WIDTH = D // (Z * YL)
HALF = TOKENS // CORE
PART = ROWS // (Z * YL)

REDUCE = (4, -3, 3, -2, 2, -1, 1, 0)
GATHER = (0, -1, 1, -2, 2, -3, 3, -4)

keep_scale = 1.45
gram_scale = 0.5

f32 = jnp.float32
bf16 = jnp.bfloat16


def dot(a, b):
    return jnp.dot(a, b, preferred_element_type=f32)


def dot_t(a, b):
    return lax.dot_general(a, b, (((1,), (1,)), ((), ())), preferred_element_type=f32)


def shift(a, axis, size, by=1):
    return lax.ppermute(a, axis, [(i, (i + by) % size) for i in range(size)])


def kernel_call(body, outs, *args, index=None, unread=(), flops=0, spec=pl.BlockSpec(memory_space=pltpu.VMEM)):
    specs = [spec] * len(args)
    specs += [pl.BlockSpec(memory_space=pl.ANY)] * len(unread)
    if index is not None:
        specs = [pl.BlockSpec(memory_space=pltpu.SMEM)] + specs
        args = (jnp.stack([i.astype(jnp.int32) for i in index]),) + args
    size = sum(a.size * a.dtype.itemsize for a in args)
    return pl.pallas_call(
        body,
        out_shape=[jax.ShapeDtypeStruct(shape, dtype) for shape, dtype in outs],
        in_specs=specs,
        out_specs=[pl.BlockSpec(memory_space=pltpu.VMEM)] * len(outs),
        compiler_params=pltpu.CompilerParams(vmem_limit_bytes=48 * 2**20),
        cost_estimate=pl.CostEstimate(flops=flops, bytes_accessed=size, transcendentals=0),
    )(*args, *unread)


def tied(a, other):
    anywhere = pl.BlockSpec(memory_space=pl.ANY)
    return pl.pallas_call(
        lambda *refs: None,
        out_shape=jax.ShapeDtypeStruct(a.shape, a.dtype),
        in_specs=[anywhere, anywhere],
        out_specs=anywhere,
        input_output_aliases={0: 0},
    )(a, other)


def project_away(which, acts, cots, act_factor, grad_factor, out):
    rows = pl.ds(pl.multiple_of(which[0] * HALF, HALF), HALF)
    out[:, :WIDTH] = dot(acts[rows, :], act_factor[...]).astype(bf16)
    out[:, WIDTH:] = dot(cots[rows, :], grad_factor[...]).astype(bf16)


def project_own(which, acts, cots, act_factor, grad_factor, came, out):
    rows = pl.ds(pl.multiple_of(which[0] * HALF, HALF), HALF)
    for rows_ref, factor, start in ((acts, act_factor, 0), (cots, grad_factor, WIDTH)):
        cols = slice(start, start + WIDTH)
        total = dot(rows_ref[rows, :], factor[...]) + came[:, cols].astype(f32)
        out[:, cols] = total.astype(bf16)


def project_sum(parts, copies, squares):
    total = parts[0].astype(f32)
    for k in range(1, X * YH):
        total = total + parts[k].astype(f32)
    own = total.astype(bf16)
    for k in range(X * YH):
        copies[k] = own
    own = jnp.square(own.astype(f32))
    row = lax.broadcasted_iota(jnp.int32, (8, 128), 0)
    squares[...] = jnp.where(row == 0, jnp.sum(own[:, :WIDTH]), jnp.sum(own[:, WIDTH:]))


def factor_columns(f):
    return slice(f * WIDTH, (f + 1) * WIDTH)


def image_rows(factor, z, side, mine, other, f):
    rows = [factor[pl.ds(lax.rem(z + (e + Z), Z), 1), pl.ds(side, 1)].reshape(PART, WIDTH) for e in REDUCE]
    rows = jnp.concatenate(rows, axis=0)
    return (
        dot_t(rows, mine[:, factor_columns(f)]),
        dot_t(rows, other[:, factor_columns(f)]),
    )


def image_away(at, act_factor, grad_factor, mine, other, *outs):
    for f, factor in enumerate((act_factor, grad_factor)):
        first, second = image_rows(factor, at[0], 1 - at[1], mine, other, f)
        for k in range(Z):
            rows = slice(k * PART, (k + 1) * PART)
            outs[k // 2][k % 2, f, :, :HALF] = first[rows].astype(bf16)
            outs[k // 2][k % 2, f, :, HALF:] = second[rows].astype(bf16)


def image_own(at, act_factor, grad_factor, mine, other, *outs):
    for f, factor in enumerate((act_factor, grad_factor)):
        first, second = image_rows(factor, at[0], at[1], mine, other, f)
        for k in range(Z):
            rows = slice(k * PART, (k + 1) * PART)
            outs[k][f, :, :HALF] = first[rows]
            outs[k][f, :, HALF:] = second[rows]


def last_sum(own, away, up, down, _, out):
    total = own[...] + away[1].astype(f32) + up[...].astype(f32) + down[...].astype(f32)
    out[...] = total.astype(bf16)


def update(at, squares, act_factor, grad_factor, mine, other, *refs):
    chunks, outs = refs[: 2 * Z], refs[2 * Z :]
    for f, (factor, out) in enumerate(((act_factor, outs[0]), (grad_factor, outs[1]))):
        scale = squares[1 - f : 2 - f, :1] / (TOKENS * D) * (gram_scale / TOKENS)
        for side in range(YL):
            image = jnp.concatenate([c[f] for c in chunks[side * Z : (side + 1) * Z]], axis=0)
            change = dot(image[:, :HALF], mine[:, factor_columns(f)])
            change += dot(image[:, HALF:], other[:, factor_columns(f)])
            half = pl.ds(at[1] if side == 0 else 1 - at[1], 1)
            for k, e in enumerate(GATHER):
                place = (pl.ds(lax.rem(at[0] + (e + Z), Z), 1), half)
                kept = factor[place].reshape(PART, WIDTH).astype(f32)
                new = keep_scale * kept - scale * change[k * PART : (k + 1) * PART]
                out[place] = new.astype(bf16).reshape(1, 1, PART, WIDTH)


def local(activations, cotangents, act_factor, grad_factor):
    core, z, yl = (lax.axis_index(name) for name in ("core", "z", "yl"))
    product = 4 * HALF * ROWS * WIDTH
    given = (activations, cotangents, act_factor, grad_factor)
    sent = [((HALF, 2 * WIDTH), bf16)]
    (away,) = kernel_call(project_away, sent, *given, index=[1 - core], flops=product, spec=pl.BlockSpec())
    came = shift(away, "core", CORE)
    (total,) = kernel_call(project_own, sent, *given, came, index=[core], flops=product, spec=pl.BlockSpec())
    group = X * YH
    chunks = (group, HALF // group, 2 * WIDTH)
    parts = lax.all_to_all(total.reshape(chunks), ("x", "yh"), 0, 0, tiled=True)
    copies, squares = kernel_call(project_sum, [(chunks, bf16), ((8, 128), f32)], parts)
    mine = lax.all_to_all(copies, ("x", "yh"), 0, 0, tiled=True).reshape(HALF, 2 * WIDTH)
    for by in (1, 2, 4):
        squares = squares + shift(squares, "z", Z, by)
    mine = tied(mine, squares)
    other = shift(mine, "core", CORE)
    for axis, size, by in (("x", X, 1), ("x", X, 2), ("core", CORE, 1), ("yh", YH, 1), ("yl", YL, 1)):
        squares = squares + shift(squares, axis, size, by)

    factors = [f.reshape(Z, YL, PART, WIDTH) for f in (act_factor, grad_factor)]
    shape = (2, PART, TOKENS)
    sent = [((2,) + shape, bf16)] * (Z // 2)
    away = kernel_call(image_away, sent, *factors, mine, other, index=[z, yl], flops=product)
    away = [shift(a, "yl", YL) for a in away]
    own = kernel_call(image_own, [(shape, f32)] * Z, *factors, mine, other, index=[z, yl], flops=product)
    up, down = (own[k] + away[0][k].astype(f32) for k in (0, 1))
    for step in (1, 2, 3):
        up = shift(up.astype(bf16), "z", Z, 1)
        down = shift(down.astype(bf16), "z", Z, -1)
        up = own[2 * step] + away[step][0].astype(f32) + up.astype(f32)
        if step < 3:
            down = own[2 * step + 1] + away[step][1].astype(f32) + down.astype(f32)
    up = shift(up.astype(bf16), "z", Z, 1)
    (up,) = kernel_call(last_sum, [(shape, bf16)], own[7], away[3], up, down, unread=(squares,))
    down = up
    gathered = [up]
    for step in (1, 2, 3):
        up, down = shift(up, "z", Z, 1), shift(down, "z", Z, -1)
        gathered += [up, down]
    gathered.append(shift(up, "z", Z, 1))
    gathered += [shift(a, "yl", YL) for a in gathered]
    outs = kernel_call(
        update, [((Z, YL, PART, WIDTH), bf16)] * 2, squares, *factors, mine, other, *gathered, index=[z, yl], flops=2 * product
    )
    return tuple(out.reshape(ROWS, WIDTH) for out in outs)


def solution(mesh):
    fine = Mesh(mesh.devices.reshape(X, YH, CORE, Z, YL), ROW + COL)
    return jax.shard_map(
        local,
        mesh=fine,
        in_specs=(P(None, ROW), P(None, ROW), P(ROW, COL), P(ROW, COL)),
        out_specs=(P(ROW, COL), P(ROW, COL)),
        check_vma=False,
    )
```

time: 186 us -> 154 us (0.83)
  blocking collectives: 42.2 us -> 23 us
  waiting for transfers between devices: 81.5 us -> 62.5 us
  starting transfers between devices: 39.4 us -> 50.7 us
  Pallas kernels: 11.2 us -> 7.9 us
  local copies, waits for them, and re-layouts: 9.96 us -> 7.11 us
    ppermute x14 -> x36, starting transfers between devices: 15.3 us -> 47.2 us  [shift(): return lax.ppermute(a, axis, [(i, (i + by) % size) for i in range(size)])]
    all_to_all x4 -> x1, waiting for transfers between devices: 24.1 us -> 0.01 us  [local(): lax.all_to_all(copies, ('x', 'yh'), 0, 0, tiled=True)]
    all_to_all x4 -> x1, starting transfers between devices: 24.1 us -> 3.56 us  [local(): lax.all_to_all(copies, ('x', 'yh'), 0, 0, tiled=True)]
    all_to_all x1 -> x0, blocking collectives: 19.2 us -> none  [local(): lax.all_to_all(copies, ('x', 'yh'), 0, 0, tiled=True)]
    ppermute x14 -> x36, waiting for transfers between devices: 57.4 us -> 62.5 us  [shift(): return lax.ppermute(a, axis, [(i, (i + by) % size) for i in range(size)])]
    pallas_call x10 -> x7, Pallas kernels: 11.2 us -> 7.9 us  [kernel_call(): pl.pallas_call(body, out_shape=[jax.ShapeDtypeStruct(shape, dtype) for sh...]
    unnamed x26 -> x18, local copies, waits for them, and re-layouts: 9.96 us -> 7.11 us
  transfers between devices with their start and end apart: 18 -> 37, of which waited for: 15 -> 25; matrix products, arithmetic and copies ran while one was open for 0% -> 1% of each run, Pallas kernels for 2% -> 1%
where the time goes in v4:
time: 154 us; the launch traced here: 153 us
  waiting for transfers between devices  62.5 us (41%)
  starting transfers between devices  50.7 us (33%)
  blocking collectives  23 us (15%)
  Pallas kernels  7.9 us (5%)
  local copies, waits for them, and re-layouts  7.11 us (5%)
    ppermute x36, waiting for transfers between devices, shift(): return lax.ppermute(a, axis, [(i, (i + by) % size) for i in range(size)])  62.5 us
    ppermute x36, starting transfers between devices, shift(): return lax.ppermute(a, axis, [(i, (i + by) % size) for i in range(size)])  47.2 us
    all_to_all x1, blocking collectives, local(): parts = lax.all_to_all(total.reshape(chunks), ('x', 'yh'), 0, 0, tiled=True)  23 us
    pallas_call x7, Pallas kernels, kernel_call(): pl.pallas_call(body, out_shape=[jax.ShapeDtypeStruct(shape, dtype) for sh...  7.9 us
    unnamed x18, local copies, waits for them, and re-layouts  7.11 us
    all_to_all x1, starting transfers between devices, local(): lax.all_to_all(copies, ('x', 'yh'), 0, 0, tiled=True)  3.56 us
  transfers between devices with their start and end apart: 37, of which 25 were waited for; matrix products, arithmetic and copies ran while one was open for 1% of the time, Pallas kernels for 1%

profile of v4, /device:TPU:8, one launch (start us, length us, event | category | flops | bytes accessed | tf_op | source)
XLA Modules:
  0.0 153.0 jit_solution(14358035726544287433)
XLA Ops:
  6.0 2.6 %collective-permute-done.came = bf16[512,1024]{1,0:T(8,128)(2,1)S(1)} collective-permute-done((bf16[512,1024]{1,0:T(8,128)(2,1)S(1)}, bf16[512,1024]{1,0:T(8,128)(2,1)S(1)}, u32[]{:S(2)}, u32[]{:S(2)}) %collective-permute-start) | collective-permute-done | bytes 1048608 | tf_op jit(solution)/shard_map/ppermute | solution.py:37
  9.4 23.0 %all_to_all.10.parts = bf16[8,64,1024]{2,1,0:T(8,128)(2,1)S(1)} all-to-all(bf16[8,64,1024]{2,1,0:T(8,128)(2,1)S(1)} %bitcast.52), channel_id=1, replica_groups=mesh['x'=4,'yh'=2,'core'=2,'z'=8,'yl'=2] {'x','yh'}, dimensions={0} | all-to-all | bytes 2097152 | tf_op jit(solution)/shard_map/all_to_all | solution.py:156
  33.6 3.6 %all-to-all-start.1 = ((bf16[8,64,1024]{2,1,0:T(8,128)(2,1)}), bf16[8,64,1024]{2,1,0:T(8,128)(2,1)S(1)}, u32[]{:S(2)}, u32[]{:S(2)}) async-start(bf16[8,64,1024]{2,1,0:T(8,128)(2,1)} %get-tuple-element.19), calls=%async_computation.1 | async-start | bytes 2097152 | tf_op jit(solution)/shard_map/all_to_all | solution.py:158
  39.1 5.5 %collective-permute-done.1 = f32[8,128]{1,0:T(8,128)S(1)} collective-permute-done((f32[8,128]{1,0:T(8,128)S(1)}, f32[8,128]{1,0:T(8,128)S(1)}, u32[]{:S(2)}, u32[]{:S(2)}) %collective-permute-start.1) | collective-permute-done | bytes 4128 | tf_op jit(solution)/shard_map/ppermute | solution.py:37
  44.7 5.7 %collective-permute-done.2 = f32[8,128]{1,0:T(8,128)S(1)} collective-permute-done((f32[8,128]{1,0:T(8,128)S(1)}, f32[8,128]{1,0:T(8,128)S(1)}, u32[]{:S(2)}, u32[]{:S(2)}) %collective-permute-start.2) | collective-permute-done | bytes 4128 | tf_op jit(solution)/shard_map/ppermute | solution.py:37
  50.4 4.6 %collective-permute-start.3 = (f32[8,128]{1,0:T(8,128)S(1)}, f32[8,128]{1,0:T(8,128)S(1)}, u32[]{:S(2)}, u32[]{:S(2)}) collective-permute-start(f32[8,128]{1,0:T(8,128)S(1)} %add.61), channel_id=1, source_target_pairs={{0,8},{2,10},{4,12},{6,14},{8,0},{10,2},{12,4},{14,6},{1,9},{3,11}... | collective-permute-start | bytes 12296 | tf_op jit(solution)/shard_map/ppermute | solution.py:37
  55.0 2.9 %collective-permute-done.3 = f32[8,128]{1,0:T(8,128)S(1)} collective-permute-done((f32[8,128]{1,0:T(8,128)S(1)}, f32[8,128]{1,0:T(8,128)S(1)}, u32[]{:S(2)}, u32[]{:S(2)}) %collective-permute-start.3) | collective-permute-done | bytes 4128 | tf_op jit(solution)/shard_map/ppermute | solution.py:37
  59.6 2.8 %collective-permute-done.9.other = bf16[512,1024]{1,0:T(8,128)(2,1)S(1)} collective-permute-done((bf16[512,1024]{1,0:T(8,128)(2,1)}, bf16[512,1024]{1,0:T(8,128)(2,1)S(1)}, u32[]{:S(2)}, u32[]{:S(2)}) %collective-permute-start.9) | collective-permute-done | bytes 1048608 | tf_op jit(solution)/shard_map/ppermute | solution.py:37
  68.3 5.8 %collective-permute-done.13 = bf16[2,2,32,1024]{3,2,1,0:T(8,128)(2,1)S(1)} collective-permute-done((bf16[2,2,32,1024]{3,2,1,0:T(8,128)(2,1)S(1)}, bf16[2,2,32,1024]{3,2,1,0:T(8,128)(2,1)S(1)}, u32[]{:S(2)}, u32[]{:S(2)}) %collective-permute-start.13) | collective-permute-done | bytes 262176 | tf_op jit(solution)/shard_map/ppermute | solution.py:37
  77.6 2.1 %collective-permute-done.12 = bf16[2,2,32,1024]{3,2,1,0:T(8,128)(2,1)S(1)} collective-permute-done((bf16[2,2,32,1024]{3,2,1,0:T(8,128)(2,1)S(1)}, bf16[2,2,32,1024]{3,2,1,0:T(8,128)(2,1)S(1)}, u32[]{:S(2)}, u32[]{:S(2)}) %collective-permute-start.12) | collective-permute-done | bytes 262176 | tf_op jit(solution)/shard_map/ppermute | solution.py:37
  87.8 2.1 %collective-permute-start.16 = (bf16[2,32,1024]{2,1,0:T(8,128)(2,1)S(1)}, bf16[2,32,1024]{2,1,0:T(8,128)(2,1)S(1)}, u32[]{:S(2)}, u32[]{:S(2)}) collective-permute-start(bf16[2,32,1024]{2,1,0:T(8,128)(2,1)S(1)} %get-tuple-element.35), channel_id=1, source_target_pairs={{0,2},{2,4},{4,6},{6,8},{8,10},{10,12},{12,14},{14,0},{1,3},{3,5},... | collective-permute-start | bytes 393224 | tf_op jit(solution)/shard_map/ppermute | solution.py:37
  91.3 4.0 %collective-permute-done.16 = bf16[2,32,1024]{2,1,0:T(8,128)(2,1)S(1)} collective-permute-done((bf16[2,32,1024]{2,1,0:T(8,128)(2,1)S(1)}, bf16[2,32,1024]{2,1,0:T(8,128)(2,1)S(1)}, u32[]{:S(2)}, u32[]{:S(2)}) %collective-permute-start.16) | collective-permute-done | bytes 131104 | tf_op jit(solution)/shard_map/ppermute | solution.py:37
  97.8 3.0 %collective-permute-done.4 = f32[8,128]{1,0:T(8,128)S(1)} collective-permute-done((f32[8,128]{1,0:T(8,128)S(1)}, f32[8,128]{1,0:T(8,128)S(1)}, u32[]{:S(2)}, u32[]{:S(2)}) %collective-permute-start.4) | collective-permute-done | bytes 4128 | tf_op jit(solution)/shard_map/ppermute | solution.py:37
  100.8 2.1 %collective-permute-start.5 = (f32[8,128]{1,0:T(8,128)S(1)}, f32[8,128]{1,0:T(8,128)S(1)}, u32[]{:S(2)}, u32[]{:S(2)}) collective-permute-start(f32[8,128]{1,0:T(8,128)S(1)} %add.63), channel_id=1, source_target_pairs={{0,128},{64,192},{128,0},{192,64},{1,129},{65,193},{129,1},{193,65... | collective-permute-start | bytes 12296 | tf_op jit(solution)/shard_map/ppermute | solution.py:37
  103.0 3.0 %collective-permute-done.5 = f32[8,128]{1,0:T(8,128)S(1)} collective-permute-done((f32[8,128]{1,0:T(8,128)S(1)}, f32[8,128]{1,0:T(8,128)S(1)}, u32[]{:S(2)}, u32[]{:S(2)}) %collective-permute-start.5) | collective-permute-done | bytes 4128 | tf_op jit(solution)/shard_map/ppermute | solution.py:37
  107.1 3.3 %collective-permute-start.7 = (f32[8,128]{1,0:T(8,128)S(1)}, f32[8,128]{1,0:T(8,128)S(1)}, u32[]{:S(2)}, u32[]{:S(2)}) collective-permute-start(f32[8,128]{1,0:T(8,128)S(1)} %add.65), channel_id=1, source_target_pairs={{0,32},{32,0},{1,33},{33,1},{2,34},{34,2},{3,35},{35,3},{4,36},{36... | collective-permute-start | bytes 12296 | tf_op jit(solution)/shard_map/ppermute | solution.py:37
  113.5 2.3 %collective-permute-done.8 = f32[8,128]{1,0:T(8,128)S(1)} collective-permute-done((f32[8,128]{1,0:T(8,128)S(1)}, f32[8,128]{1,0:T(8,128)S(1)}, u32[]{:S(2)}, u32[]{:S(2)}) %collective-permute-start.8) | collective-permute-done | bytes 4128 | tf_op jit(solution)/shard_map/ppermute | solution.py:37
  116.2 3.0 %collective-permute-start.22 = (bf16[2,32,1024]{2,1,0:T(8,128)(2,1)S(1)}, bf16[2,32,1024]{2,1,0:T(8,128)(2,1)S(1)}, u32[]{:S(2)}, u32[]{:S(2)}) collective-permute-start(bf16[2,32,1024]{2,1,0:T(8,128)(2,1)S(1)} %shard_map.65.refs_0_), channel_id=1, source_target_pairs={{0,14},{2,0},{4,2},{6,4},{8,6},{10,8},{12,10},{14,12},{1,15},{3,1}... | collective-permute-start | bytes 393224 | tf_op jit(solution)/shard_map/ppermute | solution.py:37
  119.2 2.9 %collective-permute-done.21.refs_1_ = bf16[2,32,1024]{2,1,0:T(8,128)(2,1)S(1)} collective-permute-done((bf16[2,32,1024]{2,1,0:T(8,128)(2,1)S(1)}, bf16[2,32,1024]{2,1,0:T(8,128)(2,1)S(1)}, u32[]{:S(2)}, u32[]{:S(2)}) %collective-permute-start.21) | collective-permute-done | bytes 131104 | tf_op jit(solution)/shard_map/ppermute | solution.py:37
  122.2 3.2 %collective-permute-start.24 = (bf16[2,32,1024]{2,1,0:T(8,128)(2,1)S(1)}, bf16[2,32,1024]{2,1,0:T(8,128)(2,1)S(1)}, u32[]{:S(2)}, u32[]{:S(2)}) collective-permute-start(bf16[2,32,1024]{2,1,0:T(8,128)(2,1)S(1)} %collective-permute-done.22.refs_2_), channel_id=1, source_target_pairs={{0,14},{2,0},{4,2},{6,4},{8,6},{10,8},{12,10},{14,12},{1,15},{3,1}... | collective-permute-start | bytes 393224 | tf_op jit(solution)/shard_map/ppermute | solution.py:37
  125.4 3.5 %collective-permute-done.23.refs_3_ = bf16[2,32,1024]{2,1,0:T(8,128)(2,1)S(1)} collective-permute-done((bf16[2,32,1024]{2,1,0:T(8,128)(2,1)S(1)}, bf16[2,32,1024]{2,1,0:T(8,128)(2,1)S(1)}, u32[]{:S(2)}, u32[]{:S(2)}) %collective-permute-start.23) | collective-permute-done | bytes 131104 | tf_op jit(solution)/shard_map/ppermute | solution.py:37
  132.2 3.2 %collective-permute-start.26 = (bf16[2,32,1024]{2,1,0:T(8,128)(2,1)S(1)}, bf16[2,32,1024]{2,1,0:T(8,128)(2,1)S(1)}, u32[]{:S(2)}, u32[]{:S(2)}) collective-permute-start(bf16[2,32,1024]{2,1,0:T(8,128)(2,1)S(1)} %collective-permute-done.24.refs_4_), channel_id=1, source_target_pairs={{0,14},{2,0},{4,2},{6,4},{8,6},{10,8},{12,10},{14,12},{1,15},{3,1}... | collective-permute-start | bytes 393224 | tf_op jit(solution)/shard_map/ppermute | solution.py:37
  146.2 2.8 %collective-permute-done.34.refs_14_ = bf16[2,32,1024]{2,1,0:T(8,128)(2,1)S(1)} collective-permute-done((bf16[2,32,1024]{2,1,0:T(8,128)(2,1)S(1)}, bf16[2,32,1024]{2,1,0:T(8,128)(2,1)S(1)}, u32[]{:S(2)}, u32[]{:S(2)}) %collective-permute-start.34) | collective-permute-done | bytes 131104 | tf_op jit(solution)/shard_map/ppermute | solution.py:37
  150.4 2.6 %shard_map.66 = (bf16[8,2,32,512]{3,2,1,0:T(8,128)(2,1)}, bf16[8,2,32,512]{3,2,1,0:T(8,128)(2,1)}) custom-call(s32[2]{0:T(128)S(1)} %pad_add_fusion.at, f32[8,128]{1,0:T(8,128)S(1)} %add.67._.squares, bf16[8,2,32,512]{3,2,1,0:T(8,128)(2,1)S(1)} %bitcast.48, bf16[8,2,32,512]{3,2,1,0:T(8,128)(2,1)S(1)} %bitcast.51, bf16[512,1024]{1,0:T(8,128)(2,1)S(1)} %copy-done.1, ...), custom_call_target="tpu_custom_call" | custom-call | flops 1073741824 | bytes 5246984 | tf_op jit(solution)/shard_map/pallas_call | solution.py:47
  (90 shorter events, 52.5 us)
Async XLA Ops:
  33.6 24.9 %all-to-all-start.1 = ((bf16[8,64,1024]{2,1,0:T(8,128)(2,1)}), bf16[8,64,1024]{2,1,0:T(8,128)(2,1)S(1)}, u32[]{:S(2)}, u32[]{:S(2)}) async-start(bf16[8,64,1024]{2,1,0:T(8,128)(2,1)} %get-tuple-element.19), calls=%async_computation.1 | async-start | bytes 2097152 | tf_op jit(solution)/shard_map/all_to_all | solution.py:158
  37.1 7.5 %collective-permute-start.1 = (f32[8,128]{1,0:T(8,128)S(1)}, f32[8,128]{1,0:T(8,128)S(1)}, u32[]{:S(2)}, u32[]{:S(2)}) collective-permute-start(f32[8,128]{1,0:T(8,128)S(1)} %get-tuple-element.18), channel_id=1, source_target_pairs={{0,2},{2,4},{4,6},{6,8},{8,10},{10,12},{12,14},{14,0},{1,3},{3,5},... | collective-permute-start | bytes 12296 | tf_op jit(solution)/shard_map/ppermute | solution.py:37
  50.4 7.5 %collective-permute-start.3 = (f32[8,128]{1,0:T(8,128)S(1)}, f32[8,128]{1,0:T(8,128)S(1)}, u32[]{:S(2)}, u32[]{:S(2)}) collective-permute-start(f32[8,128]{1,0:T(8,128)S(1)} %add.61), channel_id=1, source_target_pairs={{0,8},{2,10},{4,12},{6,14},{8,0},{10,2},{12,4},{14,6},{1,9},{3,11}... | collective-permute-start | bytes 12296 | tf_op jit(solution)/shard_map/ppermute | solution.py:37
  64.9 9.2 %collective-permute-start.13 = (bf16[2,2,32,1024]{3,2,1,0:T(8,128)(2,1)S(1)}, bf16[2,2,32,1024]{3,2,1,0:T(8,128)(2,1)S(1)}, u32[]{:S(2)}, u32[]{:S(2)}) collective-permute-start(bf16[2,2,32,1024]{3,2,1,0:T(8,128)(2,1)S(1)} %get-tuple-element.28), channel_id=1, source_target_pairs={{0,1},{1,0},{2,3},{3,2},{4,5},{5,4},{6,7},{7,6},{8,9},{9,8},{10,11... | collective-permute-start | bytes 786440 | tf_op jit(solution)/shard_map/ppermute | solution.py:37
  66.3 13.4 %collective-permute-start.12 = (bf16[2,2,32,1024]{3,2,1,0:T(8,128)(2,1)S(1)}, bf16[2,2,32,1024]{3,2,1,0:T(8,128)(2,1)S(1)}, u32[]{:S(2)}, u32[]{:S(2)}) collective-permute-start(bf16[2,2,32,1024]{3,2,1,0:T(8,128)(2,1)S(1)} %get-tuple-element.26), channel_id=1, source_target_pairs={{0,1},{1,0},{2,3},{3,2},{4,5},{5,4},{6,7},{7,6},{8,9},{9,8},{10,11... | collective-permute-start | bytes 786440 | tf_op jit(solution)/shard_map/ppermute | solution.py:37
  76.3 9.2 %collective-permute-start.11 = (bf16[2,2,32,1024]{3,2,1,0:T(8,128)(2,1)S(1)}, bf16[2,2,32,1024]{3,2,1,0:T(8,128)(2,1)S(1)}, u32[]{:S(2)}, u32[]{:S(2)}) collective-permute-start(bf16[2,2,32,1024]{3,2,1,0:T(8,128)(2,1)S(1)} %get-tuple-element.24), channel_id=1, source_target_pairs={{0,1},{1,0},{2,3},{3,2},{4,5},{5,4},{6,7},{7,6},{8,9},{9,8},{10,11... | collective-permute-start | bytes 786440 | tf_op jit(solution)/shard_map/ppermute | solution.py:37
  81.5 6.3 %collective-permute-start.15 = (bf16[2,32,1024]{2,1,0:T(8,128)(2,1)S(1)}, bf16[2,32,1024]{2,1,0:T(8,128)(2,1)S(1)}, u32[]{:S(2)}, u32[]{:S(2)}) collective-permute-start(bf16[2,32,1024]{2,1,0:T(8,128)(2,1)S(1)} %get-tuple-element.37), channel_id=1, source_target_pairs={{0,2},{2,4},{4,6},{6,8},{8,10},{10,12},{12,14},{14,0},{1,3},{3,5},... | collective-permute-start | bytes 393224 | tf_op jit(solution)/shard_map/ppermute | solution.py:37
  83.5 7.9 %collective-permute-start.10 = (bf16[2,2,32,1024]{3,2,1,0:T(8,128)(2,1)S(1)}, bf16[2,2,32,1024]{3,2,1,0:T(8,128)(2,1)S(1)}, u32[]{:S(2)}, u32[]{:S(2)}) collective-permute-start(bf16[2,2,32,1024]{3,2,1,0:T(8,128)(2,1)S(1)} %get-tuple-element.21), channel_id=1, source_target_pairs={{0,1},{1,0},{2,3},{3,2},{4,5},{5,4},{6,7},{7,6},{8,9},{9,8},{10,11... | collective-permute-start | bytes 786440 | tf_op jit(solution)/shard_map/ppermute | solution.py:37
  87.8 7.5 %collective-permute-start.16 = (bf16[2,32,1024]{2,1,0:T(8,128)(2,1)S(1)}, bf16[2,32,1024]{2,1,0:T(8,128)(2,1)S(1)}, u32[]{:S(2)}, u32[]{:S(2)}) collective-permute-start(bf16[2,32,1024]{2,1,0:T(8,128)(2,1)S(1)} %get-tuple-element.35), channel_id=1, source_target_pairs={{0,2},{2,4},{4,6},{6,8},{8,10},{10,12},{12,14},{14,0},{1,3},{3,5},... | collective-permute-start | bytes 393224 | tf_op jit(solution)/shard_map/ppermute | solution.py:37
  89.9 25.9 %collective-permute-start.20 = (bf16[2,32,1024]{2,1,0:T(8,128)(2,1)S(1)}, bf16[2,32,1024]{2,1,0:T(8,128)(2,1)S(1)}, u32[]{:S(2)}, u32[]{:S(2)}) collective-permute-start(bf16[2,32,1024]{2,1,0:T(8,128)(2,1)S(1)} %get-tuple-element.34), channel_id=1, source_target_pairs={{0,14},{2,0},{4,2},{6,4},{8,6},{10,8},{12,10},{14,12},{1,15},{3,1}... | collective-permute-start | bytes 393224 | tf_op jit(solution)/shard_map/ppermute | solution.py:37
  95.3 20.5 %collective-permute-start.17 = (bf16[2,32,1024]{2,1,0:T(8,128)(2,1)S(1)}, bf16[2,32,1024]{2,1,0:T(8,128)(2,1)S(1)}, u32[]{:S(2)}, u32[]{:S(2)}) collective-permute-start(bf16[2,32,1024]{2,1,0:T(8,128)(2,1)S(1)} %fusion.11), channel_id=1, source_target_pairs={{0,2},{2,4},{4,6},{6,8},{8,10},{10,12},{12,14},{14,0},{1,3},{3,5},... | collective-permute-start | bytes 393224 | tf_op jit(solution)/shard_map/ppermute | solution.py:37
  122.2 6.7 %collective-permute-start.23 = (bf16[2,32,1024]{2,1,0:T(8,128)(2,1)S(1)}, bf16[2,32,1024]{2,1,0:T(8,128)(2,1)S(1)}, u32[]{:S(2)}, u32[]{:S(2)}) collective-permute-start(bf16[2,32,1024]{2,1,0:T(8,128)(2,1)S(1)} %collective-permute-done.21.refs_1_), channel_id=1, source_target_pairs={{0,2},{2,4},{4,6},{6,8},{8,10},{10,12},{12,14},{14,0},{1,3},{3,5},... | collective-permute-start | bytes 393224 | tf_op jit(solution)/shard_map/ppermute | solution.py:37
  122.2 10.1 %collective-permute-start.24 = (bf16[2,32,1024]{2,1,0:T(8,128)(2,1)S(1)}, bf16[2,32,1024]{2,1,0:T(8,128)(2,1)S(1)}, u32[]{:S(2)}, u32[]{:S(2)}) collective-permute-start(bf16[2,32,1024]{2,1,0:T(8,128)(2,1)S(1)} %collective-permute-done.22.refs_2_), channel_id=1, source_target_pairs={{0,14},{2,0},{4,2},{6,4},{8,6},{10,8},{12,10},{14,12},{1,15},{3,1}... | collective-permute-start | bytes 393224 | tf_op jit(solution)/shard_map/ppermute | solution.py:37
  128.9 7.3 %collective-permute-start.25 = (bf16[2,32,1024]{2,1,0:T(8,128)(2,1)S(1)}, bf16[2,32,1024]{2,1,0:T(8,128)(2,1)S(1)}, u32[]{:S(2)}, u32[]{:S(2)}) collective-permute-start(bf16[2,32,1024]{2,1,0:T(8,128)(2,1)S(1)} %collective-permute-done.23.refs_3_), channel_id=1, source_target_pairs={{0,2},{2,4},{4,6},{6,8},{8,10},{10,12},{12,14},{14,0},{1,3},{3,5},... | collective-permute-start | bytes 393224 | tf_op jit(solution)/shard_map/ppermute | solution.py:37
  128.9 7.3 %collective-permute-start.28 = (bf16[2,32,1024]{2,1,0:T(8,128)(2,1)S(1)}, bf16[2,32,1024]{2,1,0:T(8,128)(2,1)S(1)}, u32[]{:S(2)}, u32[]{:S(2)}) collective-permute-start(bf16[2,32,1024]{2,1,0:T(8,128)(2,1)S(1)} %shard_map.65.refs_0_), channel_id=1, source_target_pairs={{0,1},{1,0},{2,3},{3,2},{4,5},{5,4},{6,7},{7,6},{8,9},{9,8},{10,11... | collective-permute-start | bytes 393224 | tf_op jit(solution)/shard_map/ppermute | solution.py:37
  130.2 7.9 %collective-permute-start.30 = (bf16[2,32,1024]{2,1,0:T(8,128)(2,1)S(1)}, bf16[2,32,1024]{2,1,0:T(8,128)(2,1)S(1)}, u32[]{:S(2)}, u32[]{:S(2)}) collective-permute-start(bf16[2,32,1024]{2,1,0:T(8,128)(2,1)S(1)} %collective-permute-done.22.refs_2_), channel_id=1, source_target_pairs={{0,1},{1,0},{2,3},{3,2},{4,5},{5,4},{6,7},{7,6},{8,9},{9,8},{10,11... | collective-permute-start | bytes 393224 | tf_op jit(solution)/shard_map/ppermute | solution.py:37
  131.0 9.9 %collective-permute-start.29 = (bf16[2,32,1024]{2,1,0:T(8,128)(2,1)S(1)}, bf16[2,32,1024]{2,1,0:T(8,128)(2,1)S(1)}, u32[]{:S(2)}, u32[]{:S(2)}) collective-permute-start(bf16[2,32,1024]{2,1,0:T(8,128)(2,1)S(1)} %collective-permute-done.21.refs_1_), channel_id=1, source_target_pairs={{0,1},{1,0},{2,3},{3,2},{4,5},{5,4},{6,7},{7,6},{8,9},{9,8},{10,11... | collective-permute-start | bytes 393224 | tf_op jit(solution)/shard_map/ppermute | solution.py:37
  132.2 10.0 %collective-permute-start.26 = (bf16[2,32,1024]{2,1,0:T(8,128)(2,1)S(1)}, bf16[2,32,1024]{2,1,0:T(8,128)(2,1)S(1)}, u32[]{:S(2)}, u32[]{:S(2)}) collective-permute-start(bf16[2,32,1024]{2,1,0:T(8,128)(2,1)S(1)} %collective-permute-done.24.refs_4_), channel_id=1, source_target_pairs={{0,14},{2,0},{4,2},{6,4},{8,6},{10,8},{12,10},{14,12},{1,15},{3,1}... | collective-permute-start | bytes 393224 | tf_op jit(solution)/shard_map/ppermute | solution.py:37
  136.2 6.8 %collective-permute-start.27 = (bf16[2,32,1024]{2,1,0:T(8,128)(2,1)S(1)}, bf16[2,32,1024]{2,1,0:T(8,128)(2,1)S(1)}, u32[]{:S(2)}, u32[]{:S(2)}) collective-permute-start(bf16[2,32,1024]{2,1,0:T(8,128)(2,1)S(1)} %collective-permute-done.25.refs_5_), channel_id=1, source_target_pairs={{0,2},{2,4},{4,6},{6,8},{8,10},{10,12},{12,14},{14,0},{1,3},{3,5},... | collective-permute-start | bytes 393224 | tf_op jit(solution)/shard_map/ppermute | solution.py:37
  136.2 8.1 %collective-permute-start.32 = (bf16[2,32,1024]{2,1,0:T(8,128)(2,1)S(1)}, bf16[2,32,1024]{2,1,0:T(8,128)(2,1)S(1)}, u32[]{:S(2)}, u32[]{:S(2)}) collective-permute-start(bf16[2,32,1024]{2,1,0:T(8,128)(2,1)S(1)} %collective-permute-done.24.refs_4_), channel_id=1, source_target_pairs={{0,1},{1,0},{2,3},{3,2},{4,5},{5,4},{6,7},{7,6},{8,9},{9,8},{10,11... | collective-permute-start | bytes 393224 | tf_op jit(solution)/shard_map/ppermute | solution.py:37
  138.1 8.1 %collective-permute-start.31 = (bf16[2,32,1024]{2,1,0:T(8,128)(2,1)S(1)}, bf16[2,32,1024]{2,1,0:T(8,128)(2,1)S(1)}, u32[]{:S(2)}, u32[]{:S(2)}) collective-permute-start(bf16[2,32,1024]{2,1,0:T(8,128)(2,1)S(1)} %collective-permute-done.23.refs_3_), channel_id=1, source_target_pairs={{0,1},{1,0},{2,3},{3,2},{4,5},{5,4},{6,7},{7,6},{8,9},{9,8},{10,11... | collective-permute-start | bytes 393224 | tf_op jit(solution)/shard_map/ppermute | solution.py:37
  140.9 8.1 %collective-permute-start.33 = (bf16[2,32,1024]{2,1,0:T(8,128)(2,1)S(1)}, bf16[2,32,1024]{2,1,0:T(8,128)(2,1)S(1)}, u32[]{:S(2)}, u32[]{:S(2)}) collective-permute-start(bf16[2,32,1024]{2,1,0:T(8,128)(2,1)S(1)} %collective-permute-done.25.refs_5_), channel_id=1, source_target_pairs={{0,1},{1,0},{2,3},{3,2},{4,5},{5,4},{6,7},{7,6},{8,9},{9,8},{10,11... | collective-permute-start | bytes 393224 | tf_op jit(solution)/shard_map/ppermute | solution.py:37
  142.2 6.8 %collective-permute-start.34 = (bf16[2,32,1024]{2,1,0:T(8,128)(2,1)S(1)}, bf16[2,32,1024]{2,1,0:T(8,128)(2,1)S(1)}, u32[]{:S(2)}, u32[]{:S(2)}) collective-permute-start(bf16[2,32,1024]{2,1,0:T(8,128)(2,1)S(1)} %collective-permute-done.26.refs_6_), channel_id=1, source_target_pairs={{0,1},{1,0},{2,3},{3,2},{4,5},{5,4},{6,7},{7,6},{8,9},{9,8},{10,11... | collective-permute-start | bytes 393224 | tf_op jit(solution)/shard_map/ppermute | solution.py:37
  142.9 7.5 %collective-permute-start.35 = (bf16[2,32,1024]{2,1,0:T(8,128)(2,1)S(1)}, bf16[2,32,1024]{2,1,0:T(8,128)(2,1)S(1)}, u32[]{:S(2)}, u32[]{:S(2)}) collective-permute-start(bf16[2,32,1024]{2,1,0:T(8,128)(2,1)S(1)} %collective-permute-done.27.refs_7_), channel_id=1, source_target_pairs={{0,1},{1,0},{2,3},{3,2},{4,5},{5,4},{6,7},{7,6},{8,9},{9,8},{10,11... | collective-permute-start | bytes 393224 | tf_op jit(solution)/shard_map/ppermute | solution.py:37
  (22 other events, 74.5 us)

commit v5 on v4

v5 whole, which is shorter than its diff:
```python
import jax
import jax.numpy as jnp
from jax import lax
from jax.experimental import pallas as pl
from jax.experimental.pallas import tpu as pltpu
from jax.sharding import Mesh, PartitionSpec as P

D = 8192
TOKENS = 1024
X, YH, CORE, Z, YL = 4, 2, 2, 8, 2
ROW = ("x", "yh", "core")
COL = ("z", "yl")
ROWS = D // (X * YH * CORE)
WIDTH = D // (Z * YL)
HALF = TOKENS // CORE
EXTRA = 128
PART = ROWS // (Z * YL)

REDUCE = (4, -3, 3, -2, 2, -1, 1, 0)
PLACES = ((0, 0), (1, 0), (1, 1), (2, 0), (2, 1), (3, 0), (3, 1), (4, 0))
GATHER = (0, -1, 1, -2, 2, -3, 3, -4)

keep_scale = 1.45
gram_scale = 0.5

f32 = jnp.float32
bf16 = jnp.bfloat16


def dot(a, b):
    return jnp.dot(a, b, preferred_element_type=f32)


def dot_t(a, b):
    return lax.dot_general(a, b, (((1,), (1,)), ((), ())), preferred_element_type=f32)


def shift(a, axis, size, by=1):
    return lax.ppermute(a, axis, [(i, (i + by) % size) for i in range(size)])


def kernel_call(body, outs, *args, index=None, flops=0, memory=pltpu.VMEM, scratch=(), room=48):
    specs = [pl.BlockSpec(memory_space=memory)] * len(args)
    if index is not None:
        specs = [pl.BlockSpec(memory_space=pltpu.SMEM)] + specs
        args = (jnp.stack([i.astype(jnp.int32) for i in index]),) + args
    size = sum(a.size * a.dtype.itemsize for a in args)
    return pl.pallas_call(
        body,
        out_shape=[jax.ShapeDtypeStruct(shape, dtype) for shape, dtype in outs],
        in_specs=specs,
        out_specs=[pl.BlockSpec(memory_space=pltpu.VMEM)] * len(outs),
        scratch_shapes=scratch,
        compiler_params=pltpu.CompilerParams(vmem_limit_bytes=room * 2**20),
        cost_estimate=pl.CostEstimate(flops=flops, bytes_accessed=size, transcendentals=0),
    )(*args)


def projected(which, given, bufs, sems):
    rows = pl.ds(pl.multiple_of(which[0] * HALF, HALF), HALF)
    refs = (given[0].at[rows], given[2], given[1].at[rows], given[3])
    copies = [pltpu.make_async_copy(r, buf, sems.at[i]) for i, (r, buf) in enumerate(zip(refs, bufs))]
    for copy in copies:
        copy.start()
    for f in range(2):
        copies[2 * f].wait()
        copies[2 * f + 1].wait()
        yield f, dot(bufs[2 * f][...], bufs[2 * f + 1][...])


def project(which, acts, cots, act_factor, grad_factor, out, *scratch):
    for f, total in projected(which, (acts, cots, act_factor, grad_factor), scratch[:4], scratch[4]):
        out[:, factor_columns(f)] = total.astype(out.dtype)


def project_sum(parts, copies):
    total = parts[0].astype(f32)
    for k in range(1, X * YH):
        total = total + parts[k].astype(f32)
    own = total.astype(bf16)
    for k in range(X * YH):
        copies[k] = own


def factor_columns(f):
    return slice(f * WIDTH, (f + 1) * WIDTH)


def image_rows(factor, z, side, mine, other, f):
    rows = [factor[pl.ds(lax.rem(z + (e + Z), Z), 1), pl.ds(side, 1)].reshape(PART, WIDTH) for e in REDUCE]
    rows = jnp.concatenate(rows, axis=0)
    return (
        dot_t(rows, mine[:, factor_columns(f)]),
        dot_t(rows, other[:, factor_columns(f)]),
    )


def image_away(at, act_factor, grad_factor, mine, other, *outs):
    for f, factor in enumerate((act_factor, grad_factor)):
        first, second = image_rows(factor, at[0], 1 - at[1], mine, other, f)
        for n, (group, k) in enumerate(PLACES):
            rows = slice(n * PART, (n + 1) * PART)
            outs[group][k, f, :, :HALF] = first[rows].astype(bf16)
            outs[group][k, f, :, HALF:] = second[rows].astype(bf16)


def image_own(at, act_factor, grad_factor, mine, other, *outs):
    for f, factor in enumerate((act_factor, grad_factor)):
        first, second = image_rows(factor, at[0], at[1], mine, other, f)
        for k in range(Z):
            rows = slice(k * PART, (k + 1) * PART)
            outs[k][f, :, :HALF] = first[rows]
            outs[k][f, :, HALF:] = second[rows]
        square = sum(jnp.square(part[:, factor_columns(f)].astype(f32)) for part in (mine, other))
        outs[Z][f : f + 1] = jnp.sum(square, axis=0, keepdims=True)


def last_sum(own, away, up, down, squares, out):
    total = own[...] + away[0].astype(f32) + up[...].astype(f32) + down[...].astype(f32)
    out[:, :, :TOKENS] = total.astype(bf16)
    row = lax.broadcasted_iota(jnp.int32, (PART, EXTRA), 0)
    for f in range(2):
        rest = jnp.full((PART, EXTRA), jnp.sum(squares[f : f + 1]))
        parts = jnp.zeros((PART, EXTRA), f32)
        for k in range(3):
            part = rest.astype(bf16).astype(f32)
            parts = jnp.where(row == k, part, parts)
            rest = rest - part
        out[f, :, TOKENS:] = parts.astype(bf16)


def changes(chunks, mine, other, f):
    image = jnp.concatenate([c[f, :, :TOKENS] for c in chunks], axis=0)
    change = dot(image[:, :HALF], mine[:, factor_columns(f)])
    return change + dot(image[:, HALF:], other[:, factor_columns(f)])


def own_changes(mine, other, *refs):
    chunks, (out, squares) = refs[:Z], refs[Z:]
    for f in range(2):
        out[f] = changes(chunks, mine, other, f)
        squares[f : f + 1] = share_sum(chunks, f)


def share_sum(chunks, f):
    return sum(jnp.sum(c[f, :, TOKENS:].astype(f32), axis=0, keepdims=True) for c in chunks)


def update(at, act_factor, grad_factor, mine, other, own_change, squares, *refs):
    chunks, outs = refs[:Z], refs[Z:]
    for f, (factor, out) in enumerate(((act_factor, outs[0]), (grad_factor, outs[1]))):
        total = squares[1 - f : 2 - f] + share_sum(chunks, 1 - f)
        scale = total[:, :1] / (TOKENS * D) * (gram_scale / TOKENS)
        for side in range(YL):
            change = own_change[f] if side == 0 else changes(chunks, mine, other, f)
            half = pl.ds(at[1] if side == 0 else 1 - at[1], 1)
            for k, e in enumerate(GATHER):
                place = (pl.ds(lax.rem(at[0] + (e + Z), Z), 1), half)
                kept = factor[place].reshape(PART, WIDTH).astype(f32)
                new = keep_scale * kept - scale * change[k * PART : (k + 1) * PART]
                out[place] = new.astype(bf16).reshape(1, 1, PART, WIDTH)


def after(a, *others):
    for other in others:
        a = a + jnp.minimum(jnp.abs(other), 0)
    return a


def local(activations, cotangents, act_factor, grad_factor):
    core, z, yl = (lax.axis_index(name) for name in ("core", "z", "yl"))
    product = 4 * HALF * ROWS * WIDTH
    given = (activations, cotangents, act_factor, grad_factor)
    scratch = [pltpu.VMEM((HALF, ROWS), bf16), pltpu.VMEM((ROWS, WIDTH), bf16)] * 2
    scratch.append(pltpu.SemaphoreType.DMA((4,)))
    setup = dict(flops=product, memory=pltpu.HBM, scratch=scratch, room=58)
    (away,) = kernel_call(project, [((HALF, 2 * WIDTH), bf16)], *given, index=[1 - core], **setup)
    came = shift(away, "core", CORE)
    (total,) = kernel_call(project, [((HALF, 2 * WIDTH), f32)], *given, index=[core], **setup)
    total = (total + came.astype(f32)).astype(bf16)
    group = X * YH
    chunks = (group, HALF // group, 2 * WIDTH)
    parts = lax.all_to_all(total.reshape(chunks), ("x", "yh"), 0, 0, tiled=True)
    (copies,) = kernel_call(project_sum, [(chunks, bf16)], parts)
    mine = lax.all_to_all(copies, ("x", "yh"), 0, 0, tiled=True).reshape(HALF, 2 * WIDTH)
    other = shift(mine, "core", CORE)

    factors = [f.reshape(Z, YL, PART, WIDTH) for f in (act_factor, grad_factor)]
    shape = (2, PART, TOKENS)
    sent = [((sum(g == group for g, _ in PLACES),) + shape, bf16) for group in range(5)]
    away = kernel_call(image_away, sent, *factors, mine, other, index=[z, yl], flops=product)
    away = [shift(a, "yl", YL) for a in away]
    *own, squares = kernel_call(
        image_own, [(shape, f32)] * Z + [((2, WIDTH), f32)], *factors, mine, other, index=[z, yl], flops=product
    )
    up = own[0] + away[0][0].astype(f32)
    down = own[1] + away[1][0].astype(f32)
    for step in (1, 2, 3):
        up = shift(up.astype(bf16), "z", Z, 1)
        up = own[2 * step] + away[step][1].astype(f32) + up.astype(f32)
        down = shift(down.astype(bf16), "z", Z, -1)
        if step < 3:
            down = own[2 * step + 1] + away[step + 1][0].astype(f32) + down.astype(f32)
    up = shift(up.astype(bf16), "z", Z, 1)
    shape = (2, PART, TOKENS + EXTRA)
    (up,) = kernel_call(last_sum, [(shape, bf16)], own[7], away[4], up, down, squares)

    down = up
    held, crossed = [up], [shift(up, "yl", YL)]
    for step in (1, 2, 3):
        if step == 3:
            up, down = after(up, crossed[0]), after(down, crossed[0])
        up, down = shift(up, "z", Z, 1), shift(down, "z", Z, -1)
        held += [up, down]
        crossed += [shift(up, "yl", YL), shift(down, "yl", YL)]
    up = shift(after(up, crossed[1], crossed[2]), "z", Z, 1)
    held.append(up)
    crossed.append(shift(up, "yl", YL))
    changed, squares = kernel_call(
        own_changes, [((2, ROWS // YL, WIDTH), f32), ((2, EXTRA), f32)], mine, other, *held, flops=product
    )
    outs = kernel_call(
        update, [((Z, YL, PART, WIDTH), bf16)] * 2, *factors, mine, other, changed, squares, *crossed, index=[z, yl], flops=product
    )
    return tuple(out.reshape(ROWS, WIDTH) for out in outs)


def solution(mesh):
    fine = Mesh(mesh.devices.reshape(X, YH, CORE, Z, YL), ROW + COL)
    return jax.shard_map(
        local,
        mesh=fine,
        in_specs=(P(None, ROW), P(None, ROW), P(ROW, COL), P(ROW, COL)),
        out_specs=(P(ROW, COL), P(ROW, COL)),
        check_vma=False,
    )
```

time: 154 us -> 130 us (0.84)
  waiting for transfers between devices: 62.5 us -> 35.4 us
  blocking collectives: 23 us -> 42.8 us
  starting transfers between devices: 50.7 us -> 35.6 us
  local copies, waits for them, and re-layouts: 7.11 us -> 0.01 us
  Pallas kernels: 7.9 us -> 12.9 us
    ppermute x36 -> x29, waiting for transfers between devices: 62.5 us -> 35.4 us  [shift(): return lax.ppermute(a, axis, [(i, (i + by) % size) for i in range(size)])]
    all_to_all x0 -> x1, blocking collectives: none -> 19.4 us  [local(): lax.all_to_all(copies, ('x', 'yh'), 0, 0, tiled=True)]
    ppermute x36 -> x29, starting transfers between devices: 47.2 us -> 35.6 us  [shift(): return lax.ppermute(a, axis, [(i, (i + by) % size) for i in range(size)])]
    unnamed x18 -> x4, local copies, waits for them, and re-layouts: 7.11 us -> 0.01 us
    pallas_call x7 -> x8, Pallas kernels: 7.9 us -> 12.9 us  [kernel_call(): pl.pallas_call(body, out_shape=[jax.ShapeDtypeStruct(shape, dtype) for sh...]
    all_to_all x1 -> x0, starting transfers between devices: 3.56 us -> none  [local(): lax.all_to_all(copies, ('x', 'yh'), 0, 0, tiled=True)]
    convert_element_type x0 -> x1, other arithmetic: none -> 1.92 us  [local(): total = (total + came.astype(f32)).astype(bf16)]
  transfers between devices with their start and end apart: 37 -> 29, of which waited for: 25 -> 17; matrix products, arithmetic and copies ran while one was open for 1% -> 0% of each run, Pallas kernels for 1% -> 5%
where the time goes in v5:
time: 130 us
  blocking collectives  42.8 us (33%)
  starting transfers between devices  35.6 us (27%)
  waiting for transfers between devices  35.4 us (27%)
  Pallas kernels  12.9 us (10%)
  other arithmetic  2.38 us (2%)
    ppermute x29, starting transfers between devices, shift(): return lax.ppermute(a, axis, [(i, (i + by) % size) for i in range(size)])  35.6 us
    ppermute x29, waiting for transfers between devices, shift(): return lax.ppermute(a, axis, [(i, (i + by) % size) for i in range(size)])  35.4 us
    all_to_all x1, blocking collectives, local(): parts = lax.all_to_all(total.reshape(chunks), ('x', 'yh'), 0, 0, tiled=True)  23.3 us
    all_to_all x1, blocking collectives, local(): lax.all_to_all(copies, ('x', 'yh'), 0, 0, tiled=True)  19.4 us
    pallas_call x8, Pallas kernels, kernel_call(): pl.pallas_call(body, out_shape=[jax.ShapeDtypeStruct(shape, dtype) for sh...  12.9 us
  transfers between devices with their start and end apart: 29, of which 17 were waited for; matrix products, arithmetic and copies ran while one was open for 0% of the time, Pallas kernels for 5%

profile of v5, /device:TPU:8, one launch (start us, length us, event | category | flops | bytes accessed | tf_op | source)
XLA Modules:
  0.0 129.8 jit_solution(3260910336787400217)
XLA Ops:
  0.6 3.1 %shard_map.60 = bf16[512,1024]{1,0:T(8,128)(2,1)} custom-call(s32[1]{0:T(128)} %bitcast.5.which, bf16[1024,512]{1,0:T(8,128)(2,1)} %acts.3, bf16[1024,512]{1,0:T(8,128)(2,1)} %cots.3, bf16[512,512]{1,0:T(8,128)(2,1)} %act_factor.3, bf16[512,512]{1,0:T(8,128)(2,1)} %grad_factor.3), custom_call_target="tpu_custom_call" | custom-call | flops 536870912 | bytes 3145732 | tf_op jit(solution)/shard_map/pallas_call | solution.py:48
  3.8 3.5 %shard_map.59 = f32[512,1024]{1,0:T(8,128)} custom-call(s32[1]{0:T(128)} %bitcast.4.which, bf16[1024,512]{1,0:T(8,128)(2,1)} %acts.3, bf16[1024,512]{1,0:T(8,128)(2,1)} %cots.3, bf16[512,512]{1,0:T(8,128)(2,1)} %act_factor.3, bf16[512,512]{1,0:T(8,128)(2,1)} %grad_factor.3), custom_call_target="tpu_custom_call" | custom-call | flops 536870912 | bytes 3145732 | tf_op jit(solution)/shard_map/pallas_call | solution.py:48
  7.3 1.9 %add_convert_fusion = bf16[512,1024]{1,0:T(8,128)(2,1)S(1)} fusion(f32[512,1024]{1,0:T(8,128)} %shard_map.59, bf16[512,1024]{1,0:T(8,128)(2,1)S(1)} %collective-permute-done), kind=kLoop, calls=%fused_computation | loop fusion | flops 1572864 | bytes 4194304 | tf_op jit(solution)/shard_map/convert_element_type | solution.py:180
  9.3 23.3 %all_to_all.10.parts = bf16[8,64,1024]{2,1,0:T(8,128)(2,1)S(1)} all-to-all(bf16[8,64,1024]{2,1,0:T(8,128)(2,1)S(1)} %bitcast.54), channel_id=1, replica_groups=mesh['x'=4,'yh'=2,'core'=2,'z'=8,'yl'=2] {'x','yh'}, dimensions={0} | all-to-all | bytes 2097152 | tf_op jit(solution)/shard_map/all_to_all | solution.py:183
  32.8 19.4 %all_to_all.11 = bf16[8,64,1024]{2,1,0:T(8,128)(2,1)S(1)} all-to-all(bf16[8,64,1024]{2,1,0:T(8,128)(2,1)S(1)} %shard_map.61), channel_id=1, replica_groups=mesh['x'=4,'yh'=2,'core'=2,'z'=8,'yl'=2] {'x','yh'}, dimensions={0} | all-to-all | bytes 2097152 | tf_op jit(solution)/shard_map/all_to_all | solution.py:185
  52.3 2.6 %collective-permute-done.1.other = bf16[512,1024]{1,0:T(8,128)(2,1)S(1)} collective-permute-done((bf16[512,1024]{1,0:T(8,128)(2,1)S(1)}, bf16[512,1024]{1,0:T(8,128)(2,1)S(1)}, u32[]{:S(2)}, u32[]{:S(2)}) %collective-permute-start.1) | collective-permute-done | bytes 1048608 | tf_op jit(solution)/shard_map/ppermute | solution.py:39
  58.2 1.8 %shard_map.62 = (f32[2,32,1024]{2,1,0:T(8,128)S(1)}, f32[2,32,1024]{2,1,0:T(8,128)S(1)}, f32[2,32,1024]{2,1,0:T(8,128)S(1)}, f32[2,32,1024]{2,1,0:T(8,128)S(1)},...) custom-call(s32[2]{0:T(128)S(1)} %pad_add_fusion.at, ...), custom_call_target="tpu_custom_call" | custom-call | flops 536870912 | bytes 3145736 | tf_op jit(solution)/shard_map/pallas_call | solution.py:48
  60.0 2.5 %collective-permute-done.6 = bf16[1,2,32,1024]{3,2,1,0:T(8,128)(2,1)S(1)} collective-permute-done((bf16[1,2,32,1024]{3,2,1,0:T(8,128)(2,1)S(1)}, bf16[1,2,32,1024]{3,2,1,0:T(8,128)(2,1)S(1)}, u32[]{:S(2)}, u32[]{:S(2)}) %collective-permute-start.6) | collective-permute-done | bytes 131104 | tf_op jit(solution)/shard_map/ppermute | solution.py:39
  62.6 2.0 %collective-permute-start.7 = (bf16[2,32,1024]{2,1,0:T(8,128)(2,1)S(1)}, bf16[2,32,1024]{2,1,0:T(8,128)(2,1)S(1)}, u32[]{:S(2)}, u32[]{:S(2)}) collective-permute-start(bf16[2,32,1024]{2,1,0:T(8,128)(2,1)S(1)} %fusion.5), channel_id=1, source_target_pairs={{0,2},{2,4},{4,6},{6,8},{8,10},{10,12},{12,14},{14,0},{1,3},{3,5},... | collective-permute-start | bytes 393224 | tf_op jit(solution)/shard_map/ppermute | solution.py:39
  65.9 5.5 %collective-permute-done.7 = bf16[2,32,1024]{2,1,0:T(8,128)(2,1)S(1)} collective-permute-done((bf16[2,32,1024]{2,1,0:T(8,128)(2,1)S(1)}, bf16[2,32,1024]{2,1,0:T(8,128)(2,1)S(1)}, u32[]{:S(2)}, u32[]{:S(2)}) %collective-permute-start.7) | collective-permute-done | bytes 131104 | tf_op jit(solution)/shard_map/ppermute | solution.py:39
  71.6 2.6 %collective-permute-start.11 = (bf16[2,32,1024]{2,1,0:T(8,128)(2,1)S(1)}, bf16[2,32,1024]{2,1,0:T(8,128)(2,1)S(1)}, u32[]{:S(2)}, u32[]{:S(2)}) collective-permute-start(bf16[2,32,1024]{2,1,0:T(8,128)(2,1)S(1)} %get-tuple-element.42), channel_id=1, source_target_pairs={{0,14},{2,0},{4,2},{6,4},{8,6},{10,8},{12,10},{14,12},{1,15},{3,1}... | collective-permute-start | bytes 393224 | tf_op jit(solution)/shard_map/ppermute | solution.py:39
  76.7 3.7 %collective-permute-done.8 = bf16[2,32,1024]{2,1,0:T(8,128)(2,1)S(1)} collective-permute-done((bf16[2,32,1024]{2,1,0:T(8,128)(2,1)S(1)}, bf16[2,32,1024]{2,1,0:T(8,128)(2,1)S(1)}, u32[]{:S(2)}, u32[]{:S(2)}) %collective-permute-start.8) | collective-permute-done | bytes 131104 | tf_op jit(solution)/shard_map/ppermute | solution.py:39
  80.6 2.0 %collective-permute-start.9 = (bf16[2,32,1024]{2,1,0:T(8,128)(2,1)S(1)}, bf16[2,32,1024]{2,1,0:T(8,128)(2,1)S(1)}, u32[]{:S(2)}, u32[]{:S(2)}) collective-permute-start(bf16[2,32,1024]{2,1,0:T(8,128)(2,1)S(1)} %get-tuple-element.41), channel_id=1, source_target_pairs={{0,2},{2,4},{4,6},{6,8},{8,10},{10,12},{12,14},{14,0},{1,3},{3,5},... | collective-permute-start | bytes 393224 | tf_op jit(solution)/shard_map/ppermute | solution.py:39
  86.9 2.1 %collective-permute-start.10 = (bf16[2,32,1024]{2,1,0:T(8,128)(2,1)S(1)}, bf16[2,32,1024]{2,1,0:T(8,128)(2,1)S(1)}, u32[]{:S(2)}, u32[]{:S(2)}) collective-permute-start(bf16[2,32,1024]{2,1,0:T(8,128)(2,1)S(1)} %get-tuple-element.39), channel_id=1, source_target_pairs={{0,2},{2,4},{4,6},{6,8},{8,10},{10,12},{12,14},{14,0},{1,3},{3,5},... | collective-permute-start | bytes 393224 | tf_op jit(solution)/shard_map/ppermute | solution.py:39
  90.4 3.9 %collective-permute-done.10.up = bf16[2,32,1024]{2,1,0:T(8,128)(2,1)S(1)} collective-permute-done((bf16[2,32,1024]{2,1,0:T(8,128)(2,1)S(1)}, bf16[2,32,1024]{2,1,0:T(8,128)(2,1)S(1)}, u32[]{:S(2)}, u32[]{:S(2)}) %collective-permute-start.10) | collective-permute-done | bytes 131104 | tf_op jit(solution)/shard_map/ppermute | solution.py:39
  95.6 2.4 %collective-permute-start.15 = (bf16[2,32,1152]{2,1,0:T(8,128)(2,1)S(1)}, bf16[2,32,1152]{2,1,0:T(8,128)(2,1)S(1)}, u32[]{:S(2)}, u32[]{:S(2)}) collective-permute-start(bf16[2,32,1152]{2,1,0:T(8,128)(2,1)S(1)} %shard_map.64.refs_0_), channel_id=1, source_target_pairs={{0,14},{2,0},{4,2},{6,4},{8,6},{10,8},{12,10},{14,12},{1,15},{3,1}... | collective-permute-start | bytes 442376 | tf_op jit(solution)/shard_map/ppermute | solution.py:39
  99.3 2.4 %collective-permute-done.14.refs_1_ = bf16[2,32,1152]{2,1,0:T(8,128)(2,1)S(1)} collective-permute-done((bf16[2,32,1152]{2,1,0:T(8,128)(2,1)S(1)}, bf16[2,32,1152]{2,1,0:T(8,128)(2,1)S(1)}, u32[]{:S(2)}, u32[]{:S(2)}) %collective-permute-start.14) | collective-permute-done | bytes 147488 | tf_op jit(solution)/shard_map/ppermute | solution.py:39
  101.7 3.2 %collective-permute-start.17 = (bf16[2,32,1152]{2,1,0:T(8,128)(2,1)S(1)}, bf16[2,32,1152]{2,1,0:T(8,128)(2,1)S(1)}, u32[]{:S(2)}, u32[]{:S(2)}) collective-permute-start(bf16[2,32,1152]{2,1,0:T(8,128)(2,1)S(1)} %collective-permute-done.15.refs_2_), channel_id=1, source_target_pairs={{0,14},{2,0},{4,2},{6,4},{8,6},{10,8},{12,10},{14,12},{1,15},{3,1}... | collective-permute-start | bytes 442376 | tf_op jit(solution)/shard_map/ppermute | solution.py:39
  108.6 3.0 %collective-permute-start.20 = (bf16[2,32,1152]{2,1,0:T(8,128)(2,1)S(1)}, bf16[2,32,1152]{2,1,0:T(8,128)(2,1)S(1)}, u32[]{:S(2)}, u32[]{:S(2)}) collective-permute-start(bf16[2,32,1152]{2,1,0:T(8,128)(2,1)S(1)} %get-tuple-element.44), channel_id=1, source_target_pairs={{0,14},{2,0},{4,2},{6,4},{8,6},{10,8},{12,10},{14,12},{1,15},{3,1}... | collective-permute-start | bytes 442376 | tf_op jit(solution)/shard_map/ppermute | solution.py:39
  111.6 2.2 %collective-permute-done.22.refs_2_ = bf16[2,32,1152]{2,1,0:T(8,128)(2,1)S(1)} collective-permute-done((bf16[2,32,1152]{2,1,0:T(8,128)(2,1)S(1)}, bf16[2,32,1152]{2,1,0:T(8,128)(2,1)S(1)}, u32[]{:S(2)}, u32[]{:S(2)}) %collective-permute-start.22) | collective-permute-done | bytes 147488 | tf_op jit(solution)/shard_map/ppermute | solution.py:39
  119.0 2.2 %collective-permute-done.23.refs_7_ = bf16[2,32,1152]{2,1,0:T(8,128)(2,1)S(1)} collective-permute-done((bf16[2,32,1152]{2,1,0:T(8,128)(2,1)S(1)}, bf16[2,32,1152]{2,1,0:T(8,128)(2,1)S(1)}, u32[]{:S(2)}, u32[]{:S(2)}) %collective-permute-start.23) | collective-permute-done | bytes 147488 | tf_op jit(solution)/shard_map/ppermute | solution.py:39
  124.3 1.6 %collective-permute-done.27.refs_6_ = bf16[2,32,1152]{2,1,0:T(8,128)(2,1)S(1)} collective-permute-done((bf16[2,32,1152]{2,1,0:T(8,128)(2,1)S(1)}, bf16[2,32,1152]{2,1,0:T(8,128)(2,1)S(1)}, u32[]{:S(2)}, u32[]{:S(2)}) %collective-permute-start.27) | collective-permute-done | bytes 147488 | tf_op jit(solution)/shard_map/ppermute | solution.py:39
  125.9 1.6 %collective-permute-done.28.refs_7_ = bf16[2,32,1152]{2,1,0:T(8,128)(2,1)S(1)} collective-permute-done((bf16[2,32,1152]{2,1,0:T(8,128)(2,1)S(1)}, bf16[2,32,1152]{2,1,0:T(8,128)(2,1)S(1)}, u32[]{:S(2)}, u32[]{:S(2)}) %collective-permute-start.28) | collective-permute-done | bytes 147488 | tf_op jit(solution)/shard_map/ppermute | solution.py:39
  127.5 2.3 %shard_map.66 = (bf16[8,2,32,512]{3,2,1,0:T(8,128)(2,1)}, bf16[8,2,32,512]{3,2,1,0:T(8,128)(2,1)}) custom-call(s32[2]{0:T(128)S(1)} %pad_add_fusion.at, bf16[8,2,32,512]{3,2,1,0:T(8,128)(2,1)S(1)} %bitcast.50, bf16[8,2,32,512]{3,2,1,0:T(8,128)(2,1)S(1)} %bitcast.53, bf16[512,1024]{1,0:T(8,128)(2,1)S(1)} %bitcast.47, ...), custom_call_target="tpu_custom_call" | custom-call | flops 536870912 | bytes 5374984 | tf_op jit(solution)/shard_map/pallas_call | solution.py:48
  (56 shorter events, 28.1 us)
Async XLA Ops:
  56.1 6.4 %collective-permute-start.6 = (bf16[1,2,32,1024]{3,2,1,0:T(8,128)(2,1)S(1)}, bf16[1,2,32,1024]{3,2,1,0:T(8,128)(2,1)S(1)}, u32[]{:S(2)}, u32[]{:S(2)}) collective-permute-start(bf16[1,2,32,1024]{3,2,1,0:T(8,128)(2,1)S(1)} %get-tuple-element.29), channel_id=1, source_target_pairs={{0,1},{1,0},{2,3},{3,2},{4,5},{5,4},{6,7},{7,6},{8,9},{9,8},{10,11... | collective-permute-start | bytes 393224 | tf_op jit(solution)/shard_map/ppermute | solution.py:39
  57.6 13.9 %collective-permute-start.5 = (bf16[2,2,32,1024]{3,2,1,0:T(8,128)(2,1)S(1)}, bf16[2,2,32,1024]{3,2,1,0:T(8,128)(2,1)S(1)}, u32[]{:S(2)}, u32[]{:S(2)}) collective-permute-start(bf16[2,2,32,1024]{3,2,1,0:T(8,128)(2,1)S(1)} %get-tuple-element.27), channel_id=1, source_target_pairs={{0,1},{1,0},{2,3},{3,2},{4,5},{5,4},{6,7},{7,6},{8,9},{9,8},{10,11... | collective-permute-start | bytes 786440 | tf_op jit(solution)/shard_map/ppermute | solution.py:39
  62.6 8.9 %collective-permute-start.7 = (bf16[2,32,1024]{2,1,0:T(8,128)(2,1)S(1)}, bf16[2,32,1024]{2,1,0:T(8,128)(2,1)S(1)}, u32[]{:S(2)}, u32[]{:S(2)}) collective-permute-start(bf16[2,32,1024]{2,1,0:T(8,128)(2,1)S(1)} %fusion.5), channel_id=1, source_target_pairs={{0,2},{2,4},{4,6},{6,8},{8,10},{10,12},{12,14},{14,0},{1,3},{3,5},... | collective-permute-start | bytes 393224 | tf_op jit(solution)/shard_map/ppermute | solution.py:39
  64.6 11.0 %collective-permute-start.4 = (bf16[2,2,32,1024]{3,2,1,0:T(8,128)(2,1)S(1)}, bf16[2,2,32,1024]{3,2,1,0:T(8,128)(2,1)S(1)}, u32[]{:S(2)}, u32[]{:S(2)}) collective-permute-start(bf16[2,2,32,1024]{3,2,1,0:T(8,128)(2,1)S(1)} %get-tuple-element.25), channel_id=1, source_target_pairs={{0,1},{1,0},{2,3},{3,2},{4,5},{5,4},{6,7},{7,6},{8,9},{9,8},{10,11... | collective-permute-start | bytes 786440 | tf_op jit(solution)/shard_map/ppermute | solution.py:39
  74.2 6.2 %collective-permute-start.8 = (bf16[2,32,1024]{2,1,0:T(8,128)(2,1)S(1)}, bf16[2,32,1024]{2,1,0:T(8,128)(2,1)S(1)}, u32[]{:S(2)}, u32[]{:S(2)}) collective-permute-start(bf16[2,32,1024]{2,1,0:T(8,128)(2,1)S(1)} %get-tuple-element.43), channel_id=1, source_target_pairs={{0,2},{2,4},{4,6},{6,8},{8,10},{10,12},{12,14},{14,0},{1,3},{3,5},... | collective-permute-start | bytes 393224 | tf_op jit(solution)/shard_map/ppermute | solution.py:39
  74.2 9.7 %collective-permute-start.3 = (bf16[2,2,32,1024]{3,2,1,0:T(8,128)(2,1)S(1)}, bf16[2,2,32,1024]{3,2,1,0:T(8,128)(2,1)S(1)}, u32[]{:S(2)}, u32[]{:S(2)}) collective-permute-start(bf16[2,2,32,1024]{3,2,1,0:T(8,128)(2,1)S(1)} %get-tuple-element.23), channel_id=1, source_target_pairs={{0,1},{1,0},{2,3},{3,2},{4,5},{5,4},{6,7},{7,6},{8,9},{9,8},{10,11... | collective-permute-start | bytes 786440 | tf_op jit(solution)/shard_map/ppermute | solution.py:39
  80.6 6.3 %collective-permute-start.9 = (bf16[2,32,1024]{2,1,0:T(8,128)(2,1)S(1)}, bf16[2,32,1024]{2,1,0:T(8,128)(2,1)S(1)}, u32[]{:S(2)}, u32[]{:S(2)}) collective-permute-start(bf16[2,32,1024]{2,1,0:T(8,128)(2,1)S(1)} %get-tuple-element.41), channel_id=1, source_target_pairs={{0,2},{2,4},{4,6},{6,8},{8,10},{10,12},{12,14},{14,0},{1,3},{3,5},... | collective-permute-start | bytes 393224 | tf_op jit(solution)/shard_map/ppermute | solution.py:39
  82.6 7.8 %collective-permute-start.2 = (bf16[1,2,32,1024]{3,2,1,0:T(8,128)(2,1)S(1)}, bf16[1,2,32,1024]{3,2,1,0:T(8,128)(2,1)S(1)}, u32[]{:S(2)}, u32[]{:S(2)}) collective-permute-start(bf16[1,2,32,1024]{3,2,1,0:T(8,128)(2,1)S(1)} %get-tuple-element.21), channel_id=1, source_target_pairs={{0,1},{1,0},{2,3},{3,2},{4,5},{5,4},{6,7},{7,6},{8,9},{9,8},{10,11... | collective-permute-start | bytes 393224 | tf_op jit(solution)/shard_map/ppermute | solution.py:39
  86.9 7.4 %collective-permute-start.10 = (bf16[2,32,1024]{2,1,0:T(8,128)(2,1)S(1)}, bf16[2,32,1024]{2,1,0:T(8,128)(2,1)S(1)}, u32[]{:S(2)}, u32[]{:S(2)}) collective-permute-start(bf16[2,32,1024]{2,1,0:T(8,128)(2,1)S(1)} %get-tuple-element.39), channel_id=1, source_target_pairs={{0,2},{2,4},{4,6},{6,8},{8,10},{10,12},{12,14},{14,0},{1,3},{3,5},... | collective-permute-start | bytes 393224 | tf_op jit(solution)/shard_map/ppermute | solution.py:39
  94.5 7.2 %collective-permute-start.14 = (bf16[2,32,1152]{2,1,0:T(8,128)(2,1)S(1)}, bf16[2,32,1152]{2,1,0:T(8,128)(2,1)S(1)}, u32[]{:S(2)}, u32[]{:S(2)}) collective-permute-start(bf16[2,32,1152]{2,1,0:T(8,128)(2,1)S(1)} %shard_map.64.refs_0_), channel_id=1, source_target_pairs={{0,2},{2,4},{4,6},{6,8},{8,10},{10,12},{12,14},{14,0},{1,3},{3,5},... | collective-permute-start | bytes 442376 | tf_op jit(solution)/shard_map/ppermute | solution.py:39
  95.6 6.1 %collective-permute-start.15 = (bf16[2,32,1152]{2,1,0:T(8,128)(2,1)S(1)}, bf16[2,32,1152]{2,1,0:T(8,128)(2,1)S(1)}, u32[]{:S(2)}, u32[]{:S(2)}) collective-permute-start(bf16[2,32,1152]{2,1,0:T(8,128)(2,1)S(1)} %shard_map.64.refs_0_), channel_id=1, source_target_pairs={{0,14},{2,0},{4,2},{6,4},{8,6},{10,8},{12,10},{14,12},{1,15},{3,1}... | collective-permute-start | bytes 442376 | tf_op jit(solution)/shard_map/ppermute | solution.py:39
  98.0 9.0 %collective-permute-start.18 = (bf16[2,32,1152]{2,1,0:T(8,128)(2,1)S(1)}, bf16[2,32,1152]{2,1,0:T(8,128)(2,1)S(1)}, u32[]{:S(2)}, u32[]{:S(2)}) collective-permute-start(bf16[2,32,1152]{2,1,0:T(8,128)(2,1)S(1)} %shard_map.64.refs_0_), channel_id=1, source_target_pairs={{0,1},{1,0},{2,3},{3,2},{4,5},{5,4},{6,7},{7,6},{8,9},{9,8},{10,11... | collective-permute-start | bytes 442376 | tf_op jit(solution)/shard_map/ppermute | solution.py:39
  101.7 6.5 %collective-permute-start.16 = (bf16[2,32,1152]{2,1,0:T(8,128)(2,1)S(1)}, bf16[2,32,1152]{2,1,0:T(8,128)(2,1)S(1)}, u32[]{:S(2)}, u32[]{:S(2)}) collective-permute-start(bf16[2,32,1152]{2,1,0:T(8,128)(2,1)S(1)} %collective-permute-done.14.refs_1_), channel_id=1, source_target_pairs={{0,2},{2,4},{4,6},{6,8},{8,10},{10,12},{12,14},{14,0},{1,3},{3,5},... | collective-permute-start | bytes 442376 | tf_op jit(solution)/shard_map/ppermute | solution.py:39
  101.7 6.5 %collective-permute-start.17 = (bf16[2,32,1152]{2,1,0:T(8,128)(2,1)S(1)}, bf16[2,32,1152]{2,1,0:T(8,128)(2,1)S(1)}, u32[]{:S(2)}, u32[]{:S(2)}) collective-permute-start(bf16[2,32,1152]{2,1,0:T(8,128)(2,1)S(1)} %collective-permute-done.15.refs_2_), channel_id=1, source_target_pairs={{0,14},{2,0},{4,2},{6,4},{8,6},{10,8},{12,10},{14,12},{1,15},{3,1}... | collective-permute-start | bytes 442376 | tf_op jit(solution)/shard_map/ppermute | solution.py:39
  105.0 6.6 %collective-permute-start.21 = (bf16[2,32,1152]{2,1,0:T(8,128)(2,1)S(1)}, bf16[2,32,1152]{2,1,0:T(8,128)(2,1)S(1)}, u32[]{:S(2)}, u32[]{:S(2)}) collective-permute-start(bf16[2,32,1152]{2,1,0:T(8,128)(2,1)S(1)} %collective-permute-done.14.refs_1_), channel_id=1, source_target_pairs={{0,1},{1,0},{2,3},{3,2},{4,5},{5,4},{6,7},{7,6},{8,9},{9,8},{10,11... | collective-permute-start | bytes 442376 | tf_op jit(solution)/shard_map/ppermute | solution.py:39
  106.3 7.4 %collective-permute-start.22 = (bf16[2,32,1152]{2,1,0:T(8,128)(2,1)S(1)}, bf16[2,32,1152]{2,1,0:T(8,128)(2,1)S(1)}, u32[]{:S(2)}, u32[]{:S(2)}) collective-permute-start(bf16[2,32,1152]{2,1,0:T(8,128)(2,1)S(1)} %collective-permute-done.15.refs_2_), channel_id=1, source_target_pairs={{0,1},{1,0},{2,3},{3,2},{4,5},{5,4},{6,7},{7,6},{8,9},{9,8},{10,11... | collective-permute-start | bytes 442376 | tf_op jit(solution)/shard_map/ppermute | solution.py:39
  108.3 6.4 %collective-permute-start.19 = (bf16[2,32,1152]{2,1,0:T(8,128)(2,1)S(1)}, bf16[2,32,1152]{2,1,0:T(8,128)(2,1)S(1)}, u32[]{:S(2)}, u32[]{:S(2)}) collective-permute-start(bf16[2,32,1152]{2,1,0:T(8,128)(2,1)S(1)} %get-tuple-element.45), channel_id=1, source_target_pairs={{0,2},{2,4},{4,6},{6,8},{8,10},{10,12},{12,14},{14,0},{1,3},{3,5},... | collective-permute-start | bytes 442376 | tf_op jit(solution)/shard_map/ppermute | solution.py:39
  108.6 9.8 %collective-permute-start.20 = (bf16[2,32,1152]{2,1,0:T(8,128)(2,1)S(1)}, bf16[2,32,1152]{2,1,0:T(8,128)(2,1)S(1)}, u32[]{:S(2)}, u32[]{:S(2)}) collective-permute-start(bf16[2,32,1152]{2,1,0:T(8,128)(2,1)S(1)} %get-tuple-element.44), channel_id=1, source_target_pairs={{0,14},{2,0},{4,2},{6,4},{8,6},{10,8},{12,10},{14,12},{1,15},{3,1}... | collective-permute-start | bytes 442376 | tf_op jit(solution)/shard_map/ppermute | solution.py:39
  114.7 6.4 %collective-permute-start.23 = (bf16[2,32,1152]{2,1,0:T(8,128)(2,1)S(1)}, bf16[2,32,1152]{2,1,0:T(8,128)(2,1)S(1)}, u32[]{:S(2)}, u32[]{:S(2)}) collective-permute-start(bf16[2,32,1152]{2,1,0:T(8,128)(2,1)S(1)} %minimum_add_fusion), channel_id=1, source_target_pairs={{0,2},{2,4},{4,6},{6,8},{8,10},{10,12},{12,14},{14,0},{1,3},{3,5},... | collective-permute-start | bytes 442376 | tf_op jit(solution)/shard_map/ppermute | solution.py:39
  114.8 8.5 %collective-permute-start.24 = (bf16[2,32,1152]{2,1,0:T(8,128)(2,1)S(1)}, bf16[2,32,1152]{2,1,0:T(8,128)(2,1)S(1)}, u32[]{:S(2)}, u32[]{:S(2)}) collective-permute-start(bf16[2,32,1152]{2,1,0:T(8,128)(2,1)S(1)} %collective-permute-done.16.refs_3_), channel_id=1, source_target_pairs={{0,1},{1,0},{2,3},{3,2},{4,5},{5,4},{6,7},{7,6},{8,9},{9,8},{10,11... | collective-permute-start | bytes 442376 | tf_op jit(solution)/shard_map/ppermute | solution.py:39
  116.4 7.0 %collective-permute-start.25 = (bf16[2,32,1152]{2,1,0:T(8,128)(2,1)S(1)}, bf16[2,32,1152]{2,1,0:T(8,128)(2,1)S(1)}, u32[]{:S(2)}, u32[]{:S(2)}) collective-permute-start(bf16[2,32,1152]{2,1,0:T(8,128)(2,1)S(1)} %collective-permute-done.17.refs_4_), channel_id=1, source_target_pairs={{0,1},{1,0},{2,3},{3,2},{4,5},{5,4},{6,7},{7,6},{8,9},{9,8},{10,11... | collective-permute-start | bytes 442376 | tf_op jit(solution)/shard_map/ppermute | solution.py:39
  117.0 7.4 %collective-permute-start.26 = (bf16[2,32,1152]{2,1,0:T(8,128)(2,1)S(1)}, bf16[2,32,1152]{2,1,0:T(8,128)(2,1)S(1)}, u32[]{:S(2)}, u32[]{:S(2)}) collective-permute-start(bf16[2,32,1152]{2,1,0:T(8,128)(2,1)S(1)} %collective-permute-done.19.refs_5_), channel_id=1, source_target_pairs={{0,1},{1,0},{2,3},{3,2},{4,5},{5,4},{6,7},{7,6},{8,9},{9,8},{10,11... | collective-permute-start | bytes 442376 | tf_op jit(solution)/shard_map/ppermute | solution.py:39
  118.4 7.5 %collective-permute-start.27 = (bf16[2,32,1152]{2,1,0:T(8,128)(2,1)S(1)}, bf16[2,32,1152]{2,1,0:T(8,128)(2,1)S(1)}, u32[]{:S(2)}, u32[]{:S(2)}) collective-permute-start(bf16[2,32,1152]{2,1,0:T(8,128)(2,1)S(1)} %collective-permute-done.20.refs_6_), channel_id=1, source_target_pairs={{0,1},{1,0},{2,3},{3,2},{4,5},{5,4},{6,7},{7,6},{8,9},{9,8},{10,11... | collective-permute-start | bytes 442376 | tf_op jit(solution)/shard_map/ppermute | solution.py:39
  121.2 6.3 %collective-permute-start.28 = (bf16[2,32,1152]{2,1,0:T(8,128)(2,1)S(1)}, bf16[2,32,1152]{2,1,0:T(8,128)(2,1)S(1)}, u32[]{:S(2)}, u32[]{:S(2)}) collective-permute-start(bf16[2,32,1152]{2,1,0:T(8,128)(2,1)S(1)} %collective-permute-done.23.refs_7_), channel_id=1, source_target_pairs={{0,1},{1,0},{2,3},{3,2},{4,5},{5,4},{6,7},{7,6},{8,9},{9,8},{10,11... | collective-permute-start | bytes 442376 | tf_op jit(solution)/shard_map/ppermute | solution.py:39
  (7 other events, 66.3 us)

commit v6 on v5

--- a/solution.py
+++ b/solution.py
@@ -16,9 +16,9 @@
 EXTRA = 128
 PART = ROWS // (Z * YL)
 
-REDUCE = (4, -3, 3, -2, 2, -1, 1, 0)
-PLACES = ((0, 0), (1, 0), (1, 1), (2, 0), (2, 1), (3, 0), (3, 1), (4, 0))
-GATHER = (0, -1, 1, -2, 2, -3, 3, -4)
+REDUCE = (-3, 3, 4, 2, -2, 1, -1, 0)
+PLACES = ((0, 0), (0, 1), (1, 0), (1, 1), (1, 2), (2, 0), (2, 1), (2, 2))
+GATHER = (0, -1, 1, -4, -2, 2, 3, -3)
 
 keep_scale = 1.45
 gram_scale = 0.5
@@ -37,6 +37,12 @@
 
 def shift(a, axis, size, by=1):
     return lax.ppermute(a, axis, [(i, (i + by) % size) for i in range(size)])
+
+
+def add_up(first, parts):
+    for part in parts:
+        first = first + part.astype(f32)
+    return first
 
 
 def kernel_call(body, outs, *args, index=None, flops=0, memory=pltpu.VMEM, scratch=(), room=48):
@@ -115,8 +121,9 @@
         outs[Z][f : f + 1] = jnp.sum(square, axis=0, keepdims=True)
 
 
-def last_sum(own, away, up, down, squares, out):
-    total = own[...] + away[0].astype(f32) + up[...].astype(f32) + down[...].astype(f32)
+def last_sum(own, away, squares, *refs):
+    came, out = refs[:-1], refs[-1]
+    total = add_up(own[...] + away[2].astype(f32), [part[...] for part in came])
     out[:, :, :TOKENS] = total.astype(bf16)
     row = lax.broadcasted_iota(jnp.int32, (PART, EXTRA), 0)
     for f in range(2):
@@ -187,35 +194,32 @@
 
     factors = [f.reshape(Z, YL, PART, WIDTH) for f in (act_factor, grad_factor)]
     shape = (2, PART, TOKENS)
-    sent = [((sum(g == group for g, _ in PLACES),) + shape, bf16) for group in range(5)]
+    sent = [((sum(g == group for g, _ in PLACES),) + shape, bf16) for group in range(3)]
     away = kernel_call(image_away, sent, *factors, mine, other, index=[z, yl], flops=product)
-    away = [shift(a, "yl", YL) for a in away]
+    crossed = [shift(away[0], "yl", YL)]
+    crossed.append(shift(after(away[1], crossed[0][0]), "yl", YL))
     *own, squares = kernel_call(
         image_own, [(shape, f32)] * Z + [((2, WIDTH), f32)], *factors, mine, other, index=[z, yl], flops=product
     )
-    up = own[0] + away[0][0].astype(f32)
-    down = own[1] + away[1][0].astype(f32)
-    for step in (1, 2, 3):
-        up = shift(up.astype(bf16), "z", Z, 1)
-        up = own[2 * step] + away[step][1].astype(f32) + up.astype(f32)
-        down = shift(down.astype(bf16), "z", Z, -1)
-        if step < 3:
-            down = own[2 * step + 1] + away[step + 1][0].astype(f32) + down.astype(f32)
-    up = shift(up.astype(bf16), "z", Z, 1)
+    def partial(n):
+        group, k = PLACES[n]
+        return own[n] + crossed[group][k].astype(f32)
+
+    relayed = [shift(partial(n).astype(bf16), "z", Z, by) for n, by in ((0, 1), (1, -1))]
+    crossed.append(shift(after(away[2], relayed[0]), "yl", YL))
+    opposite = add_up(partial(2), relayed).astype(bf16)
+    came = [shift(opposite, "z", Z, 4)]
+    came += [shift(partial(n).astype(bf16), "z", Z, REDUCE[n]) for n in (3, 4, 5, 6)]
     shape = (2, PART, TOKENS + EXTRA)
-    (up,) = kernel_call(last_sum, [(shape, bf16)], own[7], away[4], up, down, squares)
-
-    down = up
-    held, crossed = [up], [shift(up, "yl", YL)]
-    for step in (1, 2, 3):
-        if step == 3:
-            up, down = after(up, crossed[0]), after(down, crossed[0])
-        up, down = shift(up, "z", Z, 1), shift(down, "z", Z, -1)
-        held += [up, down]
-        crossed += [shift(up, "yl", YL), shift(down, "yl", YL)]
-    up = shift(after(up, crossed[1], crossed[2]), "z", Z, 1)
-    held.append(up)
-    crossed.append(shift(up, "yl", YL))
+    (final,) = kernel_call(last_sum, [(shape, bf16)], own[7], crossed[2], squares, *came)
+
+    opposite = shift(final, "z", Z, 4)
+    held = [final] + [shift(final, "z", Z, by) for by in (1, -1)]
+    crossed = [shift(a, "yl", YL) for a in held]
+    held += [opposite] + [shift(after(final, held[1]), "z", Z, by) for by in (2, -2)]
+    opposite = after(opposite, crossed[0], crossed[1])
+    held += [shift(opposite, "z", Z, by) for by in (1, -1)]
+    crossed += [shift(a, "yl", YL) for a in held[3:]]
     changed, squares = kernel_call(
         own_changes, [((2, ROWS // YL, WIDTH), f32), ((2, EXTRA), f32)], mine, other, *held, flops=product
     )

time: 130 us -> 139 us (1.069)
  starting transfers between devices: 35.6 us -> 43.8 us
    ppermute x29 -> x27, starting transfers between devices: 35.6 us -> 43.8 us  [shift(): return lax.ppermute(a, axis, [(i, (i + by) % size) for i in range(size)])]
    ppermute x29 -> x27, waiting for transfers between devices: 35.4 us -> 35.7 us  [shift(): return lax.ppermute(a, axis, [(i, (i + by) % size) for i in range(size)])]
  transfers between devices with their start and end apart: 29 -> 27, of which waited for: 17 -> 14; matrix products, arithmetic and copies ran while one was open for 0% -> 0% of each run, Pallas kernels for 5% -> 4%
where the time goes in v6:
time: 139 us; the launch traced here: 138 us
  starting transfers between devices  43.8 us (32%)
  blocking collectives  42.8 us (31%)
  waiting for transfers between devices  35.7 us (26%)
  Pallas kernels  13 us (9%)
  other arithmetic  2.43 us (2%)
    ppermute x27, starting transfers between devices, shift(): return lax.ppermute(a, axis, [(i, (i + by) % size) for i in range(size)])  43.8 us
    ppermute x27, waiting for transfers between devices, shift(): return lax.ppermute(a, axis, [(i, (i + by) % size) for i in range(size)])  35.7 us
    all_to_all x1, blocking collectives, local(): parts = lax.all_to_all(total.reshape(chunks), ('x', 'yh'), 0, 0, tiled=True)  23.3 us
    all_to_all x1, blocking collectives, local(): lax.all_to_all(copies, ('x', 'yh'), 0, 0, tiled=True)  19.4 us
    pallas_call x8, Pallas kernels, kernel_call(): pl.pallas_call(body, out_shape=[jax.ShapeDtypeStruct(shape, dtype) for sh...  13 us
  transfers between devices with their start and end apart: 27, of which 14 were waited for; matrix products, arithmetic and copies ran while one was open for 0% of the time, Pallas kernels for 4%

profile of v6, /device:TPU:8, one launch (start us, length us, event | category | flops | bytes accessed | tf_op | source)
XLA Modules:
  0.0 138.4 jit_solution(7345295644278628032)
XLA Ops:
  0.6 3.1 %shard_map.60 = bf16[512,1024]{1,0:T(8,128)(2,1)} custom-call(s32[1]{0:T(128)} %bitcast.5.which, bf16[1024,512]{1,0:T(8,128)(2,1)} %acts.3, bf16[1024,512]{1,0:T(8,128)(2,1)} %cots.3, bf16[512,512]{1,0:T(8,128)(2,1)} %act_factor.3, bf16[512,512]{1,0:T(8,128)(2,1)} %grad_factor.3), custom_call_target="tpu_custom_call" | custom-call | flops 536870912 | bytes 3145732 | tf_op jit(solution)/shard_map/pallas_call | solution.py:54
  3.8 3.5 %shard_map.59 = f32[512,1024]{1,0:T(8,128)} custom-call(s32[1]{0:T(128)} %bitcast.4.which, bf16[1024,512]{1,0:T(8,128)(2,1)} %acts.3, bf16[1024,512]{1,0:T(8,128)(2,1)} %cots.3, bf16[512,512]{1,0:T(8,128)(2,1)} %act_factor.3, bf16[512,512]{1,0:T(8,128)(2,1)} %grad_factor.3), custom_call_target="tpu_custom_call" | custom-call | flops 536870912 | bytes 3145732 | tf_op jit(solution)/shard_map/pallas_call | solution.py:54
  7.3 1.9 %add_convert_fusion = bf16[512,1024]{1,0:T(8,128)(2,1)S(1)} fusion(f32[512,1024]{1,0:T(8,128)} %shard_map.59, bf16[512,1024]{1,0:T(8,128)(2,1)S(1)} %collective-permute-done), kind=kLoop, calls=%fused_computation | loop fusion | flops 1572864 | bytes 4194304 | tf_op jit(solution)/shard_map/convert_element_type | solution.py:187
  9.3 23.3 %all_to_all.10.parts = bf16[8,64,1024]{2,1,0:T(8,128)(2,1)S(1)} all-to-all(bf16[8,64,1024]{2,1,0:T(8,128)(2,1)S(1)} %bitcast.56), channel_id=1, replica_groups=mesh['x'=4,'yh'=2,'core'=2,'z'=8,'yl'=2] {'x','yh'}, dimensions={0} | all-to-all | bytes 2097152 | tf_op jit(solution)/shard_map/all_to_all | solution.py:190
  32.7 19.4 %all_to_all.11 = bf16[8,64,1024]{2,1,0:T(8,128)(2,1)S(1)} all-to-all(bf16[8,64,1024]{2,1,0:T(8,128)(2,1)S(1)} %shard_map.61), channel_id=1, replica_groups=mesh['x'=4,'yh'=2,'core'=2,'z'=8,'yl'=2] {'x','yh'}, dimensions={0} | all-to-all | bytes 2097152 | tf_op jit(solution)/shard_map/all_to_all | solution.py:192
  52.2 2.6 %collective-permute-done.1.other = bf16[512,1024]{1,0:T(8,128)(2,1)S(1)} collective-permute-done((bf16[512,1024]{1,0:T(8,128)(2,1)S(1)}, bf16[512,1024]{1,0:T(8,128)(2,1)S(1)}, u32[]{:S(2)}, u32[]{:S(2)}) %collective-permute-start.1) | collective-permute-done | bytes 1048608 | tf_op jit(solution)/shard_map/ppermute | solution.py:39
  57.6 1.8 %shard_map.62 = (f32[2,32,1024]{2,1,0:T(8,128)S(1)}, f32[2,32,1024]{2,1,0:T(8,128)S(1)}, f32[2,32,1024]{2,1,0:T(8,128)S(1)}, f32[2,32,1024]{2,1,0:T(8,128)S(1)},...) custom-call(s32[2]{0:T(128)S(1)} %pad_add_fusion.at, ...), custom_call_target="tpu_custom_call" | custom-call | flops 536870912 | bytes 3145736 | tf_op jit(solution)/shard_map/pallas_call | solution.py:54
  59.3 5.2 %collective-permute-done.2 = bf16[2,2,32,1024]{3,2,1,0:T(8,128)(2,1)S(1)} collective-permute-done((bf16[2,2,32,1024]{3,2,1,0:T(8,128)(2,1)S(1)}, bf16[2,2,32,1024]{3,2,1,0:T(8,128)(2,1)S(1)}, u32[]{:S(2)}, u32[]{:S(2)}) %collective-permute-start.2) | collective-permute-done | bytes 262176 | tf_op jit(solution)/shard_map/ppermute | solution.py:39
  64.6 2.0 %collective-permute-start.3 = (bf16[2,32,1024]{2,1,0:T(8,128)(2,1)S(1)}, bf16[2,32,1024]{2,1,0:T(8,128)(2,1)S(1)}, u32[]{:S(2)}, u32[]{:S(2)}) collective-permute-start(bf16[2,32,1024]{2,1,0:T(8,128)(2,1)S(1)} %get-tuple-element.40), channel_id=1, source_target_pairs={{0,2},{2,4},{4,6},{6,8},{8,10},{10,12},{12,14},{14,0},{1,3},{3,5},... | collective-permute-start | bytes 393224 | tf_op jit(solution)/shard_map/ppermute | solution.py:39
  68.1 4.0 %collective-permute-start.6 = (bf16[2,32,1024]{2,1,0:T(8,128)(2,1)S(1)}, bf16[2,32,1024]{2,1,0:T(8,128)(2,1)S(1)}, u32[]{:S(2)}, u32[]{:S(2)}) collective-permute-start(bf16[2,32,1024]{2,1,0:T(8,128)(2,1)S(1)} %get-tuple-element.39), channel_id=1, source_target_pairs={{0,14},{2,0},{4,2},{6,4},{8,6},{10,8},{12,10},{14,12},{1,15},{3,1}... | collective-permute-start | bytes 393224 | tf_op jit(solution)/shard_map/ppermute | solution.py:39
  75.0 3.8 %collective-permute-done.5 = bf16[3,2,32,1024]{3,2,1,0:T(8,128)(2,1)S(1)} collective-permute-done((bf16[3,2,32,1024]{3,2,1,0:T(8,128)(2,1)S(1)}, bf16[3,2,32,1024]{3,2,1,0:T(8,128)(2,1)S(1)}, u32[]{:S(2)}, u32[]{:S(2)}) %collective-permute-start.5) | collective-permute-done | bytes 393248 | tf_op jit(solution)/shard_map/ppermute | solution.py:39
  79.0 5.5 %collective-permute-start.9 = (bf16[2,32,1024]{2,1,0:T(8,128)(2,1)S(1)}, bf16[2,32,1024]{2,1,0:T(8,128)(2,1)S(1)}, u32[]{:S(2)}, u32[]{:S(2)}) collective-permute-start(bf16[2,32,1024]{2,1,0:T(8,128)(2,1)S(1)} %get-tuple-element.36), channel_id=1, source_target_pairs={{0,12},{2,14},{4,0},{6,2},{8,4},{10,6},{12,8},{14,10},{1,13},{3,15... | collective-permute-start | bytes 393224 | tf_op jit(solution)/shard_map/ppermute | solution.py:39
  84.5 3.8 %collective-permute-start.7 = (bf16[2,32,1024]{2,1,0:T(8,128)(2,1)S(1)}, bf16[2,32,1024]{2,1,0:T(8,128)(2,1)S(1)}, u32[]{:S(2)}, u32[]{:S(2)}) collective-permute-start(bf16[2,32,1024]{2,1,0:T(8,128)(2,1)S(1)} %get-tuple-element.38), channel_id=1, source_target_pairs={{0,8},{2,10},{4,12},{6,14},{8,0},{10,2},{12,4},{14,6},{1,9},{3,11}... | collective-permute-start | bytes 393224 | tf_op jit(solution)/shard_map/ppermute | solution.py:39
  88.3 3.5 %collective-permute-start.11 = (bf16[2,32,1024]{2,1,0:T(8,128)(2,1)S(1)}, bf16[2,32,1024]{2,1,0:T(8,128)(2,1)S(1)}, u32[]{:S(2)}, u32[]{:S(2)}) collective-permute-start(bf16[2,32,1024]{2,1,0:T(8,128)(2,1)S(1)} %get-tuple-element.34), channel_id=1, source_target_pairs={{0,14},{2,0},{4,2},{6,4},{8,6},{10,8},{12,10},{14,12},{1,15},{3,1}... | collective-permute-start | bytes 393224 | tf_op jit(solution)/shard_map/ppermute | solution.py:39
  91.8 2.2 %collective-permute-done.9.refs_2_ = bf16[2,32,1024]{2,1,0:T(8,128)(2,1)S(1)} collective-permute-done((bf16[2,32,1024]{2,1,0:T(8,128)(2,1)S(1)}, bf16[2,32,1024]{2,1,0:T(8,128)(2,1)S(1)}, u32[]{:S(2)}, u32[]{:S(2)}) %collective-permute-start.9) | collective-permute-done | bytes 131104 | tf_op jit(solution)/shard_map/ppermute | solution.py:39
  94.1 2.9 %collective-permute-done.7.refs_0_ = bf16[2,32,1024]{2,1,0:T(8,128)(2,1)S(1)} collective-permute-done((bf16[2,32,1024]{2,1,0:T(8,128)(2,1)S(1)}, bf16[2,32,1024]{2,1,0:T(8,128)(2,1)S(1)}, u32[]{:S(2)}, u32[]{:S(2)}) %collective-permute-start.7) | collective-permute-done | bytes 131104 | tf_op jit(solution)/shard_map/ppermute | solution.py:39
  100.5 3.6 %collective-permute-start.14 = (bf16[2,32,1152]{2,1,0:T(8,128)(2,1)S(1)}, bf16[2,32,1152]{2,1,0:T(8,128)(2,1)S(1)}, u32[]{:S(2)}, u32[]{:S(2)}) collective-permute-start(bf16[2,32,1152]{2,1,0:T(8,128)(2,1)S(1)} %shard_map.64.refs_0_), channel_id=1, source_target_pairs={{0,8},{2,10},{4,12},{6,14},{8,0},{10,2},{12,4},{14,6},{1,9},{3,11}... | collective-permute-start | bytes 442376 | tf_op jit(solution)/shard_map/ppermute | solution.py:39
  104.0 3.1 %collective-permute-start.13 = (bf16[2,32,1152]{2,1,0:T(8,128)(2,1)S(1)}, bf16[2,32,1152]{2,1,0:T(8,128)(2,1)S(1)}, u32[]{:S(2)}, u32[]{:S(2)}) collective-permute-start(bf16[2,32,1152]{2,1,0:T(8,128)(2,1)S(1)} %shard_map.64.refs_0_), channel_id=1, source_target_pairs={{0,14},{2,0},{4,2},{6,4},{8,6},{10,8},{12,10},{14,12},{1,15},{3,1}... | collective-permute-start | bytes 442376 | tf_op jit(solution)/shard_map/ppermute | solution.py:39
  107.1 6.5 %collective-permute-done.12.refs_1_ = bf16[2,32,1152]{2,1,0:T(8,128)(2,1)S(1)} collective-permute-done((bf16[2,32,1152]{2,1,0:T(8,128)(2,1)S(1)}, bf16[2,32,1152]{2,1,0:T(8,128)(2,1)S(1)}, u32[]{:S(2)}, u32[]{:S(2)}) %collective-permute-start.12) | collective-permute-done | bytes 147488 | tf_op jit(solution)/shard_map/ppermute | solution.py:39
  114.7 2.9 %collective-permute-start.15 = (bf16[2,32,1152]{2,1,0:T(8,128)(2,1)S(1)}, bf16[2,32,1152]{2,1,0:T(8,128)(2,1)S(1)}, u32[]{:S(2)}, u32[]{:S(2)}) collective-permute-start(bf16[2,32,1152]{2,1,0:T(8,128)(2,1)S(1)} %minimum_add_fusion.1), channel_id=1, source_target_pairs={{0,4},{2,6},{4,8},{6,10},{8,12},{10,14},{12,0},{14,2},{1,5},{3,7},... | collective-permute-start | bytes 442376 | tf_op jit(solution)/shard_map/ppermute | solution.py:39
  120.3 2.0 %collective-permute-start.19 = (bf16[2,32,1152]{2,1,0:T(8,128)(2,1)S(1)}, bf16[2,32,1152]{2,1,0:T(8,128)(2,1)S(1)}, u32[]{:S(2)}, u32[]{:S(2)}) collective-permute-start(bf16[2,32,1152]{2,1,0:T(8,128)(2,1)S(1)} %minimum_add_fusion), channel_id=1, source_target_pairs={{0,2},{2,4},{4,6},{6,8},{8,10},{10,12},{12,14},{14,0},{1,3},{3,5},... | collective-permute-start | bytes 442376 | tf_op jit(solution)/shard_map/ppermute | solution.py:39
  122.3 2.1 %collective-permute-done.22.refs_3_ = bf16[2,32,1152]{2,1,0:T(8,128)(2,1)S(1)} collective-permute-done((bf16[2,32,1152]{2,1,0:T(8,128)(2,1)S(1)}, bf16[2,32,1152]{2,1,0:T(8,128)(2,1)S(1)}, u32[]{:S(2)}, u32[]{:S(2)}) %collective-permute-start.22) | collective-permute-done | bytes 147488 | tf_op jit(solution)/shard_map/ppermute | solution.py:39
  131.4 1.6 %collective-permute-done.23.refs_4_ = bf16[2,32,1152]{2,1,0:T(8,128)(2,1)S(1)} collective-permute-done((bf16[2,32,1152]{2,1,0:T(8,128)(2,1)S(1)}, bf16[2,32,1152]{2,1,0:T(8,128)(2,1)S(1)}, u32[]{:S(2)}, u32[]{:S(2)}) %collective-permute-start.23) | collective-permute-done | bytes 147488 | tf_op jit(solution)/shard_map/ppermute | solution.py:39
  136.2 2.3 %shard_map.66 = (bf16[8,2,32,512]{3,2,1,0:T(8,128)(2,1)}, bf16[8,2,32,512]{3,2,1,0:T(8,128)(2,1)}) custom-call(s32[2]{0:T(128)S(1)} %pad_add_fusion.at, bf16[8,2,32,512]{3,2,1,0:T(8,128)(2,1)S(1)} %bitcast.52, bf16[8,2,32,512]{3,2,1,0:T(8,128)(2,1)S(1)} %bitcast.55, bf16[512,1024]{1,0:T(8,128)(2,1)S(1)} %bitcast.49, ...), custom_call_target="tpu_custom_call" | custom-call | flops 536870912 | bytes 5374984 | tf_op jit(solution)/shard_map/pallas_call | solution.py:54
  (55 shorter events, 25.1 us)
Async XLA Ops:
  56.1 8.4 %collective-permute-start.2 = (bf16[2,2,32,1024]{3,2,1,0:T(8,128)(2,1)S(1)}, bf16[2,2,32,1024]{3,2,1,0:T(8,128)(2,1)S(1)}, u32[]{:S(2)}, u32[]{:S(2)}) collective-permute-start(bf16[2,2,32,1024]{3,2,1,0:T(8,128)(2,1)S(1)} %get-tuple-element.21), channel_id=1, source_target_pairs={{0,1},{1,0},{2,3},{3,2},{4,5},{5,4},{6,7},{7,6},{8,9},{9,8},{10,11... | collective-permute-start | bytes 786440 | tf_op jit(solution)/shard_map/ppermute | solution.py:39
  64.6 8.9 %collective-permute-start.3 = (bf16[2,32,1024]{2,1,0:T(8,128)(2,1)S(1)}, bf16[2,32,1024]{2,1,0:T(8,128)(2,1)S(1)}, u32[]{:S(2)}, u32[]{:S(2)}) collective-permute-start(bf16[2,32,1024]{2,1,0:T(8,128)(2,1)S(1)} %get-tuple-element.40), channel_id=1, source_target_pairs={{0,2},{2,4},{4,6},{6,8},{8,10},{10,12},{12,14},{14,0},{1,3},{3,5},... | collective-permute-start | bytes 393224 | tf_op jit(solution)/shard_map/ppermute | solution.py:39
  66.7 12.1 %collective-permute-start.5 = (bf16[3,2,32,1024]{3,2,1,0:T(8,128)(2,1)S(1)}, bf16[3,2,32,1024]{3,2,1,0:T(8,128)(2,1)S(1)}, u32[]{:S(2)}, u32[]{:S(2)}) collective-permute-start(bf16[3,2,32,1024]{3,2,1,0:T(8,128)(2,1)S(1)} %broadcast_add_fusion), channel_id=1, source_target_pairs={{0,1},{1,0},{2,3},{3,2},{4,5},{5,4},{6,7},{7,6},{8,9},{9,8},{10,11... | collective-permute-start | bytes 1179656 | tf_op jit(solution)/shard_map/ppermute | solution.py:39
  68.1 6.9 %collective-permute-start.6 = (bf16[2,32,1024]{2,1,0:T(8,128)(2,1)S(1)}, bf16[2,32,1024]{2,1,0:T(8,128)(2,1)S(1)}, u32[]{:S(2)}, u32[]{:S(2)}) collective-permute-start(bf16[2,32,1024]{2,1,0:T(8,128)(2,1)S(1)} %get-tuple-element.39), channel_id=1, source_target_pairs={{0,14},{2,0},{4,2},{6,4},{8,6},{10,8},{12,10},{14,12},{1,15},{3,1}... | collective-permute-start | bytes 393224 | tf_op jit(solution)/shard_map/ppermute | solution.py:39
  73.6 14.7 %collective-permute-start.4 = (bf16[3,2,32,1024]{3,2,1,0:T(8,128)(2,1)S(1)}, bf16[3,2,32,1024]{3,2,1,0:T(8,128)(2,1)S(1)}, u32[]{:S(2)}, u32[]{:S(2)}) collective-permute-start(bf16[3,2,32,1024]{3,2,1,0:T(8,128)(2,1)S(1)} %broadcast_add_fusion.1), channel_id=1, source_target_pairs={{0,1},{1,0},{2,3},{3,2},{4,5},{5,4},{6,7},{7,6},{8,9},{9,8},{10,11... | collective-permute-start | bytes 1179656 | tf_op jit(solution)/shard_map/ppermute | solution.py:39
  79.0 15.1 %collective-permute-start.9 = (bf16[2,32,1024]{2,1,0:T(8,128)(2,1)S(1)}, bf16[2,32,1024]{2,1,0:T(8,128)(2,1)S(1)}, u32[]{:S(2)}, u32[]{:S(2)}) collective-permute-start(bf16[2,32,1024]{2,1,0:T(8,128)(2,1)S(1)} %get-tuple-element.36), channel_id=1, source_target_pairs={{0,12},{2,14},{4,0},{6,2},{8,4},{10,6},{12,8},{14,10},{1,13},{3,15... | collective-permute-start | bytes 393224 | tf_op jit(solution)/shard_map/ppermute | solution.py:39
  84.4 9.6 %collective-permute-start.8 = (bf16[2,32,1024]{2,1,0:T(8,128)(2,1)S(1)}, bf16[2,32,1024]{2,1,0:T(8,128)(2,1)S(1)}, u32[]{:S(2)}, u32[]{:S(2)}) collective-permute-start(bf16[2,32,1024]{2,1,0:T(8,128)(2,1)S(1)} %get-tuple-element.37), channel_id=1, source_target_pairs={{0,4},{2,6},{4,8},{6,10},{8,12},{10,14},{12,0},{14,2},{1,5},{3,7},... | collective-permute-start | bytes 393224 | tf_op jit(solution)/shard_map/ppermute | solution.py:39
  84.5 12.5 %collective-permute-start.7 = (bf16[2,32,1024]{2,1,0:T(8,128)(2,1)S(1)}, bf16[2,32,1024]{2,1,0:T(8,128)(2,1)S(1)}, u32[]{:S(2)}, u32[]{:S(2)}) collective-permute-start(bf16[2,32,1024]{2,1,0:T(8,128)(2,1)S(1)} %get-tuple-element.38), channel_id=1, source_target_pairs={{0,8},{2,10},{4,12},{6,14},{8,0},{10,2},{12,4},{14,6},{1,9},{3,11}... | collective-permute-start | bytes 393224 | tf_op jit(solution)/shard_map/ppermute | solution.py:39
  88.3 8.6 %collective-permute-start.11 = (bf16[2,32,1024]{2,1,0:T(8,128)(2,1)S(1)}, bf16[2,32,1024]{2,1,0:T(8,128)(2,1)S(1)}, u32[]{:S(2)}, u32[]{:S(2)}) collective-permute-start(bf16[2,32,1024]{2,1,0:T(8,128)(2,1)S(1)} %get-tuple-element.34), channel_id=1, source_target_pairs={{0,14},{2,0},{4,2},{6,4},{8,6},{10,8},{12,10},{14,12},{1,15},{3,1}... | collective-permute-start | bytes 393224 | tf_op jit(solution)/shard_map/ppermute | solution.py:39
  91.8 6.7 %collective-permute-start.10 = (bf16[2,32,1024]{2,1,0:T(8,128)(2,1)S(1)}, bf16[2,32,1024]{2,1,0:T(8,128)(2,1)S(1)}, u32[]{:S(2)}, u32[]{:S(2)}) collective-permute-start(bf16[2,32,1024]{2,1,0:T(8,128)(2,1)S(1)} %get-tuple-element.35), channel_id=1, source_target_pairs={{0,2},{2,4},{4,6},{6,8},{8,10},{10,12},{12,14},{14,0},{1,3},{3,5},... | collective-permute-start | bytes 393224 | tf_op jit(solution)/shard_map/ppermute | solution.py:39
  98.8 14.9 %collective-permute-start.12 = (bf16[2,32,1152]{2,1,0:T(8,128)(2,1)S(1)}, bf16[2,32,1152]{2,1,0:T(8,128)(2,1)S(1)}, u32[]{:S(2)}, u32[]{:S(2)}) collective-permute-start(bf16[2,32,1152]{2,1,0:T(8,128)(2,1)S(1)} %shard_map.64.refs_0_), channel_id=1, source_target_pairs={{0,2},{2,4},{4,6},{6,8},{8,10},{10,12},{12,14},{14,0},{1,3},{3,5},... | collective-permute-start | bytes 442376 | tf_op jit(solution)/shard_map/ppermute | solution.py:39
  99.0 15.7 %collective-permute-start.17 = (bf16[2,32,1152]{2,1,0:T(8,128)(2,1)S(1)}, bf16[2,32,1152]{2,1,0:T(8,128)(2,1)S(1)}, u32[]{:S(2)}, u32[]{:S(2)}) collective-permute-start(bf16[2,32,1152]{2,1,0:T(8,128)(2,1)S(1)} %shard_map.64.refs_0_), channel_id=1, source_target_pairs={{0,1},{1,0},{2,3},{3,2},{4,5},{5,4},{6,7},{7,6},{8,9},{9,8},{10,11... | collective-permute-start | bytes 442376 | tf_op jit(solution)/shard_map/ppermute | solution.py:39
  100.5 17.2 %collective-permute-start.14 = (bf16[2,32,1152]{2,1,0:T(8,128)(2,1)S(1)}, bf16[2,32,1152]{2,1,0:T(8,128)(2,1)S(1)}, u32[]{:S(2)}, u32[]{:S(2)}) collective-permute-start(bf16[2,32,1152]{2,1,0:T(8,128)(2,1)S(1)} %shard_map.64.refs_0_), channel_id=1, source_target_pairs={{0,8},{2,10},{4,12},{6,14},{8,0},{10,2},{12,4},{14,6},{1,9},{3,11}... | collective-permute-start | bytes 442376 | tf_op jit(solution)/shard_map/ppermute | solution.py:39
  104.0 16.3 %collective-permute-start.13 = (bf16[2,32,1152]{2,1,0:T(8,128)(2,1)S(1)}, bf16[2,32,1152]{2,1,0:T(8,128)(2,1)S(1)}, u32[]{:S(2)}, u32[]{:S(2)}) collective-permute-start(bf16[2,32,1152]{2,1,0:T(8,128)(2,1)S(1)} %shard_map.64.refs_0_), channel_id=1, source_target_pairs={{0,14},{2,0},{4,2},{6,4},{8,6},{10,8},{12,10},{14,12},{1,15},{3,1}... | collective-permute-start | bytes 442376 | tf_op jit(solution)/shard_map/ppermute | solution.py:39
  113.7 6.5 %collective-permute-start.18 = (bf16[2,32,1152]{2,1,0:T(8,128)(2,1)S(1)}, bf16[2,32,1152]{2,1,0:T(8,128)(2,1)S(1)}, u32[]{:S(2)}, u32[]{:S(2)}) collective-permute-start(bf16[2,32,1152]{2,1,0:T(8,128)(2,1)S(1)} %collective-permute-done.12.refs_1_), channel_id=1, source_target_pairs={{0,1},{1,0},{2,3},{3,2},{4,5},{5,4},{6,7},{7,6},{8,9},{9,8},{10,11... | collective-permute-start | bytes 442376 | tf_op jit(solution)/shard_map/ppermute | solution.py:39
  114.6 10.9 %collective-permute-start.16 = (bf16[2,32,1152]{2,1,0:T(8,128)(2,1)S(1)}, bf16[2,32,1152]{2,1,0:T(8,128)(2,1)S(1)}, u32[]{:S(2)}, u32[]{:S(2)}) collective-permute-start(bf16[2,32,1152]{2,1,0:T(8,128)(2,1)S(1)} %minimum_add_fusion.1), channel_id=1, source_target_pairs={{0,12},{2,14},{4,0},{6,2},{8,4},{10,6},{12,8},{14,10},{1,13},{3,15... | collective-permute-start | bytes 442376 | tf_op jit(solution)/shard_map/ppermute | solution.py:39
  114.7 11.7 %collective-permute-start.15 = (bf16[2,32,1152]{2,1,0:T(8,128)(2,1)S(1)}, bf16[2,32,1152]{2,1,0:T(8,128)(2,1)S(1)}, u32[]{:S(2)}, u32[]{:S(2)}) collective-permute-start(bf16[2,32,1152]{2,1,0:T(8,128)(2,1)S(1)} %minimum_add_fusion.1), channel_id=1, source_target_pairs={{0,4},{2,6},{4,8},{6,10},{8,12},{10,14},{12,0},{14,2},{1,5},{3,7},... | collective-permute-start | bytes 442376 | tf_op jit(solution)/shard_map/ppermute | solution.py:39
  117.6 6.8 %collective-permute-start.22 = (bf16[2,32,1152]{2,1,0:T(8,128)(2,1)S(1)}, bf16[2,32,1152]{2,1,0:T(8,128)(2,1)S(1)}, u32[]{:S(2)}, u32[]{:S(2)}) collective-permute-start(bf16[2,32,1152]{2,1,0:T(8,128)(2,1)S(1)} %collective-permute-done.14.refs_3_), channel_id=1, source_target_pairs={{0,1},{1,0},{2,3},{3,2},{4,5},{5,4},{6,7},{7,6},{8,9},{9,8},{10,11... | collective-permute-start | bytes 442376 | tf_op jit(solution)/shard_map/ppermute | solution.py:39
  120.2 7.3 %collective-permute-start.20 = (bf16[2,32,1152]{2,1,0:T(8,128)(2,1)S(1)}, bf16[2,32,1152]{2,1,0:T(8,128)(2,1)S(1)}, u32[]{:S(2)}, u32[]{:S(2)}) collective-permute-start(bf16[2,32,1152]{2,1,0:T(8,128)(2,1)S(1)} %minimum_add_fusion), channel_id=1, source_target_pairs={{0,14},{2,0},{4,2},{6,4},{8,6},{10,8},{12,10},{14,12},{1,15},{3,1}... | collective-permute-start | bytes 442376 | tf_op jit(solution)/shard_map/ppermute | solution.py:39
  120.3 8.1 %collective-permute-start.19 = (bf16[2,32,1152]{2,1,0:T(8,128)(2,1)S(1)}, bf16[2,32,1152]{2,1,0:T(8,128)(2,1)S(1)}, u32[]{:S(2)}, u32[]{:S(2)}) collective-permute-start(bf16[2,32,1152]{2,1,0:T(8,128)(2,1)S(1)} %minimum_add_fusion), channel_id=1, source_target_pairs={{0,2},{2,4},{4,6},{6,8},{8,10},{10,12},{12,14},{14,0},{1,3},{3,5},... | collective-permute-start | bytes 442376 | tf_op jit(solution)/shard_map/ppermute | solution.py:39
  125.5 5.9 %collective-permute-start.24 = (bf16[2,32,1152]{2,1,0:T(8,128)(2,1)S(1)}, bf16[2,32,1152]{2,1,0:T(8,128)(2,1)S(1)}, u32[]{:S(2)}, u32[]{:S(2)}) collective-permute-start(bf16[2,32,1152]{2,1,0:T(8,128)(2,1)S(1)} %collective-permute-done.16.refs_5_), channel_id=1, source_target_pairs={{0,1},{1,0},{2,3},{3,2},{4,5},{5,4},{6,7},{7,6},{8,9},{9,8},{10,11... | collective-permute-start | bytes 442376 | tf_op jit(solution)/shard_map/ppermute | solution.py:39
  126.4 6.6 %collective-permute-start.23 = (bf16[2,32,1152]{2,1,0:T(8,128)(2,1)S(1)}, bf16[2,32,1152]{2,1,0:T(8,128)(2,1)S(1)}, u32[]{:S(2)}, u32[]{:S(2)}) collective-permute-start(bf16[2,32,1152]{2,1,0:T(8,128)(2,1)S(1)} %collective-permute-done.15.refs_4_), channel_id=1, source_target_pairs={{0,1},{1,0},{2,3},{3,2},{4,5},{5,4},{6,7},{7,6},{8,9},{9,8},{10,11... | collective-permute-start | bytes 442376 | tf_op jit(solution)/shard_map/ppermute | solution.py:39
  127.6 7.1 %collective-permute-start.26 = (bf16[2,32,1152]{2,1,0:T(8,128)(2,1)S(1)}, bf16[2,32,1152]{2,1,0:T(8,128)(2,1)S(1)}, u32[]{:S(2)}, u32[]{:S(2)}) collective-permute-start(bf16[2,32,1152]{2,1,0:T(8,128)(2,1)S(1)} %collective-permute-done.20.refs_7_), channel_id=1, source_target_pairs={{0,1},{1,0},{2,3},{3,2},{4,5},{5,4},{6,7},{7,6},{8,9},{9,8},{10,11... | collective-permute-start | bytes 442376 | tf_op jit(solution)/shard_map/ppermute | solution.py:39
  128.5 7.7 %collective-permute-start.25 = (bf16[2,32,1152]{2,1,0:T(8,128)(2,1)S(1)}, bf16[2,32,1152]{2,1,0:T(8,128)(2,1)S(1)}, u32[]{:S(2)}, u32[]{:S(2)}) collective-permute-start(bf16[2,32,1152]{2,1,0:T(8,128)(2,1)S(1)} %collective-permute-done.19.refs_6_), channel_id=1, source_target_pairs={{0,1},{1,0},{2,3},{3,2},{4,5},{5,4},{6,7},{7,6},{8,9},{9,8},{10,11... | collective-permute-start | bytes 442376 | tf_op jit(solution)/shard_map/ppermute | solution.py:39
  (5 other events, 56.6 us)

commit v7 on v5

--- a/solution.py
+++ b/solution.py
@@ -73,6 +73,13 @@
         out[:, factor_columns(f)] = total.astype(out.dtype)
 
 
+def project_own(which, acts, cots, act_factor, grad_factor, came, out):
+    rows = pl.ds(pl.multiple_of(which[0] * HALF, HALF), HALF)
+    for f, (part, factor) in enumerate(((acts, act_factor), (cots, grad_factor))):
+        cols = factor_columns(f)
+        out[:, cols] = (dot(part[rows, :], factor[...]) + came[:, cols].astype(f32)).astype(bf16)
+
+
 def project_sum(parts, copies):
     total = parts[0].astype(f32)
     for k in range(1, X * YH):
@@ -86,8 +93,8 @@
     return slice(f * WIDTH, (f + 1) * WIDTH)
 
 
-def image_rows(factor, z, side, mine, other, f):
-    rows = [factor[pl.ds(lax.rem(z + (e + Z), Z), 1), pl.ds(side, 1)].reshape(PART, WIDTH) for e in REDUCE]
+def image_rows(factor, z, side, mine, other, f, chunks):
+    rows = [factor[pl.ds(lax.rem(z + (e + Z), Z), 1), pl.ds(side, 1)].reshape(PART, WIDTH) for e in chunks]
     rows = jnp.concatenate(rows, axis=0)
     return (
         dot_t(rows, mine[:, factor_columns(f)]),
@@ -95,18 +102,25 @@
     )
 
 
+def image_first(at, act_factor, grad_factor, mine, other, out):
+    for f, factor in enumerate((act_factor, grad_factor)):
+        first, second = image_rows(factor, at[0], 1 - at[1], mine, other, f, REDUCE[:1])
+        out[0, f, :, :HALF] = first.astype(bf16)
+        out[0, f, :, HALF:] = second.astype(bf16)
+
+
 def image_away(at, act_factor, grad_factor, mine, other, *outs):
     for f, factor in enumerate((act_factor, grad_factor)):
-        first, second = image_rows(factor, at[0], 1 - at[1], mine, other, f)
-        for n, (group, k) in enumerate(PLACES):
+        first, second = image_rows(factor, at[0], 1 - at[1], mine, other, f, REDUCE[1:])
+        for n, (group, k) in enumerate(PLACES[1:]):
             rows = slice(n * PART, (n + 1) * PART)
-            outs[group][k, f, :, :HALF] = first[rows].astype(bf16)
-            outs[group][k, f, :, HALF:] = second[rows].astype(bf16)
+            outs[group - 1][k, f, :, :HALF] = first[rows].astype(bf16)
+            outs[group - 1][k, f, :, HALF:] = second[rows].astype(bf16)
 
 
 def image_own(at, act_factor, grad_factor, mine, other, *outs):
     for f, factor in enumerate((act_factor, grad_factor)):
-        first, second = image_rows(factor, at[0], at[1], mine, other, f)
+        first, second = image_rows(factor, at[0], at[1], mine, other, f, REDUCE)
         for k in range(Z):
             rows = slice(k * PART, (k + 1) * PART)
             outs[k][f, :, :HALF] = first[rows]
@@ -176,8 +190,7 @@
     setup = dict(flops=product, memory=pltpu.HBM, scratch=scratch, room=58)
     (away,) = kernel_call(project, [((HALF, 2 * WIDTH), bf16)], *given, index=[1 - core], **setup)
     came = shift(away, "core", CORE)
-    (total,) = kernel_call(project, [((HALF, 2 * WIDTH), f32)], *given, index=[core], **setup)
-    total = (total + came.astype(f32)).astype(bf16)
+    (total,) = kernel_call(project_own, [((HALF, 2 * WIDTH), bf16)], *given, came, index=[core], flops=product)
     group = X * YH
     chunks = (group, HALF // group, 2 * WIDTH)
     parts = lax.all_to_all(total.reshape(chunks), ("x", "yh"), 0, 0, tiled=True)
@@ -188,7 +201,8 @@
     factors = [f.reshape(Z, YL, PART, WIDTH) for f in (act_factor, grad_factor)]
     shape = (2, PART, TOKENS)
     sent = [((sum(g == group for g, _ in PLACES),) + shape, bf16) for group in range(5)]
-    away = kernel_call(image_away, sent, *factors, mine, other, index=[z, yl], flops=product)
+    first = kernel_call(image_first, sent[:1], *factors, mine, other, index=[z, yl], flops=product // Z)
+    away = first + kernel_call(image_away, sent[1:], *factors, mine, other, index=[z, yl], flops=product)
     away = [shift(a, "yl", YL) for a in away]
     *own, squares = kernel_call(
         image_own, [(shape, f32)] * Z + [((2, WIDTH), f32)], *factors, mine, other, index=[z, yl], flops=product
@@ -213,7 +227,7 @@
         up, down = shift(up, "z", Z, 1), shift(down, "z", Z, -1)
         held += [up, down]
         crossed += [shift(up, "yl", YL), shift(down, "yl", YL)]
-    up = shift(after(up, crossed[1], crossed[2]), "z", Z, 1)
+    up = shift(after(up, crossed[1], crossed[2], crossed[3]), "z", Z, 1)
     held.append(up)
     crossed.append(shift(up, "yl", YL))
     changed, squares = kernel_call(

time: 130 us -> 129 us (level)
  other arithmetic: 2.38 us -> 0.49 us
  starting transfers between devices: 35.6 us -> 37.4 us
  Pallas kernels: 12.9 us -> 11.6 us
    convert_element_type x1 -> x0, other arithmetic: 1.92 us -> none  [local(): total = (total + came.astype(f32)).astype(bf16)]
    ppermute x29, starting transfers between devices: 35.6 us -> 37.4 us  [shift(): return lax.ppermute(a, axis, [(i, (i + by) % size) for i in range(size)])]
    pallas_call x8 -> x9, Pallas kernels: 12.9 us -> 11.6 us  [kernel_call(): pl.pallas_call(body, out_shape=[jax.ShapeDtypeStruct(shape, dtype) for sh...]
  transfers between devices with their start and end apart: 29 -> 29, of which waited for: 17 -> 18; matrix products, arithmetic and copies ran while one was open for 0% -> 0% of each run, Pallas kernels for 5% -> 3%
where the time goes in v7:
time: 129 us
  blocking collectives  42.2 us (33%)
  starting transfers between devices  37.4 us (29%)
  waiting for transfers between devices  36.1 us (28%)
  Pallas kernels  11.6 us (9%)
    ppermute x29, starting transfers between devices, shift(): return lax.ppermute(a, axis, [(i, (i + by) % size) for i in range(size)])  37.4 us
    ppermute x29, waiting for transfers between devices, shift(): return lax.ppermute(a, axis, [(i, (i + by) % size) for i in range(size)])  36.1 us
    all_to_all x1, blocking collectives, local(): parts = lax.all_to_all(total.reshape(chunks), ('x', 'yh'), 0, 0, tiled=True)  23 us
    all_to_all x1, blocking collectives, local(): lax.all_to_all(copies, ('x', 'yh'), 0, 0, tiled=True)  19.2 us
    pallas_call x9, Pallas kernels, kernel_call(): pl.pallas_call(body, out_shape=[jax.ShapeDtypeStruct(shape, dtype) for sh...  11.6 us
  transfers between devices with their start and end apart: 29, of which 18 were waited for; matrix products, arithmetic and copies ran while one was open for 0% of the time, Pallas kernels for 3%

profile of v7, /device:TPU:8, one launch (start us, length us, event | category | flops | bytes accessed | tf_op | source)
XLA Modules:
  0.0 128.6 jit_solution(1797997804865777984)
XLA Ops:
  0.7 3.2 %shard_map.59 = bf16[512,1024]{1,0:T(8,128)(2,1)} custom-call(s32[1]{0:T(128)} %bitcast.5.which, bf16[1024,512]{1,0:T(8,128)(2,1)} %acts.3, bf16[1024,512]{1,0:T(8,128)(2,1)} %cots.3, bf16[512,512]{1,0:T(8,128)(2,1)} %act_factor.3, bf16[512,512]{1,0:T(8,128)(2,1)} %grad_factor.3), custom_call_target="tpu_custom_call" | custom-call | flops 536870912 | bytes 3145732 | tf_op jit(solution)/shard_map/pallas_call | solution.py:48
  4.0 2.9 %collective-permute-done.came = bf16[512,1024]{1,0:T(8,128)(2,1)S(1)} collective-permute-done((bf16[512,1024]{1,0:T(8,128)(2,1)}, bf16[512,1024]{1,0:T(8,128)(2,1)S(1)}, u32[]{:S(2)}, u32[]{:S(2)}) %collective-permute-start) | collective-permute-done | bytes 1048608 | tf_op jit(solution)/shard_map/ppermute | solution.py:39
  7.6 23.0 %all_to_all.10.parts = bf16[8,64,1024]{2,1,0:T(8,128)(2,1)S(1)} all-to-all(bf16[8,64,1024]{2,1,0:T(8,128)(2,1)S(1)} %bitcast.57), channel_id=1, replica_groups=mesh['x'=4,'yh'=2,'core'=2,'z'=8,'yl'=2] {'x','yh'}, dimensions={0} | all-to-all | bytes 2097152 | tf_op jit(solution)/shard_map/all_to_all | solution.py:196
  30.7 19.2 %all_to_all.11 = bf16[8,64,1024]{2,1,0:T(8,128)(2,1)S(1)} all-to-all(bf16[8,64,1024]{2,1,0:T(8,128)(2,1)S(1)} %shard_map.61), channel_id=1, replica_groups=mesh['x'=4,'yh'=2,'core'=2,'z'=8,'yl'=2] {'x','yh'}, dimensions={0} | all-to-all | bytes 2097152 | tf_op jit(solution)/shard_map/all_to_all | solution.py:198
  50.1 2.6 %collective-permute-done.1.other = bf16[512,1024]{1,0:T(8,128)(2,1)S(1)} collective-permute-done((bf16[512,1024]{1,0:T(8,128)(2,1)S(1)}, bf16[512,1024]{1,0:T(8,128)(2,1)S(1)}, u32[]{:S(2)}, u32[]{:S(2)}) %collective-permute-start.1) | collective-permute-done | bytes 1048608 | tf_op jit(solution)/shard_map/ppermute | solution.py:39
  57.4 1.8 %shard_map.62 = (f32[2,32,1024]{2,1,0:T(8,128)S(1)}, f32[2,32,1024]{2,1,0:T(8,128)S(1)}, f32[2,32,1024]{2,1,0:T(8,128)S(1)}, f32[2,32,1024]{2,1,0:T(8,128)S(1)},...) custom-call(s32[2]{0:T(128)S(1)} %pad_add_fusion.at, ...), custom_call_target="tpu_custom_call" | custom-call | flops 536870912 | bytes 3145736 | tf_op jit(solution)/shard_map/pallas_call | solution.py:48
  59.8 2.0 %collective-permute-start.7 = (bf16[2,32,1024]{2,1,0:T(8,128)(2,1)S(1)}, bf16[2,32,1024]{2,1,0:T(8,128)(2,1)S(1)}, u32[]{:S(2)}, u32[]{:S(2)}) collective-permute-start(bf16[2,32,1024]{2,1,0:T(8,128)(2,1)S(1)} %fusion.5), channel_id=1, source_target_pairs={{0,2},{2,4},{4,6},{6,8},{8,10},{10,12},{12,14},{14,0},{1,3},{3,5},... | collective-permute-start | bytes 393224 | tf_op jit(solution)/shard_map/ppermute | solution.py:39
  61.7 1.9 %collective-permute-start.4 = (bf16[2,2,32,1024]{3,2,1,0:T(8,128)(2,1)S(1)}, bf16[2,2,32,1024]{3,2,1,0:T(8,128)(2,1)S(1)}, u32[]{:S(2)}, u32[]{:S(2)}) collective-permute-start(bf16[2,2,32,1024]{3,2,1,0:T(8,128)(2,1)S(1)} %get-tuple-element.24), channel_id=1, source_target_pairs={{0,1},{1,0},{2,3},{3,2},{4,5},{5,4},{6,7},{7,6},{8,9},{9,8},{10,11... | collective-permute-start | bytes 786440 | tf_op jit(solution)/shard_map/ppermute | solution.py:39
  63.6 5.0 %collective-permute-done.7 = bf16[2,32,1024]{2,1,0:T(8,128)(2,1)S(1)} collective-permute-done((bf16[2,32,1024]{2,1,0:T(8,128)(2,1)S(1)}, bf16[2,32,1024]{2,1,0:T(8,128)(2,1)S(1)}, u32[]{:S(2)}, u32[]{:S(2)}) %collective-permute-start.7) | collective-permute-done | bytes 131104 | tf_op jit(solution)/shard_map/ppermute | solution.py:39
  68.7 3.2 %collective-permute-start.11 = (bf16[2,32,1024]{2,1,0:T(8,128)(2,1)S(1)}, bf16[2,32,1024]{2,1,0:T(8,128)(2,1)S(1)}, u32[]{:S(2)}, u32[]{:S(2)}) collective-permute-start(bf16[2,32,1024]{2,1,0:T(8,128)(2,1)S(1)} %get-tuple-element.40), channel_id=1, source_target_pairs={{0,14},{2,0},{4,2},{6,4},{8,6},{10,8},{12,10},{14,12},{1,15},{3,1}... | collective-permute-start | bytes 393224 | tf_op jit(solution)/shard_map/ppermute | solution.py:39
  74.4 3.7 %collective-permute-done.8 = bf16[2,32,1024]{2,1,0:T(8,128)(2,1)S(1)} collective-permute-done((bf16[2,32,1024]{2,1,0:T(8,128)(2,1)S(1)}, bf16[2,32,1024]{2,1,0:T(8,128)(2,1)S(1)}, u32[]{:S(2)}, u32[]{:S(2)}) %collective-permute-start.8) | collective-permute-done | bytes 131104 | tf_op jit(solution)/shard_map/ppermute | solution.py:39
  78.3 2.0 %collective-permute-start.9 = (bf16[2,32,1024]{2,1,0:T(8,128)(2,1)S(1)}, bf16[2,32,1024]{2,1,0:T(8,128)(2,1)S(1)}, u32[]{:S(2)}, u32[]{:S(2)}) collective-permute-start(bf16[2,32,1024]{2,1,0:T(8,128)(2,1)S(1)} %get-tuple-element.39), channel_id=1, source_target_pairs={{0,2},{2,4},{4,6},{6,8},{8,10},{10,12},{12,14},{14,0},{1,3},{3,5},... | collective-permute-start | bytes 393224 | tf_op jit(solution)/shard_map/ppermute | solution.py:39
  81.7 1.6 %collective-permute-done.12 = bf16[2,32,1024]{2,1,0:T(8,128)(2,1)S(1)} collective-permute-done((bf16[2,32,1024]{2,1,0:T(8,128)(2,1)S(1)}, bf16[2,32,1024]{2,1,0:T(8,128)(2,1)S(1)}, u32[]{:S(2)}, u32[]{:S(2)}) %collective-permute-start.12) | collective-permute-done | bytes 131104 | tf_op jit(solution)/shard_map/ppermute | solution.py:39
  84.7 2.1 %collective-permute-start.10 = (bf16[2,32,1024]{2,1,0:T(8,128)(2,1)S(1)}, bf16[2,32,1024]{2,1,0:T(8,128)(2,1)S(1)}, u32[]{:S(2)}, u32[]{:S(2)}) collective-permute-start(bf16[2,32,1024]{2,1,0:T(8,128)(2,1)S(1)} %get-tuple-element.37), channel_id=1, source_target_pairs={{0,2},{2,4},{4,6},{6,8},{8,10},{10,12},{12,14},{14,0},{1,3},{3,5},... | collective-permute-start | bytes 393224 | tf_op jit(solution)/shard_map/ppermute | solution.py:39
  88.2 3.8 %collective-permute-done.10.up = bf16[2,32,1024]{2,1,0:T(8,128)(2,1)S(1)} collective-permute-done((bf16[2,32,1024]{2,1,0:T(8,128)(2,1)S(1)}, bf16[2,32,1024]{2,1,0:T(8,128)(2,1)S(1)}, u32[]{:S(2)}, u32[]{:S(2)}) %collective-permute-start.10) | collective-permute-done | bytes 131104 | tf_op jit(solution)/shard_map/ppermute | solution.py:39
  93.3 2.4 %collective-permute-start.15 = (bf16[2,32,1152]{2,1,0:T(8,128)(2,1)S(1)}, bf16[2,32,1152]{2,1,0:T(8,128)(2,1)S(1)}, u32[]{:S(2)}, u32[]{:S(2)}) collective-permute-start(bf16[2,32,1152]{2,1,0:T(8,128)(2,1)S(1)} %shard_map.65.refs_0_), channel_id=1, source_target_pairs={{0,14},{2,0},{4,2},{6,4},{8,6},{10,8},{12,10},{14,12},{1,15},{3,1}... | collective-permute-start | bytes 442376 | tf_op jit(solution)/shard_map/ppermute | solution.py:39
  97.1 2.3 %collective-permute-done.14.refs_1_ = bf16[2,32,1152]{2,1,0:T(8,128)(2,1)S(1)} collective-permute-done((bf16[2,32,1152]{2,1,0:T(8,128)(2,1)S(1)}, bf16[2,32,1152]{2,1,0:T(8,128)(2,1)S(1)}, u32[]{:S(2)}, u32[]{:S(2)}) %collective-permute-start.14) | collective-permute-done | bytes 147488 | tf_op jit(solution)/shard_map/ppermute | solution.py:39
  99.5 3.3 %collective-permute-start.17 = (bf16[2,32,1152]{2,1,0:T(8,128)(2,1)S(1)}, bf16[2,32,1152]{2,1,0:T(8,128)(2,1)S(1)}, u32[]{:S(2)}, u32[]{:S(2)}) collective-permute-start(bf16[2,32,1152]{2,1,0:T(8,128)(2,1)S(1)} %collective-permute-done.15.refs_2_), channel_id=1, source_target_pairs={{0,14},{2,0},{4,2},{6,4},{8,6},{10,8},{12,10},{14,12},{1,15},{3,1}... | collective-permute-start | bytes 442376 | tf_op jit(solution)/shard_map/ppermute | solution.py:39
  107.8 3.2 %collective-permute-start.20 = (bf16[2,32,1152]{2,1,0:T(8,128)(2,1)S(1)}, bf16[2,32,1152]{2,1,0:T(8,128)(2,1)S(1)}, u32[]{:S(2)}, u32[]{:S(2)}) collective-permute-start(bf16[2,32,1152]{2,1,0:T(8,128)(2,1)S(1)} %get-tuple-element.42), channel_id=1, source_target_pairs={{0,14},{2,0},{4,2},{6,4},{8,6},{10,8},{12,10},{14,12},{1,15},{3,1}... | collective-permute-start | bytes 442376 | tf_op jit(solution)/shard_map/ppermute | solution.py:39
  111.5 1.8 %collective-permute-done.19.refs_5_ = bf16[2,32,1152]{2,1,0:T(8,128)(2,1)S(1)} collective-permute-done((bf16[2,32,1152]{2,1,0:T(8,128)(2,1)S(1)}, bf16[2,32,1152]{2,1,0:T(8,128)(2,1)S(1)}, u32[]{:S(2)}, u32[]{:S(2)}) %collective-permute-start.19) | collective-permute-done | bytes 147488 | tf_op jit(solution)/shard_map/ppermute | solution.py:39
  114.8 1.6 %collective-permute-start.25 = (bf16[2,32,1152]{2,1,0:T(8,128)(2,1)S(1)}, bf16[2,32,1152]{2,1,0:T(8,128)(2,1)S(1)}, u32[]{:S(2)}, u32[]{:S(2)}) collective-permute-start(bf16[2,32,1152]{2,1,0:T(8,128)(2,1)S(1)} %collective-permute-done.17.refs_4_), channel_id=1, source_target_pairs={{0,1},{1,0},{2,3},{3,2},{4,5},{5,4},{6,7},{7,6},{8,9},{9,8},{10,11... | collective-permute-start | bytes 442376 | tf_op jit(solution)/shard_map/ppermute | solution.py:39
  118.5 2.7 %collective-permute-done.24.refs_7_ = bf16[2,32,1152]{2,1,0:T(8,128)(2,1)S(1)} collective-permute-done((bf16[2,32,1152]{2,1,0:T(8,128)(2,1)S(1)}, bf16[2,32,1152]{2,1,0:T(8,128)(2,1)S(1)}, u32[]{:S(2)}, u32[]{:S(2)}) %collective-permute-start.24) | collective-permute-done | bytes 147488 | tf_op jit(solution)/shard_map/ppermute | solution.py:39
  123.3 3.1 %collective-permute-done.28.refs_7_ = bf16[2,32,1152]{2,1,0:T(8,128)(2,1)S(1)} collective-permute-done((bf16[2,32,1152]{2,1,0:T(8,128)(2,1)S(1)}, bf16[2,32,1152]{2,1,0:T(8,128)(2,1)S(1)}, u32[]{:S(2)}, u32[]{:S(2)}) %collective-permute-start.28) | collective-permute-done | bytes 147488 | tf_op jit(solution)/shard_map/ppermute | solution.py:39
  126.3 2.3 %shard_map.67 = (bf16[8,2,32,512]{3,2,1,0:T(8,128)(2,1)}, bf16[8,2,32,512]{3,2,1,0:T(8,128)(2,1)}) custom-call(s32[2]{0:T(128)S(1)} %pad_add_fusion.at, bf16[8,2,32,512]{3,2,1,0:T(8,128)(2,1)S(1)} %bitcast.52, bf16[8,2,32,512]{3,2,1,0:T(8,128)(2,1)S(1)} %bitcast.56, bf16[512,1024]{1,0:T(8,128)(2,1)S(1)} %bitcast.48, ...), custom_call_target="tpu_custom_call" | custom-call | flops 536870912 | bytes 5374984 | tf_op jit(solution)/shard_map/pallas_call | solution.py:48
  (60 shorter events, 27.2 us)
Async XLA Ops:
  53.9 5.8 %collective-permute-start.6 = (bf16[1,2,32,1024]{3,2,1,0:T(8,128)(2,1)S(1)}, bf16[1,2,32,1024]{3,2,1,0:T(8,128)(2,1)S(1)}, u32[]{:S(2)}, u32[]{:S(2)}) collective-permute-start(bf16[1,2,32,1024]{3,2,1,0:T(8,128)(2,1)S(1)} %shard_map.64), channel_id=1, source_target_pairs={{0,1},{1,0},{2,3},{3,2},{4,5},{5,4},{6,7},{7,6},{8,9},{9,8},{10,11... | collective-permute-start | bytes 393224 | tf_op jit(solution)/shard_map/ppermute | solution.py:39
  56.6 12.0 %collective-permute-start.5 = (bf16[2,2,32,1024]{3,2,1,0:T(8,128)(2,1)S(1)}, bf16[2,2,32,1024]{3,2,1,0:T(8,128)(2,1)S(1)}, u32[]{:S(2)}, u32[]{:S(2)}) collective-permute-start(bf16[2,2,32,1024]{3,2,1,0:T(8,128)(2,1)S(1)} %get-tuple-element.26), channel_id=1, source_target_pairs={{0,1},{1,0},{2,3},{3,2},{4,5},{5,4},{6,7},{7,6},{8,9},{9,8},{10,11... | collective-permute-start | bytes 786440 | tf_op jit(solution)/shard_map/ppermute | solution.py:39
  59.8 8.9 %collective-permute-start.7 = (bf16[2,32,1024]{2,1,0:T(8,128)(2,1)S(1)}, bf16[2,32,1024]{2,1,0:T(8,128)(2,1)S(1)}, u32[]{:S(2)}, u32[]{:S(2)}) collective-permute-start(bf16[2,32,1024]{2,1,0:T(8,128)(2,1)S(1)} %fusion.5), channel_id=1, source_target_pairs={{0,2},{2,4},{4,6},{6,8},{8,10},{10,12},{12,14},{14,0},{1,3},{3,5},... | collective-permute-start | bytes 393224 | tf_op jit(solution)/shard_map/ppermute | solution.py:39
  61.7 11.5 %collective-permute-start.4 = (bf16[2,2,32,1024]{3,2,1,0:T(8,128)(2,1)S(1)}, bf16[2,2,32,1024]{3,2,1,0:T(8,128)(2,1)S(1)}, u32[]{:S(2)}, u32[]{:S(2)}) collective-permute-start(bf16[2,2,32,1024]{3,2,1,0:T(8,128)(2,1)S(1)} %get-tuple-element.24), channel_id=1, source_target_pairs={{0,1},{1,0},{2,3},{3,2},{4,5},{5,4},{6,7},{7,6},{8,9},{9,8},{10,11... | collective-permute-start | bytes 786440 | tf_op jit(solution)/shard_map/ppermute | solution.py:39
  68.7 5.7 %collective-permute-start.11 = (bf16[2,32,1024]{2,1,0:T(8,128)(2,1)S(1)}, bf16[2,32,1024]{2,1,0:T(8,128)(2,1)S(1)}, u32[]{:S(2)}, u32[]{:S(2)}) collective-permute-start(bf16[2,32,1024]{2,1,0:T(8,128)(2,1)S(1)} %get-tuple-element.40), channel_id=1, source_target_pairs={{0,14},{2,0},{4,2},{6,4},{8,6},{10,8},{12,10},{14,12},{1,15},{3,1}... | collective-permute-start | bytes 393224 | tf_op jit(solution)/shard_map/ppermute | solution.py:39
  71.9 6.2 %collective-permute-start.8 = (bf16[2,32,1024]{2,1,0:T(8,128)(2,1)S(1)}, bf16[2,32,1024]{2,1,0:T(8,128)(2,1)S(1)}, u32[]{:S(2)}, u32[]{:S(2)}) collective-permute-start(bf16[2,32,1024]{2,1,0:T(8,128)(2,1)S(1)} %get-tuple-element.41), channel_id=1, source_target_pairs={{0,2},{2,4},{4,6},{6,8},{8,10},{10,12},{12,14},{14,0},{1,3},{3,5},... | collective-permute-start | bytes 393224 | tf_op jit(solution)/shard_map/ppermute | solution.py:39
  71.9 9.7 %collective-permute-start.3 = (bf16[2,2,32,1024]{3,2,1,0:T(8,128)(2,1)S(1)}, bf16[2,2,32,1024]{3,2,1,0:T(8,128)(2,1)S(1)}, u32[]{:S(2)}, u32[]{:S(2)}) collective-permute-start(bf16[2,2,32,1024]{3,2,1,0:T(8,128)(2,1)S(1)} %get-tuple-element.22), channel_id=1, source_target_pairs={{0,1},{1,0},{2,3},{3,2},{4,5},{5,4},{6,7},{7,6},{8,9},{9,8},{10,11... | collective-permute-start | bytes 786440 | tf_op jit(solution)/shard_map/ppermute | solution.py:39
  78.3 6.3 %collective-permute-start.9 = (bf16[2,32,1024]{2,1,0:T(8,128)(2,1)S(1)}, bf16[2,32,1024]{2,1,0:T(8,128)(2,1)S(1)}, u32[]{:S(2)}, u32[]{:S(2)}) collective-permute-start(bf16[2,32,1024]{2,1,0:T(8,128)(2,1)S(1)} %get-tuple-element.39), channel_id=1, source_target_pairs={{0,2},{2,4},{4,6},{6,8},{8,10},{10,12},{12,14},{14,0},{1,3},{3,5},... | collective-permute-start | bytes 393224 | tf_op jit(solution)/shard_map/ppermute | solution.py:39
  80.3 7.9 %collective-permute-start.2 = (bf16[1,2,32,1024]{3,2,1,0:T(8,128)(2,1)S(1)}, bf16[1,2,32,1024]{3,2,1,0:T(8,128)(2,1)S(1)}, u32[]{:S(2)}, u32[]{:S(2)}) collective-permute-start(bf16[1,2,32,1024]{3,2,1,0:T(8,128)(2,1)S(1)} %get-tuple-element.20), channel_id=1, source_target_pairs={{0,1},{1,0},{2,3},{3,2},{4,5},{5,4},{6,7},{7,6},{8,9},{9,8},{10,11... | collective-permute-start | bytes 393224 | tf_op jit(solution)/shard_map/ppermute | solution.py:39
  84.7 7.3 %collective-permute-start.10 = (bf16[2,32,1024]{2,1,0:T(8,128)(2,1)S(1)}, bf16[2,32,1024]{2,1,0:T(8,128)(2,1)S(1)}, u32[]{:S(2)}, u32[]{:S(2)}) collective-permute-start(bf16[2,32,1024]{2,1,0:T(8,128)(2,1)S(1)} %get-tuple-element.37), channel_id=1, source_target_pairs={{0,2},{2,4},{4,6},{6,8},{8,10},{10,12},{12,14},{14,0},{1,3},{3,5},... | collective-permute-start | bytes 393224 | tf_op jit(solution)/shard_map/ppermute | solution.py:39
  92.2 7.2 %collective-permute-start.14 = (bf16[2,32,1152]{2,1,0:T(8,128)(2,1)S(1)}, bf16[2,32,1152]{2,1,0:T(8,128)(2,1)S(1)}, u32[]{:S(2)}, u32[]{:S(2)}) collective-permute-start(bf16[2,32,1152]{2,1,0:T(8,128)(2,1)S(1)} %shard_map.65.refs_0_), channel_id=1, source_target_pairs={{0,2},{2,4},{4,6},{6,8},{8,10},{10,12},{12,14},{14,0},{1,3},{3,5},... | collective-permute-start | bytes 442376 | tf_op jit(solution)/shard_map/ppermute | solution.py:39
  93.3 6.1 %collective-permute-start.15 = (bf16[2,32,1152]{2,1,0:T(8,128)(2,1)S(1)}, bf16[2,32,1152]{2,1,0:T(8,128)(2,1)S(1)}, u32[]{:S(2)}, u32[]{:S(2)}) collective-permute-start(bf16[2,32,1152]{2,1,0:T(8,128)(2,1)S(1)} %shard_map.65.refs_0_), channel_id=1, source_target_pairs={{0,14},{2,0},{4,2},{6,4},{8,6},{10,8},{12,10},{14,12},{1,15},{3,1}... | collective-permute-start | bytes 442376 | tf_op jit(solution)/shard_map/ppermute | solution.py:39
  95.8 9.0 %collective-permute-start.18 = (bf16[2,32,1152]{2,1,0:T(8,128)(2,1)S(1)}, bf16[2,32,1152]{2,1,0:T(8,128)(2,1)S(1)}, u32[]{:S(2)}, u32[]{:S(2)}) collective-permute-start(bf16[2,32,1152]{2,1,0:T(8,128)(2,1)S(1)} %shard_map.65.refs_0_), channel_id=1, source_target_pairs={{0,1},{1,0},{2,3},{3,2},{4,5},{5,4},{6,7},{7,6},{8,9},{9,8},{10,11... | collective-permute-start | bytes 442376 | tf_op jit(solution)/shard_map/ppermute | solution.py:39
  99.5 6.5 %collective-permute-start.16 = (bf16[2,32,1152]{2,1,0:T(8,128)(2,1)S(1)}, bf16[2,32,1152]{2,1,0:T(8,128)(2,1)S(1)}, u32[]{:S(2)}, u32[]{:S(2)}) collective-permute-start(bf16[2,32,1152]{2,1,0:T(8,128)(2,1)S(1)} %collective-permute-done.14.refs_1_), channel_id=1, source_target_pairs={{0,2},{2,4},{4,6},{6,8},{8,10},{10,12},{12,14},{14,0},{1,3},{3,5},... | collective-permute-start | bytes 442376 | tf_op jit(solution)/shard_map/ppermute | solution.py:39
  99.5 6.9 %collective-permute-start.17 = (bf16[2,32,1152]{2,1,0:T(8,128)(2,1)S(1)}, bf16[2,32,1152]{2,1,0:T(8,128)(2,1)S(1)}, u32[]{:S(2)}, u32[]{:S(2)}) collective-permute-start(bf16[2,32,1152]{2,1,0:T(8,128)(2,1)S(1)} %collective-permute-done.15.refs_2_), channel_id=1, source_target_pairs={{0,14},{2,0},{4,2},{6,4},{8,6},{10,8},{12,10},{14,12},{1,15},{3,1}... | collective-permute-start | bytes 442376 | tf_op jit(solution)/shard_map/ppermute | solution.py:39
  102.7 8.2 %collective-permute-start.21 = (bf16[2,32,1152]{2,1,0:T(8,128)(2,1)S(1)}, bf16[2,32,1152]{2,1,0:T(8,128)(2,1)S(1)}, u32[]{:S(2)}, u32[]{:S(2)}) collective-permute-start(bf16[2,32,1152]{2,1,0:T(8,128)(2,1)S(1)} %collective-permute-done.14.refs_1_), channel_id=1, source_target_pairs={{0,1},{1,0},{2,3},{3,2},{4,5},{5,4},{6,7},{7,6},{8,9},{9,8},{10,11... | collective-permute-start | bytes 442376 | tf_op jit(solution)/shard_map/ppermute | solution.py:39
  104.0 7.5 %collective-permute-start.22 = (bf16[2,32,1152]{2,1,0:T(8,128)(2,1)S(1)}, bf16[2,32,1152]{2,1,0:T(8,128)(2,1)S(1)}, u32[]{:S(2)}, u32[]{:S(2)}) collective-permute-start(bf16[2,32,1152]{2,1,0:T(8,128)(2,1)S(1)} %collective-permute-done.15.refs_2_), channel_id=1, source_target_pairs={{0,1},{1,0},{2,3},{3,2},{4,5},{5,4},{6,7},{7,6},{8,9},{9,8},{10,11... | collective-permute-start | bytes 442376 | tf_op jit(solution)/shard_map/ppermute | solution.py:39
  106.4 6.9 %collective-permute-start.19 = (bf16[2,32,1152]{2,1,0:T(8,128)(2,1)S(1)}, bf16[2,32,1152]{2,1,0:T(8,128)(2,1)S(1)}, u32[]{:S(2)}, u32[]{:S(2)}) collective-permute-start(bf16[2,32,1152]{2,1,0:T(8,128)(2,1)S(1)} %get-tuple-element.43), channel_id=1, source_target_pairs={{0,2},{2,4},{4,6},{6,8},{8,10},{10,12},{12,14},{14,0},{1,3},{3,5},... | collective-permute-start | bytes 442376 | tf_op jit(solution)/shard_map/ppermute | solution.py:39
  106.5 8.2 %collective-permute-start.23 = (bf16[2,32,1152]{2,1,0:T(8,128)(2,1)S(1)}, bf16[2,32,1152]{2,1,0:T(8,128)(2,1)S(1)}, u32[]{:S(2)}, u32[]{:S(2)}) collective-permute-start(bf16[2,32,1152]{2,1,0:T(8,128)(2,1)S(1)} %collective-permute-done.16.refs_3_), channel_id=1, source_target_pairs={{0,1},{1,0},{2,3},{3,2},{4,5},{5,4},{6,7},{7,6},{8,9},{9,8},{10,11... | collective-permute-start | bytes 442376 | tf_op jit(solution)/shard_map/ppermute | solution.py:39
  107.8 9.2 %collective-permute-start.20 = (bf16[2,32,1152]{2,1,0:T(8,128)(2,1)S(1)}, bf16[2,32,1152]{2,1,0:T(8,128)(2,1)S(1)}, u32[]{:S(2)}, u32[]{:S(2)}) collective-permute-start(bf16[2,32,1152]{2,1,0:T(8,128)(2,1)S(1)} %get-tuple-element.42), channel_id=1, source_target_pairs={{0,14},{2,0},{4,2},{6,4},{8,6},{10,8},{12,10},{14,12},{1,15},{3,1}... | collective-permute-start | bytes 442376 | tf_op jit(solution)/shard_map/ppermute | solution.py:39
  114.7 6.4 %collective-permute-start.24 = (bf16[2,32,1152]{2,1,0:T(8,128)(2,1)S(1)}, bf16[2,32,1152]{2,1,0:T(8,128)(2,1)S(1)}, u32[]{:S(2)}, u32[]{:S(2)}) collective-permute-start(bf16[2,32,1152]{2,1,0:T(8,128)(2,1)S(1)} %minimum_add_fusion), channel_id=1, source_target_pairs={{0,2},{2,4},{4,6},{6,8},{8,10},{10,12},{12,14},{14,0},{1,3},{3,5},... | collective-permute-start | bytes 442376 | tf_op jit(solution)/shard_map/ppermute | solution.py:39
  114.8 8.4 %collective-permute-start.25 = (bf16[2,32,1152]{2,1,0:T(8,128)(2,1)S(1)}, bf16[2,32,1152]{2,1,0:T(8,128)(2,1)S(1)}, u32[]{:S(2)}, u32[]{:S(2)}) collective-permute-start(bf16[2,32,1152]{2,1,0:T(8,128)(2,1)S(1)} %collective-permute-done.17.refs_4_), channel_id=1, source_target_pairs={{0,1},{1,0},{2,3},{3,2},{4,5},{5,4},{6,7},{7,6},{8,9},{9,8},{10,11... | collective-permute-start | bytes 442376 | tf_op jit(solution)/shard_map/ppermute | solution.py:39
  116.4 6.8 %collective-permute-start.26 = (bf16[2,32,1152]{2,1,0:T(8,128)(2,1)S(1)}, bf16[2,32,1152]{2,1,0:T(8,128)(2,1)S(1)}, u32[]{:S(2)}, u32[]{:S(2)}) collective-permute-start(bf16[2,32,1152]{2,1,0:T(8,128)(2,1)S(1)} %collective-permute-done.19.refs_5_), channel_id=1, source_target_pairs={{0,1},{1,0},{2,3},{3,2},{4,5},{5,4},{6,7},{7,6},{8,9},{9,8},{10,11... | collective-permute-start | bytes 442376 | tf_op jit(solution)/shard_map/ppermute | solution.py:39
  116.9 6.3 %collective-permute-start.27 = (bf16[2,32,1152]{2,1,0:T(8,128)(2,1)S(1)}, bf16[2,32,1152]{2,1,0:T(8,128)(2,1)S(1)}, u32[]{:S(2)}, u32[]{:S(2)}) collective-permute-start(bf16[2,32,1152]{2,1,0:T(8,128)(2,1)S(1)} %collective-permute-done.20.refs_6_), channel_id=1, source_target_pairs={{0,1},{1,0},{2,3},{3,2},{4,5},{5,4},{6,7},{7,6},{8,9},{9,8},{10,11... | collective-permute-start | bytes 442376 | tf_op jit(solution)/shard_map/ppermute | solution.py:39
  (9 other events, 46.1 us)

commit v8 on v7

--- a/solution.py
+++ b/solution.py
@@ -13,7 +13,9 @@
 ROWS = D // (X * YH * CORE)
 WIDTH = D // (Z * YL)
 HALF = TOKENS // CORE
-EXTRA = 128
+EXTRA = 16
+LANES = 128
+BLOCKS = TOKENS // LANES
 PART = ROWS // (Z * YL)
 
 REDUCE = (4, -3, 3, -2, 2, -1, 1, 0)
@@ -131,20 +133,27 @@
 
 def last_sum(own, away, up, down, squares, out):
     total = own[...] + away[0].astype(f32) + up[...].astype(f32) + down[...].astype(f32)
-    out[:, :, :TOKENS] = total.astype(bf16)
-    row = lax.broadcasted_iota(jnp.int32, (PART, EXTRA), 0)
+    total = total.astype(bf16)
+    for n in range(2 * BLOCKS):
+        f, block = divmod(n, BLOCKS)
+        out[n * PART : (n + 1) * PART, :] = total[f, :, block * LANES : (block + 1) * LANES]
+    row = lax.broadcasted_iota(jnp.int32, (EXTRA, LANES), 0)
+    parts = jnp.zeros((EXTRA, LANES), f32)
     for f in range(2):
-        rest = jnp.full((PART, EXTRA), jnp.sum(squares[f : f + 1]))
-        parts = jnp.zeros((PART, EXTRA), f32)
+        rest = jnp.full((EXTRA, LANES), jnp.sum(squares[f : f + 1]))
         for k in range(3):
             part = rest.astype(bf16).astype(f32)
-            parts = jnp.where(row == k, part, parts)
+            parts = jnp.where(row == f * EXTRA // 2 + k, part, parts)
             rest = rest - part
-        out[f, :, TOKENS:] = parts.astype(bf16)
+    out[2 * BLOCKS * PART :, :] = parts.astype(bf16)
 
 
 def changes(chunks, mine, other, f):
-    image = jnp.concatenate([c[f, :, :TOKENS] for c in chunks], axis=0)
+    def image(c):
+        first = f * BLOCKS
+        return jnp.concatenate([c[n * PART : (n + 1) * PART, :] for n in range(first, first + BLOCKS)], axis=1)
+
+    image = jnp.concatenate([image(c) for c in chunks], axis=0)
     change = dot(image[:, :HALF], mine[:, factor_columns(f)])
     return change + dot(image[:, HALF:], other[:, factor_columns(f)])
 
@@ -157,7 +166,9 @@
 
 
 def share_sum(chunks, f):
-    return sum(jnp.sum(c[f, :, TOKENS:].astype(f32), axis=0, keepdims=True) for c in chunks)
+    shares = sum(c[2 * BLOCKS * PART :, :].astype(f32) for c in chunks)
+    half = EXTRA // 2
+    return jnp.sum(shares[f * half : (f + 1) * half], axis=0, keepdims=True)
 
 
 def update(at, act_factor, grad_factor, mine, other, own_change, squares, *refs):
@@ -216,7 +227,7 @@
         if step < 3:
             down = own[2 * step + 1] + away[step + 1][0].astype(f32) + down.astype(f32)
     up = shift(up.astype(bf16), "z", Z, 1)
-    shape = (2, PART, TOKENS + EXTRA)
+    shape = (2 * BLOCKS * PART + EXTRA, LANES)
     (up,) = kernel_call(last_sum, [(shape, bf16)], own[7], away[4], up, down, squares)
 
     down = up
@@ -227,11 +238,11 @@
         up, down = shift(up, "z", Z, 1), shift(down, "z", Z, -1)
         held += [up, down]
         crossed += [shift(up, "yl", YL), shift(down, "yl", YL)]
-    up = shift(after(up, crossed[1], crossed[2], crossed[3]), "z", Z, 1)
+    up = shift(after(up, *crossed[1:5]), "z", Z, 1)
     held.append(up)
     crossed.append(shift(up, "yl", YL))
     changed, squares = kernel_call(
-        own_changes, [((2, ROWS // YL, WIDTH), f32), ((2, EXTRA), f32)], mine, other, *held, flops=product
+        own_changes, [((2, ROWS // YL, WIDTH), f32), ((2, LANES), f32)], mine, other, *held, flops=product
     )
     outs = kernel_call(
         update, [((Z, YL, PART, WIDTH), bf16)] * 2, *factors, mine, other, changed, squares, *crossed, index=[z, yl], flops=product

time: 129 us -> 130 us (level)
  transfers between devices with their start and end apart: 29 -> 29, of which waited for: 18 -> 16; matrix products, arithmetic and copies ran while one was open for 0% -> 0% of each run, Pallas kernels for 3% -> 3%
where the time goes in v8:
time: 130 us; the launch traced here: 129 us
  blocking collectives  42.2 us (32%)
  starting transfers between devices  37.3 us (29%)
  waiting for transfers between devices  36.8 us (28%)
  Pallas kernels  11.5 us (9%)
    ppermute x29, starting transfers between devices, shift(): return lax.ppermute(a, axis, [(i, (i + by) % size) for i in range(size)])  37.3 us
    ppermute x29, waiting for transfers between devices, shift(): return lax.ppermute(a, axis, [(i, (i + by) % size) for i in range(size)])  36.8 us
    all_to_all x1, blocking collectives, local(): parts = lax.all_to_all(total.reshape(chunks), ('x', 'yh'), 0, 0, tiled=True)  23 us
    all_to_all x1, blocking collectives, local(): lax.all_to_all(copies, ('x', 'yh'), 0, 0, tiled=True)  19.2 us
    pallas_call x9, Pallas kernels, kernel_call(): pl.pallas_call(body, out_shape=[jax.ShapeDtypeStruct(shape, dtype) for sh...  11.5 us
  transfers between devices with their start and end apart: 29, of which 16 were waited for; matrix products, arithmetic and copies ran while one was open for 0% of the time, Pallas kernels for 3%

profile of v8, /device:TPU:8, one launch (start us, length us, event | category | flops | bytes accessed | tf_op | source)
XLA Modules:
  0.0 129.2 jit_solution(12504230660014133391)
XLA Ops:
  0.7 3.2 %shard_map.59 = bf16[512,1024]{1,0:T(8,128)(2,1)} custom-call(s32[1]{0:T(128)} %bitcast.5.which, bf16[1024,512]{1,0:T(8,128)(2,1)} %acts.3, bf16[1024,512]{1,0:T(8,128)(2,1)} %cots.3, bf16[512,512]{1,0:T(8,128)(2,1)} %act_factor.3, bf16[512,512]{1,0:T(8,128)(2,1)} %grad_factor.3), custom_call_target="tpu_custom_call" | custom-call | flops 536870912 | bytes 3145732 | tf_op jit(solution)/shard_map/pallas_call | solution.py:50
  4.0 2.9 %collective-permute-done.came = bf16[512,1024]{1,0:T(8,128)(2,1)S(1)} collective-permute-done((bf16[512,1024]{1,0:T(8,128)(2,1)}, bf16[512,1024]{1,0:T(8,128)(2,1)S(1)}, u32[]{:S(2)}, u32[]{:S(2)}) %collective-permute-start) | collective-permute-done | bytes 1048608 | tf_op jit(solution)/shard_map/ppermute | solution.py:41
  7.6 23.0 %all_to_all.10.parts = bf16[8,64,1024]{2,1,0:T(8,128)(2,1)S(1)} all-to-all(bf16[8,64,1024]{2,1,0:T(8,128)(2,1)S(1)} %bitcast.57), channel_id=1, replica_groups=mesh['x'=4,'yh'=2,'core'=2,'z'=8,'yl'=2] {'x','yh'}, dimensions={0} | all-to-all | bytes 2097152 | tf_op jit(solution)/shard_map/all_to_all | solution.py:207
  30.7 19.2 %all_to_all.11 = bf16[8,64,1024]{2,1,0:T(8,128)(2,1)S(1)} all-to-all(bf16[8,64,1024]{2,1,0:T(8,128)(2,1)S(1)} %shard_map.61), channel_id=1, replica_groups=mesh['x'=4,'yh'=2,'core'=2,'z'=8,'yl'=2] {'x','yh'}, dimensions={0} | all-to-all | bytes 2097152 | tf_op jit(solution)/shard_map/all_to_all | solution.py:209
  50.1 2.6 %collective-permute-done.1.other = bf16[512,1024]{1,0:T(8,128)(2,1)S(1)} collective-permute-done((bf16[512,1024]{1,0:T(8,128)(2,1)S(1)}, bf16[512,1024]{1,0:T(8,128)(2,1)S(1)}, u32[]{:S(2)}, u32[]{:S(2)}) %collective-permute-start.1) | collective-permute-done | bytes 1048608 | tf_op jit(solution)/shard_map/ppermute | solution.py:41
  57.4 1.8 %shard_map.62 = (f32[2,32,1024]{2,1,0:T(8,128)S(1)}, f32[2,32,1024]{2,1,0:T(8,128)S(1)}, f32[2,32,1024]{2,1,0:T(8,128)S(1)}, f32[2,32,1024]{2,1,0:T(8,128)S(1)},...) custom-call(s32[2]{0:T(128)S(1)} %pad_add_fusion.at, ...), custom_call_target="tpu_custom_call" | custom-call | flops 536870912 | bytes 3145736 | tf_op jit(solution)/shard_map/pallas_call | solution.py:50
  59.8 2.0 %collective-permute-start.7 = (bf16[2,32,1024]{2,1,0:T(8,128)(2,1)S(1)}, bf16[2,32,1024]{2,1,0:T(8,128)(2,1)S(1)}, u32[]{:S(2)}, u32[]{:S(2)}) collective-permute-start(bf16[2,32,1024]{2,1,0:T(8,128)(2,1)S(1)} %fusion.5), channel_id=1, source_target_pairs={{0,2},{2,4},{4,6},{6,8},{8,10},{10,12},{12,14},{14,0},{1,3},{3,5},... | collective-permute-start | bytes 393224 | tf_op jit(solution)/shard_map/ppermute | solution.py:41
  61.7 1.9 %collective-permute-start.4 = (bf16[2,2,32,1024]{3,2,1,0:T(8,128)(2,1)S(1)}, bf16[2,2,32,1024]{3,2,1,0:T(8,128)(2,1)S(1)}, u32[]{:S(2)}, u32[]{:S(2)}) collective-permute-start(bf16[2,2,32,1024]{3,2,1,0:T(8,128)(2,1)S(1)} %get-tuple-element.24), channel_id=1, source_target_pairs={{0,1},{1,0},{2,3},{3,2},{4,5},{5,4},{6,7},{7,6},{8,9},{9,8},{10,11... | collective-permute-start | bytes 786440 | tf_op jit(solution)/shard_map/ppermute | solution.py:41
  63.6 5.0 %collective-permute-done.7 = bf16[2,32,1024]{2,1,0:T(8,128)(2,1)S(1)} collective-permute-done((bf16[2,32,1024]{2,1,0:T(8,128)(2,1)S(1)}, bf16[2,32,1024]{2,1,0:T(8,128)(2,1)S(1)}, u32[]{:S(2)}, u32[]{:S(2)}) %collective-permute-start.7) | collective-permute-done | bytes 131104 | tf_op jit(solution)/shard_map/ppermute | solution.py:41
  68.7 3.2 %collective-permute-start.11 = (bf16[2,32,1024]{2,1,0:T(8,128)(2,1)S(1)}, bf16[2,32,1024]{2,1,0:T(8,128)(2,1)S(1)}, u32[]{:S(2)}, u32[]{:S(2)}) collective-permute-start(bf16[2,32,1024]{2,1,0:T(8,128)(2,1)S(1)} %get-tuple-element.40), channel_id=1, source_target_pairs={{0,14},{2,0},{4,2},{6,4},{8,6},{10,8},{12,10},{14,12},{1,15},{3,1}... | collective-permute-start | bytes 393224 | tf_op jit(solution)/shard_map/ppermute | solution.py:41
  74.4 3.7 %collective-permute-done.8 = bf16[2,32,1024]{2,1,0:T(8,128)(2,1)S(1)} collective-permute-done((bf16[2,32,1024]{2,1,0:T(8,128)(2,1)S(1)}, bf16[2,32,1024]{2,1,0:T(8,128)(2,1)S(1)}, u32[]{:S(2)}, u32[]{:S(2)}) %collective-permute-start.8) | collective-permute-done | bytes 131104 | tf_op jit(solution)/shard_map/ppermute | solution.py:41
  78.3 2.0 %collective-permute-start.9 = (bf16[2,32,1024]{2,1,0:T(8,128)(2,1)S(1)}, bf16[2,32,1024]{2,1,0:T(8,128)(2,1)S(1)}, u32[]{:S(2)}, u32[]{:S(2)}) collective-permute-start(bf16[2,32,1024]{2,1,0:T(8,128)(2,1)S(1)} %get-tuple-element.39), channel_id=1, source_target_pairs={{0,2},{2,4},{4,6},{6,8},{8,10},{10,12},{12,14},{14,0},{1,3},{3,5},... | collective-permute-start | bytes 393224 | tf_op jit(solution)/shard_map/ppermute | solution.py:41
  81.7 1.6 %collective-permute-done.12 = bf16[2,32,1024]{2,1,0:T(8,128)(2,1)S(1)} collective-permute-done((bf16[2,32,1024]{2,1,0:T(8,128)(2,1)S(1)}, bf16[2,32,1024]{2,1,0:T(8,128)(2,1)S(1)}, u32[]{:S(2)}, u32[]{:S(2)}) %collective-permute-start.12) | collective-permute-done | bytes 131104 | tf_op jit(solution)/shard_map/ppermute | solution.py:41
  84.7 2.1 %collective-permute-start.10 = (bf16[2,32,1024]{2,1,0:T(8,128)(2,1)S(1)}, bf16[2,32,1024]{2,1,0:T(8,128)(2,1)S(1)}, u32[]{:S(2)}, u32[]{:S(2)}) collective-permute-start(bf16[2,32,1024]{2,1,0:T(8,128)(2,1)S(1)} %get-tuple-element.37), channel_id=1, source_target_pairs={{0,2},{2,4},{4,6},{6,8},{8,10},{10,12},{12,14},{14,0},{1,3},{3,5},... | collective-permute-start | bytes 393224 | tf_op jit(solution)/shard_map/ppermute | solution.py:41
  88.2 3.8 %collective-permute-done.10.up = bf16[2,32,1024]{2,1,0:T(8,128)(2,1)S(1)} collective-permute-done((bf16[2,32,1024]{2,1,0:T(8,128)(2,1)S(1)}, bf16[2,32,1024]{2,1,0:T(8,128)(2,1)S(1)}, u32[]{:S(2)}, u32[]{:S(2)}) %collective-permute-start.10) | collective-permute-done | bytes 131104 | tf_op jit(solution)/shard_map/ppermute | solution.py:41
  93.2 2.6 %collective-permute-start.15 = (bf16[528,128]{1,0:T(8,128)(2,1)S(1)}, bf16[528,128]{1,0:T(8,128)(2,1)S(1)}, u32[]{:S(2)}, u32[]{:S(2)}) collective-permute-start(bf16[528,128]{1,0:T(8,128)(2,1)S(1)} %shard_map.65.refs_0_), channel_id=1, source_target_pairs={{0,14},{2,0},{4,2},{6,4},{8,6},{10,8},{12,10},{14,12},{1,15},{3,1}... | collective-permute-start | bytes 405512 | tf_op jit(solution)/shard_map/ppermute | solution.py:41
  97.1 1.9 %collective-permute-done.14.refs_1_ = bf16[528,128]{1,0:T(8,128)(2,1)S(1)} collective-permute-done((bf16[528,128]{1,0:T(8,128)(2,1)S(1)}, bf16[528,128]{1,0:T(8,128)(2,1)S(1)}, u32[]{:S(2)}, u32[]{:S(2)}) %collective-permute-start.14) | collective-permute-done | bytes 135200 | tf_op jit(solution)/shard_map/ppermute | solution.py:41
  99.1 3.2 %collective-permute-start.17 = (bf16[528,128]{1,0:T(8,128)(2,1)S(1)}, bf16[528,128]{1,0:T(8,128)(2,1)S(1)}, u32[]{:S(2)}, u32[]{:S(2)}) collective-permute-start(bf16[528,128]{1,0:T(8,128)(2,1)S(1)} %collective-permute-done.15.refs_2_), channel_id=1, source_target_pairs={{0,14},{2,0},{4,2},{6,4},{8,6},{10,8},{12,10},{14,12},{1,15},{3,1}... | collective-permute-start | bytes 405512 | tf_op jit(solution)/shard_map/ppermute | solution.py:41
  106.1 1.4 %collective-permute-start.23 = (bf16[528,128]{1,0:T(8,128)(2,1)S(1)}, bf16[528,128]{1,0:T(8,128)(2,1)S(1)}, u32[]{:S(2)}, u32[]{:S(2)}) collective-permute-start(bf16[528,128]{1,0:T(8,128)(2,1)S(1)} %collective-permute-done.16.refs_3_), channel_id=1, source_target_pairs={{0,1},{1,0},{2,3},{3,2},{4,5},{5,4},{6,7},{7,6},{8,9},{9,8},{10,11... | collective-permute-start | bytes 405512 | tf_op jit(solution)/shard_map/ppermute | solution.py:41
  108.2 3.7 %collective-permute-start.20 = (bf16[528,128]{1,0:T(8,128)(2,1)S(1)}, bf16[528,128]{1,0:T(8,128)(2,1)S(1)}, u32[]{:S(2)}, u32[]{:S(2)}) collective-permute-start(bf16[528,128]{1,0:T(8,128)(2,1)S(1)} %get-tuple-element.42), channel_id=1, source_target_pairs={{0,14},{2,0},{4,2},{6,4},{8,6},{10,8},{12,10},{14,12},{1,15},{3,1}... | collective-permute-start | bytes 405512 | tf_op jit(solution)/shard_map/ppermute | solution.py:41
  112.7 2.8 %collective-permute-done.24.refs_4_ = bf16[528,128]{1,0:T(8,128)(2,1)S(1)} collective-permute-done((bf16[528,128]{1,0:T(8,128)(2,1)S(1)}, bf16[528,128]{1,0:T(8,128)(2,1)S(1)}, u32[]{:S(2)}, u32[]{:S(2)}) %collective-permute-start.24) | collective-permute-done | bytes 135200 | tf_op jit(solution)/shard_map/ppermute | solution.py:41
  117.9 4.1 %collective-permute-done.25.refs_7_ = bf16[528,128]{1,0:T(8,128)(2,1)S(1)} collective-permute-done((bf16[528,128]{1,0:T(8,128)(2,1)S(1)}, bf16[528,128]{1,0:T(8,128)(2,1)S(1)}, u32[]{:S(2)}, u32[]{:S(2)}) %collective-permute-start.25) | collective-permute-done | bytes 135200 | tf_op jit(solution)/shard_map/ppermute | solution.py:41
  124.0 2.9 %collective-permute-done.28.refs_7_ = bf16[528,128]{1,0:T(8,128)(2,1)S(1)} collective-permute-done((bf16[528,128]{1,0:T(8,128)(2,1)S(1)}, bf16[528,128]{1,0:T(8,128)(2,1)S(1)}, u32[]{:S(2)}, u32[]{:S(2)}) %collective-permute-start.28) | collective-permute-done | bytes 135200 | tf_op jit(solution)/shard_map/ppermute | solution.py:41
  127.0 2.3 %shard_map.67 = (bf16[8,2,32,512]{3,2,1,0:T(8,128)(2,1)}, bf16[8,2,32,512]{3,2,1,0:T(8,128)(2,1)}) custom-call(s32[2]{0:T(128)S(1)} %pad_add_fusion.at, bf16[8,2,32,512]{3,2,1,0:T(8,128)(2,1)S(1)} %bitcast.52, bf16[8,2,32,512]{3,2,1,0:T(8,128)(2,1)S(1)} %bitcast.56, bf16[512,1024]{1,0:T(8,128)(2,1)S(1)} %bitcast.48, ...), custom_call_target="tpu_custom_call" | custom-call | flops 536870912 | bytes 5276680 | tf_op jit(solution)/shard_map/pallas_call | solution.py:50
  (60 shorter events, 25.6 us)
Async XLA Ops:
  53.9 5.8 %collective-permute-start.6 = (bf16[1,2,32,1024]{3,2,1,0:T(8,128)(2,1)S(1)}, bf16[1,2,32,1024]{3,2,1,0:T(8,128)(2,1)S(1)}, u32[]{:S(2)}, u32[]{:S(2)}) collective-permute-start(bf16[1,2,32,1024]{3,2,1,0:T(8,128)(2,1)S(1)} %shard_map.64), channel_id=1, source_target_pairs={{0,1},{1,0},{2,3},{3,2},{4,5},{5,4},{6,7},{7,6},{8,9},{9,8},{10,11... | collective-permute-start | bytes 393224 | tf_op jit(solution)/shard_map/ppermute | solution.py:41
  56.6 12.0 %collective-permute-start.5 = (bf16[2,2,32,1024]{3,2,1,0:T(8,128)(2,1)S(1)}, bf16[2,2,32,1024]{3,2,1,0:T(8,128)(2,1)S(1)}, u32[]{:S(2)}, u32[]{:S(2)}) collective-permute-start(bf16[2,2,32,1024]{3,2,1,0:T(8,128)(2,1)S(1)} %get-tuple-element.26), channel_id=1, source_target_pairs={{0,1},{1,0},{2,3},{3,2},{4,5},{5,4},{6,7},{7,6},{8,9},{9,8},{10,11... | collective-permute-start | bytes 786440 | tf_op jit(solution)/shard_map/ppermute | solution.py:41
  59.8 8.9 %collective-permute-start.7 = (bf16[2,32,1024]{2,1,0:T(8,128)(2,1)S(1)}, bf16[2,32,1024]{2,1,0:T(8,128)(2,1)S(1)}, u32[]{:S(2)}, u32[]{:S(2)}) collective-permute-start(bf16[2,32,1024]{2,1,0:T(8,128)(2,1)S(1)} %fusion.5), channel_id=1, source_target_pairs={{0,2},{2,4},{4,6},{6,8},{8,10},{10,12},{12,14},{14,0},{1,3},{3,5},... | collective-permute-start | bytes 393224 | tf_op jit(solution)/shard_map/ppermute | solution.py:41
  61.7 11.5 %collective-permute-start.4 = (bf16[2,2,32,1024]{3,2,1,0:T(8,128)(2,1)S(1)}, bf16[2,2,32,1024]{3,2,1,0:T(8,128)(2,1)S(1)}, u32[]{:S(2)}, u32[]{:S(2)}) collective-permute-start(bf16[2,2,32,1024]{3,2,1,0:T(8,128)(2,1)S(1)} %get-tuple-element.24), channel_id=1, source_target_pairs={{0,1},{1,0},{2,3},{3,2},{4,5},{5,4},{6,7},{7,6},{8,9},{9,8},{10,11... | collective-permute-start | bytes 786440 | tf_op jit(solution)/shard_map/ppermute | solution.py:41
  68.7 5.7 %collective-permute-start.11 = (bf16[2,32,1024]{2,1,0:T(8,128)(2,1)S(1)}, bf16[2,32,1024]{2,1,0:T(8,128)(2,1)S(1)}, u32[]{:S(2)}, u32[]{:S(2)}) collective-permute-start(bf16[2,32,1024]{2,1,0:T(8,128)(2,1)S(1)} %get-tuple-element.40), channel_id=1, source_target_pairs={{0,14},{2,0},{4,2},{6,4},{8,6},{10,8},{12,10},{14,12},{1,15},{3,1}... | collective-permute-start | bytes 393224 | tf_op jit(solution)/shard_map/ppermute | solution.py:41
  71.9 6.2 %collective-permute-start.8 = (bf16[2,32,1024]{2,1,0:T(8,128)(2,1)S(1)}, bf16[2,32,1024]{2,1,0:T(8,128)(2,1)S(1)}, u32[]{:S(2)}, u32[]{:S(2)}) collective-permute-start(bf16[2,32,1024]{2,1,0:T(8,128)(2,1)S(1)} %get-tuple-element.41), channel_id=1, source_target_pairs={{0,2},{2,4},{4,6},{6,8},{8,10},{10,12},{12,14},{14,0},{1,3},{3,5},... | collective-permute-start | bytes 393224 | tf_op jit(solution)/shard_map/ppermute | solution.py:41
  71.9 9.7 %collective-permute-start.3 = (bf16[2,2,32,1024]{3,2,1,0:T(8,128)(2,1)S(1)}, bf16[2,2,32,1024]{3,2,1,0:T(8,128)(2,1)S(1)}, u32[]{:S(2)}, u32[]{:S(2)}) collective-permute-start(bf16[2,2,32,1024]{3,2,1,0:T(8,128)(2,1)S(1)} %get-tuple-element.22), channel_id=1, source_target_pairs={{0,1},{1,0},{2,3},{3,2},{4,5},{5,4},{6,7},{7,6},{8,9},{9,8},{10,11... | collective-permute-start | bytes 786440 | tf_op jit(solution)/shard_map/ppermute | solution.py:41
  78.3 6.3 %collective-permute-start.9 = (bf16[2,32,1024]{2,1,0:T(8,128)(2,1)S(1)}, bf16[2,32,1024]{2,1,0:T(8,128)(2,1)S(1)}, u32[]{:S(2)}, u32[]{:S(2)}) collective-permute-start(bf16[2,32,1024]{2,1,0:T(8,128)(2,1)S(1)} %get-tuple-element.39), channel_id=1, source_target_pairs={{0,2},{2,4},{4,6},{6,8},{8,10},{10,12},{12,14},{14,0},{1,3},{3,5},... | collective-permute-start | bytes 393224 | tf_op jit(solution)/shard_map/ppermute | solution.py:41
  80.3 7.9 %collective-permute-start.2 = (bf16[1,2,32,1024]{3,2,1,0:T(8,128)(2,1)S(1)}, bf16[1,2,32,1024]{3,2,1,0:T(8,128)(2,1)S(1)}, u32[]{:S(2)}, u32[]{:S(2)}) collective-permute-start(bf16[1,2,32,1024]{3,2,1,0:T(8,128)(2,1)S(1)} %get-tuple-element.20), channel_id=1, source_target_pairs={{0,1},{1,0},{2,3},{3,2},{4,5},{5,4},{6,7},{7,6},{8,9},{9,8},{10,11... | collective-permute-start | bytes 393224 | tf_op jit(solution)/shard_map/ppermute | solution.py:41
  84.7 7.3 %collective-permute-start.10 = (bf16[2,32,1024]{2,1,0:T(8,128)(2,1)S(1)}, bf16[2,32,1024]{2,1,0:T(8,128)(2,1)S(1)}, u32[]{:S(2)}, u32[]{:S(2)}) collective-permute-start(bf16[2,32,1024]{2,1,0:T(8,128)(2,1)S(1)} %get-tuple-element.37), channel_id=1, source_target_pairs={{0,2},{2,4},{4,6},{6,8},{8,10},{10,12},{12,14},{14,0},{1,3},{3,5},... | collective-permute-start | bytes 393224 | tf_op jit(solution)/shard_map/ppermute | solution.py:41
  92.1 6.9 %collective-permute-start.14 = (bf16[528,128]{1,0:T(8,128)(2,1)S(1)}, bf16[528,128]{1,0:T(8,128)(2,1)S(1)}, u32[]{:S(2)}, u32[]{:S(2)}) collective-permute-start(bf16[528,128]{1,0:T(8,128)(2,1)S(1)} %shard_map.65.refs_0_), channel_id=1, source_target_pairs={{0,2},{2,4},{4,6},{6,8},{8,10},{10,12},{12,14},{14,0},{1,3},{3,5},... | collective-permute-start | bytes 405512 | tf_op jit(solution)/shard_map/ppermute | solution.py:41
  93.2 5.9 %collective-permute-start.15 = (bf16[528,128]{1,0:T(8,128)(2,1)S(1)}, bf16[528,128]{1,0:T(8,128)(2,1)S(1)}, u32[]{:S(2)}, u32[]{:S(2)}) collective-permute-start(bf16[528,128]{1,0:T(8,128)(2,1)S(1)} %shard_map.65.refs_0_), channel_id=1, source_target_pairs={{0,14},{2,0},{4,2},{6,4},{8,6},{10,8},{12,10},{14,12},{1,15},{3,1}... | collective-permute-start | bytes 405512 | tf_op jit(solution)/shard_map/ppermute | solution.py:41
  95.8 8.6 %collective-permute-start.18 = (bf16[528,128]{1,0:T(8,128)(2,1)S(1)}, bf16[528,128]{1,0:T(8,128)(2,1)S(1)}, u32[]{:S(2)}, u32[]{:S(2)}) collective-permute-start(bf16[528,128]{1,0:T(8,128)(2,1)S(1)} %shard_map.65.refs_0_), channel_id=1, source_target_pairs={{0,1},{1,0},{2,3},{3,2},{4,5},{5,4},{6,7},{7,6},{8,9},{9,8},{10,11... | collective-permute-start | bytes 405512 | tf_op jit(solution)/shard_map/ppermute | solution.py:41
  99.1 6.2 %collective-permute-start.16 = (bf16[528,128]{1,0:T(8,128)(2,1)S(1)}, bf16[528,128]{1,0:T(8,128)(2,1)S(1)}, u32[]{:S(2)}, u32[]{:S(2)}) collective-permute-start(bf16[528,128]{1,0:T(8,128)(2,1)S(1)} %collective-permute-done.14.refs_1_), channel_id=1, source_target_pairs={{0,2},{2,4},{4,6},{6,8},{8,10},{10,12},{12,14},{14,0},{1,3},{3,5},... | collective-permute-start | bytes 405512 | tf_op jit(solution)/shard_map/ppermute | solution.py:41
  99.1 6.9 %collective-permute-start.17 = (bf16[528,128]{1,0:T(8,128)(2,1)S(1)}, bf16[528,128]{1,0:T(8,128)(2,1)S(1)}, u32[]{:S(2)}, u32[]{:S(2)}) collective-permute-start(bf16[528,128]{1,0:T(8,128)(2,1)S(1)} %collective-permute-done.15.refs_2_), channel_id=1, source_target_pairs={{0,14},{2,0},{4,2},{6,4},{8,6},{10,8},{12,10},{14,12},{1,15},{3,1}... | collective-permute-start | bytes 405512 | tf_op jit(solution)/shard_map/ppermute | solution.py:41
  102.3 5.9 %collective-permute-start.21 = (bf16[528,128]{1,0:T(8,128)(2,1)S(1)}, bf16[528,128]{1,0:T(8,128)(2,1)S(1)}, u32[]{:S(2)}, u32[]{:S(2)}) collective-permute-start(bf16[528,128]{1,0:T(8,128)(2,1)S(1)} %collective-permute-done.14.refs_1_), channel_id=1, source_target_pairs={{0,1},{1,0},{2,3},{3,2},{4,5},{5,4},{6,7},{7,6},{8,9},{9,8},{10,11... | collective-permute-start | bytes 405512 | tf_op jit(solution)/shard_map/ppermute | solution.py:41
  103.7 8.2 %collective-permute-start.22 = (bf16[528,128]{1,0:T(8,128)(2,1)S(1)}, bf16[528,128]{1,0:T(8,128)(2,1)S(1)}, u32[]{:S(2)}, u32[]{:S(2)}) collective-permute-start(bf16[528,128]{1,0:T(8,128)(2,1)S(1)} %collective-permute-done.15.refs_2_), channel_id=1, source_target_pairs={{0,1},{1,0},{2,3},{3,2},{4,5},{5,4},{6,7},{7,6},{8,9},{9,8},{10,11... | collective-permute-start | bytes 405512 | tf_op jit(solution)/shard_map/ppermute | solution.py:41
  106.0 6.8 %collective-permute-start.19 = (bf16[528,128]{1,0:T(8,128)(2,1)S(1)}, bf16[528,128]{1,0:T(8,128)(2,1)S(1)}, u32[]{:S(2)}, u32[]{:S(2)}) collective-permute-start(bf16[528,128]{1,0:T(8,128)(2,1)S(1)} %get-tuple-element.43), channel_id=1, source_target_pairs={{0,2},{2,4},{4,6},{6,8},{8,10},{10,12},{12,14},{14,0},{1,3},{3,5},... | collective-permute-start | bytes 405512 | tf_op jit(solution)/shard_map/ppermute | solution.py:41
  106.1 6.7 %collective-permute-start.23 = (bf16[528,128]{1,0:T(8,128)(2,1)S(1)}, bf16[528,128]{1,0:T(8,128)(2,1)S(1)}, u32[]{:S(2)}, u32[]{:S(2)}) collective-permute-start(bf16[528,128]{1,0:T(8,128)(2,1)S(1)} %collective-permute-done.16.refs_3_), channel_id=1, source_target_pairs={{0,1},{1,0},{2,3},{3,2},{4,5},{5,4},{6,7},{7,6},{8,9},{9,8},{10,11... | collective-permute-start | bytes 405512 | tf_op jit(solution)/shard_map/ppermute | solution.py:41
  107.5 8.1 %collective-permute-start.24 = (bf16[528,128]{1,0:T(8,128)(2,1)S(1)}, bf16[528,128]{1,0:T(8,128)(2,1)S(1)}, u32[]{:S(2)}, u32[]{:S(2)}) collective-permute-start(bf16[528,128]{1,0:T(8,128)(2,1)S(1)} %collective-permute-done.17.refs_4_), channel_id=1, source_target_pairs={{0,1},{1,0},{2,3},{3,2},{4,5},{5,4},{6,7},{7,6},{8,9},{9,8},{10,11... | collective-permute-start | bytes 405512 | tf_op jit(solution)/shard_map/ppermute | solution.py:41
  108.2 9.0 %collective-permute-start.20 = (bf16[528,128]{1,0:T(8,128)(2,1)S(1)}, bf16[528,128]{1,0:T(8,128)(2,1)S(1)}, u32[]{:S(2)}, u32[]{:S(2)}) collective-permute-start(bf16[528,128]{1,0:T(8,128)(2,1)S(1)} %get-tuple-element.42), channel_id=1, source_target_pairs={{0,14},{2,0},{4,2},{6,4},{8,6},{10,8},{12,10},{14,12},{1,15},{3,1}... | collective-permute-start | bytes 405512 | tf_op jit(solution)/shard_map/ppermute | solution.py:41
  115.7 6.3 %collective-permute-start.25 = (bf16[528,128]{1,0:T(8,128)(2,1)S(1)}, bf16[528,128]{1,0:T(8,128)(2,1)S(1)}, u32[]{:S(2)}, u32[]{:S(2)}) collective-permute-start(bf16[528,128]{1,0:T(8,128)(2,1)S(1)} %minimum_add_fusion), channel_id=1, source_target_pairs={{0,2},{2,4},{4,6},{6,8},{8,10},{10,12},{12,14},{14,0},{1,3},{3,5},... | collective-permute-start | bytes 405512 | tf_op jit(solution)/shard_map/ppermute | solution.py:41
  115.7 8.3 %collective-permute-start.26 = (bf16[528,128]{1,0:T(8,128)(2,1)S(1)}, bf16[528,128]{1,0:T(8,128)(2,1)S(1)}, u32[]{:S(2)}, u32[]{:S(2)}) collective-permute-start(bf16[528,128]{1,0:T(8,128)(2,1)S(1)} %collective-permute-done.19.refs_5_), channel_id=1, source_target_pairs={{0,1},{1,0},{2,3},{3,2},{4,5},{5,4},{6,7},{7,6},{8,9},{9,8},{10,11... | collective-permute-start | bytes 405512 | tf_op jit(solution)/shard_map/ppermute | solution.py:41
  117.2 6.9 %collective-permute-start.27 = (bf16[528,128]{1,0:T(8,128)(2,1)S(1)}, bf16[528,128]{1,0:T(8,128)(2,1)S(1)}, u32[]{:S(2)}, u32[]{:S(2)}) collective-permute-start(bf16[528,128]{1,0:T(8,128)(2,1)S(1)} %collective-permute-done.20.refs_6_), channel_id=1, source_target_pairs={{0,1},{1,0},{2,3},{3,2},{4,5},{5,4},{6,7},{7,6},{8,9},{9,8},{10,11... | collective-permute-start | bytes 405512 | tf_op jit(solution)/shard_map/ppermute | solution.py:41
  (9 other events, 45.9 us)

commit v9 on v8

--- a/solution.py
+++ b/solution.py
@@ -1,3 +1,5 @@
+import functools
+
 import jax
 import jax.numpy as jnp
 from jax import lax
@@ -19,7 +21,7 @@
 PART = ROWS // (Z * YL)
 
 REDUCE = (4, -3, 3, -2, 2, -1, 1, 0)
-PLACES = ((0, 0), (1, 0), (1, 1), (2, 0), (2, 1), (3, 0), (3, 1), (4, 0))
+FIRST = 3
 GATHER = (0, -1, 1, -2, 2, -3, 3, -4)
 
 keep_scale = 1.45
@@ -95,40 +97,45 @@
     return slice(f * WIDTH, (f + 1) * WIDTH)
 
 
-def image_rows(factor, z, side, mine, other, f, chunks):
+def image_rows(factor, z, side, chunks):
     rows = [factor[pl.ds(lax.rem(z + (e + Z), Z), 1), pl.ds(side, 1)].reshape(PART, WIDTH) for e in chunks]
-    rows = jnp.concatenate(rows, axis=0)
-    return (
-        dot_t(rows, mine[:, factor_columns(f)]),
-        dot_t(rows, other[:, factor_columns(f)]),
-    )
-
-
-def image_first(at, act_factor, grad_factor, mine, other, out):
+    return jnp.concatenate(rows, axis=0)
+
+
+def image_first(at, act_factor, grad_factor, part, out):
     for f, factor in enumerate((act_factor, grad_factor)):
-        first, second = image_rows(factor, at[0], 1 - at[1], mine, other, f, REDUCE[:1])
-        out[0, f, :, :HALF] = first.astype(bf16)
-        out[0, f, :, HALF:] = second.astype(bf16)
+        rows = image_rows(factor, at[0], 1 - at[1], REDUCE[:FIRST])
+        image = dot_t(rows, part[:, factor_columns(f)]).astype(bf16)
+        out[:, f] = image.reshape(FIRST, PART, HALF)
 
 
 def image_away(at, act_factor, grad_factor, mine, other, *outs):
     for f, factor in enumerate((act_factor, grad_factor)):
-        first, second = image_rows(factor, at[0], 1 - at[1], mine, other, f, REDUCE[1:])
-        for n, (group, k) in enumerate(PLACES[1:]):
-            rows = slice(n * PART, (n + 1) * PART)
-            outs[group - 1][k, f, :, :HALF] = first[rows].astype(bf16)
-            outs[group - 1][k, f, :, HALF:] = second[rows].astype(bf16)
+        rows = image_rows(factor, at[0], 1 - at[1], REDUCE[FIRST:])
+        for part, cols in ((mine, slice(0, HALF)), (other, slice(HALF, TOKENS))):
+            image = dot_t(rows, part[:, factor_columns(f)]).astype(bf16)
+            for n in range(Z - FIRST):
+                outs[n // 2][n % 2, f, :, cols] = image[n * PART : (n + 1) * PART]
 
 
 def image_own(at, act_factor, grad_factor, mine, other, *outs):
     for f, factor in enumerate((act_factor, grad_factor)):
-        first, second = image_rows(factor, at[0], at[1], mine, other, f, REDUCE)
-        for k in range(Z):
-            rows = slice(k * PART, (k + 1) * PART)
-            outs[k][f, :, :HALF] = first[rows]
-            outs[k][f, :, HALF:] = second[rows]
+        rows = image_rows(factor, at[0], at[1], REDUCE)
+        for part, cols in ((mine, slice(0, HALF)), (other, slice(HALF, TOKENS))):
+            image = dot_t(rows, part[:, factor_columns(f)])
+            for k in range(Z):
+                outs[k][f, :, cols] = image[k * PART : (k + 1) * PART]
         square = sum(jnp.square(part[:, factor_columns(f)].astype(f32)) for part in (mine, other))
         outs[Z][f : f + 1] = jnp.sum(square, axis=0, keepdims=True)
+
+
+def joined(n, own, away_mine, away_other, *refs):
+    came, out = refs[:-1], refs[-1]
+    for away, cols in ((away_mine, slice(0, HALF)), (away_other, slice(HALF, TOKENS))):
+        total = own[:, :, cols] + away[n].astype(f32)
+        for part in came:
+            total = total + part[:, :, cols].astype(f32)
+        out[:, :, cols] = total.astype(bf16)
 
 
 def last_sum(own, away, up, down, squares, out):
@@ -211,24 +218,33 @@
 
     factors = [f.reshape(Z, YL, PART, WIDTH) for f in (act_factor, grad_factor)]
     shape = (2, PART, TOKENS)
-    sent = [((sum(g == group for g, _ in PLACES),) + shape, bf16) for group in range(5)]
-    first = kernel_call(image_first, sent[:1], *factors, mine, other, index=[z, yl], flops=product // Z)
-    away = first + kernel_call(image_away, sent[1:], *factors, mine, other, index=[z, yl], flops=product)
+    at, work = [z, yl], product // 4
+    first = [((FIRST, 2, PART, HALF), bf16)]
+    (away_mine,) = kernel_call(image_first, first, *factors, mine, index=at, flops=work)
+    away_mine = shift(away_mine, "yl", YL)
+    (away_other,) = kernel_call(image_first, first, *factors, other, index=at, flops=work)
+    away_other = shift(away_other, "yl", YL)
+    sent = [((count,) + shape, bf16) for count in (2, 2, 1)]
+    away = kernel_call(image_away, sent, *factors, mine, other, index=at, flops=product)
     away = [shift(a, "yl", YL) for a in away]
     *own, squares = kernel_call(
-        image_own, [(shape, f32)] * Z + [((2, WIDTH), f32)], *factors, mine, other, index=[z, yl], flops=product
-    )
-    up = own[0] + away[0][0].astype(f32)
-    down = own[1] + away[1][0].astype(f32)
-    for step in (1, 2, 3):
-        up = shift(up.astype(bf16), "z", Z, 1)
-        up = own[2 * step] + away[step][1].astype(f32) + up.astype(f32)
-        down = shift(down.astype(bf16), "z", Z, -1)
-        if step < 3:
-            down = own[2 * step + 1] + away[step + 1][0].astype(f32) + down.astype(f32)
-    up = shift(up.astype(bf16), "z", Z, 1)
+        image_own, [(shape, f32)] * Z + [((2, WIDTH), f32)], *factors, mine, other, index=at, flops=product
+    )
+
+    def join(n, *came):
+        body = functools.partial(joined, n)
+        return kernel_call(body, [(shape, bf16)], own[n], away_mine, away_other, *came)[0]
+
+    def add(n, came):
+        group, k = divmod(n - FIRST, 2)
+        return (own[n] + away[group][k].astype(f32) + came.astype(f32)).astype(bf16)
+
+    up, down = shift(join(0), "z", Z, 1), shift(join(1), "z", Z, -1)
+    up, down = shift(join(2, up), "z", Z, 1), shift(add(3, down), "z", Z, -1)
+    up, down = shift(add(4, up), "z", Z, 1), shift(add(5, down), "z", Z, -1)
+    up = shift(add(6, up), "z", Z, 1)
     shape = (2 * BLOCKS * PART + EXTRA, LANES)
-    (up,) = kernel_call(last_sum, [(shape, bf16)], own[7], away[4], up, down, squares)
+    (up,) = kernel_call(last_sum, [(shape, bf16)], own[7], away[2], up, down, squares)
 
     down = up
     held, crossed = [up], [shift(up, "yl", YL)]
@@ -238,7 +254,7 @@
         up, down = shift(up, "z", Z, 1), shift(down, "z", Z, -1)
         held += [up, down]
         crossed += [shift(up, "yl", YL), shift(down, "yl", YL)]
-    up = shift(after(up, *crossed[1:5]), "z", Z, 1)
+    up = shift(after(up, *crossed[1:4]), "z", Z, 1)
     held.append(up)
     crossed.append(shift(up, "yl", YL))
     changed, squares = kernel_call(

time: 130 us -> 129 us (level)
  waiting for transfers between devices: 36.8 us -> 31.5 us
  starting transfers between devices: 37.3 us -> 40.5 us
    ppermute x29, waiting for transfers between devices: 36.8 us -> 31.5 us  [shift(): return lax.ppermute(a, axis, [(i, (i + by) % size) for i in range(size)])]
    ppermute x29, starting transfers between devices: 37.3 us -> 40.5 us  [shift(): return lax.ppermute(a, axis, [(i, (i + by) % size) for i in range(size)])]
    pallas_call x9 -> x13, Pallas kernels: 11.5 us -> 12.4 us  [kernel_call(): pl.pallas_call(body, out_shape=[jax.ShapeDtypeStruct(shape, dtype) for sh...]
  transfers between devices with their start and end apart: 29 -> 29, of which waited for: 16 -> 19; matrix products, arithmetic and copies ran while one was open for 0% -> 0% of each run, Pallas kernels for 3% -> 5%
where the time goes in v9:
time: 129 us; the launch traced here: 128 us
  blocking collectives  42.2 us (33%)
  starting transfers between devices  40.5 us (31%)
  waiting for transfers between devices  31.5 us (24%)
  Pallas kernels  12.4 us (10%)
    ppermute x29, starting transfers between devices, shift(): return lax.ppermute(a, axis, [(i, (i + by) % size) for i in range(size)])  40.5 us
    ppermute x29, waiting for transfers between devices, shift(): return lax.ppermute(a, axis, [(i, (i + by) % size) for i in range(size)])  31.5 us
    all_to_all x1, blocking collectives, local(): parts = lax.all_to_all(total.reshape(chunks), ('x', 'yh'), 0, 0, tiled=True)  23 us
    all_to_all x1, blocking collectives, local(): lax.all_to_all(copies, ('x', 'yh'), 0, 0, tiled=True)  19.2 us
    pallas_call x13, Pallas kernels, kernel_call(): pl.pallas_call(body, out_shape=[jax.ShapeDtypeStruct(shape, dtype) for sh...  12.4 us
  transfers between devices with their start and end apart: 29, of which 19 were waited for; matrix products, arithmetic and copies ran while one was open for 0% of the time, Pallas kernels for 5%

profile of v9, /device:TPU:8, one launch (start us, length us, event | category | flops | bytes accessed | tf_op | source)
XLA Modules:
  0.0 127.9 jit_solution(8556490205768755914)
XLA Ops:
  0.7 3.2 %shard_map.59 = bf16[512,1024]{1,0:T(8,128)(2,1)} custom-call(s32[1]{0:T(128)} %bitcast.5.which, bf16[1024,512]{1,0:T(8,128)(2,1)} %acts.3, bf16[1024,512]{1,0:T(8,128)(2,1)} %cots.3, bf16[512,512]{1,0:T(8,128)(2,1)} %act_factor.3, bf16[512,512]{1,0:T(8,128)(2,1)} %grad_factor.3), custom_call_target="tpu_custom_call" | custom-call | flops 536870912 | bytes 3145732 | tf_op jit(solution)/shard_map/pallas_call | solution.py:52
  4.0 2.9 %collective-permute-done.came = bf16[512,1024]{1,0:T(8,128)(2,1)S(1)} collective-permute-done((bf16[512,1024]{1,0:T(8,128)(2,1)}, bf16[512,1024]{1,0:T(8,128)(2,1)S(1)}, u32[]{:S(2)}, u32[]{:S(2)}) %collective-permute-start) | collective-permute-done | bytes 1048608 | tf_op jit(solution)/shard_map/ppermute | solution.py:43
  7.6 23.0 %all_to_all.10.parts = bf16[8,64,1024]{2,1,0:T(8,128)(2,1)S(1)} all-to-all(bf16[8,64,1024]{2,1,0:T(8,128)(2,1)S(1)} %bitcast.46), channel_id=1, replica_groups=mesh['x'=4,'yh'=2,'core'=2,'z'=8,'yl'=2] {'x','yh'}, dimensions={0} | all-to-all | bytes 2097152 | tf_op jit(solution)/shard_map/all_to_all | solution.py:214
  30.7 19.2 %all_to_all.11 = bf16[8,64,1024]{2,1,0:T(8,128)(2,1)S(1)} all-to-all(bf16[8,64,1024]{2,1,0:T(8,128)(2,1)S(1)} %shard_map.61), channel_id=1, replica_groups=mesh['x'=4,'yh'=2,'core'=2,'z'=8,'yl'=2] {'x','yh'}, dimensions={0} | all-to-all | bytes 2097152 | tf_op jit(solution)/shard_map/all_to_all | solution.py:216
  55.1 1.8 %shard_map.62 = (f32[2,32,1024]{2,1,0:T(8,128)S(1)}, f32[2,32,1024]{2,1,0:T(8,128)S(1)}, f32[2,32,1024]{2,1,0:T(8,128)S(1)}, f32[2,32,1024]{2,1,0:T(8,128)S(1)},...) custom-call(s32[2]{0:T(128)S(1)} %pad_add_fusion.at, ...), custom_call_target="tpu_custom_call" | custom-call | flops 536870912 | bytes 3145736 | tf_op jit(solution)/shard_map/pallas_call | solution.py:52
  58.8 3.8 %collective-permute-done.6.away_other = bf16[3,2,32,512]{3,2,1,0:T(8,128)(2,1)S(1)} collective-permute-done((bf16[3,2,32,512]{3,2,1,0:T(8,128)(2,1)S(1)}, bf16[3,2,32,512]{3,2,1,0:T(8,128)(2,1)S(1)}, u32[]{:S(2)}, u32[]{:S(2)}) %collective-permute-start.6) | collective-permute-done | bytes 196640 | tf_op jit(solution)/shard_map/ppermute | solution.py:43
  62.7 2.0 %collective-permute-start.7 = (bf16[2,32,1024]{2,1,0:T(8,128)(2,1)S(1)}, bf16[2,32,1024]{2,1,0:T(8,128)(2,1)S(1)}, u32[]{:S(2)}, u32[]{:S(2)}) collective-permute-start(bf16[2,32,1024]{2,1,0:T(8,128)(2,1)S(1)} %shard_map.66), channel_id=1, source_target_pairs={{0,2},{2,4},{4,6},{6,8},{8,10},{10,12},{12,14},{14,0},{1,3},{3,5},... | collective-permute-start | bytes 393224 | tf_op jit(solution)/shard_map/ppermute | solution.py:43
  66.1 4.1 %collective-permute-start.11 = (bf16[2,32,1024]{2,1,0:T(8,128)(2,1)S(1)}, bf16[2,32,1024]{2,1,0:T(8,128)(2,1)S(1)}, u32[]{:S(2)}, u32[]{:S(2)}) collective-permute-start(bf16[2,32,1024]{2,1,0:T(8,128)(2,1)S(1)} %shard_map.68), channel_id=1, source_target_pairs={{0,14},{2,0},{4,2},{6,4},{8,6},{10,8},{12,10},{14,12},{1,15},{3,1}... | collective-permute-start | bytes 393224 | tf_op jit(solution)/shard_map/ppermute | solution.py:43
  70.2 1.8 %collective-permute-done.7.refs_0_ = bf16[2,32,1024]{2,1,0:T(8,128)(2,1)S(1)} collective-permute-done((bf16[2,32,1024]{2,1,0:T(8,128)(2,1)S(1)}, bf16[2,32,1024]{2,1,0:T(8,128)(2,1)S(1)}, u32[]{:S(2)}, u32[]{:S(2)}) %collective-permute-start.7) | collective-permute-done | bytes 131104 | tf_op jit(solution)/shard_map/ppermute | solution.py:43
  73.6 4.7 %collective-permute-done.8 = bf16[2,32,1024]{2,1,0:T(8,128)(2,1)S(1)} collective-permute-done((bf16[2,32,1024]{2,1,0:T(8,128)(2,1)S(1)}, bf16[2,32,1024]{2,1,0:T(8,128)(2,1)S(1)}, u32[]{:S(2)}, u32[]{:S(2)}) %collective-permute-start.8) | collective-permute-done | bytes 131104 | tf_op jit(solution)/shard_map/ppermute | solution.py:43
  79.0 1.5 %collective-permute-start.9 = (bf16[2,32,1024]{2,1,0:T(8,128)(2,1)S(1)}, bf16[2,32,1024]{2,1,0:T(8,128)(2,1)S(1)}, u32[]{:S(2)}, u32[]{:S(2)}) collective-permute-start(bf16[2,32,1024]{2,1,0:T(8,128)(2,1)S(1)} %get-tuple-element.37), channel_id=1, source_target_pairs={{0,2},{2,4},{4,6},{6,8},{8,10},{10,12},{12,14},{14,0},{1,3},{3,5},... | collective-permute-start | bytes 393224 | tf_op jit(solution)/shard_map/ppermute | solution.py:43
  81.9 1.6 %collective-permute-done.12 = bf16[2,32,1024]{2,1,0:T(8,128)(2,1)S(1)} collective-permute-done((bf16[2,32,1024]{2,1,0:T(8,128)(2,1)S(1)}, bf16[2,32,1024]{2,1,0:T(8,128)(2,1)S(1)}, u32[]{:S(2)}, u32[]{:S(2)}) %collective-permute-start.12) | collective-permute-done | bytes 131104 | tf_op jit(solution)/shard_map/ppermute | solution.py:43
  83.5 1.7 %collective-permute-done.9 = bf16[2,32,1024]{2,1,0:T(8,128)(2,1)S(1)} collective-permute-done((bf16[2,32,1024]{2,1,0:T(8,128)(2,1)S(1)}, bf16[2,32,1024]{2,1,0:T(8,128)(2,1)S(1)}, u32[]{:S(2)}, u32[]{:S(2)}) %collective-permute-start.9) | collective-permute-done | bytes 131104 | tf_op jit(solution)/shard_map/ppermute | solution.py:43
  86.0 2.8 %collective-permute-start.13 = (bf16[2,32,1024]{2,1,0:T(8,128)(2,1)S(1)}, bf16[2,32,1024]{2,1,0:T(8,128)(2,1)S(1)}, u32[]{:S(2)}, u32[]{:S(2)}) collective-permute-start(bf16[2,32,1024]{2,1,0:T(8,128)(2,1)S(1)} %get-tuple-element.34), channel_id=1, source_target_pairs={{0,14},{2,0},{4,2},{6,4},{8,6},{10,8},{12,10},{14,12},{1,15},{3,1}... | collective-permute-start | bytes 393224 | tf_op jit(solution)/shard_map/ppermute | solution.py:43
  88.8 3.6 %collective-permute-done.10.up = bf16[2,32,1024]{2,1,0:T(8,128)(2,1)S(1)} collective-permute-done((bf16[2,32,1024]{2,1,0:T(8,128)(2,1)S(1)}, bf16[2,32,1024]{2,1,0:T(8,128)(2,1)S(1)}, u32[]{:S(2)}, u32[]{:S(2)}) %collective-permute-start.10) | collective-permute-done | bytes 131104 | tf_op jit(solution)/shard_map/ppermute | solution.py:43
  92.6 3.5 %collective-permute-start.15 = (bf16[528,128]{1,0:T(8,128)(2,1)S(1)}, bf16[528,128]{1,0:T(8,128)(2,1)S(1)}, u32[]{:S(2)}, u32[]{:S(2)}) collective-permute-start(bf16[528,128]{1,0:T(8,128)(2,1)S(1)} %shard_map.69.refs_0_), channel_id=1, source_target_pairs={{0,14},{2,0},{4,2},{6,4},{8,6},{10,8},{12,10},{14,12},{1,15},{3,1}... | collective-permute-start | bytes 405512 | tf_op jit(solution)/shard_map/ppermute | solution.py:43
  97.5 2.2 %collective-permute-done.14.refs_1_ = bf16[528,128]{1,0:T(8,128)(2,1)S(1)} collective-permute-done((bf16[528,128]{1,0:T(8,128)(2,1)S(1)}, bf16[528,128]{1,0:T(8,128)(2,1)S(1)}, u32[]{:S(2)}, u32[]{:S(2)}) %collective-permute-start.14) | collective-permute-done | bytes 135200 | tf_op jit(solution)/shard_map/ppermute | solution.py:43
  99.8 3.2 %collective-permute-start.17 = (bf16[528,128]{1,0:T(8,128)(2,1)S(1)}, bf16[528,128]{1,0:T(8,128)(2,1)S(1)}, u32[]{:S(2)}, u32[]{:S(2)}) collective-permute-start(bf16[528,128]{1,0:T(8,128)(2,1)S(1)} %collective-permute-done.15.refs_2_), channel_id=1, source_target_pairs={{0,14},{2,0},{4,2},{6,4},{8,6},{10,8},{12,10},{14,12},{1,15},{3,1}... | collective-permute-start | bytes 405512 | tf_op jit(solution)/shard_map/ppermute | solution.py:43
  106.7 2.1 %collective-permute-start.23 = (bf16[528,128]{1,0:T(8,128)(2,1)S(1)}, bf16[528,128]{1,0:T(8,128)(2,1)S(1)}, u32[]{:S(2)}, u32[]{:S(2)}) collective-permute-start(bf16[528,128]{1,0:T(8,128)(2,1)S(1)} %collective-permute-done.16.refs_3_), channel_id=1, source_target_pairs={{0,1},{1,0},{2,3},{3,2},{4,5},{5,4},{6,7},{7,6},{8,9},{9,8},{10,11... | collective-permute-start | bytes 405512 | tf_op jit(solution)/shard_map/ppermute | solution.py:43
  108.8 2.3 %collective-permute-start.20 = (bf16[528,128]{1,0:T(8,128)(2,1)S(1)}, bf16[528,128]{1,0:T(8,128)(2,1)S(1)}, u32[]{:S(2)}, u32[]{:S(2)}) collective-permute-start(bf16[528,128]{1,0:T(8,128)(2,1)S(1)} %get-tuple-element.38), channel_id=1, source_target_pairs={{0,14},{2,0},{4,2},{6,4},{8,6},{10,8},{12,10},{14,12},{1,15},{3,1}... | collective-permute-start | bytes 405512 | tf_op jit(solution)/shard_map/ppermute | solution.py:43
  111.3 2.0 %collective-permute-done.19.refs_5_ = bf16[528,128]{1,0:T(8,128)(2,1)S(1)} collective-permute-done((bf16[528,128]{1,0:T(8,128)(2,1)S(1)}, bf16[528,128]{1,0:T(8,128)(2,1)S(1)}, u32[]{:S(2)}, u32[]{:S(2)}) %collective-permute-start.19) | collective-permute-done | bytes 135200 | tf_op jit(solution)/shard_map/ppermute | solution.py:43
  115.6 2.1 %collective-permute-start.25 = (bf16[528,128]{1,0:T(8,128)(2,1)S(1)}, bf16[528,128]{1,0:T(8,128)(2,1)S(1)}, u32[]{:S(2)}, u32[]{:S(2)}) collective-permute-start(bf16[528,128]{1,0:T(8,128)(2,1)S(1)} %collective-permute-done.17.refs_4_), channel_id=1, source_target_pairs={{0,1},{1,0},{2,3},{3,2},{4,5},{5,4},{6,7},{7,6},{8,9},{9,8},{10,11... | collective-permute-start | bytes 405512 | tf_op jit(solution)/shard_map/ppermute | solution.py:43
  117.7 2.0 %collective-permute-start.27 = (bf16[528,128]{1,0:T(8,128)(2,1)S(1)}, bf16[528,128]{1,0:T(8,128)(2,1)S(1)}, u32[]{:S(2)}, u32[]{:S(2)}) collective-permute-start(bf16[528,128]{1,0:T(8,128)(2,1)S(1)} %collective-permute-done.20.refs_6_), channel_id=1, source_target_pairs={{0,1},{1,0},{2,3},{3,2},{4,5},{5,4},{6,7},{7,6},{8,9},{9,8},{10,11... | collective-permute-start | bytes 405512 | tf_op jit(solution)/shard_map/ppermute | solution.py:43
  125.6 2.3 %shard_map.71 = (bf16[8,2,32,512]{3,2,1,0:T(8,128)(2,1)}, bf16[8,2,32,512]{3,2,1,0:T(8,128)(2,1)}) custom-call(s32[2]{0:T(128)S(1)} %pad_add_fusion.at, bf16[8,2,32,512]{3,2,1,0:T(8,128)(2,1)S(1)} %bitcast.40, bf16[8,2,32,512]{3,2,1,0:T(8,128)(2,1)S(1)} %bitcast.45, bf16[512,1024]{1,0:T(8,128)(2,1)S(1)} %bitcast.35, ...), custom_call_target="tpu_custom_call" | custom-call | flops 536870912 | bytes 5276680 | tf_op jit(solution)/shard_map/pallas_call | solution.py:52
  (62 shorter events, 27.5 us)
Async XLA Ops:
  51.1 7.8 %collective-permute-start.5 = (bf16[3,2,32,512]{3,2,1,0:T(8,128)(2,1)S(1)}, bf16[3,2,32,512]{3,2,1,0:T(8,128)(2,1)S(1)}, u32[]{:S(2)}, u32[]{:S(2)}) collective-permute-start(bf16[3,2,32,512]{3,2,1,0:T(8,128)(2,1)S(1)} %shard_map.64), channel_id=1, source_target_pairs={{0,1},{1,0},{2,3},{3,2},{4,5},{5,4},{6,7},{7,6},{8,9},{9,8},{10,11... | collective-permute-start | bytes 589832 | tf_op jit(solution)/shard_map/ppermute | solution.py:43
  53.6 9.0 %collective-permute-start.6 = (bf16[3,2,32,512]{3,2,1,0:T(8,128)(2,1)S(1)}, bf16[3,2,32,512]{3,2,1,0:T(8,128)(2,1)S(1)}, u32[]{:S(2)}, u32[]{:S(2)}) collective-permute-start(bf16[3,2,32,512]{3,2,1,0:T(8,128)(2,1)S(1)} %shard_map.65), channel_id=1, source_target_pairs={{0,1},{1,0},{2,3},{3,2},{4,5},{5,4},{6,7},{7,6},{8,9},{9,8},{10,11... | collective-permute-start | bytes 589832 | tf_op jit(solution)/shard_map/ppermute | solution.py:43
  62.7 9.3 %collective-permute-start.7 = (bf16[2,32,1024]{2,1,0:T(8,128)(2,1)S(1)}, bf16[2,32,1024]{2,1,0:T(8,128)(2,1)S(1)}, u32[]{:S(2)}, u32[]{:S(2)}) collective-permute-start(bf16[2,32,1024]{2,1,0:T(8,128)(2,1)S(1)} %shard_map.66), channel_id=1, source_target_pairs={{0,2},{2,4},{4,6},{6,8},{8,10},{10,12},{12,14},{14,0},{1,3},{3,5},... | collective-permute-start | bytes 393224 | tf_op jit(solution)/shard_map/ppermute | solution.py:43
  64.7 8.9 %collective-permute-start.4 = (bf16[2,2,32,1024]{3,2,1,0:T(8,128)(2,1)S(1)}, bf16[2,2,32,1024]{3,2,1,0:T(8,128)(2,1)S(1)}, u32[]{:S(2)}, u32[]{:S(2)}) collective-permute-start(bf16[2,2,32,1024]{3,2,1,0:T(8,128)(2,1)S(1)} %get-tuple-element.23), channel_id=1, source_target_pairs={{0,1},{1,0},{2,3},{3,2},{4,5},{5,4},{6,7},{7,6},{8,9},{9,8},{10,11... | collective-permute-start | bytes 786440 | tf_op jit(solution)/shard_map/ppermute | solution.py:43
  66.1 7.5 %collective-permute-start.11 = (bf16[2,32,1024]{2,1,0:T(8,128)(2,1)S(1)}, bf16[2,32,1024]{2,1,0:T(8,128)(2,1)S(1)}, u32[]{:S(2)}, u32[]{:S(2)}) collective-permute-start(bf16[2,32,1024]{2,1,0:T(8,128)(2,1)S(1)} %shard_map.68), channel_id=1, source_target_pairs={{0,14},{2,0},{4,2},{6,4},{8,6},{10,8},{12,10},{14,12},{1,15},{3,1}... | collective-permute-start | bytes 393224 | tf_op jit(solution)/shard_map/ppermute | solution.py:43
  72.1 6.3 %collective-permute-start.8 = (bf16[2,32,1024]{2,1,0:T(8,128)(2,1)S(1)}, bf16[2,32,1024]{2,1,0:T(8,128)(2,1)S(1)}, u32[]{:S(2)}, u32[]{:S(2)}) collective-permute-start(bf16[2,32,1024]{2,1,0:T(8,128)(2,1)S(1)} %shard_map.67), channel_id=1, source_target_pairs={{0,2},{2,4},{4,6},{6,8},{8,10},{10,12},{12,14},{14,0},{1,3},{3,5},... | collective-permute-start | bytes 393224 | tf_op jit(solution)/shard_map/ppermute | solution.py:43
  72.2 9.7 %collective-permute-start.3 = (bf16[2,2,32,1024]{3,2,1,0:T(8,128)(2,1)S(1)}, bf16[2,2,32,1024]{3,2,1,0:T(8,128)(2,1)S(1)}, u32[]{:S(2)}, u32[]{:S(2)}) collective-permute-start(bf16[2,2,32,1024]{3,2,1,0:T(8,128)(2,1)S(1)} %get-tuple-element.21), channel_id=1, source_target_pairs={{0,1},{1,0},{2,3},{3,2},{4,5},{5,4},{6,7},{7,6},{8,9},{9,8},{10,11... | collective-permute-start | bytes 786440 | tf_op jit(solution)/shard_map/ppermute | solution.py:43
  79.0 6.2 %collective-permute-start.9 = (bf16[2,32,1024]{2,1,0:T(8,128)(2,1)S(1)}, bf16[2,32,1024]{2,1,0:T(8,128)(2,1)S(1)}, u32[]{:S(2)}, u32[]{:S(2)}) collective-permute-start(bf16[2,32,1024]{2,1,0:T(8,128)(2,1)S(1)} %get-tuple-element.37), channel_id=1, source_target_pairs={{0,2},{2,4},{4,6},{6,8},{8,10},{10,12},{12,14},{14,0},{1,3},{3,5},... | collective-permute-start | bytes 393224 | tf_op jit(solution)/shard_map/ppermute | solution.py:43
  80.5 8.3 %collective-permute-start.2 = (bf16[1,2,32,1024]{3,2,1,0:T(8,128)(2,1)S(1)}, bf16[1,2,32,1024]{3,2,1,0:T(8,128)(2,1)S(1)}, u32[]{:S(2)}, u32[]{:S(2)}) collective-permute-start(bf16[1,2,32,1024]{3,2,1,0:T(8,128)(2,1)S(1)} %get-tuple-element.19), channel_id=1, source_target_pairs={{0,1},{1,0},{2,3},{3,2},{4,5},{5,4},{6,7},{7,6},{8,9},{9,8},{10,11... | collective-permute-start | bytes 393224 | tf_op jit(solution)/shard_map/ppermute | solution.py:43
  85.3 7.1 %collective-permute-start.10 = (bf16[2,32,1024]{2,1,0:T(8,128)(2,1)S(1)}, bf16[2,32,1024]{2,1,0:T(8,128)(2,1)S(1)}, u32[]{:S(2)}, u32[]{:S(2)}) collective-permute-start(bf16[2,32,1024]{2,1,0:T(8,128)(2,1)S(1)} %get-tuple-element.35), channel_id=1, source_target_pairs={{0,2},{2,4},{4,6},{6,8},{8,10},{10,12},{12,14},{14,0},{1,3},{3,5},... | collective-permute-start | bytes 393224 | tf_op jit(solution)/shard_map/ppermute | solution.py:43
  86.0 6.4 %collective-permute-start.13 = (bf16[2,32,1024]{2,1,0:T(8,128)(2,1)S(1)}, bf16[2,32,1024]{2,1,0:T(8,128)(2,1)S(1)}, u32[]{:S(2)}, u32[]{:S(2)}) collective-permute-start(bf16[2,32,1024]{2,1,0:T(8,128)(2,1)S(1)} %get-tuple-element.34), channel_id=1, source_target_pairs={{0,14},{2,0},{4,2},{6,4},{8,6},{10,8},{12,10},{14,12},{1,15},{3,1}... | collective-permute-start | bytes 393224 | tf_op jit(solution)/shard_map/ppermute | solution.py:43
  92.5 7.2 %collective-permute-start.14 = (bf16[528,128]{1,0:T(8,128)(2,1)S(1)}, bf16[528,128]{1,0:T(8,128)(2,1)S(1)}, u32[]{:S(2)}, u32[]{:S(2)}) collective-permute-start(bf16[528,128]{1,0:T(8,128)(2,1)S(1)} %shard_map.69.refs_0_), channel_id=1, source_target_pairs={{0,2},{2,4},{4,6},{6,8},{8,10},{10,12},{12,14},{14,0},{1,3},{3,5},... | collective-permute-start | bytes 405512 | tf_op jit(solution)/shard_map/ppermute | solution.py:43
  92.6 7.1 %collective-permute-start.15 = (bf16[528,128]{1,0:T(8,128)(2,1)S(1)}, bf16[528,128]{1,0:T(8,128)(2,1)S(1)}, u32[]{:S(2)}, u32[]{:S(2)}) collective-permute-start(bf16[528,128]{1,0:T(8,128)(2,1)S(1)} %shard_map.69.refs_0_), channel_id=1, source_target_pairs={{0,14},{2,0},{4,2},{6,4},{8,6},{10,8},{12,10},{14,12},{1,15},{3,1}... | collective-permute-start | bytes 405512 | tf_op jit(solution)/shard_map/ppermute | solution.py:43
  96.2 8.9 %collective-permute-start.18 = (bf16[528,128]{1,0:T(8,128)(2,1)S(1)}, bf16[528,128]{1,0:T(8,128)(2,1)S(1)}, u32[]{:S(2)}, u32[]{:S(2)}) collective-permute-start(bf16[528,128]{1,0:T(8,128)(2,1)S(1)} %shard_map.69.refs_0_), channel_id=1, source_target_pairs={{0,1},{1,0},{2,3},{3,2},{4,5},{5,4},{6,7},{7,6},{8,9},{9,8},{10,11... | collective-permute-start | bytes 405512 | tf_op jit(solution)/shard_map/ppermute | solution.py:43
  99.8 6.3 %collective-permute-start.16 = (bf16[528,128]{1,0:T(8,128)(2,1)S(1)}, bf16[528,128]{1,0:T(8,128)(2,1)S(1)}, u32[]{:S(2)}, u32[]{:S(2)}) collective-permute-start(bf16[528,128]{1,0:T(8,128)(2,1)S(1)} %collective-permute-done.14.refs_1_), channel_id=1, source_target_pairs={{0,2},{2,4},{4,6},{6,8},{8,10},{10,12},{12,14},{14,0},{1,3},{3,5},... | collective-permute-start | bytes 405512 | tf_op jit(solution)/shard_map/ppermute | solution.py:43
  99.8 6.7 %collective-permute-start.17 = (bf16[528,128]{1,0:T(8,128)(2,1)S(1)}, bf16[528,128]{1,0:T(8,128)(2,1)S(1)}, u32[]{:S(2)}, u32[]{:S(2)}) collective-permute-start(bf16[528,128]{1,0:T(8,128)(2,1)S(1)} %collective-permute-done.15.refs_2_), channel_id=1, source_target_pairs={{0,14},{2,0},{4,2},{6,4},{8,6},{10,8},{12,10},{14,12},{1,15},{3,1}... | collective-permute-start | bytes 405512 | tf_op jit(solution)/shard_map/ppermute | solution.py:43
  103.0 8.1 %collective-permute-start.21 = (bf16[528,128]{1,0:T(8,128)(2,1)S(1)}, bf16[528,128]{1,0:T(8,128)(2,1)S(1)}, u32[]{:S(2)}, u32[]{:S(2)}) collective-permute-start(bf16[528,128]{1,0:T(8,128)(2,1)S(1)} %collective-permute-done.14.refs_1_), channel_id=1, source_target_pairs={{0,1},{1,0},{2,3},{3,2},{4,5},{5,4},{6,7},{7,6},{8,9},{9,8},{10,11... | collective-permute-start | bytes 405512 | tf_op jit(solution)/shard_map/ppermute | solution.py:43
  104.3 6.9 %collective-permute-start.22 = (bf16[528,128]{1,0:T(8,128)(2,1)S(1)}, bf16[528,128]{1,0:T(8,128)(2,1)S(1)}, u32[]{:S(2)}, u32[]{:S(2)}) collective-permute-start(bf16[528,128]{1,0:T(8,128)(2,1)S(1)} %collective-permute-done.15.refs_2_), channel_id=1, source_target_pairs={{0,1},{1,0},{2,3},{3,2},{4,5},{5,4},{6,7},{7,6},{8,9},{9,8},{10,11... | collective-permute-start | bytes 405512 | tf_op jit(solution)/shard_map/ppermute | solution.py:43
  106.5 6.8 %collective-permute-start.19 = (bf16[528,128]{1,0:T(8,128)(2,1)S(1)}, bf16[528,128]{1,0:T(8,128)(2,1)S(1)}, u32[]{:S(2)}, u32[]{:S(2)}) collective-permute-start(bf16[528,128]{1,0:T(8,128)(2,1)S(1)} %get-tuple-element.39), channel_id=1, source_target_pairs={{0,2},{2,4},{4,6},{6,8},{8,10},{10,12},{12,14},{14,0},{1,3},{3,5},... | collective-permute-start | bytes 405512 | tf_op jit(solution)/shard_map/ppermute | solution.py:43
  106.7 7.4 %collective-permute-start.23 = (bf16[528,128]{1,0:T(8,128)(2,1)S(1)}, bf16[528,128]{1,0:T(8,128)(2,1)S(1)}, u32[]{:S(2)}, u32[]{:S(2)}) collective-permute-start(bf16[528,128]{1,0:T(8,128)(2,1)S(1)} %collective-permute-done.16.refs_3_), channel_id=1, source_target_pairs={{0,1},{1,0},{2,3},{3,2},{4,5},{5,4},{6,7},{7,6},{8,9},{9,8},{10,11... | collective-permute-start | bytes 405512 | tf_op jit(solution)/shard_map/ppermute | solution.py:43
  108.8 8.9 %collective-permute-start.20 = (bf16[528,128]{1,0:T(8,128)(2,1)S(1)}, bf16[528,128]{1,0:T(8,128)(2,1)S(1)}, u32[]{:S(2)}, u32[]{:S(2)}) collective-permute-start(bf16[528,128]{1,0:T(8,128)(2,1)S(1)} %get-tuple-element.38), channel_id=1, source_target_pairs={{0,14},{2,0},{4,2},{6,4},{8,6},{10,8},{12,10},{14,12},{1,15},{3,1}... | collective-permute-start | bytes 405512 | tf_op jit(solution)/shard_map/ppermute | solution.py:43
  114.2 6.3 %collective-permute-start.24 = (bf16[528,128]{1,0:T(8,128)(2,1)S(1)}, bf16[528,128]{1,0:T(8,128)(2,1)S(1)}, u32[]{:S(2)}, u32[]{:S(2)}) collective-permute-start(bf16[528,128]{1,0:T(8,128)(2,1)S(1)} %minimum_add_fusion), channel_id=1, source_target_pairs={{0,2},{2,4},{4,6},{6,8},{8,10},{10,12},{12,14},{14,0},{1,3},{3,5},... | collective-permute-start | bytes 405512 | tf_op jit(solution)/shard_map/ppermute | solution.py:43
  115.6 7.0 %collective-permute-start.25 = (bf16[528,128]{1,0:T(8,128)(2,1)S(1)}, bf16[528,128]{1,0:T(8,128)(2,1)S(1)}, u32[]{:S(2)}, u32[]{:S(2)}) collective-permute-start(bf16[528,128]{1,0:T(8,128)(2,1)S(1)} %collective-permute-done.17.refs_4_), channel_id=1, source_target_pairs={{0,1},{1,0},{2,3},{3,2},{4,5},{5,4},{6,7},{7,6},{8,9},{9,8},{10,11... | collective-permute-start | bytes 405512 | tf_op jit(solution)/shard_map/ppermute | solution.py:43
  117.7 6.4 %collective-permute-start.27 = (bf16[528,128]{1,0:T(8,128)(2,1)S(1)}, bf16[528,128]{1,0:T(8,128)(2,1)S(1)}, u32[]{:S(2)}, u32[]{:S(2)}) collective-permute-start(bf16[528,128]{1,0:T(8,128)(2,1)S(1)} %collective-permute-done.20.refs_6_), channel_id=1, source_target_pairs={{0,1},{1,0},{2,3},{3,2},{4,5},{5,4},{6,7},{7,6},{8,9},{9,8},{10,11... | collective-permute-start | bytes 405512 | tf_op jit(solution)/shard_map/ppermute | solution.py:43
  (9 other events, 45.7 us)

commit v10 on v8

--- a/solution.py
+++ b/solution.py
@@ -238,7 +238,7 @@
         up, down = shift(up, "z", Z, 1), shift(down, "z", Z, -1)
         held += [up, down]
         crossed += [shift(up, "yl", YL), shift(down, "yl", YL)]
-    up = shift(after(up, *crossed[1:5]), "z", Z, 1)
+    up = shift(after(up, *crossed[1:3]), "z", Z, 1)
     held.append(up)
     crossed.append(shift(up, "yl", YL))
     changed, squares = kernel_call(

time: 130 us -> 126 us (0.969)
  waiting for transfers between devices: 36.8 us -> 33.6 us
    ppermute x29, waiting for transfers between devices: 36.8 us -> 33.6 us  [shift(): return lax.ppermute(a, axis, [(i, (i + by) % size) for i in range(size)])]
  transfers between devices with their start and end apart: 29 -> 29, of which waited for: 16 -> 17; matrix products, arithmetic and copies ran while one was open for 0% -> 0% of each run, Pallas kernels for 3% -> 3%
where the time goes in v10:
time: 126 us
  blocking collectives  42.2 us (33%)
  starting transfers between devices  36.8 us (29%)
  waiting for transfers between devices  33.6 us (27%)
  Pallas kernels  11.6 us (9%)
    ppermute x29, starting transfers between devices, shift(): return lax.ppermute(a, axis, [(i, (i + by) % size) for i in range(size)])  36.8 us
    ppermute x29, waiting for transfers between devices, shift(): return lax.ppermute(a, axis, [(i, (i + by) % size) for i in range(size)])  33.6 us
    all_to_all x1, blocking collectives, local(): parts = lax.all_to_all(total.reshape(chunks), ('x', 'yh'), 0, 0, tiled=True)  23 us
    all_to_all x1, blocking collectives, local(): lax.all_to_all(copies, ('x', 'yh'), 0, 0, tiled=True)  19.2 us
    pallas_call x9, Pallas kernels, kernel_call(): pl.pallas_call(body, out_shape=[jax.ShapeDtypeStruct(shape, dtype) for sh...  11.6 us
  transfers between devices with their start and end apart: 29, of which 17 were waited for; matrix products, arithmetic and copies ran while one was open for 0% of the time, Pallas kernels for 3%

profile of v10, /device:TPU:8, one launch (start us, length us, event | category | flops | bytes accessed | tf_op | source)
XLA Modules:
  0.0 125.5 jit_solution(8728827127410384484)
XLA Ops:
  0.7 3.2 %shard_map.59 = bf16[512,1024]{1,0:T(8,128)(2,1)} custom-call(s32[1]{0:T(128)} %bitcast.5.which, bf16[1024,512]{1,0:T(8,128)(2,1)} %acts.3, bf16[1024,512]{1,0:T(8,128)(2,1)} %cots.3, bf16[512,512]{1,0:T(8,128)(2,1)} %act_factor.3, bf16[512,512]{1,0:T(8,128)(2,1)} %grad_factor.3), custom_call_target="tpu_custom_call" | custom-call | flops 536870912 | bytes 3145732 | tf_op jit(solution)/shard_map/pallas_call | solution.py:50
  4.0 2.9 %collective-permute-done.came = bf16[512,1024]{1,0:T(8,128)(2,1)S(1)} collective-permute-done((bf16[512,1024]{1,0:T(8,128)(2,1)}, bf16[512,1024]{1,0:T(8,128)(2,1)S(1)}, u32[]{:S(2)}, u32[]{:S(2)}) %collective-permute-start) | collective-permute-done | bytes 1048608 | tf_op jit(solution)/shard_map/ppermute | solution.py:41
  7.6 23.0 %all_to_all.10.parts = bf16[8,64,1024]{2,1,0:T(8,128)(2,1)S(1)} all-to-all(bf16[8,64,1024]{2,1,0:T(8,128)(2,1)S(1)} %bitcast.57), channel_id=1, replica_groups=mesh['x'=4,'yh'=2,'core'=2,'z'=8,'yl'=2] {'x','yh'}, dimensions={0} | all-to-all | bytes 2097152 | tf_op jit(solution)/shard_map/all_to_all | solution.py:207
  30.7 19.2 %all_to_all.11 = bf16[8,64,1024]{2,1,0:T(8,128)(2,1)S(1)} all-to-all(bf16[8,64,1024]{2,1,0:T(8,128)(2,1)S(1)} %shard_map.61), channel_id=1, replica_groups=mesh['x'=4,'yh'=2,'core'=2,'z'=8,'yl'=2] {'x','yh'}, dimensions={0} | all-to-all | bytes 2097152 | tf_op jit(solution)/shard_map/all_to_all | solution.py:209
  50.1 2.6 %collective-permute-done.1.other = bf16[512,1024]{1,0:T(8,128)(2,1)S(1)} collective-permute-done((bf16[512,1024]{1,0:T(8,128)(2,1)S(1)}, bf16[512,1024]{1,0:T(8,128)(2,1)S(1)}, u32[]{:S(2)}, u32[]{:S(2)}) %collective-permute-start.1) | collective-permute-done | bytes 1048608 | tf_op jit(solution)/shard_map/ppermute | solution.py:41
  57.4 1.8 %shard_map.62 = (f32[2,32,1024]{2,1,0:T(8,128)S(1)}, f32[2,32,1024]{2,1,0:T(8,128)S(1)}, f32[2,32,1024]{2,1,0:T(8,128)S(1)}, f32[2,32,1024]{2,1,0:T(8,128)S(1)},...) custom-call(s32[2]{0:T(128)S(1)} %pad_add_fusion.at, ...), custom_call_target="tpu_custom_call" | custom-call | flops 536870912 | bytes 3145736 | tf_op jit(solution)/shard_map/pallas_call | solution.py:50
  59.8 2.0 %collective-permute-start.7 = (bf16[2,32,1024]{2,1,0:T(8,128)(2,1)S(1)}, bf16[2,32,1024]{2,1,0:T(8,128)(2,1)S(1)}, u32[]{:S(2)}, u32[]{:S(2)}) collective-permute-start(bf16[2,32,1024]{2,1,0:T(8,128)(2,1)S(1)} %fusion.5), channel_id=1, source_target_pairs={{0,2},{2,4},{4,6},{6,8},{8,10},{10,12},{12,14},{14,0},{1,3},{3,5},... | collective-permute-start | bytes 393224 | tf_op jit(solution)/shard_map/ppermute | solution.py:41
  61.7 1.9 %collective-permute-start.4 = (bf16[2,2,32,1024]{3,2,1,0:T(8,128)(2,1)S(1)}, bf16[2,2,32,1024]{3,2,1,0:T(8,128)(2,1)S(1)}, u32[]{:S(2)}, u32[]{:S(2)}) collective-permute-start(bf16[2,2,32,1024]{3,2,1,0:T(8,128)(2,1)S(1)} %get-tuple-element.24), channel_id=1, source_target_pairs={{0,1},{1,0},{2,3},{3,2},{4,5},{5,4},{6,7},{7,6},{8,9},{9,8},{10,11... | collective-permute-start | bytes 786440 | tf_op jit(solution)/shard_map/ppermute | solution.py:41
  63.6 5.0 %collective-permute-done.7 = bf16[2,32,1024]{2,1,0:T(8,128)(2,1)S(1)} collective-permute-done((bf16[2,32,1024]{2,1,0:T(8,128)(2,1)S(1)}, bf16[2,32,1024]{2,1,0:T(8,128)(2,1)S(1)}, u32[]{:S(2)}, u32[]{:S(2)}) %collective-permute-start.7) | collective-permute-done | bytes 131104 | tf_op jit(solution)/shard_map/ppermute | solution.py:41
  68.7 3.2 %collective-permute-start.11 = (bf16[2,32,1024]{2,1,0:T(8,128)(2,1)S(1)}, bf16[2,32,1024]{2,1,0:T(8,128)(2,1)S(1)}, u32[]{:S(2)}, u32[]{:S(2)}) collective-permute-start(bf16[2,32,1024]{2,1,0:T(8,128)(2,1)S(1)} %get-tuple-element.40), channel_id=1, source_target_pairs={{0,14},{2,0},{4,2},{6,4},{8,6},{10,8},{12,10},{14,12},{1,15},{3,1}... | collective-permute-start | bytes 393224 | tf_op jit(solution)/shard_map/ppermute | solution.py:41
  74.4 3.7 %collective-permute-done.8 = bf16[2,32,1024]{2,1,0:T(8,128)(2,1)S(1)} collective-permute-done((bf16[2,32,1024]{2,1,0:T(8,128)(2,1)S(1)}, bf16[2,32,1024]{2,1,0:T(8,128)(2,1)S(1)}, u32[]{:S(2)}, u32[]{:S(2)}) %collective-permute-start.8) | collective-permute-done | bytes 131104 | tf_op jit(solution)/shard_map/ppermute | solution.py:41
  78.3 2.0 %collective-permute-start.9 = (bf16[2,32,1024]{2,1,0:T(8,128)(2,1)S(1)}, bf16[2,32,1024]{2,1,0:T(8,128)(2,1)S(1)}, u32[]{:S(2)}, u32[]{:S(2)}) collective-permute-start(bf16[2,32,1024]{2,1,0:T(8,128)(2,1)S(1)} %get-tuple-element.39), channel_id=1, source_target_pairs={{0,2},{2,4},{4,6},{6,8},{8,10},{10,12},{12,14},{14,0},{1,3},{3,5},... | collective-permute-start | bytes 393224 | tf_op jit(solution)/shard_map/ppermute | solution.py:41
  81.7 1.6 %collective-permute-done.12 = bf16[2,32,1024]{2,1,0:T(8,128)(2,1)S(1)} collective-permute-done((bf16[2,32,1024]{2,1,0:T(8,128)(2,1)S(1)}, bf16[2,32,1024]{2,1,0:T(8,128)(2,1)S(1)}, u32[]{:S(2)}, u32[]{:S(2)}) %collective-permute-start.12) | collective-permute-done | bytes 131104 | tf_op jit(solution)/shard_map/ppermute | solution.py:41
  84.7 2.1 %collective-permute-start.10 = (bf16[2,32,1024]{2,1,0:T(8,128)(2,1)S(1)}, bf16[2,32,1024]{2,1,0:T(8,128)(2,1)S(1)}, u32[]{:S(2)}, u32[]{:S(2)}) collective-permute-start(bf16[2,32,1024]{2,1,0:T(8,128)(2,1)S(1)} %get-tuple-element.37), channel_id=1, source_target_pairs={{0,2},{2,4},{4,6},{6,8},{8,10},{10,12},{12,14},{14,0},{1,3},{3,5},... | collective-permute-start | bytes 393224 | tf_op jit(solution)/shard_map/ppermute | solution.py:41
  88.2 3.8 %collective-permute-done.10.up = bf16[2,32,1024]{2,1,0:T(8,128)(2,1)S(1)} collective-permute-done((bf16[2,32,1024]{2,1,0:T(8,128)(2,1)S(1)}, bf16[2,32,1024]{2,1,0:T(8,128)(2,1)S(1)}, u32[]{:S(2)}, u32[]{:S(2)}) %collective-permute-start.10) | collective-permute-done | bytes 131104 | tf_op jit(solution)/shard_map/ppermute | solution.py:41
  93.2 2.6 %collective-permute-start.15 = (bf16[528,128]{1,0:T(8,128)(2,1)S(1)}, bf16[528,128]{1,0:T(8,128)(2,1)S(1)}, u32[]{:S(2)}, u32[]{:S(2)}) collective-permute-start(bf16[528,128]{1,0:T(8,128)(2,1)S(1)} %shard_map.65.refs_0_), channel_id=1, source_target_pairs={{0,14},{2,0},{4,2},{6,4},{8,6},{10,8},{12,10},{14,12},{1,15},{3,1}... | collective-permute-start | bytes 405512 | tf_op jit(solution)/shard_map/ppermute | solution.py:41
  97.1 1.9 %collective-permute-done.14.refs_1_ = bf16[528,128]{1,0:T(8,128)(2,1)S(1)} collective-permute-done((bf16[528,128]{1,0:T(8,128)(2,1)S(1)}, bf16[528,128]{1,0:T(8,128)(2,1)S(1)}, u32[]{:S(2)}, u32[]{:S(2)}) %collective-permute-start.14) | collective-permute-done | bytes 135200 | tf_op jit(solution)/shard_map/ppermute | solution.py:41
  99.1 3.2 %collective-permute-start.17 = (bf16[528,128]{1,0:T(8,128)(2,1)S(1)}, bf16[528,128]{1,0:T(8,128)(2,1)S(1)}, u32[]{:S(2)}, u32[]{:S(2)}) collective-permute-start(bf16[528,128]{1,0:T(8,128)(2,1)S(1)} %collective-permute-done.15.refs_2_), channel_id=1, source_target_pairs={{0,14},{2,0},{4,2},{6,4},{8,6},{10,8},{12,10},{14,12},{1,15},{3,1}... | collective-permute-start | bytes 405512 | tf_op jit(solution)/shard_map/ppermute | solution.py:41
  105.4 3.3 %collective-permute-start.20 = (bf16[528,128]{1,0:T(8,128)(2,1)S(1)}, bf16[528,128]{1,0:T(8,128)(2,1)S(1)}, u32[]{:S(2)}, u32[]{:S(2)}) collective-permute-start(bf16[528,128]{1,0:T(8,128)(2,1)S(1)} %get-tuple-element.42), channel_id=1, source_target_pairs={{0,14},{2,0},{4,2},{6,4},{8,6},{10,8},{12,10},{14,12},{1,15},{3,1}... | collective-permute-start | bytes 405512 | tf_op jit(solution)/shard_map/ppermute | solution.py:41
  108.7 2.6 %collective-permute-done.22.refs_2_ = bf16[528,128]{1,0:T(8,128)(2,1)S(1)} collective-permute-done((bf16[528,128]{1,0:T(8,128)(2,1)S(1)}, bf16[528,128]{1,0:T(8,128)(2,1)S(1)}, u32[]{:S(2)}, u32[]{:S(2)}) %collective-permute-start.22) | collective-permute-done | bytes 135200 | tf_op jit(solution)/shard_map/ppermute | solution.py:41
  115.9 2.1 %collective-permute-done.23.refs_7_ = bf16[528,128]{1,0:T(8,128)(2,1)S(1)} collective-permute-done((bf16[528,128]{1,0:T(8,128)(2,1)S(1)}, bf16[528,128]{1,0:T(8,128)(2,1)S(1)}, u32[]{:S(2)}, u32[]{:S(2)}) %collective-permute-start.23) | collective-permute-done | bytes 135200 | tf_op jit(solution)/shard_map/ppermute | solution.py:41
  120.3 1.4 %collective-permute-done.27.refs_6_ = bf16[528,128]{1,0:T(8,128)(2,1)S(1)} collective-permute-done((bf16[528,128]{1,0:T(8,128)(2,1)S(1)}, bf16[528,128]{1,0:T(8,128)(2,1)S(1)}, u32[]{:S(2)}, u32[]{:S(2)}) %collective-permute-start.27) | collective-permute-done | bytes 135200 | tf_op jit(solution)/shard_map/ppermute | solution.py:41
  121.8 1.4 %collective-permute-done.28.refs_7_ = bf16[528,128]{1,0:T(8,128)(2,1)S(1)} collective-permute-done((bf16[528,128]{1,0:T(8,128)(2,1)S(1)}, bf16[528,128]{1,0:T(8,128)(2,1)S(1)}, u32[]{:S(2)}, u32[]{:S(2)}) %collective-permute-start.28) | collective-permute-done | bytes 135200 | tf_op jit(solution)/shard_map/ppermute | solution.py:41
  123.2 2.3 %shard_map.67 = (bf16[8,2,32,512]{3,2,1,0:T(8,128)(2,1)}, bf16[8,2,32,512]{3,2,1,0:T(8,128)(2,1)}) custom-call(s32[2]{0:T(128)S(1)} %pad_add_fusion.at, bf16[8,2,32,512]{3,2,1,0:T(8,128)(2,1)S(1)} %bitcast.52, bf16[8,2,32,512]{3,2,1,0:T(8,128)(2,1)S(1)} %bitcast.56, bf16[512,1024]{1,0:T(8,128)(2,1)S(1)} %bitcast.48, ...), custom_call_target="tpu_custom_call" | custom-call | flops 536870912 | bytes 5276680 | tf_op jit(solution)/shard_map/pallas_call | solution.py:50
  (60 shorter events, 26.0 us)
Async XLA Ops:
  53.9 5.8 %collective-permute-start.6 = (bf16[1,2,32,1024]{3,2,1,0:T(8,128)(2,1)S(1)}, bf16[1,2,32,1024]{3,2,1,0:T(8,128)(2,1)S(1)}, u32[]{:S(2)}, u32[]{:S(2)}) collective-permute-start(bf16[1,2,32,1024]{3,2,1,0:T(8,128)(2,1)S(1)} %shard_map.64), channel_id=1, source_target_pairs={{0,1},{1,0},{2,3},{3,2},{4,5},{5,4},{6,7},{7,6},{8,9},{9,8},{10,11... | collective-permute-start | bytes 393224 | tf_op jit(solution)/shard_map/ppermute | solution.py:41
  56.6 12.0 %collective-permute-start.5 = (bf16[2,2,32,1024]{3,2,1,0:T(8,128)(2,1)S(1)}, bf16[2,2,32,1024]{3,2,1,0:T(8,128)(2,1)S(1)}, u32[]{:S(2)}, u32[]{:S(2)}) collective-permute-start(bf16[2,2,32,1024]{3,2,1,0:T(8,128)(2,1)S(1)} %get-tuple-element.26), channel_id=1, source_target_pairs={{0,1},{1,0},{2,3},{3,2},{4,5},{5,4},{6,7},{7,6},{8,9},{9,8},{10,11... | collective-permute-start | bytes 786440 | tf_op jit(solution)/shard_map/ppermute | solution.py:41
  59.8 8.9 %collective-permute-start.7 = (bf16[2,32,1024]{2,1,0:T(8,128)(2,1)S(1)}, bf16[2,32,1024]{2,1,0:T(8,128)(2,1)S(1)}, u32[]{:S(2)}, u32[]{:S(2)}) collective-permute-start(bf16[2,32,1024]{2,1,0:T(8,128)(2,1)S(1)} %fusion.5), channel_id=1, source_target_pairs={{0,2},{2,4},{4,6},{6,8},{8,10},{10,12},{12,14},{14,0},{1,3},{3,5},... | collective-permute-start | bytes 393224 | tf_op jit(solution)/shard_map/ppermute | solution.py:41
  61.7 11.5 %collective-permute-start.4 = (bf16[2,2,32,1024]{3,2,1,0:T(8,128)(2,1)S(1)}, bf16[2,2,32,1024]{3,2,1,0:T(8,128)(2,1)S(1)}, u32[]{:S(2)}, u32[]{:S(2)}) collective-permute-start(bf16[2,2,32,1024]{3,2,1,0:T(8,128)(2,1)S(1)} %get-tuple-element.24), channel_id=1, source_target_pairs={{0,1},{1,0},{2,3},{3,2},{4,5},{5,4},{6,7},{7,6},{8,9},{9,8},{10,11... | collective-permute-start | bytes 786440 | tf_op jit(solution)/shard_map/ppermute | solution.py:41
  68.7 5.7 %collective-permute-start.11 = (bf16[2,32,1024]{2,1,0:T(8,128)(2,1)S(1)}, bf16[2,32,1024]{2,1,0:T(8,128)(2,1)S(1)}, u32[]{:S(2)}, u32[]{:S(2)}) collective-permute-start(bf16[2,32,1024]{2,1,0:T(8,128)(2,1)S(1)} %get-tuple-element.40), channel_id=1, source_target_pairs={{0,14},{2,0},{4,2},{6,4},{8,6},{10,8},{12,10},{14,12},{1,15},{3,1}... | collective-permute-start | bytes 393224 | tf_op jit(solution)/shard_map/ppermute | solution.py:41
  71.9 6.2 %collective-permute-start.8 = (bf16[2,32,1024]{2,1,0:T(8,128)(2,1)S(1)}, bf16[2,32,1024]{2,1,0:T(8,128)(2,1)S(1)}, u32[]{:S(2)}, u32[]{:S(2)}) collective-permute-start(bf16[2,32,1024]{2,1,0:T(8,128)(2,1)S(1)} %get-tuple-element.41), channel_id=1, source_target_pairs={{0,2},{2,4},{4,6},{6,8},{8,10},{10,12},{12,14},{14,0},{1,3},{3,5},... | collective-permute-start | bytes 393224 | tf_op jit(solution)/shard_map/ppermute | solution.py:41
  71.9 9.7 %collective-permute-start.3 = (bf16[2,2,32,1024]{3,2,1,0:T(8,128)(2,1)S(1)}, bf16[2,2,32,1024]{3,2,1,0:T(8,128)(2,1)S(1)}, u32[]{:S(2)}, u32[]{:S(2)}) collective-permute-start(bf16[2,2,32,1024]{3,2,1,0:T(8,128)(2,1)S(1)} %get-tuple-element.22), channel_id=1, source_target_pairs={{0,1},{1,0},{2,3},{3,2},{4,5},{5,4},{6,7},{7,6},{8,9},{9,8},{10,11... | collective-permute-start | bytes 786440 | tf_op jit(solution)/shard_map/ppermute | solution.py:41
  78.3 6.3 %collective-permute-start.9 = (bf16[2,32,1024]{2,1,0:T(8,128)(2,1)S(1)}, bf16[2,32,1024]{2,1,0:T(8,128)(2,1)S(1)}, u32[]{:S(2)}, u32[]{:S(2)}) collective-permute-start(bf16[2,32,1024]{2,1,0:T(8,128)(2,1)S(1)} %get-tuple-element.39), channel_id=1, source_target_pairs={{0,2},{2,4},{4,6},{6,8},{8,10},{10,12},{12,14},{14,0},{1,3},{3,5},... | collective-permute-start | bytes 393224 | tf_op jit(solution)/shard_map/ppermute | solution.py:41
  80.3 7.9 %collective-permute-start.2 = (bf16[1,2,32,1024]{3,2,1,0:T(8,128)(2,1)S(1)}, bf16[1,2,32,1024]{3,2,1,0:T(8,128)(2,1)S(1)}, u32[]{:S(2)}, u32[]{:S(2)}) collective-permute-start(bf16[1,2,32,1024]{3,2,1,0:T(8,128)(2,1)S(1)} %get-tuple-element.20), channel_id=1, source_target_pairs={{0,1},{1,0},{2,3},{3,2},{4,5},{5,4},{6,7},{7,6},{8,9},{9,8},{10,11... | collective-permute-start | bytes 393224 | tf_op jit(solution)/shard_map/ppermute | solution.py:41
  84.7 7.3 %collective-permute-start.10 = (bf16[2,32,1024]{2,1,0:T(8,128)(2,1)S(1)}, bf16[2,32,1024]{2,1,0:T(8,128)(2,1)S(1)}, u32[]{:S(2)}, u32[]{:S(2)}) collective-permute-start(bf16[2,32,1024]{2,1,0:T(8,128)(2,1)S(1)} %get-tuple-element.37), channel_id=1, source_target_pairs={{0,2},{2,4},{4,6},{6,8},{8,10},{10,12},{12,14},{14,0},{1,3},{3,5},... | collective-permute-start | bytes 393224 | tf_op jit(solution)/shard_map/ppermute | solution.py:41
  92.1 6.9 %collective-permute-start.14 = (bf16[528,128]{1,0:T(8,128)(2,1)S(1)}, bf16[528,128]{1,0:T(8,128)(2,1)S(1)}, u32[]{:S(2)}, u32[]{:S(2)}) collective-permute-start(bf16[528,128]{1,0:T(8,128)(2,1)S(1)} %shard_map.65.refs_0_), channel_id=1, source_target_pairs={{0,2},{2,4},{4,6},{6,8},{8,10},{10,12},{12,14},{14,0},{1,3},{3,5},... | collective-permute-start | bytes 405512 | tf_op jit(solution)/shard_map/ppermute | solution.py:41
  93.2 5.9 %collective-permute-start.15 = (bf16[528,128]{1,0:T(8,128)(2,1)S(1)}, bf16[528,128]{1,0:T(8,128)(2,1)S(1)}, u32[]{:S(2)}, u32[]{:S(2)}) collective-permute-start(bf16[528,128]{1,0:T(8,128)(2,1)S(1)} %shard_map.65.refs_0_), channel_id=1, source_target_pairs={{0,14},{2,0},{4,2},{6,4},{8,6},{10,8},{12,10},{14,12},{1,15},{3,1}... | collective-permute-start | bytes 405512 | tf_op jit(solution)/shard_map/ppermute | solution.py:41
  95.8 8.6 %collective-permute-start.18 = (bf16[528,128]{1,0:T(8,128)(2,1)S(1)}, bf16[528,128]{1,0:T(8,128)(2,1)S(1)}, u32[]{:S(2)}, u32[]{:S(2)}) collective-permute-start(bf16[528,128]{1,0:T(8,128)(2,1)S(1)} %shard_map.65.refs_0_), channel_id=1, source_target_pairs={{0,1},{1,0},{2,3},{3,2},{4,5},{5,4},{6,7},{7,6},{8,9},{9,8},{10,11... | collective-permute-start | bytes 405512 | tf_op jit(solution)/shard_map/ppermute | solution.py:41
  99.1 6.2 %collective-permute-start.16 = (bf16[528,128]{1,0:T(8,128)(2,1)S(1)}, bf16[528,128]{1,0:T(8,128)(2,1)S(1)}, u32[]{:S(2)}, u32[]{:S(2)}) collective-permute-start(bf16[528,128]{1,0:T(8,128)(2,1)S(1)} %collective-permute-done.14.refs_1_), channel_id=1, source_target_pairs={{0,2},{2,4},{4,6},{6,8},{8,10},{10,12},{12,14},{14,0},{1,3},{3,5},... | collective-permute-start | bytes 405512 | tf_op jit(solution)/shard_map/ppermute | solution.py:41
  99.1 6.2 %collective-permute-start.17 = (bf16[528,128]{1,0:T(8,128)(2,1)S(1)}, bf16[528,128]{1,0:T(8,128)(2,1)S(1)}, u32[]{:S(2)}, u32[]{:S(2)}) collective-permute-start(bf16[528,128]{1,0:T(8,128)(2,1)S(1)} %collective-permute-done.15.refs_2_), channel_id=1, source_target_pairs={{0,14},{2,0},{4,2},{6,4},{8,6},{10,8},{12,10},{14,12},{1,15},{3,1}... | collective-permute-start | bytes 405512 | tf_op jit(solution)/shard_map/ppermute | solution.py:41
  102.3 6.4 %collective-permute-start.21 = (bf16[528,128]{1,0:T(8,128)(2,1)S(1)}, bf16[528,128]{1,0:T(8,128)(2,1)S(1)}, u32[]{:S(2)}, u32[]{:S(2)}) collective-permute-start(bf16[528,128]{1,0:T(8,128)(2,1)S(1)} %collective-permute-done.14.refs_1_), channel_id=1, source_target_pairs={{0,1},{1,0},{2,3},{3,2},{4,5},{5,4},{6,7},{7,6},{8,9},{9,8},{10,11... | collective-permute-start | bytes 405512 | tf_op jit(solution)/shard_map/ppermute | solution.py:41
  103.7 7.6 %collective-permute-start.22 = (bf16[528,128]{1,0:T(8,128)(2,1)S(1)}, bf16[528,128]{1,0:T(8,128)(2,1)S(1)}, u32[]{:S(2)}, u32[]{:S(2)}) collective-permute-start(bf16[528,128]{1,0:T(8,128)(2,1)S(1)} %collective-permute-done.15.refs_2_), channel_id=1, source_target_pairs={{0,1},{1,0},{2,3},{3,2},{4,5},{5,4},{6,7},{7,6},{8,9},{9,8},{10,11... | collective-permute-start | bytes 405512 | tf_op jit(solution)/shard_map/ppermute | solution.py:41
  105.3 6.3 %collective-permute-start.19 = (bf16[528,128]{1,0:T(8,128)(2,1)S(1)}, bf16[528,128]{1,0:T(8,128)(2,1)S(1)}, u32[]{:S(2)}, u32[]{:S(2)}) collective-permute-start(bf16[528,128]{1,0:T(8,128)(2,1)S(1)} %get-tuple-element.43), channel_id=1, source_target_pairs={{0,2},{2,4},{4,6},{6,8},{8,10},{10,12},{12,14},{14,0},{1,3},{3,5},... | collective-permute-start | bytes 405512 | tf_op jit(solution)/shard_map/ppermute | solution.py:41
  105.4 9.8 %collective-permute-start.20 = (bf16[528,128]{1,0:T(8,128)(2,1)S(1)}, bf16[528,128]{1,0:T(8,128)(2,1)S(1)}, u32[]{:S(2)}, u32[]{:S(2)}) collective-permute-start(bf16[528,128]{1,0:T(8,128)(2,1)S(1)} %get-tuple-element.42), channel_id=1, source_target_pairs={{0,14},{2,0},{4,2},{6,4},{8,6},{10,8},{12,10},{14,12},{1,15},{3,1}... | collective-permute-start | bytes 405512 | tf_op jit(solution)/shard_map/ppermute | solution.py:41
  111.7 6.3 %collective-permute-start.23 = (bf16[528,128]{1,0:T(8,128)(2,1)S(1)}, bf16[528,128]{1,0:T(8,128)(2,1)S(1)}, u32[]{:S(2)}, u32[]{:S(2)}) collective-permute-start(bf16[528,128]{1,0:T(8,128)(2,1)S(1)} %minimum_add_fusion), channel_id=1, source_target_pairs={{0,2},{2,4},{4,6},{6,8},{8,10},{10,12},{12,14},{14,0},{1,3},{3,5},... | collective-permute-start | bytes 405512 | tf_op jit(solution)/shard_map/ppermute | solution.py:41
  111.8 8.3 %collective-permute-start.24 = (bf16[528,128]{1,0:T(8,128)(2,1)S(1)}, bf16[528,128]{1,0:T(8,128)(2,1)S(1)}, u32[]{:S(2)}, u32[]{:S(2)}) collective-permute-start(bf16[528,128]{1,0:T(8,128)(2,1)S(1)} %collective-permute-done.16.refs_3_), channel_id=1, source_target_pairs={{0,1},{1,0},{2,3},{3,2},{4,5},{5,4},{6,7},{7,6},{8,9},{9,8},{10,11... | collective-permute-start | bytes 405512 | tf_op jit(solution)/shard_map/ppermute | solution.py:41
  113.2 6.9 %collective-permute-start.25 = (bf16[528,128]{1,0:T(8,128)(2,1)S(1)}, bf16[528,128]{1,0:T(8,128)(2,1)S(1)}, u32[]{:S(2)}, u32[]{:S(2)}) collective-permute-start(bf16[528,128]{1,0:T(8,128)(2,1)S(1)} %collective-permute-done.17.refs_4_), channel_id=1, source_target_pairs={{0,1},{1,0},{2,3},{3,2},{4,5},{5,4},{6,7},{7,6},{8,9},{9,8},{10,11... | collective-permute-start | bytes 405512 | tf_op jit(solution)/shard_map/ppermute | solution.py:41
  113.9 6.5 %collective-permute-start.26 = (bf16[528,128]{1,0:T(8,128)(2,1)S(1)}, bf16[528,128]{1,0:T(8,128)(2,1)S(1)}, u32[]{:S(2)}, u32[]{:S(2)}) collective-permute-start(bf16[528,128]{1,0:T(8,128)(2,1)S(1)} %collective-permute-done.19.refs_5_), channel_id=1, source_target_pairs={{0,1},{1,0},{2,3},{3,2},{4,5},{5,4},{6,7},{7,6},{8,9},{9,8},{10,11... | collective-permute-start | bytes 405512 | tf_op jit(solution)/shard_map/ppermute | solution.py:41
  115.2 6.6 %collective-permute-start.27 = (bf16[528,128]{1,0:T(8,128)(2,1)S(1)}, bf16[528,128]{1,0:T(8,128)(2,1)S(1)}, u32[]{:S(2)}, u32[]{:S(2)}) collective-permute-start(bf16[528,128]{1,0:T(8,128)(2,1)S(1)} %collective-permute-done.20.refs_6_), channel_id=1, source_target_pairs={{0,1},{1,0},{2,3},{3,2},{4,5},{5,4},{6,7},{7,6},{8,9},{9,8},{10,11... | collective-permute-start | bytes 405512 | tf_op jit(solution)/shard_map/ppermute | solution.py:41
  (9 other events, 46.2 us)

commit v11 on v10

--- a/solution.py
+++ b/solution.py
@@ -95,38 +95,36 @@
     return slice(f * WIDTH, (f + 1) * WIDTH)
 
 
-def image_rows(factor, z, side, mine, other, f, chunks):
+def image_rows(factor, z, side, chunks):
     rows = [factor[pl.ds(lax.rem(z + (e + Z), Z), 1), pl.ds(side, 1)].reshape(PART, WIDTH) for e in chunks]
-    rows = jnp.concatenate(rows, axis=0)
-    return (
-        dot_t(rows, mine[:, factor_columns(f)]),
-        dot_t(rows, other[:, factor_columns(f)]),
-    )
-
-
-def image_first(at, act_factor, grad_factor, mine, other, out):
+    return jnp.concatenate(rows, axis=0)
+
+
+def image_first(at, act_factor, grad_factor, mine, other, *outs):
     for f, factor in enumerate((act_factor, grad_factor)):
-        first, second = image_rows(factor, at[0], 1 - at[1], mine, other, f, REDUCE[:1])
-        out[0, f, :, :HALF] = first.astype(bf16)
-        out[0, f, :, HALF:] = second.astype(bf16)
+        rows = image_rows(factor, at[0], 1 - at[1], REDUCE[:4])
+        for part, cols in ((mine, slice(0, HALF)), (other, slice(HALF, TOKENS))):
+            image = dot_t(part[:, factor_columns(f)], rows).T.astype(bf16)
+            for n, (group, k) in enumerate(PLACES[:3]):
+                outs[group][k, f, :, cols] = image[n * PART : (n + 1) * PART]
 
 
 def image_away(at, act_factor, grad_factor, mine, other, *outs):
     for f, factor in enumerate((act_factor, grad_factor)):
-        first, second = image_rows(factor, at[0], 1 - at[1], mine, other, f, REDUCE[1:])
-        for n, (group, k) in enumerate(PLACES[1:]):
-            rows = slice(n * PART, (n + 1) * PART)
-            outs[group - 1][k, f, :, :HALF] = first[rows].astype(bf16)
-            outs[group - 1][k, f, :, HALF:] = second[rows].astype(bf16)
+        rows = image_rows(factor, at[0], 1 - at[1], REDUCE[3:])
+        for part, cols in ((mine, slice(0, HALF)), (other, slice(HALF, TOKENS))):
+            image = dot_t(rows, part[:, factor_columns(f)]).astype(bf16)
+            for n, (group, k) in enumerate(PLACES[3:]):
+                outs[group - 2][k, f, :, cols] = image[n * PART : (n + 1) * PART]
 
 
 def image_own(at, act_factor, grad_factor, mine, other, *outs):
     for f, factor in enumerate((act_factor, grad_factor)):
-        first, second = image_rows(factor, at[0], at[1], mine, other, f, REDUCE)
-        for k in range(Z):
-            rows = slice(k * PART, (k + 1) * PART)
-            outs[k][f, :, :HALF] = first[rows]
-            outs[k][f, :, HALF:] = second[rows]
+        rows = image_rows(factor, at[0], at[1], REDUCE)
+        for part, cols in ((mine, slice(0, HALF)), (other, slice(HALF, TOKENS))):
+            image = dot_t(rows, part[:, factor_columns(f)])
+            for k in range(Z):
+                outs[k][f, :, cols] = image[k * PART : (k + 1) * PART]
         square = sum(jnp.square(part[:, factor_columns(f)].astype(f32)) for part in (mine, other))
         outs[Z][f : f + 1] = jnp.sum(square, axis=0, keepdims=True)
 
@@ -212,8 +210,8 @@
     factors = [f.reshape(Z, YL, PART, WIDTH) for f in (act_factor, grad_factor)]
     shape = (2, PART, TOKENS)
     sent = [((sum(g == group for g, _ in PLACES),) + shape, bf16) for group in range(5)]
-    first = kernel_call(image_first, sent[:1], *factors, mine, other, index=[z, yl], flops=product // Z)
-    away = first + kernel_call(image_away, sent[1:], *factors, mine, other, index=[z, yl], flops=product)
+    first = kernel_call(image_first, sent[:2], *factors, mine, other, index=[z, yl], flops=product // 2)
+    away = first + kernel_call(image_away, sent[2:], *factors, mine, other, index=[z, yl], flops=product)
     away = [shift(a, "yl", YL) for a in away]
     *own, squares = kernel_call(
         image_own, [(shape, f32)] * Z + [((2, WIDTH), f32)], *factors, mine, other, index=[z, yl], flops=product

time: 126 us -> 126 us (level)
  no operation moved by 1% of the time
where the time goes in v11:
time: 126 us
  blocking collectives  42.2 us (33%)
  starting transfers between devices  35.8 us (28%)
  waiting for transfers between devices  34.7 us (28%)
  Pallas kernels  11.7 us (9%)
    ppermute x29, starting transfers between devices, shift(): return lax.ppermute(a, axis, [(i, (i + by) % size) for i in range(size)])  35.8 us
    ppermute x29, waiting for transfers between devices, shift(): return lax.ppermute(a, axis, [(i, (i + by) % size) for i in range(size)])  34.7 us
    all_to_all x1, blocking collectives, local(): parts = lax.all_to_all(total.reshape(chunks), ('x', 'yh'), 0, 0, tiled=True)  23 us
    all_to_all x1, blocking collectives, local(): lax.all_to_all(copies, ('x', 'yh'), 0, 0, tiled=True)  19.2 us
    pallas_call x9, Pallas kernels, kernel_call(): pl.pallas_call(body, out_shape=[jax.ShapeDtypeStruct(shape, dtype) for sh...  11.7 us
  transfers between devices with their start and end apart: 29, of which 17 were waited for; matrix products, arithmetic and copies ran while one was open for 0% of the time, Pallas kernels for 3%

profile of v11, /device:TPU:8, one launch (start us, length us, event | category | flops | bytes accessed | tf_op | source)
XLA Modules:
  0.0 125.7 jit_solution(14093773105252798935)
XLA Ops:
  0.7 3.3 %shard_map.59 = bf16[512,1024]{1,0:T(8,128)(2,1)} custom-call(s32[1]{0:T(128)} %bitcast.5.which, bf16[1024,512]{1,0:T(8,128)(2,1)} %acts.3, bf16[1024,512]{1,0:T(8,128)(2,1)} %cots.3, bf16[512,512]{1,0:T(8,128)(2,1)} %act_factor.3, bf16[512,512]{1,0:T(8,128)(2,1)} %grad_factor.3), custom_call_target="tpu_custom_call" | custom-call | flops 536870912 | bytes 3145732 | tf_op jit(solution)/shard_map/pallas_call | solution.py:50
  4.0 2.9 %collective-permute-done.came = bf16[512,1024]{1,0:T(8,128)(2,1)S(1)} collective-permute-done((bf16[512,1024]{1,0:T(8,128)(2,1)}, bf16[512,1024]{1,0:T(8,128)(2,1)S(1)}, u32[]{:S(2)}, u32[]{:S(2)}) %collective-permute-start) | collective-permute-done | bytes 1048608 | tf_op jit(solution)/shard_map/ppermute | solution.py:41
  7.6 23.0 %all_to_all.10.parts = bf16[8,64,1024]{2,1,0:T(8,128)(2,1)S(1)} all-to-all(bf16[8,64,1024]{2,1,0:T(8,128)(2,1)S(1)} %bitcast.57), channel_id=1, replica_groups=mesh['x'=4,'yh'=2,'core'=2,'z'=8,'yl'=2] {'x','yh'}, dimensions={0} | all-to-all | bytes 2097152 | tf_op jit(solution)/shard_map/all_to_all | solution.py:205
  30.8 19.2 %all_to_all.11 = bf16[8,64,1024]{2,1,0:T(8,128)(2,1)S(1)} all-to-all(bf16[8,64,1024]{2,1,0:T(8,128)(2,1)S(1)} %shard_map.61), channel_id=1, replica_groups=mesh['x'=4,'yh'=2,'core'=2,'z'=8,'yl'=2] {'x','yh'}, dimensions={0} | all-to-all | bytes 2097152 | tf_op jit(solution)/shard_map/all_to_all | solution.py:207
  50.1 2.6 %collective-permute-done.1.other = bf16[512,1024]{1,0:T(8,128)(2,1)S(1)} collective-permute-done((bf16[512,1024]{1,0:T(8,128)(2,1)S(1)}, bf16[512,1024]{1,0:T(8,128)(2,1)S(1)}, u32[]{:S(2)}, u32[]{:S(2)}) %collective-permute-start.1) | collective-permute-done | bytes 1048608 | tf_op jit(solution)/shard_map/ppermute | solution.py:41
  56.1 1.8 %shard_map.62 = (f32[2,32,1024]{2,1,0:T(8,128)S(1)}, f32[2,32,1024]{2,1,0:T(8,128)S(1)}, f32[2,32,1024]{2,1,0:T(8,128)S(1)}, f32[2,32,1024]{2,1,0:T(8,128)S(1)},...) custom-call(s32[2]{0:T(128)S(1)} %pad_add_fusion.at, ...), custom_call_target="tpu_custom_call" | custom-call | flops 536870912 | bytes 3145736 | tf_op jit(solution)/shard_map/pallas_call | solution.py:50
  57.9 2.6 %collective-permute-done.6 = bf16[1,2,32,1024]{3,2,1,0:T(8,128)(2,1)S(1)} collective-permute-done((bf16[1,2,32,1024]{3,2,1,0:T(8,128)(2,1)S(1)}, bf16[1,2,32,1024]{3,2,1,0:T(8,128)(2,1)S(1)}, u32[]{:S(2)}, u32[]{:S(2)}) %collective-permute-start.6) | collective-permute-done | bytes 131104 | tf_op jit(solution)/shard_map/ppermute | solution.py:41
  60.5 2.0 %collective-permute-start.7 = (bf16[2,32,1024]{2,1,0:T(8,128)(2,1)S(1)}, bf16[2,32,1024]{2,1,0:T(8,128)(2,1)S(1)}, u32[]{:S(2)}, u32[]{:S(2)}) collective-permute-start(bf16[2,32,1024]{2,1,0:T(8,128)(2,1)S(1)} %fusion.5), channel_id=1, source_target_pairs={{0,2},{2,4},{4,6},{6,8},{8,10},{10,12},{12,14},{14,0},{1,3},{3,5},... | collective-permute-start | bytes 393224 | tf_op jit(solution)/shard_map/ppermute | solution.py:41
  65.3 4.1 %collective-permute-done.7 = bf16[2,32,1024]{2,1,0:T(8,128)(2,1)S(1)} collective-permute-done((bf16[2,32,1024]{2,1,0:T(8,128)(2,1)S(1)}, bf16[2,32,1024]{2,1,0:T(8,128)(2,1)S(1)}, u32[]{:S(2)}, u32[]{:S(2)}) %collective-permute-start.7) | collective-permute-done | bytes 131104 | tf_op jit(solution)/shard_map/ppermute | solution.py:41
  69.4 2.6 %collective-permute-start.11 = (bf16[2,32,1024]{2,1,0:T(8,128)(2,1)S(1)}, bf16[2,32,1024]{2,1,0:T(8,128)(2,1)S(1)}, u32[]{:S(2)}, u32[]{:S(2)}) collective-permute-start(bf16[2,32,1024]{2,1,0:T(8,128)(2,1)S(1)} %get-tuple-element.42), channel_id=1, source_target_pairs={{0,14},{2,0},{4,2},{6,4},{8,6},{10,8},{12,10},{14,12},{1,15},{3,1}... | collective-permute-start | bytes 393224 | tf_op jit(solution)/shard_map/ppermute | solution.py:41
  74.6 3.7 %collective-permute-done.8 = bf16[2,32,1024]{2,1,0:T(8,128)(2,1)S(1)} collective-permute-done((bf16[2,32,1024]{2,1,0:T(8,128)(2,1)S(1)}, bf16[2,32,1024]{2,1,0:T(8,128)(2,1)S(1)}, u32[]{:S(2)}, u32[]{:S(2)}) %collective-permute-start.8) | collective-permute-done | bytes 131104 | tf_op jit(solution)/shard_map/ppermute | solution.py:41
  78.4 2.0 %collective-permute-start.9 = (bf16[2,32,1024]{2,1,0:T(8,128)(2,1)S(1)}, bf16[2,32,1024]{2,1,0:T(8,128)(2,1)S(1)}, u32[]{:S(2)}, u32[]{:S(2)}) collective-permute-start(bf16[2,32,1024]{2,1,0:T(8,128)(2,1)S(1)} %get-tuple-element.41), channel_id=1, source_target_pairs={{0,2},{2,4},{4,6},{6,8},{8,10},{10,12},{12,14},{14,0},{1,3},{3,5},... | collective-permute-start | bytes 393224 | tf_op jit(solution)/shard_map/ppermute | solution.py:41
  81.8 1.6 %collective-permute-done.12 = bf16[2,32,1024]{2,1,0:T(8,128)(2,1)S(1)} collective-permute-done((bf16[2,32,1024]{2,1,0:T(8,128)(2,1)S(1)}, bf16[2,32,1024]{2,1,0:T(8,128)(2,1)S(1)}, u32[]{:S(2)}, u32[]{:S(2)}) %collective-permute-start.12) | collective-permute-done | bytes 131104 | tf_op jit(solution)/shard_map/ppermute | solution.py:41
  84.8 2.1 %collective-permute-start.10 = (bf16[2,32,1024]{2,1,0:T(8,128)(2,1)S(1)}, bf16[2,32,1024]{2,1,0:T(8,128)(2,1)S(1)}, u32[]{:S(2)}, u32[]{:S(2)}) collective-permute-start(bf16[2,32,1024]{2,1,0:T(8,128)(2,1)S(1)} %get-tuple-element.39), channel_id=1, source_target_pairs={{0,2},{2,4},{4,6},{6,8},{8,10},{10,12},{12,14},{14,0},{1,3},{3,5},... | collective-permute-start | bytes 393224 | tf_op jit(solution)/shard_map/ppermute | solution.py:41
  88.3 3.9 %collective-permute-done.10.up = bf16[2,32,1024]{2,1,0:T(8,128)(2,1)S(1)} collective-permute-done((bf16[2,32,1024]{2,1,0:T(8,128)(2,1)S(1)}, bf16[2,32,1024]{2,1,0:T(8,128)(2,1)S(1)}, u32[]{:S(2)}, u32[]{:S(2)}) %collective-permute-start.10) | collective-permute-done | bytes 131104 | tf_op jit(solution)/shard_map/ppermute | solution.py:41
  93.0 2.9 %collective-permute-start.15 = (bf16[528,128]{1,0:T(8,128)(2,1)S(1)}, bf16[528,128]{1,0:T(8,128)(2,1)S(1)}, u32[]{:S(2)}, u32[]{:S(2)}) collective-permute-start(bf16[528,128]{1,0:T(8,128)(2,1)S(1)} %shard_map.65.refs_0_), channel_id=1, source_target_pairs={{0,14},{2,0},{4,2},{6,4},{8,6},{10,8},{12,10},{14,12},{1,15},{3,1}... | collective-permute-start | bytes 405512 | tf_op jit(solution)/shard_map/ppermute | solution.py:41
  97.3 1.9 %collective-permute-done.14.refs_1_ = bf16[528,128]{1,0:T(8,128)(2,1)S(1)} collective-permute-done((bf16[528,128]{1,0:T(8,128)(2,1)S(1)}, bf16[528,128]{1,0:T(8,128)(2,1)S(1)}, u32[]{:S(2)}, u32[]{:S(2)}) %collective-permute-start.14) | collective-permute-done | bytes 135200 | tf_op jit(solution)/shard_map/ppermute | solution.py:41
  99.2 3.2 %collective-permute-start.17 = (bf16[528,128]{1,0:T(8,128)(2,1)S(1)}, bf16[528,128]{1,0:T(8,128)(2,1)S(1)}, u32[]{:S(2)}, u32[]{:S(2)}) collective-permute-start(bf16[528,128]{1,0:T(8,128)(2,1)S(1)} %collective-permute-done.15.refs_2_), channel_id=1, source_target_pairs={{0,14},{2,0},{4,2},{6,4},{8,6},{10,8},{12,10},{14,12},{1,15},{3,1}... | collective-permute-start | bytes 405512 | tf_op jit(solution)/shard_map/ppermute | solution.py:41
  105.6 3.3 %collective-permute-start.20 = (bf16[528,128]{1,0:T(8,128)(2,1)S(1)}, bf16[528,128]{1,0:T(8,128)(2,1)S(1)}, u32[]{:S(2)}, u32[]{:S(2)}) collective-permute-start(bf16[528,128]{1,0:T(8,128)(2,1)S(1)} %get-tuple-element.44), channel_id=1, source_target_pairs={{0,14},{2,0},{4,2},{6,4},{8,6},{10,8},{12,10},{14,12},{1,15},{3,1}... | collective-permute-start | bytes 405512 | tf_op jit(solution)/shard_map/ppermute | solution.py:41
  108.9 2.6 %collective-permute-done.22.refs_2_ = bf16[528,128]{1,0:T(8,128)(2,1)S(1)} collective-permute-done((bf16[528,128]{1,0:T(8,128)(2,1)S(1)}, bf16[528,128]{1,0:T(8,128)(2,1)S(1)}, u32[]{:S(2)}, u32[]{:S(2)}) %collective-permute-start.22) | collective-permute-done | bytes 135200 | tf_op jit(solution)/shard_map/ppermute | solution.py:41
  116.1 2.1 %collective-permute-done.23.refs_7_ = bf16[528,128]{1,0:T(8,128)(2,1)S(1)} collective-permute-done((bf16[528,128]{1,0:T(8,128)(2,1)S(1)}, bf16[528,128]{1,0:T(8,128)(2,1)S(1)}, u32[]{:S(2)}, u32[]{:S(2)}) %collective-permute-start.23) | collective-permute-done | bytes 135200 | tf_op jit(solution)/shard_map/ppermute | solution.py:41
  120.5 1.4 %collective-permute-done.27.refs_6_ = bf16[528,128]{1,0:T(8,128)(2,1)S(1)} collective-permute-done((bf16[528,128]{1,0:T(8,128)(2,1)S(1)}, bf16[528,128]{1,0:T(8,128)(2,1)S(1)}, u32[]{:S(2)}, u32[]{:S(2)}) %collective-permute-start.27) | collective-permute-done | bytes 135200 | tf_op jit(solution)/shard_map/ppermute | solution.py:41
  122.0 1.4 %collective-permute-done.28.refs_7_ = bf16[528,128]{1,0:T(8,128)(2,1)S(1)} collective-permute-done((bf16[528,128]{1,0:T(8,128)(2,1)S(1)}, bf16[528,128]{1,0:T(8,128)(2,1)S(1)}, u32[]{:S(2)}, u32[]{:S(2)}) %collective-permute-start.28) | collective-permute-done | bytes 135200 | tf_op jit(solution)/shard_map/ppermute | solution.py:41
  123.4 2.3 %shard_map.67 = (bf16[8,2,32,512]{3,2,1,0:T(8,128)(2,1)}, bf16[8,2,32,512]{3,2,1,0:T(8,128)(2,1)}) custom-call(s32[2]{0:T(128)S(1)} %pad_add_fusion.at, bf16[8,2,32,512]{3,2,1,0:T(8,128)(2,1)S(1)} %bitcast.52, bf16[8,2,32,512]{3,2,1,0:T(8,128)(2,1)S(1)} %bitcast.56, bf16[512,1024]{1,0:T(8,128)(2,1)S(1)} %bitcast.48, ...), custom_call_target="tpu_custom_call" | custom-call | flops 536870912 | bytes 5276680 | tf_op jit(solution)/shard_map/pallas_call | solution.py:50
  (60 shorter events, 26.5 us)
Async XLA Ops:
  54.0 6.4 %collective-permute-start.6 = (bf16[1,2,32,1024]{3,2,1,0:T(8,128)(2,1)S(1)}, bf16[1,2,32,1024]{3,2,1,0:T(8,128)(2,1)S(1)}, u32[]{:S(2)}, u32[]{:S(2)}) collective-permute-start(bf16[1,2,32,1024]{3,2,1,0:T(8,128)(2,1)S(1)} %get-tuple-element.29), channel_id=1, source_target_pairs={{0,1},{1,0},{2,3},{3,2},{4,5},{5,4},{6,7},{7,6},{8,9},{9,8},{10,11... | collective-permute-start | bytes 393224 | tf_op jit(solution)/shard_map/ppermute | solution.py:41
  55.4 13.9 %collective-permute-start.5 = (bf16[2,2,32,1024]{3,2,1,0:T(8,128)(2,1)S(1)}, bf16[2,2,32,1024]{3,2,1,0:T(8,128)(2,1)S(1)}, u32[]{:S(2)}, u32[]{:S(2)}) collective-permute-start(bf16[2,2,32,1024]{3,2,1,0:T(8,128)(2,1)S(1)} %get-tuple-element.27), channel_id=1, source_target_pairs={{0,1},{1,0},{2,3},{3,2},{4,5},{5,4},{6,7},{7,6},{8,9},{9,8},{10,11... | collective-permute-start | bytes 786440 | tf_op jit(solution)/shard_map/ppermute | solution.py:41
  60.5 8.9 %collective-permute-start.7 = (bf16[2,32,1024]{2,1,0:T(8,128)(2,1)S(1)}, bf16[2,32,1024]{2,1,0:T(8,128)(2,1)S(1)}, u32[]{:S(2)}, u32[]{:S(2)}) collective-permute-start(bf16[2,32,1024]{2,1,0:T(8,128)(2,1)S(1)} %fusion.5), channel_id=1, source_target_pairs={{0,2},{2,4},{4,6},{6,8},{8,10},{10,12},{12,14},{14,0},{1,3},{3,5},... | collective-permute-start | bytes 393224 | tf_op jit(solution)/shard_map/ppermute | solution.py:41
  63.8 9.6 %collective-permute-start.4 = (bf16[2,2,32,1024]{3,2,1,0:T(8,128)(2,1)S(1)}, bf16[2,2,32,1024]{3,2,1,0:T(8,128)(2,1)S(1)}, u32[]{:S(2)}, u32[]{:S(2)}) collective-permute-start(bf16[2,2,32,1024]{3,2,1,0:T(8,128)(2,1)S(1)} %get-tuple-element.25), channel_id=1, source_target_pairs={{0,1},{1,0},{2,3},{3,2},{4,5},{5,4},{6,7},{7,6},{8,9},{9,8},{10,11... | collective-permute-start | bytes 786440 | tf_op jit(solution)/shard_map/ppermute | solution.py:41
  72.1 6.2 %collective-permute-start.8 = (bf16[2,32,1024]{2,1,0:T(8,128)(2,1)S(1)}, bf16[2,32,1024]{2,1,0:T(8,128)(2,1)S(1)}, u32[]{:S(2)}, u32[]{:S(2)}) collective-permute-start(bf16[2,32,1024]{2,1,0:T(8,128)(2,1)S(1)} %get-tuple-element.43), channel_id=1, source_target_pairs={{0,2},{2,4},{4,6},{6,8},{8,10},{10,12},{12,14},{14,0},{1,3},{3,5},... | collective-permute-start | bytes 393224 | tf_op jit(solution)/shard_map/ppermute | solution.py:41
  72.1 9.7 %collective-permute-start.3 = (bf16[2,2,32,1024]{3,2,1,0:T(8,128)(2,1)S(1)}, bf16[2,2,32,1024]{3,2,1,0:T(8,128)(2,1)S(1)}, u32[]{:S(2)}, u32[]{:S(2)}) collective-permute-start(bf16[2,2,32,1024]{3,2,1,0:T(8,128)(2,1)S(1)} %get-tuple-element.23), channel_id=1, source_target_pairs={{0,1},{1,0},{2,3},{3,2},{4,5},{5,4},{6,7},{7,6},{8,9},{9,8},{10,11... | collective-permute-start | bytes 786440 | tf_op jit(solution)/shard_map/ppermute | solution.py:41
  78.4 6.3 %collective-permute-start.9 = (bf16[2,32,1024]{2,1,0:T(8,128)(2,1)S(1)}, bf16[2,32,1024]{2,1,0:T(8,128)(2,1)S(1)}, u32[]{:S(2)}, u32[]{:S(2)}) collective-permute-start(bf16[2,32,1024]{2,1,0:T(8,128)(2,1)S(1)} %get-tuple-element.41), channel_id=1, source_target_pairs={{0,2},{2,4},{4,6},{6,8},{8,10},{10,12},{12,14},{14,0},{1,3},{3,5},... | collective-permute-start | bytes 393224 | tf_op jit(solution)/shard_map/ppermute | solution.py:41
  80.5 7.8 %collective-permute-start.2 = (bf16[1,2,32,1024]{3,2,1,0:T(8,128)(2,1)S(1)}, bf16[1,2,32,1024]{3,2,1,0:T(8,128)(2,1)S(1)}, u32[]{:S(2)}, u32[]{:S(2)}) collective-permute-start(bf16[1,2,32,1024]{3,2,1,0:T(8,128)(2,1)S(1)} %get-tuple-element.21), channel_id=1, source_target_pairs={{0,1},{1,0},{2,3},{3,2},{4,5},{5,4},{6,7},{7,6},{8,9},{9,8},{10,11... | collective-permute-start | bytes 393224 | tf_op jit(solution)/shard_map/ppermute | solution.py:41
  84.8 7.4 %collective-permute-start.10 = (bf16[2,32,1024]{2,1,0:T(8,128)(2,1)S(1)}, bf16[2,32,1024]{2,1,0:T(8,128)(2,1)S(1)}, u32[]{:S(2)}, u32[]{:S(2)}) collective-permute-start(bf16[2,32,1024]{2,1,0:T(8,128)(2,1)S(1)} %get-tuple-element.39), channel_id=1, source_target_pairs={{0,2},{2,4},{4,6},{6,8},{8,10},{10,12},{12,14},{14,0},{1,3},{3,5},... | collective-permute-start | bytes 393224 | tf_op jit(solution)/shard_map/ppermute | solution.py:41
  92.3 6.9 %collective-permute-start.14 = (bf16[528,128]{1,0:T(8,128)(2,1)S(1)}, bf16[528,128]{1,0:T(8,128)(2,1)S(1)}, u32[]{:S(2)}, u32[]{:S(2)}) collective-permute-start(bf16[528,128]{1,0:T(8,128)(2,1)S(1)} %shard_map.65.refs_0_), channel_id=1, source_target_pairs={{0,2},{2,4},{4,6},{6,8},{8,10},{10,12},{12,14},{14,0},{1,3},{3,5},... | collective-permute-start | bytes 405512 | tf_op jit(solution)/shard_map/ppermute | solution.py:41
  93.0 6.2 %collective-permute-start.15 = (bf16[528,128]{1,0:T(8,128)(2,1)S(1)}, bf16[528,128]{1,0:T(8,128)(2,1)S(1)}, u32[]{:S(2)}, u32[]{:S(2)}) collective-permute-start(bf16[528,128]{1,0:T(8,128)(2,1)S(1)} %shard_map.65.refs_0_), channel_id=1, source_target_pairs={{0,14},{2,0},{4,2},{6,4},{8,6},{10,8},{12,10},{14,12},{1,15},{3,1}... | collective-permute-start | bytes 405512 | tf_op jit(solution)/shard_map/ppermute | solution.py:41
  95.9 8.6 %collective-permute-start.18 = (bf16[528,128]{1,0:T(8,128)(2,1)S(1)}, bf16[528,128]{1,0:T(8,128)(2,1)S(1)}, u32[]{:S(2)}, u32[]{:S(2)}) collective-permute-start(bf16[528,128]{1,0:T(8,128)(2,1)S(1)} %shard_map.65.refs_0_), channel_id=1, source_target_pairs={{0,1},{1,0},{2,3},{3,2},{4,5},{5,4},{6,7},{7,6},{8,9},{9,8},{10,11... | collective-permute-start | bytes 405512 | tf_op jit(solution)/shard_map/ppermute | solution.py:41
  99.2 6.2 %collective-permute-start.16 = (bf16[528,128]{1,0:T(8,128)(2,1)S(1)}, bf16[528,128]{1,0:T(8,128)(2,1)S(1)}, u32[]{:S(2)}, u32[]{:S(2)}) collective-permute-start(bf16[528,128]{1,0:T(8,128)(2,1)S(1)} %collective-permute-done.14.refs_1_), channel_id=1, source_target_pairs={{0,2},{2,4},{4,6},{6,8},{8,10},{10,12},{12,14},{14,0},{1,3},{3,5},... | collective-permute-start | bytes 405512 | tf_op jit(solution)/shard_map/ppermute | solution.py:41
  99.2 6.2 %collective-permute-start.17 = (bf16[528,128]{1,0:T(8,128)(2,1)S(1)}, bf16[528,128]{1,0:T(8,128)(2,1)S(1)}, u32[]{:S(2)}, u32[]{:S(2)}) collective-permute-start(bf16[528,128]{1,0:T(8,128)(2,1)S(1)} %collective-permute-done.15.refs_2_), channel_id=1, source_target_pairs={{0,14},{2,0},{4,2},{6,4},{8,6},{10,8},{12,10},{14,12},{1,15},{3,1}... | collective-permute-start | bytes 405512 | tf_op jit(solution)/shard_map/ppermute | solution.py:41
  102.5 6.4 %collective-permute-start.21 = (bf16[528,128]{1,0:T(8,128)(2,1)S(1)}, bf16[528,128]{1,0:T(8,128)(2,1)S(1)}, u32[]{:S(2)}, u32[]{:S(2)}) collective-permute-start(bf16[528,128]{1,0:T(8,128)(2,1)S(1)} %collective-permute-done.14.refs_1_), channel_id=1, source_target_pairs={{0,1},{1,0},{2,3},{3,2},{4,5},{5,4},{6,7},{7,6},{8,9},{9,8},{10,11... | collective-permute-start | bytes 405512 | tf_op jit(solution)/shard_map/ppermute | solution.py:41
  103.8 7.7 %collective-permute-start.22 = (bf16[528,128]{1,0:T(8,128)(2,1)S(1)}, bf16[528,128]{1,0:T(8,128)(2,1)S(1)}, u32[]{:S(2)}, u32[]{:S(2)}) collective-permute-start(bf16[528,128]{1,0:T(8,128)(2,1)S(1)} %collective-permute-done.15.refs_2_), channel_id=1, source_target_pairs={{0,1},{1,0},{2,3},{3,2},{4,5},{5,4},{6,7},{7,6},{8,9},{9,8},{10,11... | collective-permute-start | bytes 405512 | tf_op jit(solution)/shard_map/ppermute | solution.py:41
  105.5 6.3 %collective-permute-start.19 = (bf16[528,128]{1,0:T(8,128)(2,1)S(1)}, bf16[528,128]{1,0:T(8,128)(2,1)S(1)}, u32[]{:S(2)}, u32[]{:S(2)}) collective-permute-start(bf16[528,128]{1,0:T(8,128)(2,1)S(1)} %get-tuple-element.45), channel_id=1, source_target_pairs={{0,2},{2,4},{4,6},{6,8},{8,10},{10,12},{12,14},{14,0},{1,3},{3,5},... | collective-permute-start | bytes 405512 | tf_op jit(solution)/shard_map/ppermute | solution.py:41
  105.6 9.8 %collective-permute-start.20 = (bf16[528,128]{1,0:T(8,128)(2,1)S(1)}, bf16[528,128]{1,0:T(8,128)(2,1)S(1)}, u32[]{:S(2)}, u32[]{:S(2)}) collective-permute-start(bf16[528,128]{1,0:T(8,128)(2,1)S(1)} %get-tuple-element.44), channel_id=1, source_target_pairs={{0,14},{2,0},{4,2},{6,4},{8,6},{10,8},{12,10},{14,12},{1,15},{3,1}... | collective-permute-start | bytes 405512 | tf_op jit(solution)/shard_map/ppermute | solution.py:41
  111.8 6.3 %collective-permute-start.23 = (bf16[528,128]{1,0:T(8,128)(2,1)S(1)}, bf16[528,128]{1,0:T(8,128)(2,1)S(1)}, u32[]{:S(2)}, u32[]{:S(2)}) collective-permute-start(bf16[528,128]{1,0:T(8,128)(2,1)S(1)} %minimum_add_fusion), channel_id=1, source_target_pairs={{0,2},{2,4},{4,6},{6,8},{8,10},{10,12},{12,14},{14,0},{1,3},{3,5},... | collective-permute-start | bytes 405512 | tf_op jit(solution)/shard_map/ppermute | solution.py:41
  111.9 8.3 %collective-permute-start.24 = (bf16[528,128]{1,0:T(8,128)(2,1)S(1)}, bf16[528,128]{1,0:T(8,128)(2,1)S(1)}, u32[]{:S(2)}, u32[]{:S(2)}) collective-permute-start(bf16[528,128]{1,0:T(8,128)(2,1)S(1)} %collective-permute-done.16.refs_3_), channel_id=1, source_target_pairs={{0,1},{1,0},{2,3},{3,2},{4,5},{5,4},{6,7},{7,6},{8,9},{9,8},{10,11... | collective-permute-start | bytes 405512 | tf_op jit(solution)/shard_map/ppermute | solution.py:41
  113.3 6.9 %collective-permute-start.25 = (bf16[528,128]{1,0:T(8,128)(2,1)S(1)}, bf16[528,128]{1,0:T(8,128)(2,1)S(1)}, u32[]{:S(2)}, u32[]{:S(2)}) collective-permute-start(bf16[528,128]{1,0:T(8,128)(2,1)S(1)} %collective-permute-done.17.refs_4_), channel_id=1, source_target_pairs={{0,1},{1,0},{2,3},{3,2},{4,5},{5,4},{6,7},{7,6},{8,9},{9,8},{10,11... | collective-permute-start | bytes 405512 | tf_op jit(solution)/shard_map/ppermute | solution.py:41
  114.0 6.5 %collective-permute-start.26 = (bf16[528,128]{1,0:T(8,128)(2,1)S(1)}, bf16[528,128]{1,0:T(8,128)(2,1)S(1)}, u32[]{:S(2)}, u32[]{:S(2)}) collective-permute-start(bf16[528,128]{1,0:T(8,128)(2,1)S(1)} %collective-permute-done.19.refs_5_), channel_id=1, source_target_pairs={{0,1},{1,0},{2,3},{3,2},{4,5},{5,4},{6,7},{7,6},{8,9},{9,8},{10,11... | collective-permute-start | bytes 405512 | tf_op jit(solution)/shard_map/ppermute | solution.py:41
  115.4 6.6 %collective-permute-start.27 = (bf16[528,128]{1,0:T(8,128)(2,1)S(1)}, bf16[528,128]{1,0:T(8,128)(2,1)S(1)}, u32[]{:S(2)}, u32[]{:S(2)}) collective-permute-start(bf16[528,128]{1,0:T(8,128)(2,1)S(1)} %collective-permute-done.20.refs_6_), channel_id=1, source_target_pairs={{0,1},{1,0},{2,3},{3,2},{4,5},{5,4},{6,7},{7,6},{8,9},{9,8},{10,11... | collective-permute-start | bytes 405512 | tf_op jit(solution)/shard_map/ppermute | solution.py:41
  118.1 5.3 %collective-permute-start.28 = (bf16[528,128]{1,0:T(8,128)(2,1)S(1)}, bf16[528,128]{1,0:T(8,128)(2,1)S(1)}, u32[]{:S(2)}, u32[]{:S(2)}) collective-permute-start(bf16[528,128]{1,0:T(8,128)(2,1)S(1)} %collective-permute-done.23.refs_7_), channel_id=1, source_target_pairs={{0,1},{1,0},{2,3},{3,2},{4,5},{5,4},{6,7},{7,6},{8,9},{9,8},{10,11... | collective-permute-start | bytes 405512 | tf_op jit(solution)/shard_map/ppermute | solution.py:41
  (9 other events, 46.1 us)

commit v12 on v11

--- a/solution.py
+++ b/solution.py
@@ -170,7 +170,8 @@
 
 
 def update(at, act_factor, grad_factor, mine, other, own_change, squares, *refs):
-    chunks, outs = refs[:Z], refs[Z:]
+    chunks, outs = refs[:-2], refs[-2:]
+    chunks = [*chunks[:3], chunks[3].at[0], chunks[3].at[1], *chunks[4:]]
     for f, (factor, out) in enumerate(((act_factor, outs[0]), (grad_factor, outs[1]))):
         total = squares[1 - f : 2 - f] + share_sum(chunks, 1 - f)
         scale = total[:, :1] / (TOKENS * D) * (gram_scale / TOKENS)
@@ -235,7 +236,10 @@
             up, down = after(up, crossed[0]), after(down, crossed[0])
         up, down = shift(up, "z", Z, 1), shift(down, "z", Z, -1)
         held += [up, down]
-        crossed += [shift(up, "yl", YL), shift(down, "yl", YL)]
+        if step == 2:
+            crossed.append(shift(jnp.stack([up, down]), "yl", YL))
+        else:
+            crossed += [shift(up, "yl", YL), shift(down, "yl", YL)]
     up = shift(after(up, *crossed[1:3]), "z", Z, 1)
     held.append(up)
     crossed.append(shift(up, "yl", YL))

time: 126 us -> 126 us (level)
  waiting for transfers between devices: 34.7 us -> 36.6 us
  starting transfers between devices: 35.8 us -> 34.3 us
    ppermute x29 -> x28, waiting for transfers between devices: 34.7 us -> 36.6 us  [shift(): return lax.ppermute(a, axis, [(i, (i + by) % size) for i in range(size)])]
    ppermute x29 -> x28, starting transfers between devices: 35.8 us -> 34.3 us  [shift(): return lax.ppermute(a, axis, [(i, (i + by) % size) for i in range(size)])]
  transfers between devices with their start and end apart: 29 -> 28, of which waited for: 17 -> 16; matrix products, arithmetic and copies ran while one was open for 0% -> 0% of each run, Pallas kernels for 3% -> 3%
where the time goes in v12:
time: 126 us
  blocking collectives  42.2 us (33%)
  waiting for transfers between devices  36.6 us (29%)
  starting transfers between devices  34.3 us (27%)
  Pallas kernels  11.7 us (9%)
    ppermute x28, waiting for transfers between devices, shift(): return lax.ppermute(a, axis, [(i, (i + by) % size) for i in range(size)])  36.6 us
    ppermute x28, starting transfers between devices, shift(): return lax.ppermute(a, axis, [(i, (i + by) % size) for i in range(size)])  34.3 us
    all_to_all x1, blocking collectives, local(): parts = lax.all_to_all(total.reshape(chunks), ('x', 'yh'), 0, 0, tiled=True)  23 us
    all_to_all x1, blocking collectives, local(): lax.all_to_all(copies, ('x', 'yh'), 0, 0, tiled=True)  19.2 us
    pallas_call x9, Pallas kernels, kernel_call(): pl.pallas_call(body, out_shape=[jax.ShapeDtypeStruct(shape, dtype) for sh...  11.7 us
  transfers between devices with their start and end apart: 28, of which 16 were waited for; matrix products, arithmetic and copies ran while one was open for 0% of the time, Pallas kernels for 3%

profile of v12, /device:TPU:8, one launch (start us, length us, event | category | flops | bytes accessed | tf_op | source)
XLA Modules:
  0.0 126.1 jit_solution(933804555290068524)
XLA Ops:
  0.7 3.2 %shard_map.59 = bf16[512,1024]{1,0:T(8,128)(2,1)} custom-call(s32[1]{0:T(128)} %bitcast.5.which, bf16[1024,512]{1,0:T(8,128)(2,1)} %acts.3, bf16[1024,512]{1,0:T(8,128)(2,1)} %cots.3, bf16[512,512]{1,0:T(8,128)(2,1)} %act_factor.3, bf16[512,512]{1,0:T(8,128)(2,1)} %grad_factor.3), custom_call_target="tpu_custom_call" | custom-call | flops 536870912 | bytes 3145732 | tf_op jit(solution)/shard_map/pallas_call | solution.py:50
  4.0 2.9 %collective-permute-done.came = bf16[512,1024]{1,0:T(8,128)(2,1)S(1)} collective-permute-done((bf16[512,1024]{1,0:T(8,128)(2,1)}, bf16[512,1024]{1,0:T(8,128)(2,1)S(1)}, u32[]{:S(2)}, u32[]{:S(2)}) %collective-permute-start) | collective-permute-done | bytes 1048608 | tf_op jit(solution)/shard_map/ppermute | solution.py:41
  7.6 23.0 %all_to_all.10.parts = bf16[8,64,1024]{2,1,0:T(8,128)(2,1)S(1)} all-to-all(bf16[8,64,1024]{2,1,0:T(8,128)(2,1)S(1)} %bitcast.59), channel_id=1, replica_groups=mesh['x'=4,'yh'=2,'core'=2,'z'=8,'yl'=2] {'x','yh'}, dimensions={0} | all-to-all | bytes 2097152 | tf_op jit(solution)/shard_map/all_to_all | solution.py:206
  30.7 19.2 %all_to_all.11 = bf16[8,64,1024]{2,1,0:T(8,128)(2,1)S(1)} all-to-all(bf16[8,64,1024]{2,1,0:T(8,128)(2,1)S(1)} %shard_map.61), channel_id=1, replica_groups=mesh['x'=4,'yh'=2,'core'=2,'z'=8,'yl'=2] {'x','yh'}, dimensions={0} | all-to-all | bytes 2097152 | tf_op jit(solution)/shard_map/all_to_all | solution.py:208
  50.1 2.6 %collective-permute-done.1.other = bf16[512,1024]{1,0:T(8,128)(2,1)S(1)} collective-permute-done((bf16[512,1024]{1,0:T(8,128)(2,1)S(1)}, bf16[512,1024]{1,0:T(8,128)(2,1)S(1)}, u32[]{:S(2)}, u32[]{:S(2)}) %collective-permute-start.1) | collective-permute-done | bytes 1048608 | tf_op jit(solution)/shard_map/ppermute | solution.py:41
  54.0 1.4 %collective-permute-start.6 = (bf16[1,2,32,1024]{3,2,1,0:T(8,128)(2,1)S(1)}, bf16[1,2,32,1024]{3,2,1,0:T(8,128)(2,1)S(1)}, u32[]{:S(2)}, u32[]{:S(2)}) collective-permute-start(bf16[1,2,32,1024]{3,2,1,0:T(8,128)(2,1)S(1)} %get-tuple-element.29), channel_id=1, source_target_pairs={{0,1},{1,0},{2,3},{3,2},{4,5},{5,4},{6,7},{7,6},{8,9},{9,8},{10,11... | collective-permute-start | bytes 393224 | tf_op jit(solution)/shard_map/ppermute | solution.py:41
  56.1 1.8 %shard_map.62 = (f32[2,32,1024]{2,1,0:T(8,128)S(1)}, f32[2,32,1024]{2,1,0:T(8,128)S(1)}, f32[2,32,1024]{2,1,0:T(8,128)S(1)}, f32[2,32,1024]{2,1,0:T(8,128)S(1)},...) custom-call(s32[2]{0:T(128)S(1)} %pad_add_fusion.at, ...), custom_call_target="tpu_custom_call" | custom-call | flops 536870912 | bytes 3145736 | tf_op jit(solution)/shard_map/pallas_call | solution.py:50
  57.9 2.5 %collective-permute-done.6 = bf16[1,2,32,1024]{3,2,1,0:T(8,128)(2,1)S(1)} collective-permute-done((bf16[1,2,32,1024]{3,2,1,0:T(8,128)(2,1)S(1)}, bf16[1,2,32,1024]{3,2,1,0:T(8,128)(2,1)S(1)}, u32[]{:S(2)}, u32[]{:S(2)}) %collective-permute-start.6) | collective-permute-done | bytes 131104 | tf_op jit(solution)/shard_map/ppermute | solution.py:41
  60.5 2.0 %collective-permute-start.7 = (bf16[2,32,1024]{2,1,0:T(8,128)(2,1)S(1)}, bf16[2,32,1024]{2,1,0:T(8,128)(2,1)S(1)}, u32[]{:S(2)}, u32[]{:S(2)}) collective-permute-start(bf16[2,32,1024]{2,1,0:T(8,128)(2,1)S(1)} %fusion.5), channel_id=1, source_target_pairs={{0,2},{2,4},{4,6},{6,8},{8,10},{10,12},{12,14},{14,0},{1,3},{3,5},... | collective-permute-start | bytes 393224 | tf_op jit(solution)/shard_map/ppermute | solution.py:41
  65.3 4.1 %collective-permute-done.7 = bf16[2,32,1024]{2,1,0:T(8,128)(2,1)S(1)} collective-permute-done((bf16[2,32,1024]{2,1,0:T(8,128)(2,1)S(1)}, bf16[2,32,1024]{2,1,0:T(8,128)(2,1)S(1)}, u32[]{:S(2)}, u32[]{:S(2)}) %collective-permute-start.7) | collective-permute-done | bytes 131104 | tf_op jit(solution)/shard_map/ppermute | solution.py:41
  69.4 2.6 %collective-permute-start.11 = (bf16[2,32,1024]{2,1,0:T(8,128)(2,1)S(1)}, bf16[2,32,1024]{2,1,0:T(8,128)(2,1)S(1)}, u32[]{:S(2)}, u32[]{:S(2)}) collective-permute-start(bf16[2,32,1024]{2,1,0:T(8,128)(2,1)S(1)} %get-tuple-element.42), channel_id=1, source_target_pairs={{0,14},{2,0},{4,2},{6,4},{8,6},{10,8},{12,10},{14,12},{1,15},{3,1}... | collective-permute-start | bytes 393224 | tf_op jit(solution)/shard_map/ppermute | solution.py:41
  74.6 3.7 %collective-permute-done.8 = bf16[2,32,1024]{2,1,0:T(8,128)(2,1)S(1)} collective-permute-done((bf16[2,32,1024]{2,1,0:T(8,128)(2,1)S(1)}, bf16[2,32,1024]{2,1,0:T(8,128)(2,1)S(1)}, u32[]{:S(2)}, u32[]{:S(2)}) %collective-permute-start.8) | collective-permute-done | bytes 131104 | tf_op jit(solution)/shard_map/ppermute | solution.py:41
  78.4 2.0 %collective-permute-start.9 = (bf16[2,32,1024]{2,1,0:T(8,128)(2,1)S(1)}, bf16[2,32,1024]{2,1,0:T(8,128)(2,1)S(1)}, u32[]{:S(2)}, u32[]{:S(2)}) collective-permute-start(bf16[2,32,1024]{2,1,0:T(8,128)(2,1)S(1)} %get-tuple-element.41), channel_id=1, source_target_pairs={{0,2},{2,4},{4,6},{6,8},{8,10},{10,12},{12,14},{14,0},{1,3},{3,5},... | collective-permute-start | bytes 393224 | tf_op jit(solution)/shard_map/ppermute | solution.py:41
  81.8 1.6 %collective-permute-done.12 = bf16[2,32,1024]{2,1,0:T(8,128)(2,1)S(1)} collective-permute-done((bf16[2,32,1024]{2,1,0:T(8,128)(2,1)S(1)}, bf16[2,32,1024]{2,1,0:T(8,128)(2,1)S(1)}, u32[]{:S(2)}, u32[]{:S(2)}) %collective-permute-start.12) | collective-permute-done | bytes 131104 | tf_op jit(solution)/shard_map/ppermute | solution.py:41
  84.8 2.1 %collective-permute-start.10 = (bf16[2,32,1024]{2,1,0:T(8,128)(2,1)S(1)}, bf16[2,32,1024]{2,1,0:T(8,128)(2,1)S(1)}, u32[]{:S(2)}, u32[]{:S(2)}) collective-permute-start(bf16[2,32,1024]{2,1,0:T(8,128)(2,1)S(1)} %get-tuple-element.39), channel_id=1, source_target_pairs={{0,2},{2,4},{4,6},{6,8},{8,10},{10,12},{12,14},{14,0},{1,3},{3,5},... | collective-permute-start | bytes 393224 | tf_op jit(solution)/shard_map/ppermute | solution.py:41
  86.8 1.4 %collective-permute-start.13 = (bf16[2,32,1024]{2,1,0:T(8,128)(2,1)S(1)}, bf16[2,32,1024]{2,1,0:T(8,128)(2,1)S(1)}, u32[]{:S(2)}, u32[]{:S(2)}) collective-permute-start(bf16[2,32,1024]{2,1,0:T(8,128)(2,1)S(1)} %get-tuple-element.38), channel_id=1, source_target_pairs={{0,14},{2,0},{4,2},{6,4},{8,6},{10,8},{12,10},{14,12},{1,15},{3,1}... | collective-permute-start | bytes 393224 | tf_op jit(solution)/shard_map/ppermute | solution.py:41
  88.3 3.8 %collective-permute-done.10.up = bf16[2,32,1024]{2,1,0:T(8,128)(2,1)S(1)} collective-permute-done((bf16[2,32,1024]{2,1,0:T(8,128)(2,1)S(1)}, bf16[2,32,1024]{2,1,0:T(8,128)(2,1)S(1)}, u32[]{:S(2)}, u32[]{:S(2)}) %collective-permute-start.10) | collective-permute-done | bytes 131104 | tf_op jit(solution)/shard_map/ppermute | solution.py:41
  93.0 2.9 %collective-permute-start.15 = (bf16[528,128]{1,0:T(8,128)(2,1)S(1)}, bf16[528,128]{1,0:T(8,128)(2,1)S(1)}, u32[]{:S(2)}, u32[]{:S(2)}) collective-permute-start(bf16[528,128]{1,0:T(8,128)(2,1)S(1)} %shard_map.65.refs_0_), channel_id=1, source_target_pairs={{0,14},{2,0},{4,2},{6,4},{8,6},{10,8},{12,10},{14,12},{1,15},{3,1}... | collective-permute-start | bytes 405512 | tf_op jit(solution)/shard_map/ppermute | solution.py:41
  97.2 1.9 %collective-permute-done.14.refs_1_ = bf16[528,128]{1,0:T(8,128)(2,1)S(1)} collective-permute-done((bf16[528,128]{1,0:T(8,128)(2,1)S(1)}, bf16[528,128]{1,0:T(8,128)(2,1)S(1)}, u32[]{:S(2)}, u32[]{:S(2)}) %collective-permute-start.14) | collective-permute-done | bytes 135200 | tf_op jit(solution)/shard_map/ppermute | solution.py:41
  99.2 3.2 %collective-permute-start.17 = (bf16[528,128]{1,0:T(8,128)(2,1)S(1)}, bf16[528,128]{1,0:T(8,128)(2,1)S(1)}, u32[]{:S(2)}, u32[]{:S(2)}) collective-permute-start(bf16[528,128]{1,0:T(8,128)(2,1)S(1)} %collective-permute-done.15.refs_2_), channel_id=1, source_target_pairs={{0,14},{2,0},{4,2},{6,4},{8,6},{10,8},{12,10},{14,12},{1,15},{3,1}... | collective-permute-start | bytes 405512 | tf_op jit(solution)/shard_map/ppermute | solution.py:41
  107.0 3.3 %collective-permute-start.20 = (bf16[528,128]{1,0:T(8,128)(2,1)S(1)}, bf16[528,128]{1,0:T(8,128)(2,1)S(1)}, u32[]{:S(2)}, u32[]{:S(2)}) collective-permute-start(bf16[528,128]{1,0:T(8,128)(2,1)S(1)} %get-tuple-element.44), channel_id=1, source_target_pairs={{0,14},{2,0},{4,2},{6,4},{8,6},{10,8},{12,10},{14,12},{1,15},{3,1}... | collective-permute-start | bytes 405512 | tf_op jit(solution)/shard_map/ppermute | solution.py:41
  114.8 4.1 %collective-permute-done.23.refs_7_ = bf16[528,128]{1,0:T(8,128)(2,1)S(1)} collective-permute-done((bf16[528,128]{1,0:T(8,128)(2,1)S(1)}, bf16[528,128]{1,0:T(8,128)(2,1)S(1)}, u32[]{:S(2)}, u32[]{:S(2)}) %collective-permute-start.23) | collective-permute-done | bytes 135200 | tf_op jit(solution)/shard_map/ppermute | solution.py:41
  120.3 3.6 %collective-permute-done.27.refs_6_ = bf16[528,128]{1,0:T(8,128)(2,1)S(1)} collective-permute-done((bf16[528,128]{1,0:T(8,128)(2,1)S(1)}, bf16[528,128]{1,0:T(8,128)(2,1)S(1)}, u32[]{:S(2)}, u32[]{:S(2)}) %collective-permute-start.27) | collective-permute-done | bytes 135200 | tf_op jit(solution)/shard_map/ppermute | solution.py:41
  123.9 2.3 %shard_map.67 = (bf16[8,2,32,512]{3,2,1,0:T(8,128)(2,1)}, bf16[8,2,32,512]{3,2,1,0:T(8,128)(2,1)}) custom-call(s32[2]{0:T(128)S(1)} %pad_add_fusion.at, bf16[8,2,32,512]{3,2,1,0:T(8,128)(2,1)S(1)} %bitcast.54, bf16[8,2,32,512]{3,2,1,0:T(8,128)(2,1)S(1)} %bitcast.58, bf16[512,1024]{1,0:T(8,128)(2,1)S(1)} %bitcast.50, ...), custom_call_target="tpu_custom_call" | custom-call | flops 536870912 | bytes 5276680 | tf_op jit(solution)/shard_map/pallas_call | solution.py:50
  (59 shorter events, 24.1 us)
Async XLA Ops:
  54.0 6.4 %collective-permute-start.6 = (bf16[1,2,32,1024]{3,2,1,0:T(8,128)(2,1)S(1)}, bf16[1,2,32,1024]{3,2,1,0:T(8,128)(2,1)S(1)}, u32[]{:S(2)}, u32[]{:S(2)}) collective-permute-start(bf16[1,2,32,1024]{3,2,1,0:T(8,128)(2,1)S(1)} %get-tuple-element.29), channel_id=1, source_target_pairs={{0,1},{1,0},{2,3},{3,2},{4,5},{5,4},{6,7},{7,6},{8,9},{9,8},{10,11... | collective-permute-start | bytes 393224 | tf_op jit(solution)/shard_map/ppermute | solution.py:41
  55.4 13.9 %collective-permute-start.5 = (bf16[2,2,32,1024]{3,2,1,0:T(8,128)(2,1)S(1)}, bf16[2,2,32,1024]{3,2,1,0:T(8,128)(2,1)S(1)}, u32[]{:S(2)}, u32[]{:S(2)}) collective-permute-start(bf16[2,2,32,1024]{3,2,1,0:T(8,128)(2,1)S(1)} %get-tuple-element.27), channel_id=1, source_target_pairs={{0,1},{1,0},{2,3},{3,2},{4,5},{5,4},{6,7},{7,6},{8,9},{9,8},{10,11... | collective-permute-start | bytes 786440 | tf_op jit(solution)/shard_map/ppermute | solution.py:41
  60.5 8.9 %collective-permute-start.7 = (bf16[2,32,1024]{2,1,0:T(8,128)(2,1)S(1)}, bf16[2,32,1024]{2,1,0:T(8,128)(2,1)S(1)}, u32[]{:S(2)}, u32[]{:S(2)}) collective-permute-start(bf16[2,32,1024]{2,1,0:T(8,128)(2,1)S(1)} %fusion.5), channel_id=1, source_target_pairs={{0,2},{2,4},{4,6},{6,8},{8,10},{10,12},{12,14},{14,0},{1,3},{3,5},... | collective-permute-start | bytes 393224 | tf_op jit(solution)/shard_map/ppermute | solution.py:41
  63.8 9.6 %collective-permute-start.4 = (bf16[2,2,32,1024]{3,2,1,0:T(8,128)(2,1)S(1)}, bf16[2,2,32,1024]{3,2,1,0:T(8,128)(2,1)S(1)}, u32[]{:S(2)}, u32[]{:S(2)}) collective-permute-start(bf16[2,2,32,1024]{3,2,1,0:T(8,128)(2,1)S(1)} %get-tuple-element.25), channel_id=1, source_target_pairs={{0,1},{1,0},{2,3},{3,2},{4,5},{5,4},{6,7},{7,6},{8,9},{9,8},{10,11... | collective-permute-start | bytes 786440 | tf_op jit(solution)/shard_map/ppermute | solution.py:41
  69.4 5.2 %collective-permute-start.11 = (bf16[2,32,1024]{2,1,0:T(8,128)(2,1)S(1)}, bf16[2,32,1024]{2,1,0:T(8,128)(2,1)S(1)}, u32[]{:S(2)}, u32[]{:S(2)}) collective-permute-start(bf16[2,32,1024]{2,1,0:T(8,128)(2,1)S(1)} %get-tuple-element.42), channel_id=1, source_target_pairs={{0,14},{2,0},{4,2},{6,4},{8,6},{10,8},{12,10},{14,12},{1,15},{3,1}... | collective-permute-start | bytes 393224 | tf_op jit(solution)/shard_map/ppermute | solution.py:41
  72.0 6.2 %collective-permute-start.8 = (bf16[2,32,1024]{2,1,0:T(8,128)(2,1)S(1)}, bf16[2,32,1024]{2,1,0:T(8,128)(2,1)S(1)}, u32[]{:S(2)}, u32[]{:S(2)}) collective-permute-start(bf16[2,32,1024]{2,1,0:T(8,128)(2,1)S(1)} %get-tuple-element.43), channel_id=1, source_target_pairs={{0,2},{2,4},{4,6},{6,8},{8,10},{10,12},{12,14},{14,0},{1,3},{3,5},... | collective-permute-start | bytes 393224 | tf_op jit(solution)/shard_map/ppermute | solution.py:41
  72.1 9.7 %collective-permute-start.3 = (bf16[2,2,32,1024]{3,2,1,0:T(8,128)(2,1)S(1)}, bf16[2,2,32,1024]{3,2,1,0:T(8,128)(2,1)S(1)}, u32[]{:S(2)}, u32[]{:S(2)}) collective-permute-start(bf16[2,2,32,1024]{3,2,1,0:T(8,128)(2,1)S(1)} %get-tuple-element.23), channel_id=1, source_target_pairs={{0,1},{1,0},{2,3},{3,2},{4,5},{5,4},{6,7},{7,6},{8,9},{9,8},{10,11... | collective-permute-start | bytes 786440 | tf_op jit(solution)/shard_map/ppermute | solution.py:41
  78.4 6.3 %collective-permute-start.9 = (bf16[2,32,1024]{2,1,0:T(8,128)(2,1)S(1)}, bf16[2,32,1024]{2,1,0:T(8,128)(2,1)S(1)}, u32[]{:S(2)}, u32[]{:S(2)}) collective-permute-start(bf16[2,32,1024]{2,1,0:T(8,128)(2,1)S(1)} %get-tuple-element.41), channel_id=1, source_target_pairs={{0,2},{2,4},{4,6},{6,8},{8,10},{10,12},{12,14},{14,0},{1,3},{3,5},... | collective-permute-start | bytes 393224 | tf_op jit(solution)/shard_map/ppermute | solution.py:41
  80.4 7.8 %collective-permute-start.2 = (bf16[1,2,32,1024]{3,2,1,0:T(8,128)(2,1)S(1)}, bf16[1,2,32,1024]{3,2,1,0:T(8,128)(2,1)S(1)}, u32[]{:S(2)}, u32[]{:S(2)}) collective-permute-start(bf16[1,2,32,1024]{3,2,1,0:T(8,128)(2,1)S(1)} %get-tuple-element.21), channel_id=1, source_target_pairs={{0,1},{1,0},{2,3},{3,2},{4,5},{5,4},{6,7},{7,6},{8,9},{9,8},{10,11... | collective-permute-start | bytes 393224 | tf_op jit(solution)/shard_map/ppermute | solution.py:41
  84.8 7.3 %collective-permute-start.10 = (bf16[2,32,1024]{2,1,0:T(8,128)(2,1)S(1)}, bf16[2,32,1024]{2,1,0:T(8,128)(2,1)S(1)}, u32[]{:S(2)}, u32[]{:S(2)}) collective-permute-start(bf16[2,32,1024]{2,1,0:T(8,128)(2,1)S(1)} %get-tuple-element.39), channel_id=1, source_target_pairs={{0,2},{2,4},{4,6},{6,8},{8,10},{10,12},{12,14},{14,0},{1,3},{3,5},... | collective-permute-start | bytes 393224 | tf_op jit(solution)/shard_map/ppermute | solution.py:41
  86.8 5.3 %collective-permute-start.13 = (bf16[2,32,1024]{2,1,0:T(8,128)(2,1)S(1)}, bf16[2,32,1024]{2,1,0:T(8,128)(2,1)S(1)}, u32[]{:S(2)}, u32[]{:S(2)}) collective-permute-start(bf16[2,32,1024]{2,1,0:T(8,128)(2,1)S(1)} %get-tuple-element.38), channel_id=1, source_target_pairs={{0,14},{2,0},{4,2},{6,4},{8,6},{10,8},{12,10},{14,12},{1,15},{3,1}... | collective-permute-start | bytes 393224 | tf_op jit(solution)/shard_map/ppermute | solution.py:41
  92.3 6.9 %collective-permute-start.14 = (bf16[528,128]{1,0:T(8,128)(2,1)S(1)}, bf16[528,128]{1,0:T(8,128)(2,1)S(1)}, u32[]{:S(2)}, u32[]{:S(2)}) collective-permute-start(bf16[528,128]{1,0:T(8,128)(2,1)S(1)} %shard_map.65.refs_0_), channel_id=1, source_target_pairs={{0,2},{2,4},{4,6},{6,8},{8,10},{10,12},{12,14},{14,0},{1,3},{3,5},... | collective-permute-start | bytes 405512 | tf_op jit(solution)/shard_map/ppermute | solution.py:41
  93.0 6.2 %collective-permute-start.15 = (bf16[528,128]{1,0:T(8,128)(2,1)S(1)}, bf16[528,128]{1,0:T(8,128)(2,1)S(1)}, u32[]{:S(2)}, u32[]{:S(2)}) collective-permute-start(bf16[528,128]{1,0:T(8,128)(2,1)S(1)} %shard_map.65.refs_0_), channel_id=1, source_target_pairs={{0,14},{2,0},{4,2},{6,4},{8,6},{10,8},{12,10},{14,12},{1,15},{3,1}... | collective-permute-start | bytes 405512 | tf_op jit(solution)/shard_map/ppermute | solution.py:41
  95.9 8.6 %collective-permute-start.18 = (bf16[528,128]{1,0:T(8,128)(2,1)S(1)}, bf16[528,128]{1,0:T(8,128)(2,1)S(1)}, u32[]{:S(2)}, u32[]{:S(2)}) collective-permute-start(bf16[528,128]{1,0:T(8,128)(2,1)S(1)} %shard_map.65.refs_0_), channel_id=1, source_target_pairs={{0,1},{1,0},{2,3},{3,2},{4,5},{5,4},{6,7},{7,6},{8,9},{9,8},{10,11... | collective-permute-start | bytes 405512 | tf_op jit(solution)/shard_map/ppermute | solution.py:41
  99.2 6.2 %collective-permute-start.16 = (bf16[528,128]{1,0:T(8,128)(2,1)S(1)}, bf16[528,128]{1,0:T(8,128)(2,1)S(1)}, u32[]{:S(2)}, u32[]{:S(2)}) collective-permute-start(bf16[528,128]{1,0:T(8,128)(2,1)S(1)} %collective-permute-done.14.refs_1_), channel_id=1, source_target_pairs={{0,2},{2,4},{4,6},{6,8},{8,10},{10,12},{12,14},{14,0},{1,3},{3,5},... | collective-permute-start | bytes 405512 | tf_op jit(solution)/shard_map/ppermute | solution.py:41
  99.2 6.5 %collective-permute-start.17 = (bf16[528,128]{1,0:T(8,128)(2,1)S(1)}, bf16[528,128]{1,0:T(8,128)(2,1)S(1)}, u32[]{:S(2)}, u32[]{:S(2)}) collective-permute-start(bf16[528,128]{1,0:T(8,128)(2,1)S(1)} %collective-permute-done.15.refs_2_), channel_id=1, source_target_pairs={{0,14},{2,0},{4,2},{6,4},{8,6},{10,8},{12,10},{14,12},{1,15},{3,1}... | collective-permute-start | bytes 405512 | tf_op jit(solution)/shard_map/ppermute | solution.py:41
  102.4 7.9 %collective-permute-start.21 = (bf16[528,128]{1,0:T(8,128)(2,1)S(1)}, bf16[528,128]{1,0:T(8,128)(2,1)S(1)}, u32[]{:S(2)}, u32[]{:S(2)}) collective-permute-start(bf16[528,128]{1,0:T(8,128)(2,1)S(1)} %collective-permute-done.14.refs_1_), channel_id=1, source_target_pairs={{0,1},{1,0},{2,3},{3,2},{4,5},{5,4},{6,7},{7,6},{8,9},{9,8},{10,11... | collective-permute-start | bytes 405512 | tf_op jit(solution)/shard_map/ppermute | solution.py:41
  103.8 7.6 %collective-permute-start.22 = (bf16[528,128]{1,0:T(8,128)(2,1)S(1)}, bf16[528,128]{1,0:T(8,128)(2,1)S(1)}, u32[]{:S(2)}, u32[]{:S(2)}) collective-permute-start(bf16[528,128]{1,0:T(8,128)(2,1)S(1)} %collective-permute-done.15.refs_2_), channel_id=1, source_target_pairs={{0,1},{1,0},{2,3},{3,2},{4,5},{5,4},{6,7},{7,6},{8,9},{9,8},{10,11... | collective-permute-start | bytes 405512 | tf_op jit(solution)/shard_map/ppermute | solution.py:41
  105.7 6.8 %collective-permute-start.19 = (bf16[528,128]{1,0:T(8,128)(2,1)S(1)}, bf16[528,128]{1,0:T(8,128)(2,1)S(1)}, u32[]{:S(2)}, u32[]{:S(2)}) collective-permute-start(bf16[528,128]{1,0:T(8,128)(2,1)S(1)} %get-tuple-element.45), channel_id=1, source_target_pairs={{0,2},{2,4},{4,6},{6,8},{8,10},{10,12},{12,14},{14,0},{1,3},{3,5},... | collective-permute-start | bytes 405512 | tf_op jit(solution)/shard_map/ppermute | solution.py:41
  106.0 14.3 %collective-permute-start.24 = (bf16[2,528,128]{2,1,0:T(8,128)(2,1)S(1)}, bf16[2,528,128]{2,1,0:T(8,128)(2,1)S(1)}, u32[]{:S(2)}, u32[]{:S(2)}) collective-permute-start(bf16[2,528,128]{2,1,0:T(8,128)(2,1)S(1)} %pad_maximum_fusion), channel_id=1, source_target_pairs={{0,1},{1,0},{2,3},{3,2},{4,5},{5,4},{6,7},{7,6},{8,9},{9,8},{10,11... | collective-permute-start | bytes 811016 | tf_op jit(solution)/shard_map/ppermute | solution.py:41
  107.0 6.4 %collective-permute-start.20 = (bf16[528,128]{1,0:T(8,128)(2,1)S(1)}, bf16[528,128]{1,0:T(8,128)(2,1)S(1)}, u32[]{:S(2)}, u32[]{:S(2)}) collective-permute-start(bf16[528,128]{1,0:T(8,128)(2,1)S(1)} %get-tuple-element.44), channel_id=1, source_target_pairs={{0,14},{2,0},{4,2},{6,4},{8,6},{10,8},{12,10},{14,12},{1,15},{3,1}... | collective-permute-start | bytes 405512 | tf_op jit(solution)/shard_map/ppermute | solution.py:41
  112.6 6.3 %collective-permute-start.23 = (bf16[528,128]{1,0:T(8,128)(2,1)S(1)}, bf16[528,128]{1,0:T(8,128)(2,1)S(1)}, u32[]{:S(2)}, u32[]{:S(2)}) collective-permute-start(bf16[528,128]{1,0:T(8,128)(2,1)S(1)} %minimum_add_fusion), channel_id=1, source_target_pairs={{0,2},{2,4},{4,6},{6,8},{8,10},{10,12},{12,14},{14,0},{1,3},{3,5},... | collective-permute-start | bytes 405512 | tf_op jit(solution)/shard_map/ppermute | solution.py:41
  112.6 7.6 %collective-permute-start.25 = (bf16[528,128]{1,0:T(8,128)(2,1)S(1)}, bf16[528,128]{1,0:T(8,128)(2,1)S(1)}, u32[]{:S(2)}, u32[]{:S(2)}) collective-permute-start(bf16[528,128]{1,0:T(8,128)(2,1)S(1)} %collective-permute-done.19.refs_5_), channel_id=1, source_target_pairs={{0,1},{1,0},{2,3},{3,2},{4,5},{5,4},{6,7},{7,6},{8,9},{9,8},{10,11... | collective-permute-start | bytes 405512 | tf_op jit(solution)/shard_map/ppermute | solution.py:41
  113.4 6.9 %collective-permute-start.26 = (bf16[528,128]{1,0:T(8,128)(2,1)S(1)}, bf16[528,128]{1,0:T(8,128)(2,1)S(1)}, u32[]{:S(2)}, u32[]{:S(2)}) collective-permute-start(bf16[528,128]{1,0:T(8,128)(2,1)S(1)} %collective-permute-done.20.refs_6_), channel_id=1, source_target_pairs={{0,1},{1,0},{2,3},{3,2},{4,5},{5,4},{6,7},{7,6},{8,9},{9,8},{10,11... | collective-permute-start | bytes 405512 | tf_op jit(solution)/shard_map/ppermute | solution.py:41
  (8 other events, 40.6 us)

commit v13 on v12

--- a/solution.py
+++ b/solution.py
@@ -171,7 +171,7 @@
 
 def update(at, act_factor, grad_factor, mine, other, own_change, squares, *refs):
     chunks, outs = refs[:-2], refs[-2:]
-    chunks = [*chunks[:3], chunks[3].at[0], chunks[3].at[1], *chunks[4:]]
+    chunks = [chunks[0], *(pair.at[k] for pair in chunks[1:3] for k in range(2)), *chunks[3:]]
     for f, (factor, out) in enumerate(((act_factor, outs[0]), (grad_factor, outs[1]))):
         total = squares[1 - f : 2 - f] + share_sum(chunks, 1 - f)
         scale = total[:, :1] / (TOKENS * D) * (gram_scale / TOKENS)
@@ -236,11 +236,11 @@
             up, down = after(up, crossed[0]), after(down, crossed[0])
         up, down = shift(up, "z", Z, 1), shift(down, "z", Z, -1)
         held += [up, down]
-        if step == 2:
+        if step < 3:
             crossed.append(shift(jnp.stack([up, down]), "yl", YL))
         else:
             crossed += [shift(up, "yl", YL), shift(down, "yl", YL)]
-    up = shift(after(up, *crossed[1:3]), "z", Z, 1)
+    up = shift(after(up, crossed[1][0]), "z", Z, 1)
     held.append(up)
     crossed.append(shift(up, "yl", YL))
     changed, squares = kernel_call(

time: 126 us -> 126 us (level)
    ppermute x28 -> x27, starting transfers between devices: 34.3 us -> 33.6 us  [shift(): return lax.ppermute(a, axis, [(i, (i + by) % size) for i in range(size)])]
    ppermute x28 -> x27, waiting for transfers between devices: 36.6 us -> 37.2 us  [shift(): return lax.ppermute(a, axis, [(i, (i + by) % size) for i in range(size)])]
  transfers between devices with their start and end apart: 28 -> 27, of which waited for: 16 -> 15; matrix products, arithmetic and copies ran while one was open for 0% -> 0% of each run, Pallas kernels for 3% -> 3%
where the time goes in v13:
time: 126 us
  blocking collectives  42.2 us (33%)
  waiting for transfers between devices  37.2 us (30%)
  starting transfers between devices  33.6 us (27%)
  Pallas kernels  11.7 us (9%)
    ppermute x27, waiting for transfers between devices, shift(): return lax.ppermute(a, axis, [(i, (i + by) % size) for i in range(size)])  37.2 us
    ppermute x27, starting transfers between devices, shift(): return lax.ppermute(a, axis, [(i, (i + by) % size) for i in range(size)])  33.6 us
    all_to_all x1, blocking collectives, local(): parts = lax.all_to_all(total.reshape(chunks), ('x', 'yh'), 0, 0, tiled=True)  23 us
    all_to_all x1, blocking collectives, local(): lax.all_to_all(copies, ('x', 'yh'), 0, 0, tiled=True)  19.2 us
    pallas_call x9, Pallas kernels, kernel_call(): pl.pallas_call(body, out_shape=[jax.ShapeDtypeStruct(shape, dtype) for sh...  11.7 us
  transfers between devices with their start and end apart: 27, of which 15 were waited for; matrix products, arithmetic and copies ran while one was open for 0% of the time, Pallas kernels for 3%

profile of v13, /device:TPU:8, one launch (start us, length us, event | category | flops | bytes accessed | tf_op | source)
XLA Modules:
  0.0 126.1 jit_solution(9407726122782271388)
XLA Ops:
  0.7 3.2 %shard_map.59 = bf16[512,1024]{1,0:T(8,128)(2,1)} custom-call(s32[1]{0:T(128)} %bitcast.5.which, bf16[1024,512]{1,0:T(8,128)(2,1)} %acts.3, bf16[1024,512]{1,0:T(8,128)(2,1)} %cots.3, bf16[512,512]{1,0:T(8,128)(2,1)} %act_factor.3, bf16[512,512]{1,0:T(8,128)(2,1)} %grad_factor.3), custom_call_target="tpu_custom_call" | custom-call | flops 536870912 | bytes 3145732 | tf_op jit(solution)/shard_map/pallas_call | solution.py:50
  4.0 2.9 %collective-permute-done.came = bf16[512,1024]{1,0:T(8,128)(2,1)S(1)} collective-permute-done((bf16[512,1024]{1,0:T(8,128)(2,1)}, bf16[512,1024]{1,0:T(8,128)(2,1)S(1)}, u32[]{:S(2)}, u32[]{:S(2)}) %collective-permute-start) | collective-permute-done | bytes 1048608 | tf_op jit(solution)/shard_map/ppermute | solution.py:41
  7.6 23.0 %all_to_all.10.parts = bf16[8,64,1024]{2,1,0:T(8,128)(2,1)S(1)} all-to-all(bf16[8,64,1024]{2,1,0:T(8,128)(2,1)S(1)} %bitcast.65), channel_id=1, replica_groups=mesh['x'=4,'yh'=2,'core'=2,'z'=8,'yl'=2] {'x','yh'}, dimensions={0} | all-to-all | bytes 2097152 | tf_op jit(solution)/shard_map/all_to_all | solution.py:206
  30.8 19.2 %all_to_all.11 = bf16[8,64,1024]{2,1,0:T(8,128)(2,1)S(1)} all-to-all(bf16[8,64,1024]{2,1,0:T(8,128)(2,1)S(1)} %shard_map.61), channel_id=1, replica_groups=mesh['x'=4,'yh'=2,'core'=2,'z'=8,'yl'=2] {'x','yh'}, dimensions={0} | all-to-all | bytes 2097152 | tf_op jit(solution)/shard_map/all_to_all | solution.py:208
  50.1 2.6 %collective-permute-done.1.other = bf16[512,1024]{1,0:T(8,128)(2,1)S(1)} collective-permute-done((bf16[512,1024]{1,0:T(8,128)(2,1)S(1)}, bf16[512,1024]{1,0:T(8,128)(2,1)S(1)}, u32[]{:S(2)}, u32[]{:S(2)}) %collective-permute-start.1) | collective-permute-done | bytes 1048608 | tf_op jit(solution)/shard_map/ppermute | solution.py:41
  56.1 1.8 %shard_map.62 = (f32[2,32,1024]{2,1,0:T(8,128)S(1)}, f32[2,32,1024]{2,1,0:T(8,128)S(1)}, f32[2,32,1024]{2,1,0:T(8,128)S(1)}, f32[2,32,1024]{2,1,0:T(8,128)S(1)},...) custom-call(s32[2]{0:T(128)S(1)} %pad_add_fusion.at, ...), custom_call_target="tpu_custom_call" | custom-call | flops 536870912 | bytes 3145736 | tf_op jit(solution)/shard_map/pallas_call | solution.py:50
  57.9 2.6 %collective-permute-done.6 = bf16[1,2,32,1024]{3,2,1,0:T(8,128)(2,1)S(1)} collective-permute-done((bf16[1,2,32,1024]{3,2,1,0:T(8,128)(2,1)S(1)}, bf16[1,2,32,1024]{3,2,1,0:T(8,128)(2,1)S(1)}, u32[]{:S(2)}, u32[]{:S(2)}) %collective-permute-start.6) | collective-permute-done | bytes 131104 | tf_op jit(solution)/shard_map/ppermute | solution.py:41
  60.5 2.0 %collective-permute-start.7 = (bf16[2,32,1024]{2,1,0:T(8,128)(2,1)S(1)}, bf16[2,32,1024]{2,1,0:T(8,128)(2,1)S(1)}, u32[]{:S(2)}, u32[]{:S(2)}) collective-permute-start(bf16[2,32,1024]{2,1,0:T(8,128)(2,1)S(1)} %fusion.5), channel_id=1, source_target_pairs={{0,2},{2,4},{4,6},{6,8},{8,10},{10,12},{12,14},{14,0},{1,3},{3,5},... | collective-permute-start | bytes 393224 | tf_op jit(solution)/shard_map/ppermute | solution.py:41
  65.3 4.1 %collective-permute-done.7 = bf16[2,32,1024]{2,1,0:T(8,128)(2,1)S(1)} collective-permute-done((bf16[2,32,1024]{2,1,0:T(8,128)(2,1)S(1)}, bf16[2,32,1024]{2,1,0:T(8,128)(2,1)S(1)}, u32[]{:S(2)}, u32[]{:S(2)}) %collective-permute-start.7) | collective-permute-done | bytes 131104 | tf_op jit(solution)/shard_map/ppermute | solution.py:41
  69.4 2.6 %collective-permute-start.11 = (bf16[2,32,1024]{2,1,0:T(8,128)(2,1)S(1)}, bf16[2,32,1024]{2,1,0:T(8,128)(2,1)S(1)}, u32[]{:S(2)}, u32[]{:S(2)}) collective-permute-start(bf16[2,32,1024]{2,1,0:T(8,128)(2,1)S(1)} %get-tuple-element.42), channel_id=1, source_target_pairs={{0,14},{2,0},{4,2},{6,4},{8,6},{10,8},{12,10},{14,12},{1,15},{3,1}... | collective-permute-start | bytes 393224 | tf_op jit(solution)/shard_map/ppermute | solution.py:41
  74.6 3.7 %collective-permute-done.8 = bf16[2,32,1024]{2,1,0:T(8,128)(2,1)S(1)} collective-permute-done((bf16[2,32,1024]{2,1,0:T(8,128)(2,1)S(1)}, bf16[2,32,1024]{2,1,0:T(8,128)(2,1)S(1)}, u32[]{:S(2)}, u32[]{:S(2)}) %collective-permute-start.8) | collective-permute-done | bytes 131104 | tf_op jit(solution)/shard_map/ppermute | solution.py:41
  78.4 2.0 %collective-permute-start.9 = (bf16[2,32,1024]{2,1,0:T(8,128)(2,1)S(1)}, bf16[2,32,1024]{2,1,0:T(8,128)(2,1)S(1)}, u32[]{:S(2)}, u32[]{:S(2)}) collective-permute-start(bf16[2,32,1024]{2,1,0:T(8,128)(2,1)S(1)} %get-tuple-element.41), channel_id=1, source_target_pairs={{0,2},{2,4},{4,6},{6,8},{8,10},{10,12},{12,14},{14,0},{1,3},{3,5},... | collective-permute-start | bytes 393224 | tf_op jit(solution)/shard_map/ppermute | solution.py:41
  81.8 1.6 %collective-permute-done.12 = bf16[2,32,1024]{2,1,0:T(8,128)(2,1)S(1)} collective-permute-done((bf16[2,32,1024]{2,1,0:T(8,128)(2,1)S(1)}, bf16[2,32,1024]{2,1,0:T(8,128)(2,1)S(1)}, u32[]{:S(2)}, u32[]{:S(2)}) %collective-permute-start.12) | collective-permute-done | bytes 131104 | tf_op jit(solution)/shard_map/ppermute | solution.py:41
  84.8 2.1 %collective-permute-start.10 = (bf16[2,32,1024]{2,1,0:T(8,128)(2,1)S(1)}, bf16[2,32,1024]{2,1,0:T(8,128)(2,1)S(1)}, u32[]{:S(2)}, u32[]{:S(2)}) collective-permute-start(bf16[2,32,1024]{2,1,0:T(8,128)(2,1)S(1)} %get-tuple-element.39), channel_id=1, source_target_pairs={{0,2},{2,4},{4,6},{6,8},{8,10},{10,12},{12,14},{14,0},{1,3},{3,5},... | collective-permute-start | bytes 393224 | tf_op jit(solution)/shard_map/ppermute | solution.py:41
  88.3 3.9 %collective-permute-done.10.up = bf16[2,32,1024]{2,1,0:T(8,128)(2,1)S(1)} collective-permute-done((bf16[2,32,1024]{2,1,0:T(8,128)(2,1)S(1)}, bf16[2,32,1024]{2,1,0:T(8,128)(2,1)S(1)}, u32[]{:S(2)}, u32[]{:S(2)}) %collective-permute-start.10) | collective-permute-done | bytes 131104 | tf_op jit(solution)/shard_map/ppermute | solution.py:41
  93.0 2.9 %collective-permute-start.15 = (bf16[528,128]{1,0:T(8,128)(2,1)S(1)}, bf16[528,128]{1,0:T(8,128)(2,1)S(1)}, u32[]{:S(2)}, u32[]{:S(2)}) collective-permute-start(bf16[528,128]{1,0:T(8,128)(2,1)S(1)} %shard_map.65.refs_0_), channel_id=1, source_target_pairs={{0,14},{2,0},{4,2},{6,4},{8,6},{10,8},{12,10},{14,12},{1,15},{3,1}... | collective-permute-start | bytes 405512 | tf_op jit(solution)/shard_map/ppermute | solution.py:41
  97.3 1.9 %collective-permute-done.14.refs_1_ = bf16[528,128]{1,0:T(8,128)(2,1)S(1)} collective-permute-done((bf16[528,128]{1,0:T(8,128)(2,1)S(1)}, bf16[528,128]{1,0:T(8,128)(2,1)S(1)}, u32[]{:S(2)}, u32[]{:S(2)}) %collective-permute-start.14) | collective-permute-done | bytes 135200 | tf_op jit(solution)/shard_map/ppermute | solution.py:41
  99.2 3.2 %collective-permute-start.17 = (bf16[528,128]{1,0:T(8,128)(2,1)S(1)}, bf16[528,128]{1,0:T(8,128)(2,1)S(1)}, u32[]{:S(2)}, u32[]{:S(2)}) collective-permute-start(bf16[528,128]{1,0:T(8,128)(2,1)S(1)} %collective-permute-done.15.refs_2_), channel_id=1, source_target_pairs={{0,14},{2,0},{4,2},{6,4},{8,6},{10,8},{12,10},{14,12},{1,15},{3,1}... | collective-permute-start | bytes 405512 | tf_op jit(solution)/shard_map/ppermute | solution.py:41
  103.9 1.5 %collective-permute-done.16.refs_3_ = bf16[528,128]{1,0:T(8,128)(2,1)S(1)} collective-permute-done((bf16[528,128]{1,0:T(8,128)(2,1)S(1)}, bf16[528,128]{1,0:T(8,128)(2,1)S(1)}, u32[]{:S(2)}, u32[]{:S(2)}) %collective-permute-start.16) | collective-permute-done | bytes 135200 | tf_op jit(solution)/shard_map/ppermute | solution.py:41
  107.0 3.3 %collective-permute-start.20 = (bf16[528,128]{1,0:T(8,128)(2,1)S(1)}, bf16[528,128]{1,0:T(8,128)(2,1)S(1)}, u32[]{:S(2)}, u32[]{:S(2)}) collective-permute-start(bf16[528,128]{1,0:T(8,128)(2,1)S(1)} %get-tuple-element.44), channel_id=1, source_target_pairs={{0,14},{2,0},{4,2},{6,4},{8,6},{10,8},{12,10},{14,12},{1,15},{3,1}... | collective-permute-start | bytes 405512 | tf_op jit(solution)/shard_map/ppermute | solution.py:41
  110.3 2.2 %collective-permute-done.19.refs_5_ = bf16[528,128]{1,0:T(8,128)(2,1)S(1)} collective-permute-done((bf16[528,128]{1,0:T(8,128)(2,1)S(1)}, bf16[528,128]{1,0:T(8,128)(2,1)S(1)}, u32[]{:S(2)}, u32[]{:S(2)}) %collective-permute-start.19) | collective-permute-done | bytes 135200 | tf_op jit(solution)/shard_map/ppermute | solution.py:41
  114.7 4.1 %collective-permute-done.22.refs_7_ = bf16[528,128]{1,0:T(8,128)(2,1)S(1)} collective-permute-done((bf16[528,128]{1,0:T(8,128)(2,1)S(1)}, bf16[528,128]{1,0:T(8,128)(2,1)S(1)}, u32[]{:S(2)}, u32[]{:S(2)}) %collective-permute-start.22) | collective-permute-done | bytes 135200 | tf_op jit(solution)/shard_map/ppermute | solution.py:41
  120.3 3.6 %collective-permute-done.26.refs_5_ = bf16[528,128]{1,0:T(8,128)(2,1)S(1)} collective-permute-done((bf16[528,128]{1,0:T(8,128)(2,1)S(1)}, bf16[528,128]{1,0:T(8,128)(2,1)S(1)}, u32[]{:S(2)}, u32[]{:S(2)}) %collective-permute-start.26) | collective-permute-done | bytes 135200 | tf_op jit(solution)/shard_map/ppermute | solution.py:41
  123.8 2.3 %shard_map.67 = (bf16[8,2,32,512]{3,2,1,0:T(8,128)(2,1)}, bf16[8,2,32,512]{3,2,1,0:T(8,128)(2,1)}) custom-call(s32[2]{0:T(128)S(1)} %pad_add_fusion.at, bf16[8,2,32,512]{3,2,1,0:T(8,128)(2,1)S(1)} %bitcast.60, bf16[8,2,32,512]{3,2,1,0:T(8,128)(2,1)S(1)} %bitcast.64, bf16[512,1024]{1,0:T(8,128)(2,1)S(1)} %bitcast.56, ...), custom_call_target="tpu_custom_call" | custom-call | flops 536870912 | bytes 5276680 | tf_op jit(solution)/shard_map/pallas_call | solution.py:50
  (58 shorter events, 23.2 us)
Async XLA Ops:
  54.0 6.4 %collective-permute-start.6 = (bf16[1,2,32,1024]{3,2,1,0:T(8,128)(2,1)S(1)}, bf16[1,2,32,1024]{3,2,1,0:T(8,128)(2,1)S(1)}, u32[]{:S(2)}, u32[]{:S(2)}) collective-permute-start(bf16[1,2,32,1024]{3,2,1,0:T(8,128)(2,1)S(1)} %get-tuple-element.29), channel_id=1, source_target_pairs={{0,1},{1,0},{2,3},{3,2},{4,5},{5,4},{6,7},{7,6},{8,9},{9,8},{10,11... | collective-permute-start | bytes 393224 | tf_op jit(solution)/shard_map/ppermute | solution.py:41
  55.4 13.9 %collective-permute-start.5 = (bf16[2,2,32,1024]{3,2,1,0:T(8,128)(2,1)S(1)}, bf16[2,2,32,1024]{3,2,1,0:T(8,128)(2,1)S(1)}, u32[]{:S(2)}, u32[]{:S(2)}) collective-permute-start(bf16[2,2,32,1024]{3,2,1,0:T(8,128)(2,1)S(1)} %get-tuple-element.27), channel_id=1, source_target_pairs={{0,1},{1,0},{2,3},{3,2},{4,5},{5,4},{6,7},{7,6},{8,9},{9,8},{10,11... | collective-permute-start | bytes 786440 | tf_op jit(solution)/shard_map/ppermute | solution.py:41
  60.5 8.9 %collective-permute-start.7 = (bf16[2,32,1024]{2,1,0:T(8,128)(2,1)S(1)}, bf16[2,32,1024]{2,1,0:T(8,128)(2,1)S(1)}, u32[]{:S(2)}, u32[]{:S(2)}) collective-permute-start(bf16[2,32,1024]{2,1,0:T(8,128)(2,1)S(1)} %fusion.5), channel_id=1, source_target_pairs={{0,2},{2,4},{4,6},{6,8},{8,10},{10,12},{12,14},{14,0},{1,3},{3,5},... | collective-permute-start | bytes 393224 | tf_op jit(solution)/shard_map/ppermute | solution.py:41
  63.8 9.6 %collective-permute-start.4 = (bf16[2,2,32,1024]{3,2,1,0:T(8,128)(2,1)S(1)}, bf16[2,2,32,1024]{3,2,1,0:T(8,128)(2,1)S(1)}, u32[]{:S(2)}, u32[]{:S(2)}) collective-permute-start(bf16[2,2,32,1024]{3,2,1,0:T(8,128)(2,1)S(1)} %get-tuple-element.25), channel_id=1, source_target_pairs={{0,1},{1,0},{2,3},{3,2},{4,5},{5,4},{6,7},{7,6},{8,9},{9,8},{10,11... | collective-permute-start | bytes 786440 | tf_op jit(solution)/shard_map/ppermute | solution.py:41
  69.4 5.2 %collective-permute-start.11 = (bf16[2,32,1024]{2,1,0:T(8,128)(2,1)S(1)}, bf16[2,32,1024]{2,1,0:T(8,128)(2,1)S(1)}, u32[]{:S(2)}, u32[]{:S(2)}) collective-permute-start(bf16[2,32,1024]{2,1,0:T(8,128)(2,1)S(1)} %get-tuple-element.42), channel_id=1, source_target_pairs={{0,14},{2,0},{4,2},{6,4},{8,6},{10,8},{12,10},{14,12},{1,15},{3,1}... | collective-permute-start | bytes 393224 | tf_op jit(solution)/shard_map/ppermute | solution.py:41
  72.1 6.2 %collective-permute-start.8 = (bf16[2,32,1024]{2,1,0:T(8,128)(2,1)S(1)}, bf16[2,32,1024]{2,1,0:T(8,128)(2,1)S(1)}, u32[]{:S(2)}, u32[]{:S(2)}) collective-permute-start(bf16[2,32,1024]{2,1,0:T(8,128)(2,1)S(1)} %get-tuple-element.43), channel_id=1, source_target_pairs={{0,2},{2,4},{4,6},{6,8},{8,10},{10,12},{12,14},{14,0},{1,3},{3,5},... | collective-permute-start | bytes 393224 | tf_op jit(solution)/shard_map/ppermute | solution.py:41
  72.1 9.7 %collective-permute-start.3 = (bf16[2,2,32,1024]{3,2,1,0:T(8,128)(2,1)S(1)}, bf16[2,2,32,1024]{3,2,1,0:T(8,128)(2,1)S(1)}, u32[]{:S(2)}, u32[]{:S(2)}) collective-permute-start(bf16[2,2,32,1024]{3,2,1,0:T(8,128)(2,1)S(1)} %get-tuple-element.23), channel_id=1, source_target_pairs={{0,1},{1,0},{2,3},{3,2},{4,5},{5,4},{6,7},{7,6},{8,9},{9,8},{10,11... | collective-permute-start | bytes 786440 | tf_op jit(solution)/shard_map/ppermute | solution.py:41
  78.3 5.0 %collective-permute-start.12 = (bf16[2,32,1024]{2,1,0:T(8,128)(2,1)S(1)}, bf16[2,32,1024]{2,1,0:T(8,128)(2,1)S(1)}, u32[]{:S(2)}, u32[]{:S(2)}) collective-permute-start(bf16[2,32,1024]{2,1,0:T(8,128)(2,1)S(1)} %get-tuple-element.40), channel_id=1, source_target_pairs={{0,14},{2,0},{4,2},{6,4},{8,6},{10,8},{12,10},{14,12},{1,15},{3,1}... | collective-permute-start | bytes 393224 | tf_op jit(solution)/shard_map/ppermute | solution.py:41
  78.4 6.3 %collective-permute-start.9 = (bf16[2,32,1024]{2,1,0:T(8,128)(2,1)S(1)}, bf16[2,32,1024]{2,1,0:T(8,128)(2,1)S(1)}, u32[]{:S(2)}, u32[]{:S(2)}) collective-permute-start(bf16[2,32,1024]{2,1,0:T(8,128)(2,1)S(1)} %get-tuple-element.41), channel_id=1, source_target_pairs={{0,2},{2,4},{4,6},{6,8},{8,10},{10,12},{12,14},{14,0},{1,3},{3,5},... | collective-permute-start | bytes 393224 | tf_op jit(solution)/shard_map/ppermute | solution.py:41
  80.5 7.8 %collective-permute-start.2 = (bf16[1,2,32,1024]{3,2,1,0:T(8,128)(2,1)S(1)}, bf16[1,2,32,1024]{3,2,1,0:T(8,128)(2,1)S(1)}, u32[]{:S(2)}, u32[]{:S(2)}) collective-permute-start(bf16[1,2,32,1024]{3,2,1,0:T(8,128)(2,1)S(1)} %get-tuple-element.21), channel_id=1, source_target_pairs={{0,1},{1,0},{2,3},{3,2},{4,5},{5,4},{6,7},{7,6},{8,9},{9,8},{10,11... | collective-permute-start | bytes 393224 | tf_op jit(solution)/shard_map/ppermute | solution.py:41
  84.8 7.4 %collective-permute-start.10 = (bf16[2,32,1024]{2,1,0:T(8,128)(2,1)S(1)}, bf16[2,32,1024]{2,1,0:T(8,128)(2,1)S(1)}, u32[]{:S(2)}, u32[]{:S(2)}) collective-permute-start(bf16[2,32,1024]{2,1,0:T(8,128)(2,1)S(1)} %get-tuple-element.39), channel_id=1, source_target_pairs={{0,2},{2,4},{4,6},{6,8},{8,10},{10,12},{12,14},{14,0},{1,3},{3,5},... | collective-permute-start | bytes 393224 | tf_op jit(solution)/shard_map/ppermute | solution.py:41
  86.9 5.3 %collective-permute-start.13 = (bf16[2,32,1024]{2,1,0:T(8,128)(2,1)S(1)}, bf16[2,32,1024]{2,1,0:T(8,128)(2,1)S(1)}, u32[]{:S(2)}, u32[]{:S(2)}) collective-permute-start(bf16[2,32,1024]{2,1,0:T(8,128)(2,1)S(1)} %get-tuple-element.38), channel_id=1, source_target_pairs={{0,14},{2,0},{4,2},{6,4},{8,6},{10,8},{12,10},{14,12},{1,15},{3,1}... | collective-permute-start | bytes 393224 | tf_op jit(solution)/shard_map/ppermute | solution.py:41
  92.3 6.9 %collective-permute-start.14 = (bf16[528,128]{1,0:T(8,128)(2,1)S(1)}, bf16[528,128]{1,0:T(8,128)(2,1)S(1)}, u32[]{:S(2)}, u32[]{:S(2)}) collective-permute-start(bf16[528,128]{1,0:T(8,128)(2,1)S(1)} %shard_map.65.refs_0_), channel_id=1, source_target_pairs={{0,2},{2,4},{4,6},{6,8},{8,10},{10,12},{12,14},{14,0},{1,3},{3,5},... | collective-permute-start | bytes 405512 | tf_op jit(solution)/shard_map/ppermute | solution.py:41
  93.0 6.2 %collective-permute-start.15 = (bf16[528,128]{1,0:T(8,128)(2,1)S(1)}, bf16[528,128]{1,0:T(8,128)(2,1)S(1)}, u32[]{:S(2)}, u32[]{:S(2)}) collective-permute-start(bf16[528,128]{1,0:T(8,128)(2,1)S(1)} %shard_map.65.refs_0_), channel_id=1, source_target_pairs={{0,14},{2,0},{4,2},{6,4},{8,6},{10,8},{12,10},{14,12},{1,15},{3,1}... | collective-permute-start | bytes 405512 | tf_op jit(solution)/shard_map/ppermute | solution.py:41
  95.9 8.0 %collective-permute-start.18 = (bf16[528,128]{1,0:T(8,128)(2,1)S(1)}, bf16[528,128]{1,0:T(8,128)(2,1)S(1)}, u32[]{:S(2)}, u32[]{:S(2)}) collective-permute-start(bf16[528,128]{1,0:T(8,128)(2,1)S(1)} %shard_map.65.refs_0_), channel_id=1, source_target_pairs={{0,1},{1,0},{2,3},{3,2},{4,5},{5,4},{6,7},{7,6},{8,9},{9,8},{10,11... | collective-permute-start | bytes 405512 | tf_op jit(solution)/shard_map/ppermute | solution.py:41
  99.2 6.2 %collective-permute-start.16 = (bf16[528,128]{1,0:T(8,128)(2,1)S(1)}, bf16[528,128]{1,0:T(8,128)(2,1)S(1)}, u32[]{:S(2)}, u32[]{:S(2)}) collective-permute-start(bf16[528,128]{1,0:T(8,128)(2,1)S(1)} %collective-permute-done.14.refs_1_), channel_id=1, source_target_pairs={{0,2},{2,4},{4,6},{6,8},{8,10},{10,12},{12,14},{14,0},{1,3},{3,5},... | collective-permute-start | bytes 405512 | tf_op jit(solution)/shard_map/ppermute | solution.py:41
  99.2 6.5 %collective-permute-start.17 = (bf16[528,128]{1,0:T(8,128)(2,1)S(1)}, bf16[528,128]{1,0:T(8,128)(2,1)S(1)}, u32[]{:S(2)}, u32[]{:S(2)}) collective-permute-start(bf16[528,128]{1,0:T(8,128)(2,1)S(1)} %collective-permute-done.15.refs_2_), channel_id=1, source_target_pairs={{0,14},{2,0},{4,2},{6,4},{8,6},{10,8},{12,10},{14,12},{1,15},{3,1}... | collective-permute-start | bytes 405512 | tf_op jit(solution)/shard_map/ppermute | solution.py:41
  102.5 10.0 %collective-permute-start.21 = (bf16[2,528,128]{2,1,0:T(8,128)(2,1)S(1)}, bf16[2,528,128]{2,1,0:T(8,128)(2,1)S(1)}, u32[]{:S(2)}, u32[]{:S(2)}) collective-permute-start(bf16[2,528,128]{2,1,0:T(8,128)(2,1)S(1)} %pad_maximum_fusion), channel_id=1, source_target_pairs={{0,1},{1,0},{2,3},{3,2},{4,5},{5,4},{6,7},{7,6},{8,9},{9,8},{10,11... | collective-permute-start | bytes 811016 | tf_op jit(solution)/shard_map/ppermute | solution.py:41
  105.7 6.8 %collective-permute-start.19 = (bf16[528,128]{1,0:T(8,128)(2,1)S(1)}, bf16[528,128]{1,0:T(8,128)(2,1)S(1)}, u32[]{:S(2)}, u32[]{:S(2)}) collective-permute-start(bf16[528,128]{1,0:T(8,128)(2,1)S(1)} %get-tuple-element.45), channel_id=1, source_target_pairs={{0,2},{2,4},{4,6},{6,8},{8,10},{10,12},{12,14},{14,0},{1,3},{3,5},... | collective-permute-start | bytes 405512 | tf_op jit(solution)/shard_map/ppermute | solution.py:41
  105.9 14.3 %collective-permute-start.23 = (bf16[2,528,128]{2,1,0:T(8,128)(2,1)S(1)}, bf16[2,528,128]{2,1,0:T(8,128)(2,1)S(1)}, u32[]{:S(2)}, u32[]{:S(2)}) collective-permute-start(bf16[2,528,128]{2,1,0:T(8,128)(2,1)S(1)} %pad_maximum_fusion.1), channel_id=1, source_target_pairs={{0,1},{1,0},{2,3},{3,2},{4,5},{5,4},{6,7},{7,6},{8,9},{9,8},{10,11... | collective-permute-start | bytes 811016 | tf_op jit(solution)/shard_map/ppermute | solution.py:41
  107.0 6.4 %collective-permute-start.20 = (bf16[528,128]{1,0:T(8,128)(2,1)S(1)}, bf16[528,128]{1,0:T(8,128)(2,1)S(1)}, u32[]{:S(2)}, u32[]{:S(2)}) collective-permute-start(bf16[528,128]{1,0:T(8,128)(2,1)S(1)} %get-tuple-element.44), channel_id=1, source_target_pairs={{0,14},{2,0},{4,2},{6,4},{8,6},{10,8},{12,10},{14,12},{1,15},{3,1}... | collective-permute-start | bytes 405512 | tf_op jit(solution)/shard_map/ppermute | solution.py:41
  112.5 6.3 %collective-permute-start.22 = (bf16[528,128]{1,0:T(8,128)(2,1)S(1)}, bf16[528,128]{1,0:T(8,128)(2,1)S(1)}, u32[]{:S(2)}, u32[]{:S(2)}) collective-permute-start(bf16[528,128]{1,0:T(8,128)(2,1)S(1)} %fusion.14), channel_id=1, source_target_pairs={{0,2},{2,4},{4,6},{6,8},{8,10},{10,12},{12,14},{14,0},{1,3},{3,5},... | collective-permute-start | bytes 405512 | tf_op jit(solution)/shard_map/ppermute | solution.py:41
  112.6 7.6 %collective-permute-start.24 = (bf16[528,128]{1,0:T(8,128)(2,1)S(1)}, bf16[528,128]{1,0:T(8,128)(2,1)S(1)}, u32[]{:S(2)}, u32[]{:S(2)}) collective-permute-start(bf16[528,128]{1,0:T(8,128)(2,1)S(1)} %collective-permute-done.19.refs_5_), channel_id=1, source_target_pairs={{0,1},{1,0},{2,3},{3,2},{4,5},{5,4},{6,7},{7,6},{8,9},{9,8},{10,11... | collective-permute-start | bytes 405512 | tf_op jit(solution)/shard_map/ppermute | solution.py:41
  113.4 6.9 %collective-permute-start.25 = (bf16[528,128]{1,0:T(8,128)(2,1)S(1)}, bf16[528,128]{1,0:T(8,128)(2,1)S(1)}, u32[]{:S(2)}, u32[]{:S(2)}) collective-permute-start(bf16[528,128]{1,0:T(8,128)(2,1)S(1)} %collective-permute-done.20.refs_6_), channel_id=1, source_target_pairs={{0,1},{1,0},{2,3},{3,2},{4,5},{5,4},{6,7},{7,6},{8,9},{9,8},{10,11... | collective-permute-start | bytes 405512 | tf_op jit(solution)/shard_map/ppermute | solution.py:41
  (7 other events, 35.6 us)

commit v14 on v11

--- a/solution.py
+++ b/solution.py
@@ -41,7 +41,7 @@
     return lax.ppermute(a, axis, [(i, (i + by) % size) for i in range(size)])
 
 
-def kernel_call(body, outs, *args, index=None, flops=0, memory=pltpu.VMEM, scratch=(), room=48):
+def kernel_call(body, outs, *args, index=None, flops=0, memory=pltpu.VMEM, out_memory=pltpu.VMEM, scratch=(), room=48):
     specs = [pl.BlockSpec(memory_space=memory)] * len(args)
     if index is not None:
         specs = [pl.BlockSpec(memory_space=pltpu.SMEM)] + specs
@@ -51,7 +51,7 @@
         body,
         out_shape=[jax.ShapeDtypeStruct(shape, dtype) for shape, dtype in outs],
         in_specs=specs,
-        out_specs=[pl.BlockSpec(memory_space=pltpu.VMEM)] * len(outs),
+        out_specs=[pl.BlockSpec(memory_space=out_memory)] * len(outs),
         scratch_shapes=scratch,
         compiler_params=pltpu.CompilerParams(vmem_limit_bytes=room * 2**20),
         cost_estimate=pl.CostEstimate(flops=flops, bytes_accessed=size, transcendentals=0),
@@ -170,7 +170,8 @@
 
 
 def update(at, act_factor, grad_factor, mine, other, own_change, squares, *refs):
-    chunks, outs = refs[:Z], refs[Z:]
+    chunks, results, outs, sems = refs[:Z], refs[Z : Z + 2], refs[Z + 2 : Z + 4], refs[Z + 4]
+    copies = [pltpu.make_async_copy(outs[f], results[f], sems.at[f]) for f in range(2)]
     for f, (factor, out) in enumerate(((act_factor, outs[0]), (grad_factor, outs[1]))):
         total = squares[1 - f : 2 - f] + share_sum(chunks, 1 - f)
         scale = total[:, :1] / (TOKENS * D) * (gram_scale / TOKENS)
@@ -182,6 +183,9 @@
                 kept = factor[place].reshape(PART, WIDTH).astype(f32)
                 new = keep_scale * kept - scale * change[k * PART : (k + 1) * PART]
                 out[place] = new.astype(bf16).reshape(1, 1, PART, WIDTH)
+        copies[f].start()
+    for copy in copies:
+        copy.wait()
 
 
 def after(a, *others):
@@ -243,7 +247,8 @@
         own_changes, [((2, ROWS // YL, WIDTH), f32), ((2, LANES), f32)], mine, other, *held, flops=product
     )
     outs = kernel_call(
-        update, [((Z, YL, PART, WIDTH), bf16)] * 2, *factors, mine, other, changed, squares, *crossed, index=[z, yl], flops=product
+        update, [((Z, YL, PART, WIDTH), bf16)] * 2, *factors, mine, other, changed, squares, *crossed, index=[z, yl], flops=product,
+        out_memory=pltpu.HBM, scratch=[pltpu.VMEM((Z, YL, PART, WIDTH), bf16)] * 2 + [pltpu.SemaphoreType.DMA((2,))],
     )
     return tuple(out.reshape(ROWS, WIDTH) for out in outs)
 

time: 126 us -> 126 us (level)
  no operation moved by 1% of the time
where the time goes in v14:
time: 126 us
  blocking collectives  42.2 us (33%)
  starting transfers between devices  35.8 us (28%)
  waiting for transfers between devices  34.7 us (28%)
  Pallas kernels  11.7 us (9%)
    ppermute x29, starting transfers between devices, shift(): return lax.ppermute(a, axis, [(i, (i + by) % size) for i in range(size)])  35.8 us
    ppermute x29, waiting for transfers between devices, shift(): return lax.ppermute(a, axis, [(i, (i + by) % size) for i in range(size)])  34.7 us
    all_to_all x1, blocking collectives, local(): parts = lax.all_to_all(total.reshape(chunks), ('x', 'yh'), 0, 0, tiled=True)  23 us
    all_to_all x1, blocking collectives, local(): lax.all_to_all(copies, ('x', 'yh'), 0, 0, tiled=True)  19.2 us
    pallas_call x9, Pallas kernels, kernel_call(): pl.pallas_call(body, out_shape=[jax.ShapeDtypeStruct(shape, dtype) for sh...  11.7 us
  transfers between devices with their start and end apart: 29, of which 17 were waited for; matrix products, arithmetic and copies ran while one was open for 0% of the time, Pallas kernels for 3%

profile of v14, /device:TPU:8, one launch (start us, length us, event | category | flops | bytes accessed | tf_op | source)
XLA Modules:
  0.0 125.8 jit_solution(525773738986159082)
XLA Ops:
  0.7 3.3 %shard_map.59 = bf16[512,1024]{1,0:T(8,128)(2,1)} custom-call(s32[1]{0:T(128)} %bitcast.5.which, bf16[1024,512]{1,0:T(8,128)(2,1)} %acts.3, bf16[1024,512]{1,0:T(8,128)(2,1)} %cots.3, bf16[512,512]{1,0:T(8,128)(2,1)} %act_factor.3, bf16[512,512]{1,0:T(8,128)(2,1)} %grad_factor.3), custom_call_target="tpu_custom_call" | custom-call | flops 536870912 | bytes 3145732 | tf_op jit(solution)/shard_map/pallas_call | solution.py:50
  4.0 2.9 %collective-permute-done.came = bf16[512,1024]{1,0:T(8,128)(2,1)S(1)} collective-permute-done((bf16[512,1024]{1,0:T(8,128)(2,1)}, bf16[512,1024]{1,0:T(8,128)(2,1)S(1)}, u32[]{:S(2)}, u32[]{:S(2)}) %collective-permute-start) | collective-permute-done | bytes 1048608 | tf_op jit(solution)/shard_map/ppermute | solution.py:41
  7.6 23.0 %all_to_all.10.parts = bf16[8,64,1024]{2,1,0:T(8,128)(2,1)S(1)} all-to-all(bf16[8,64,1024]{2,1,0:T(8,128)(2,1)S(1)} %bitcast.57), channel_id=1, replica_groups=mesh['x'=4,'yh'=2,'core'=2,'z'=8,'yl'=2] {'x','yh'}, dimensions={0} | all-to-all | bytes 2097152 | tf_op jit(solution)/shard_map/all_to_all | solution.py:209
  30.8 19.2 %all_to_all.11 = bf16[8,64,1024]{2,1,0:T(8,128)(2,1)S(1)} all-to-all(bf16[8,64,1024]{2,1,0:T(8,128)(2,1)S(1)} %shard_map.61), channel_id=1, replica_groups=mesh['x'=4,'yh'=2,'core'=2,'z'=8,'yl'=2] {'x','yh'}, dimensions={0} | all-to-all | bytes 2097152 | tf_op jit(solution)/shard_map/all_to_all | solution.py:211
  50.1 2.6 %collective-permute-done.1.other = bf16[512,1024]{1,0:T(8,128)(2,1)S(1)} collective-permute-done((bf16[512,1024]{1,0:T(8,128)(2,1)S(1)}, bf16[512,1024]{1,0:T(8,128)(2,1)S(1)}, u32[]{:S(2)}, u32[]{:S(2)}) %collective-permute-start.1) | collective-permute-done | bytes 1048608 | tf_op jit(solution)/shard_map/ppermute | solution.py:41
  56.1 1.8 %shard_map.62 = (f32[2,32,1024]{2,1,0:T(8,128)S(1)}, f32[2,32,1024]{2,1,0:T(8,128)S(1)}, f32[2,32,1024]{2,1,0:T(8,128)S(1)}, f32[2,32,1024]{2,1,0:T(8,128)S(1)},...) custom-call(s32[2]{0:T(128)S(1)} %pad_add_fusion.at, ...), custom_call_target="tpu_custom_call" | custom-call | flops 536870912 | bytes 3145736 | tf_op jit(solution)/shard_map/pallas_call | solution.py:50
  57.9 2.6 %collective-permute-done.6 = bf16[1,2,32,1024]{3,2,1,0:T(8,128)(2,1)S(1)} collective-permute-done((bf16[1,2,32,1024]{3,2,1,0:T(8,128)(2,1)S(1)}, bf16[1,2,32,1024]{3,2,1,0:T(8,128)(2,1)S(1)}, u32[]{:S(2)}, u32[]{:S(2)}) %collective-permute-start.6) | collective-permute-done | bytes 131104 | tf_op jit(solution)/shard_map/ppermute | solution.py:41
  60.5 2.0 %collective-permute-start.7 = (bf16[2,32,1024]{2,1,0:T(8,128)(2,1)S(1)}, bf16[2,32,1024]{2,1,0:T(8,128)(2,1)S(1)}, u32[]{:S(2)}, u32[]{:S(2)}) collective-permute-start(bf16[2,32,1024]{2,1,0:T(8,128)(2,1)S(1)} %fusion.5), channel_id=1, source_target_pairs={{0,2},{2,4},{4,6},{6,8},{8,10},{10,12},{12,14},{14,0},{1,3},{3,5},... | collective-permute-start | bytes 393224 | tf_op jit(solution)/shard_map/ppermute | solution.py:41
  65.3 4.1 %collective-permute-done.7 = bf16[2,32,1024]{2,1,0:T(8,128)(2,1)S(1)} collective-permute-done((bf16[2,32,1024]{2,1,0:T(8,128)(2,1)S(1)}, bf16[2,32,1024]{2,1,0:T(8,128)(2,1)S(1)}, u32[]{:S(2)}, u32[]{:S(2)}) %collective-permute-start.7) | collective-permute-done | bytes 131104 | tf_op jit(solution)/shard_map/ppermute | solution.py:41
  69.4 2.6 %collective-permute-start.11 = (bf16[2,32,1024]{2,1,0:T(8,128)(2,1)S(1)}, bf16[2,32,1024]{2,1,0:T(8,128)(2,1)S(1)}, u32[]{:S(2)}, u32[]{:S(2)}) collective-permute-start(bf16[2,32,1024]{2,1,0:T(8,128)(2,1)S(1)} %get-tuple-element.42), channel_id=1, source_target_pairs={{0,14},{2,0},{4,2},{6,4},{8,6},{10,8},{12,10},{14,12},{1,15},{3,1}... | collective-permute-start | bytes 393224 | tf_op jit(solution)/shard_map/ppermute | solution.py:41
  74.6 3.7 %collective-permute-done.8 = bf16[2,32,1024]{2,1,0:T(8,128)(2,1)S(1)} collective-permute-done((bf16[2,32,1024]{2,1,0:T(8,128)(2,1)S(1)}, bf16[2,32,1024]{2,1,0:T(8,128)(2,1)S(1)}, u32[]{:S(2)}, u32[]{:S(2)}) %collective-permute-start.8) | collective-permute-done | bytes 131104 | tf_op jit(solution)/shard_map/ppermute | solution.py:41
  78.4 2.0 %collective-permute-start.9 = (bf16[2,32,1024]{2,1,0:T(8,128)(2,1)S(1)}, bf16[2,32,1024]{2,1,0:T(8,128)(2,1)S(1)}, u32[]{:S(2)}, u32[]{:S(2)}) collective-permute-start(bf16[2,32,1024]{2,1,0:T(8,128)(2,1)S(1)} %get-tuple-element.41), channel_id=1, source_target_pairs={{0,2},{2,4},{4,6},{6,8},{8,10},{10,12},{12,14},{14,0},{1,3},{3,5},... | collective-permute-start | bytes 393224 | tf_op jit(solution)/shard_map/ppermute | solution.py:41
  81.8 1.6 %collective-permute-done.12 = bf16[2,32,1024]{2,1,0:T(8,128)(2,1)S(1)} collective-permute-done((bf16[2,32,1024]{2,1,0:T(8,128)(2,1)S(1)}, bf16[2,32,1024]{2,1,0:T(8,128)(2,1)S(1)}, u32[]{:S(2)}, u32[]{:S(2)}) %collective-permute-start.12) | collective-permute-done | bytes 131104 | tf_op jit(solution)/shard_map/ppermute | solution.py:41
  84.8 2.1 %collective-permute-start.10 = (bf16[2,32,1024]{2,1,0:T(8,128)(2,1)S(1)}, bf16[2,32,1024]{2,1,0:T(8,128)(2,1)S(1)}, u32[]{:S(2)}, u32[]{:S(2)}) collective-permute-start(bf16[2,32,1024]{2,1,0:T(8,128)(2,1)S(1)} %get-tuple-element.39), channel_id=1, source_target_pairs={{0,2},{2,4},{4,6},{6,8},{8,10},{10,12},{12,14},{14,0},{1,3},{3,5},... | collective-permute-start | bytes 393224 | tf_op jit(solution)/shard_map/ppermute | solution.py:41
  88.3 3.9 %collective-permute-done.10.up = bf16[2,32,1024]{2,1,0:T(8,128)(2,1)S(1)} collective-permute-done((bf16[2,32,1024]{2,1,0:T(8,128)(2,1)S(1)}, bf16[2,32,1024]{2,1,0:T(8,128)(2,1)S(1)}, u32[]{:S(2)}, u32[]{:S(2)}) %collective-permute-start.10) | collective-permute-done | bytes 131104 | tf_op jit(solution)/shard_map/ppermute | solution.py:41
  93.0 2.9 %collective-permute-start.15 = (bf16[528,128]{1,0:T(8,128)(2,1)S(1)}, bf16[528,128]{1,0:T(8,128)(2,1)S(1)}, u32[]{:S(2)}, u32[]{:S(2)}) collective-permute-start(bf16[528,128]{1,0:T(8,128)(2,1)S(1)} %shard_map.65.refs_0_), channel_id=1, source_target_pairs={{0,14},{2,0},{4,2},{6,4},{8,6},{10,8},{12,10},{14,12},{1,15},{3,1}... | collective-permute-start | bytes 405512 | tf_op jit(solution)/shard_map/ppermute | solution.py:41
  97.3 1.9 %collective-permute-done.14.refs_1_ = bf16[528,128]{1,0:T(8,128)(2,1)S(1)} collective-permute-done((bf16[528,128]{1,0:T(8,128)(2,1)S(1)}, bf16[528,128]{1,0:T(8,128)(2,1)S(1)}, u32[]{:S(2)}, u32[]{:S(2)}) %collective-permute-start.14) | collective-permute-done | bytes 135200 | tf_op jit(solution)/shard_map/ppermute | solution.py:41
  99.2 3.2 %collective-permute-start.17 = (bf16[528,128]{1,0:T(8,128)(2,1)S(1)}, bf16[528,128]{1,0:T(8,128)(2,1)S(1)}, u32[]{:S(2)}, u32[]{:S(2)}) collective-permute-start(bf16[528,128]{1,0:T(8,128)(2,1)S(1)} %collective-permute-done.15.refs_2_), channel_id=1, source_target_pairs={{0,14},{2,0},{4,2},{6,4},{8,6},{10,8},{12,10},{14,12},{1,15},{3,1}... | collective-permute-start | bytes 405512 | tf_op jit(solution)/shard_map/ppermute | solution.py:41
  105.6 3.3 %collective-permute-start.20 = (bf16[528,128]{1,0:T(8,128)(2,1)S(1)}, bf16[528,128]{1,0:T(8,128)(2,1)S(1)}, u32[]{:S(2)}, u32[]{:S(2)}) collective-permute-start(bf16[528,128]{1,0:T(8,128)(2,1)S(1)} %get-tuple-element.44), channel_id=1, source_target_pairs={{0,14},{2,0},{4,2},{6,4},{8,6},{10,8},{12,10},{14,12},{1,15},{3,1}... | collective-permute-start | bytes 405512 | tf_op jit(solution)/shard_map/ppermute | solution.py:41
  108.9 2.6 %collective-permute-done.22.refs_2_ = bf16[528,128]{1,0:T(8,128)(2,1)S(1)} collective-permute-done((bf16[528,128]{1,0:T(8,128)(2,1)S(1)}, bf16[528,128]{1,0:T(8,128)(2,1)S(1)}, u32[]{:S(2)}, u32[]{:S(2)}) %collective-permute-start.22) | collective-permute-done | bytes 135200 | tf_op jit(solution)/shard_map/ppermute | solution.py:41
  116.1 2.1 %collective-permute-done.23.refs_7_ = bf16[528,128]{1,0:T(8,128)(2,1)S(1)} collective-permute-done((bf16[528,128]{1,0:T(8,128)(2,1)S(1)}, bf16[528,128]{1,0:T(8,128)(2,1)S(1)}, u32[]{:S(2)}, u32[]{:S(2)}) %collective-permute-start.23) | collective-permute-done | bytes 135200 | tf_op jit(solution)/shard_map/ppermute | solution.py:41
  120.5 1.4 %collective-permute-done.27.refs_6_ = bf16[528,128]{1,0:T(8,128)(2,1)S(1)} collective-permute-done((bf16[528,128]{1,0:T(8,128)(2,1)S(1)}, bf16[528,128]{1,0:T(8,128)(2,1)S(1)}, u32[]{:S(2)}, u32[]{:S(2)}) %collective-permute-start.27) | collective-permute-done | bytes 135200 | tf_op jit(solution)/shard_map/ppermute | solution.py:41
  122.0 1.4 %collective-permute-done.28.refs_7_ = bf16[528,128]{1,0:T(8,128)(2,1)S(1)} collective-permute-done((bf16[528,128]{1,0:T(8,128)(2,1)S(1)}, bf16[528,128]{1,0:T(8,128)(2,1)S(1)}, u32[]{:S(2)}, u32[]{:S(2)}) %collective-permute-start.28) | collective-permute-done | bytes 135200 | tf_op jit(solution)/shard_map/ppermute | solution.py:41
  123.4 2.3 %shard_map.67 = (bf16[8,2,32,512]{3,2,1,0:T(8,128)(2,1)}, bf16[8,2,32,512]{3,2,1,0:T(8,128)(2,1)}) custom-call(s32[2]{0:T(128)S(1)} %pad_add_fusion.at, bf16[8,2,32,512]{3,2,1,0:T(8,128)(2,1)S(1)} %bitcast.52, bf16[8,2,32,512]{3,2,1,0:T(8,128)(2,1)S(1)} %bitcast.56, bf16[512,1024]{1,0:T(8,128)(2,1)S(1)} %bitcast.48, ...), custom_call_target="tpu_custom_call" | custom-call | flops 536870912 | bytes 5276680 | tf_op jit(solution)/shard_map/pallas_call | solution.py:50
  (60 shorter events, 26.5 us)
Async XLA Ops:
  54.0 6.4 %collective-permute-start.6 = (bf16[1,2,32,1024]{3,2,1,0:T(8,128)(2,1)S(1)}, bf16[1,2,32,1024]{3,2,1,0:T(8,128)(2,1)S(1)}, u32[]{:S(2)}, u32[]{:S(2)}) collective-permute-start(bf16[1,2,32,1024]{3,2,1,0:T(8,128)(2,1)S(1)} %get-tuple-element.29), channel_id=1, source_target_pairs={{0,1},{1,0},{2,3},{3,2},{4,5},{5,4},{6,7},{7,6},{8,9},{9,8},{10,11... | collective-permute-start | bytes 393224 | tf_op jit(solution)/shard_map/ppermute | solution.py:41
  55.4 13.9 %collective-permute-start.5 = (bf16[2,2,32,1024]{3,2,1,0:T(8,128)(2,1)S(1)}, bf16[2,2,32,1024]{3,2,1,0:T(8,128)(2,1)S(1)}, u32[]{:S(2)}, u32[]{:S(2)}) collective-permute-start(bf16[2,2,32,1024]{3,2,1,0:T(8,128)(2,1)S(1)} %get-tuple-element.27), channel_id=1, source_target_pairs={{0,1},{1,0},{2,3},{3,2},{4,5},{5,4},{6,7},{7,6},{8,9},{9,8},{10,11... | collective-permute-start | bytes 786440 | tf_op jit(solution)/shard_map/ppermute | solution.py:41
  60.5 8.9 %collective-permute-start.7 = (bf16[2,32,1024]{2,1,0:T(8,128)(2,1)S(1)}, bf16[2,32,1024]{2,1,0:T(8,128)(2,1)S(1)}, u32[]{:S(2)}, u32[]{:S(2)}) collective-permute-start(bf16[2,32,1024]{2,1,0:T(8,128)(2,1)S(1)} %fusion.5), channel_id=1, source_target_pairs={{0,2},{2,4},{4,6},{6,8},{8,10},{10,12},{12,14},{14,0},{1,3},{3,5},... | collective-permute-start | bytes 393224 | tf_op jit(solution)/shard_map/ppermute | solution.py:41
  63.8 9.6 %collective-permute-start.4 = (bf16[2,2,32,1024]{3,2,1,0:T(8,128)(2,1)S(1)}, bf16[2,2,32,1024]{3,2,1,0:T(8,128)(2,1)S(1)}, u32[]{:S(2)}, u32[]{:S(2)}) collective-permute-start(bf16[2,2,32,1024]{3,2,1,0:T(8,128)(2,1)S(1)} %get-tuple-element.25), channel_id=1, source_target_pairs={{0,1},{1,0},{2,3},{3,2},{4,5},{5,4},{6,7},{7,6},{8,9},{9,8},{10,11... | collective-permute-start | bytes 786440 | tf_op jit(solution)/shard_map/ppermute | solution.py:41
  72.1 6.2 %collective-permute-start.8 = (bf16[2,32,1024]{2,1,0:T(8,128)(2,1)S(1)}, bf16[2,32,1024]{2,1,0:T(8,128)(2,1)S(1)}, u32[]{:S(2)}, u32[]{:S(2)}) collective-permute-start(bf16[2,32,1024]{2,1,0:T(8,128)(2,1)S(1)} %get-tuple-element.43), channel_id=1, source_target_pairs={{0,2},{2,4},{4,6},{6,8},{8,10},{10,12},{12,14},{14,0},{1,3},{3,5},... | collective-permute-start | bytes 393224 | tf_op jit(solution)/shard_map/ppermute | solution.py:41
  72.1 9.7 %collective-permute-start.3 = (bf16[2,2,32,1024]{3,2,1,0:T(8,128)(2,1)S(1)}, bf16[2,2,32,1024]{3,2,1,0:T(8,128)(2,1)S(1)}, u32[]{:S(2)}, u32[]{:S(2)}) collective-permute-start(bf16[2,2,32,1024]{3,2,1,0:T(8,128)(2,1)S(1)} %get-tuple-element.23), channel_id=1, source_target_pairs={{0,1},{1,0},{2,3},{3,2},{4,5},{5,4},{6,7},{7,6},{8,9},{9,8},{10,11... | collective-permute-start | bytes 786440 | tf_op jit(solution)/shard_map/ppermute | solution.py:41
  78.4 6.3 %collective-permute-start.9 = (bf16[2,32,1024]{2,1,0:T(8,128)(2,1)S(1)}, bf16[2,32,1024]{2,1,0:T(8,128)(2,1)S(1)}, u32[]{:S(2)}, u32[]{:S(2)}) collective-permute-start(bf16[2,32,1024]{2,1,0:T(8,128)(2,1)S(1)} %get-tuple-element.41), channel_id=1, source_target_pairs={{0,2},{2,4},{4,6},{6,8},{8,10},{10,12},{12,14},{14,0},{1,3},{3,5},... | collective-permute-start | bytes 393224 | tf_op jit(solution)/shard_map/ppermute | solution.py:41
  80.5 7.8 %collective-permute-start.2 = (bf16[1,2,32,1024]{3,2,1,0:T(8,128)(2,1)S(1)}, bf16[1,2,32,1024]{3,2,1,0:T(8,128)(2,1)S(1)}, u32[]{:S(2)}, u32[]{:S(2)}) collective-permute-start(bf16[1,2,32,1024]{3,2,1,0:T(8,128)(2,1)S(1)} %get-tuple-element.21), channel_id=1, source_target_pairs={{0,1},{1,0},{2,3},{3,2},{4,5},{5,4},{6,7},{7,6},{8,9},{9,8},{10,11... | collective-permute-start | bytes 393224 | tf_op jit(solution)/shard_map/ppermute | solution.py:41
  84.8 7.4 %collective-permute-start.10 = (bf16[2,32,1024]{2,1,0:T(8,128)(2,1)S(1)}, bf16[2,32,1024]{2,1,0:T(8,128)(2,1)S(1)}, u32[]{:S(2)}, u32[]{:S(2)}) collective-permute-start(bf16[2,32,1024]{2,1,0:T(8,128)(2,1)S(1)} %get-tuple-element.39), channel_id=1, source_target_pairs={{0,2},{2,4},{4,6},{6,8},{8,10},{10,12},{12,14},{14,0},{1,3},{3,5},... | collective-permute-start | bytes 393224 | tf_op jit(solution)/shard_map/ppermute | solution.py:41
  92.3 6.9 %collective-permute-start.14 = (bf16[528,128]{1,0:T(8,128)(2,1)S(1)}, bf16[528,128]{1,0:T(8,128)(2,1)S(1)}, u32[]{:S(2)}, u32[]{:S(2)}) collective-permute-start(bf16[528,128]{1,0:T(8,128)(2,1)S(1)} %shard_map.65.refs_0_), channel_id=1, source_target_pairs={{0,2},{2,4},{4,6},{6,8},{8,10},{10,12},{12,14},{14,0},{1,3},{3,5},... | collective-permute-start | bytes 405512 | tf_op jit(solution)/shard_map/ppermute | solution.py:41
  93.0 6.2 %collective-permute-start.15 = (bf16[528,128]{1,0:T(8,128)(2,1)S(1)}, bf16[528,128]{1,0:T(8,128)(2,1)S(1)}, u32[]{:S(2)}, u32[]{:S(2)}) collective-permute-start(bf16[528,128]{1,0:T(8,128)(2,1)S(1)} %shard_map.65.refs_0_), channel_id=1, source_target_pairs={{0,14},{2,0},{4,2},{6,4},{8,6},{10,8},{12,10},{14,12},{1,15},{3,1}... | collective-permute-start | bytes 405512 | tf_op jit(solution)/shard_map/ppermute | solution.py:41
  95.9 8.6 %collective-permute-start.18 = (bf16[528,128]{1,0:T(8,128)(2,1)S(1)}, bf16[528,128]{1,0:T(8,128)(2,1)S(1)}, u32[]{:S(2)}, u32[]{:S(2)}) collective-permute-start(bf16[528,128]{1,0:T(8,128)(2,1)S(1)} %shard_map.65.refs_0_), channel_id=1, source_target_pairs={{0,1},{1,0},{2,3},{3,2},{4,5},{5,4},{6,7},{7,6},{8,9},{9,8},{10,11... | collective-permute-start | bytes 405512 | tf_op jit(solution)/shard_map/ppermute | solution.py:41
  99.2 6.2 %collective-permute-start.16 = (bf16[528,128]{1,0:T(8,128)(2,1)S(1)}, bf16[528,128]{1,0:T(8,128)(2,1)S(1)}, u32[]{:S(2)}, u32[]{:S(2)}) collective-permute-start(bf16[528,128]{1,0:T(8,128)(2,1)S(1)} %collective-permute-done.14.refs_1_), channel_id=1, source_target_pairs={{0,2},{2,4},{4,6},{6,8},{8,10},{10,12},{12,14},{14,0},{1,3},{3,5},... | collective-permute-start | bytes 405512 | tf_op jit(solution)/shard_map/ppermute | solution.py:41
  99.2 6.2 %collective-permute-start.17 = (bf16[528,128]{1,0:T(8,128)(2,1)S(1)}, bf16[528,128]{1,0:T(8,128)(2,1)S(1)}, u32[]{:S(2)}, u32[]{:S(2)}) collective-permute-start(bf16[528,128]{1,0:T(8,128)(2,1)S(1)} %collective-permute-done.15.refs_2_), channel_id=1, source_target_pairs={{0,14},{2,0},{4,2},{6,4},{8,6},{10,8},{12,10},{14,12},{1,15},{3,1}... | collective-permute-start | bytes 405512 | tf_op jit(solution)/shard_map/ppermute | solution.py:41
  102.5 6.4 %collective-permute-start.21 = (bf16[528,128]{1,0:T(8,128)(2,1)S(1)}, bf16[528,128]{1,0:T(8,128)(2,1)S(1)}, u32[]{:S(2)}, u32[]{:S(2)}) collective-permute-start(bf16[528,128]{1,0:T(8,128)(2,1)S(1)} %collective-permute-done.14.refs_1_), channel_id=1, source_target_pairs={{0,1},{1,0},{2,3},{3,2},{4,5},{5,4},{6,7},{7,6},{8,9},{9,8},{10,11... | collective-permute-start | bytes 405512 | tf_op jit(solution)/shard_map/ppermute | solution.py:41
  103.8 7.7 %collective-permute-start.22 = (bf16[528,128]{1,0:T(8,128)(2,1)S(1)}, bf16[528,128]{1,0:T(8,128)(2,1)S(1)}, u32[]{:S(2)}, u32[]{:S(2)}) collective-permute-start(bf16[528,128]{1,0:T(8,128)(2,1)S(1)} %collective-permute-done.15.refs_2_), channel_id=1, source_target_pairs={{0,1},{1,0},{2,3},{3,2},{4,5},{5,4},{6,7},{7,6},{8,9},{9,8},{10,11... | collective-permute-start | bytes 405512 | tf_op jit(solution)/shard_map/ppermute | solution.py:41
  105.5 6.3 %collective-permute-start.19 = (bf16[528,128]{1,0:T(8,128)(2,1)S(1)}, bf16[528,128]{1,0:T(8,128)(2,1)S(1)}, u32[]{:S(2)}, u32[]{:S(2)}) collective-permute-start(bf16[528,128]{1,0:T(8,128)(2,1)S(1)} %get-tuple-element.45), channel_id=1, source_target_pairs={{0,2},{2,4},{4,6},{6,8},{8,10},{10,12},{12,14},{14,0},{1,3},{3,5},... | collective-permute-start | bytes 405512 | tf_op jit(solution)/shard_map/ppermute | solution.py:41
  105.6 9.8 %collective-permute-start.20 = (bf16[528,128]{1,0:T(8,128)(2,1)S(1)}, bf16[528,128]{1,0:T(8,128)(2,1)S(1)}, u32[]{:S(2)}, u32[]{:S(2)}) collective-permute-start(bf16[528,128]{1,0:T(8,128)(2,1)S(1)} %get-tuple-element.44), channel_id=1, source_target_pairs={{0,14},{2,0},{4,2},{6,4},{8,6},{10,8},{12,10},{14,12},{1,15},{3,1}... | collective-permute-start | bytes 405512 | tf_op jit(solution)/shard_map/ppermute | solution.py:41
  111.8 6.3 %collective-permute-start.23 = (bf16[528,128]{1,0:T(8,128)(2,1)S(1)}, bf16[528,128]{1,0:T(8,128)(2,1)S(1)}, u32[]{:S(2)}, u32[]{:S(2)}) collective-permute-start(bf16[528,128]{1,0:T(8,128)(2,1)S(1)} %minimum_add_fusion), channel_id=1, source_target_pairs={{0,2},{2,4},{4,6},{6,8},{8,10},{10,12},{12,14},{14,0},{1,3},{3,5},... | collective-permute-start | bytes 405512 | tf_op jit(solution)/shard_map/ppermute | solution.py:41
  111.9 8.3 %collective-permute-start.24 = (bf16[528,128]{1,0:T(8,128)(2,1)S(1)}, bf16[528,128]{1,0:T(8,128)(2,1)S(1)}, u32[]{:S(2)}, u32[]{:S(2)}) collective-permute-start(bf16[528,128]{1,0:T(8,128)(2,1)S(1)} %collective-permute-done.16.refs_3_), channel_id=1, source_target_pairs={{0,1},{1,0},{2,3},{3,2},{4,5},{5,4},{6,7},{7,6},{8,9},{9,8},{10,11... | collective-permute-start | bytes 405512 | tf_op jit(solution)/shard_map/ppermute | solution.py:41
  113.3 6.9 %collective-permute-start.25 = (bf16[528,128]{1,0:T(8,128)(2,1)S(1)}, bf16[528,128]{1,0:T(8,128)(2,1)S(1)}, u32[]{:S(2)}, u32[]{:S(2)}) collective-permute-start(bf16[528,128]{1,0:T(8,128)(2,1)S(1)} %collective-permute-done.17.refs_4_), channel_id=1, source_target_pairs={{0,1},{1,0},{2,3},{3,2},{4,5},{5,4},{6,7},{7,6},{8,9},{9,8},{10,11... | collective-permute-start | bytes 405512 | tf_op jit(solution)/shard_map/ppermute | solution.py:41
  114.0 6.5 %collective-permute-start.26 = (bf16[528,128]{1,0:T(8,128)(2,1)S(1)}, bf16[528,128]{1,0:T(8,128)(2,1)S(1)}, u32[]{:S(2)}, u32[]{:S(2)}) collective-permute-start(bf16[528,128]{1,0:T(8,128)(2,1)S(1)} %collective-permute-done.19.refs_5_), channel_id=1, source_target_pairs={{0,1},{1,0},{2,3},{3,2},{4,5},{5,4},{6,7},{7,6},{8,9},{9,8},{10,11... | collective-permute-start | bytes 405512 | tf_op jit(solution)/shard_map/ppermute | solution.py:41
  115.4 6.6 %collective-permute-start.27 = (bf16[528,128]{1,0:T(8,128)(2,1)S(1)}, bf16[528,128]{1,0:T(8,128)(2,1)S(1)}, u32[]{:S(2)}, u32[]{:S(2)}) collective-permute-start(bf16[528,128]{1,0:T(8,128)(2,1)S(1)} %collective-permute-done.20.refs_6_), channel_id=1, source_target_pairs={{0,1},{1,0},{2,3},{3,2},{4,5},{5,4},{6,7},{7,6},{8,9},{9,8},{10,11... | collective-permute-start | bytes 405512 | tf_op jit(solution)/shard_map/ppermute | solution.py:41
  118.1 5.3 %collective-permute-start.28 = (bf16[528,128]{1,0:T(8,128)(2,1)S(1)}, bf16[528,128]{1,0:T(8,128)(2,1)S(1)}, u32[]{:S(2)}, u32[]{:S(2)}) collective-permute-start(bf16[528,128]{1,0:T(8,128)(2,1)S(1)} %collective-permute-done.23.refs_7_), channel_id=1, source_target_pairs={{0,1},{1,0},{2,3},{3,2},{4,5},{5,4},{6,7},{7,6},{8,9},{9,8},{10,11... | collective-permute-start | bytes 405512 | tf_op jit(solution)/shard_map/ppermute | solution.py:41
  (9 other events, 46.1 us)
